TPU v7x, 128 devices: a whole 4x4x4 slice. The times are simulated.
128 devices in a mesh: dp: 16 (over y, z), tp: 8 (over x, core).
Axes of the slice: x: 4, y: 4, z: 4, core: 2. Of those that a mesh axis runs over, the one named last changes fastest.
Arguments:
- residual_in: bfloat16 [1024, 7168], P(('dp', 'tp')), may hold values from -6 to 6
- query_latent: bfloat16 [1024, 64, 576], P(('dp', 'tp')), may hold values from -48 to 48
- latent_cache: bfloat16 [1024, 384, 576], P(('dp', 'tp')), may hold values from -6 to 6
- new_latent: bfloat16 [1024, 576], P(('dp', 'tp')), may hold values from -6 to 6
- context_lengths: int32 [1024], P(('dp', 'tp')), may hold values from 1 to 384, 196608 in all
- value_up: bfloat16 [64, 512, 128], P('tp'), may hold values from -0.25 to 0.25
- out_proj: bfloat16 [8192, 7168], P('tp'), may hold values from -0.0625 to 0.0625
- norm_gain: bfloat16 [7168], replicated, may hold values from 0.099609375 to 1.8984375
- expert_ids: int32 [1024, 8], P(('dp', 'tp')), may hold values from 0 to 15, all different within a row
- route_scores: float32 [1024, 8], P(('dp', 'tp')), may hold values from 0.2 to 1
- expert_slots: int32 [16], replicated, may hold values from 0 to 15, each once
- expert_gate_up: bfloat16 [16, 2, 7168, 1024], P('dp', None, None, 'tp'), may hold values from -0.0625 to 0.0625
- expert_down: bfloat16 [16, 1024, 7168], P('dp', 'tp'), may hold values from -0.1875 to 0.1875
Outputs:
- attention_out: bfloat16 [1024, 7168], P(('dp', 'tp'))
- layer_output: bfloat16 [1024, 7168], P(('dp', 'tp'))
All inputs are finite; a program needn't handle non-finite values. No bound on the sum of `context_lengths` on one device may be relied on, other than what follows from the above.
Results may differ from a plain program's by a relative error of at most 0.02.
Values may be sent and summed in bfloat16 or wider, within the bound.
No kernel may reach another device: no remote copies, remote signals or barrier semaphores. Data moves between devices by JAX's collectives and lax.ppermute only.
A program may use at most 128 MiB of HBM per device.

v0:
```python
import jax
import jax.numpy as jnp
from jax import lax
from jax.sharding import PartitionSpec as P

score_scale = 192.0 ** (-0.5)
route_scale = 2.5
norm_eps = 1e-06


def attend(query_rows, cache_rows, fresh_key, context_lengths, latent_width):
    scores = (
        jnp.einsum("rhc,rtc->rht", query_rows, cache_rows, preferred_element_type=jnp.float32)
        * score_scale
    )
    own_score = (
        jnp.einsum("rhc,rc->rh", query_rows, fresh_key, preferred_element_type=jnp.float32)
        * score_scale
    )
    positions = lax.broadcasted_iota(jnp.int32, scores.shape, 2)
    scores = jnp.where(positions < context_lengths[:, None, None], scores, -jnp.inf)
    row_max = jnp.maximum(jnp.max(scores, axis=2), own_score)
    cache_weights = jnp.exp(scores - row_max[:, :, None])
    own_weight = jnp.exp(own_score - row_max)
    denominator = jnp.sum(cache_weights, axis=2) + own_weight
    cache_weights = (cache_weights / denominator[:, :, None]).astype(jnp.bfloat16)
    own_weight = (own_weight / denominator).astype(jnp.bfloat16)
    own_weight = lax.optimization_barrier(own_weight).astype(jnp.float32)
    result = jnp.einsum(
        "rht,rtl->rhl",
        cache_weights,
        cache_rows[:, :, :latent_width],
        preferred_element_type=jnp.float32,
    )
    result = result + own_weight[:, :, None] * fresh_key[:, None, :latent_width].astype(jnp.float32)
    return result.astype(jnp.bfloat16)


def combine_table(expert_ids, gates, expert_slots):
    slot_count = expert_slots.shape[0]
    labels = lax.broadcasted_iota(jnp.int32, (1, 1, slot_count), 2)
    slot_of = jnp.sum(
        jnp.where(expert_ids[:, :, None] == labels, expert_slots[None, None, :], 0), axis=2
    )
    slot_hits = slot_of[:, :, None] == labels
    weight_table = jnp.sum(jnp.where(slot_hits, gates[:, :, None].astype(jnp.float32), 0.0), axis=1)
    return weight_table.astype(jnp.bfloat16)


def expert_partial(arrived, expert_gate_up, expert_down):
    gate_part = jnp.einsum(
        "gsld,ldf->gslf", arrived, expert_gate_up[:, 0], preferred_element_type=jnp.float32
    )
    up_part = jnp.einsum(
        "gsld,ldf->gslf", arrived, expert_gate_up[:, 1], preferred_element_type=jnp.float32
    )
    activated = (jax.nn.silu(gate_part) * up_part).astype(jnp.bfloat16)
    return jnp.einsum("gslf,lfd->gsld", activated, expert_down, preferred_element_type=jnp.float32)


def per_device(
    residual_in,
    query_latent,
    latent_cache,
    new_latent,
    context_lengths,
    value_up,
    out_proj,
    norm_gain,
    expert_ids,
    route_scores,
    expert_slots,
    expert_gate_up,
    expert_down,
):
    model_width = residual_in.shape[1]
    latent_width = value_up.shape[1]
    owners = lax.axis_size("dp")
    local_experts = expert_gate_up.shape[0]
    latent_out = attend(query_latent, latent_cache, new_latent, context_lengths, latent_width)
    exchanged = lax.all_to_all(latent_out, "tp", split_axis=1, concat_axis=0, tiled=True)
    values = jnp.einsum(
        "thl,hlv->thv", exchanged, value_up, preferred_element_type=jnp.float32
    ).astype(jnp.bfloat16)
    values = values.reshape(values.shape[0], values.shape[1] * values.shape[2])
    attention_sum = lax.psum_scatter(
        jnp.dot(values, out_proj, preferred_element_type=jnp.float32).astype(jnp.bfloat16),
        "tp",
        scatter_dimension=0,
        tiled=True,
    )
    residual_mid = (residual_in.astype(jnp.float32) + attention_sum.astype(jnp.float32)).astype(
        jnp.bfloat16
    )
    residual_f32 = residual_mid.astype(jnp.float32)
    scaling = lax.rsqrt(jnp.mean(residual_f32 * residual_f32, axis=1, keepdims=True) + norm_eps)
    normed = (residual_f32 * scaling * norm_gain.astype(jnp.float32)[None, :]).astype(jnp.bfloat16)
    gates = (route_scale * route_scores / jnp.sum(route_scores, axis=1, keepdims=True)).astype(
        jnp.bfloat16
    )
    weight_table = combine_table(expert_ids, gates, expert_slots)
    zero_value = jnp.zeros((), jnp.bfloat16)
    group_rows, group_table = (
        lax.all_gather(normed, "tp", axis=0, tiled=True),
        lax.all_gather(weight_table, "tp", axis=0, tiled=True),
    )
    group_count = group_rows.shape[0]
    buffer = jnp.where(group_table[:, :, None] != 0, group_rows[:, None, :], zero_value)
    buffer = buffer.reshape(group_count, owners, local_experts, model_width)
    partial_value = expert_partial(
        lax.all_to_all(buffer, "dp", split_axis=1, concat_axis=1, tiled=True),
        expert_gate_up,
        expert_down,
    ).astype(jnp.bfloat16)
    returned = lax.all_to_all(partial_value, "dp", split_axis=1, concat_axis=1, tiled=True)
    returned = returned.reshape(group_count, owners * local_experts, model_width)
    weighted = jnp.sum(
        returned.astype(jnp.float32) * group_table[:, :, None].astype(jnp.float32), axis=1
    )
    expert_sum = lax.psum_scatter(
        weighted.astype(jnp.bfloat16), "tp", scatter_dimension=0, tiled=True
    ).astype(jnp.float32)
    layer_output = (residual_mid.astype(jnp.float32) + expert_sum).astype(jnp.bfloat16)
    return (attention_sum, layer_output)


def solution(mesh):
    placed = (
        P(("dp", "tp"), None),
        P(("dp", "tp"), None, None),
        P(("dp", "tp"), None, None),
        P(("dp", "tp"), None),
        P(("dp", "tp")),
        P("tp", None, None),
        P("tp", None),
        P(),
        P(("dp", "tp"), None),
        P(("dp", "tp"), None),
        P(),
        P("dp", None, None, "tp"),
        P("dp", "tp", None),
    )
    return jax.shard_map(
        per_device,
        mesh=mesh,
        in_specs=placed,
        out_specs=(P(("dp", "tp"), None), P(("dp", "tp"), None)),
        check_vma=False,
    )
```

profile of v0, /device:TPU:1, one launch (start us, length us, event | category | flops | bytes accessed | tf_op | source)
XLA Modules:
  0.0 631.5 jit_solution(15721573368258930166)
XLA Ops:
  7.2 0.0 copy-start
  7.2 0.0 copy-start.3
  7.2 0.0 reduce-scatter.3.cloned.1.call-start
  7.2 0.0 copy-start.2
  7.2 0.9 slice_convert_fusion
  8.1 1.9 fusion.68
  10.0 3.5 fusion.73
  13.5 0.3 fusion.51
  13.9 0.0 copy-start.8
  13.9 0.0 copy-start.7
  13.9 0.0 copy-start.9
  13.9 0.0 copy-start.10
  13.9 0.0 copy-start.4
  13.9 3.1 fusion.17
  17.0 0.3 copy.43
  17.3 15.0 %all_to_all.28 = bf16[8,64,512]{2,0,1:T(8,128)(2,1)S(1)} all-to-all(bf16[8,64,512]{2,0,1:T(8,128)(2,1)S(1)} %copy.43), channel_id=1, replica_groups=mesh['dp'=16,'tp'=8] {'tp'}, dimensions={1} | all-to-all | bytes 1048576 | tf_op jit(solution)/shard_map/all_to_all | solution.py:81
  32.3 0.0 copy-done.3
  32.3 0.3 fusion.50
  32.6 3.6 convolution_convert_fusion
  36.2 0.0 reduce-scatter.3.cloned.1.call-update
  36.2 0.0 copy-done.8
  36.2 0.1 reduce_sum.56
  36.4 0.3 select_reduce_fusion.1
  36.7 0.1 fusion.70
  36.7 0.1 select_reduce_fusion
  36.8 12.1 %all_gather.6 = bf16[64,16]{1,0:T(8,128)(2,1)S(1)} all-gather(bf16[8,16]{1,0:T(8,128)(2,1)S(1)} %select_reduce_fusion), channel_id=1, replica_groups=mesh['dp'=16,'tp'=8] {'tp'}, dimensions={0}, use_global_device_ids=true | all-gather | bytes 2304 | tf_op jit(solution)/shard_map/all_gather | solution.py:105
  48.9 0.1 copy.46
  49.0 17.0 %reduce-scatter.3.cloned.1.call-done = bf16[8,7168]{1,0:T(8,128)(2,1)} async-done(((bf16[64,7168]{1,0:T(8,128)(2,1)}), bf16[8,7168]{1,0:T(8,128)(2,1)}) %reduce-scatter.3.cloned.1.call-update) | async-done | bytes 114704 | tf_op jit(solution)/shard_map/reduce_scatter | solution.py:86
  66.0 1.1 fusion.62
  67.1 1.0 fusion.64
  68.1 16.9 %all_gather.7 = bf16[64,7168]{1,0:T(8,128)(2,1)S(1)} all-gather(bf16[8,7168]{1,0:T(8,128)(2,1)S(1)} %fusion.64), channel_id=1, replica_groups=mesh['dp'=16,'tp'=8] {'tp'}, dimensions={0}, use_global_device_ids=true | all-gather | bytes 1032192 | tf_op jit(solution)/shard_map/all_gather | solution.py:104
  85.0 6.6 %broadcast_select_fusion = bf16[64,16,1,7168]{3,0,2,1:T(8,128)(2,1)} fusion(pred[64,16]{0,1:T(8,128)(4,1)S(1)} %broadcast_compare_fusion, bf16[64,7168]{1,0:T(8,128)(2,1)S(1)} %all_gather.7), kind=kLoop, calls=%fused_computation.7 | loop fusion | flops 7340032 | bytes 15598592 | tf_op jit(solution)/shard_map/jit(_where)/select_n | solution.py:108
  91.6 168.8 %all_to_all.29 = bf16[64,16,1,7168]{3,0,2,1:T(8,128)(2,1)S(1)} all-to-all(bf16[64,16,1,7168]{3,0,2,1:T(8,128)(2,1)} %broadcast_select_fusion), channel_id=1, replica_groups=mesh['dp'=16,'tp'=8] {'dp'}, dimensions={1} | all-to-all | bytes 29360128 | tf_op jit(solution)/shard_map/all_to_all | solution.py:111
  260.4 5.2 copy-done.1
  265.6 0.0 copy-done.6
  265.6 7.8 %fusion.21 = f32[64,16,1,128]{3,1,0,2:T(8,128)S(1)} fusion(bf16[1,2,7168,128]{3,2,1,0:T(8,128)(2,1)S(1)} %copy-done.6, bf16[64,16,1,7168]{3,0,2,1:T(8,128)(2,1)S(1)} %all_to_all.29), kind=kOutput, calls=%fused_computation.22 | convolution fusion | flops 1879048192 | bytes 17039360 | tf_op jit(solution)/shard_map/gsld,ldf->gslf/dot_general | solution.py:51
  273.4 0.0 copy-done
  273.4 26.1 %convert_bitcast_fusion = bf16[64,16,1,7168]{3,1,0,2:T(8,128)(2,1)} fusion(bf16[1,128,7168]{2,1,0:T(8,128)(2,1)S(1)} %copy-done, bf16[1,2,7168,128]{3,2,1,0:T(8,128)(2,1)} %param.24, bf16[64,16,1,7168]{3,0,2,1:T(8,128)(2,1)} %copy-done.1, f32[64,16,1,128]{3,1,0,2:T(8,128)S(1)} %fusion.21), kind=kOutput, calls=%fused_computation.6 | convolution fusion | flops 3766222848 | bytes 33554432 | tf_op jit(solution)/shard_map/gslf,lfd->gsld/dot_general | solution.py:58
  299.5 16.7 %copy.48 = bf16[64,16,1,7168]{3,0,2,1:T(8,128)(2,1)} copy(bf16[64,16,1,7168]{3,1,0,2:T(8,128)(2,1)} %convert_bitcast_fusion) | data formatting | bytes 29360128 | tf_op jit(solution)/shard_map/convert_element_type | solution.py:114
  316.2 5.0 all-to-all-start.2
  321.3 0.0 copy-start.5
  321.3 0.3 reduce-scatter.5.cloned.1.call-start
  321.6 255.5 %all-to-all-done.2 = bf16[64,16,1,7168]{3,0,2,1:T(8,128)(2,1)} async-done(((bf16[64,16,1,7168]{3,0,2,1:T(8,128)(2,1)}), bf16[64,16,1,7168]{3,0,2,1:T(8,128)(2,1)}, u32[]{:S(2)}, u32[]{:S(2)}) %all-to-all-start.2) | async-done | bytes 14680096 | tf_op jit(solution)/shard_map/all_to_all | solution.py:115
  577.1 10.5 %fusion = bf16[64,7168]{1,0:T(8,128)(2,1)} fusion(bf16[64,16,1,7168]{3,0,2,1:T(8,128)(2,1)} %all-to-all-done.2, f32[64,16]{0,1:T(8,128)S(1)} %convert_element_type.112), kind=kLoop, calls=%fused_computation.1 | loop fusion | flops 21561344 | bytes 15601664 | tf_op jit(solution)/shard_map/reduce_sum | solution.py:117
  587.6 0.0 reduce-scatter.5.cloned.1.call-update
  587.6 35.5 %reduce-scatter.5.cloned.1.call-done = bf16[8,7168]{1,0:T(8,128)(2,1)} async-done(((bf16[64,7168]{1,0:T(8,128)(2,1)}), bf16[8,7168]{1,0:T(8,128)(2,1)}) %reduce-scatter.5.cloned.1.call-update) | async-done | bytes 114704 | tf_op jit(solution)/shard_map/reduce_scatter | solution.py:120
  623.1 0.0 copy-done.5
  623.1 1.6 fusion.65
  (14 shorter events, 0.1 us)
Async XLA Ops:
  7.2 266.3 %copy-start = (bf16[1,128,7168]{2,1,0:T(8,128)(2,1)S(1)}, bf16[1,128,7168]{2,1,0:T(8,128)(2,1)}, u32[]{:S(2)}) copy-start(bf16[1,128,7168]{2,1,0:T(8,128)(2,1)} %param.25) | copy-start | bytes 5505028
  7.2 25.1 %copy-start.3 = (bf16[8,512,128]{2,1,0:T(8,128)(2,1)S(1)}, bf16[8,512,128]{2,1,0:T(8,128)(2,1)}, u32[]{:S(2)}) copy-start(bf16[8,512,128]{2,1,0:T(8,128)(2,1)} %param.18) | copy-start | bytes 3145732
  7.2 58.8 %reduce-scatter.3.cloned.1.call-start = ((), (), s32[]{:S(2)}) async-start(), calls=%async_computation.5 | async-start | bytes 1032192 | tf_op jit(solution)/shard_map/reduce_scatter | solution.py:86
  7.2 25.4 %copy-start.2 = (bf16[1024,7168]{1,0:T(8,128)(2,1)S(1)}, bf16[1024,7168]{1,0:T(8,128)(2,1)}, u32[]{:S(2)}) copy-start(bf16[1024,7168]{1,0:T(8,128)(2,1)} %param.19) | copy-start | bytes 44040196
  13.9 22.3 %copy-start.8 = (bf16[7168]{0:T(1024)(128)(2,1)S(1)}, bf16[7168]{0:T(1024)(128)(2,1)}, u32[]{:S(2)}) copy-start(bf16[7168]{0:T(1024)(128)(2,1)} %param.20) | copy-start | bytes 43012
  13.9 22.4 %copy-start.7 = (f32[8,8]{1,0:T(8,128)S(1)}, f32[8,8]{1,0:T(8,128)}, u32[]{:S(2)}) copy-start(f32[8,8]{1,0:T(8,128)} %param.22) | copy-start | bytes 772
  13.9 22.5 %copy-start.9 = (s32[8,8]{1,0:T(8,128)S(1)}, s32[8,8]{1,0:T(8,128)}, u32[]{:S(2)}) copy-start(s32[8,8]{1,0:T(8,128)} %param.21) | copy-start | bytes 772
  13.9 22.5 %copy-start.10 = (s32[16]{0:T(128)S(1)}, s32[16]{0:T(128)}, u32[]{:S(2)}) copy-start(s32[16]{0:T(128)} %param.23) | copy-start | bytes 196
  13.9 52.1 %copy-start.4 = (bf16[8,7168]{1,0:T(8,128)(2,1)S(1)}, bf16[8,7168]{1,0:T(8,128)(2,1)}, u32[]{:S(2)}) copy-start(bf16[8,7168]{1,0:T(8,128)(2,1)} %param.13) | copy-start | bytes 344068
  91.6 174.0 %copy-start.6 = (bf16[1,2,7168,128]{3,2,1,0:T(8,128)(2,1)S(1)}, bf16[1,2,7168,128]{3,2,1,0:T(8,128)(2,1)}, u32[]{:S(2)}) copy-start(bf16[1,2,7168,128]{3,2,1,0:T(8,128)(2,1)} %param.24) | copy-start | bytes 11010052
  260.4 5.2 copy-start.1
  316.2 260.9 %all-to-all-start.2 = ((bf16[64,16,1,7168]{3,0,2,1:T(8,128)(2,1)}), bf16[64,16,1,7168]{3,0,2,1:T(8,128)(2,1)}, u32[]{:S(2)}, u32[]{:S(2)}) async-start(bf16[64,16,1,7168]{3,0,2,1:T(8,128)(2,1)} %copy.48), calls=%async_computation.3 | async-start | bytes 29360128 | tf_op jit(solution)/shard_map/all_to_all | solution.py:115
  321.3 301.8 %copy-start.5 = (bf16[8,7168]{1,0:T(8,128)(2,1)S(1)}, bf16[8,7168]{1,0:T(8,128)(2,1)}, u32[]{:S(2)}) copy-start(bf16[8,7168]{1,0:T(8,128)(2,1)} %reduce-scatter.3.cloned.1.call-done) | copy-start | bytes 344068
  321.3 301.8 %reduce-scatter.5.cloned.1.call-start = ((), (), s32[]{:S(2)}) async-start(), calls=%async_computation.6 | async-start | bytes 1032192 | tf_op jit(solution)/shard_map/reduce_scatter | solution.py:120
Sparse Core Ops, SparseCore 0:
  36.3 29.6 reduce-scatter.2
  587.7 35.3 reduce-scatter.4
where the time goes:
time: 634 us; the launch traced here: 632 us
  waiting for transfers between devices  308 us (49%)
  blocking collectives  213 us (34%)
  matrix products  46.3 us (7%)
  other arithmetic  22.5 us (4%)
  local copies, waits for them, and re-layouts  22.3 us (4%)
  between operations  14.2 us (2%)
    all_to_all x1, waiting for transfers between devices, per_device(): lax.all_to_all(partial_value, 'dp', split_axis=1, concat_axis=1, tiled=True)  255 us
    all_to_all x1, blocking collectives, per_device(): lax.all_to_all(buffer, 'dp', split_axis=1, concat_axis=1, tiled=True)  169 us
    reduce_scatter x1, waiting for transfers between devices, per_device(): lax.psum_scatter(weighted.astype(jnp.bfloat16), 'tp', scatter_dimension=0...  35.5 us
    dot_general x1, matrix products, expert_partial(): jnp.einsum('gslf,lfd->gsld', activated, expert_down, preferred_element_ty...  26.1 us
    reduce_scatter x1, waiting for transfers between devices, per_device(): lax.psum_scatter(jnp.dot(values, out_proj, preferred_element_type=jnp.flo...  17 us
    all_gather x1, blocking collectives, per_device(): lax.all_gather(normed, 'tp', axis=0, tiled=True)  16.9 us
    convert_element_type x1, local copies, waits for them, and re-layouts, per_device(): partial_value = expert_partial(lax.all_to_all(buffer, 'dp', split_axis=1,...  16.7 us
    all_to_all x1, blocking collectives, per_device(): lax.all_to_all(latent_out, 'tp', split_axis=1, concat_axis=0, tiled=True)  15 us
  transfers between devices with their start and end apart: 3, of which 3 were waited for; matrix products, arithmetic and copies ran while one was open for 0% of the time, Pallas kernels for 0%

commit v1 on v0

v1 whole, which is shorter than its diff:
```python
import jax
import jax.numpy as jnp
from jax import lax
from jax.sharding import Mesh, PartitionSpec as P

score_scale = 192.0 ** (-0.5)
route_scale = 2.5
norm_eps = 1e-06
f32 = jnp.float32
bf16 = jnp.bfloat16


def attend(query_rows, cache_rows, fresh_key, context_lengths, latent_width):
    scores = (
        jnp.einsum("rhc,rtc->rht", query_rows, cache_rows, preferred_element_type=jnp.float32)
        * score_scale
    )
    own_score = (
        jnp.einsum("rhc,rc->rh", query_rows, fresh_key, preferred_element_type=jnp.float32)
        * score_scale
    )
    positions = lax.broadcasted_iota(jnp.int32, scores.shape, 2)
    scores = jnp.where(positions < context_lengths[:, None, None], scores, -jnp.inf)
    row_max = jnp.maximum(jnp.max(scores, axis=2), own_score)
    cache_weights = jnp.exp(scores - row_max[:, :, None])
    own_weight = jnp.exp(own_score - row_max)
    denominator = jnp.sum(cache_weights, axis=2) + own_weight
    cache_weights = (cache_weights / denominator[:, :, None]).astype(jnp.bfloat16)
    own_weight = (own_weight / denominator).astype(jnp.bfloat16)
    own_weight = lax.optimization_barrier(own_weight).astype(jnp.float32)
    result = jnp.einsum(
        "rht,rtl->rhl",
        cache_weights,
        cache_rows[:, :, :latent_width],
        preferred_element_type=jnp.float32,
    )
    result = result + own_weight[:, :, None] * fresh_key[:, None, :latent_width].astype(jnp.float32)
    return result.astype(jnp.bfloat16)


def combine_table(expert_ids, gates, expert_slots):
    slot_count = expert_slots.shape[0]
    labels = lax.broadcasted_iota(jnp.int32, (1, 1, slot_count), 2)
    slot_of = jnp.sum(
        jnp.where(expert_ids[:, :, None] == labels, expert_slots[None, None, :], 0), axis=2
    )
    slot_hits = slot_of[:, :, None] == labels
    weight_table = jnp.sum(jnp.where(slot_hits, gates[:, :, None].astype(jnp.float32), 0.0), axis=1)
    return weight_table.astype(jnp.bfloat16)


def shift(value, axis, distance):
    count = lax.axis_size(axis)
    return lax.ppermute(value, axis, [((i + distance) % count, i) for i in range(count)])


def swap(value):
    return lax.ppermute(value, "core", [(0, 1), (1, 0)])


def total(*terms):
    return sum(term.astype(f32) for term in terms)


def gather_near(block, axis):
    return jnp.concatenate(
        [block, shift(block, axis, 1), shift(block, axis, 2), shift(block, axis, -1)], axis=0
    )


def gather_far(block, axis):
    half = block.shape[0] // 2
    right, left = shift(block, axis, 1), shift(block, axis, -1)
    low, high = shift(right[:half], axis, 1), shift(left[half:], axis, -1)
    return [block, right, jnp.concatenate([low, high], axis=0), left]


def scatter_far(own, right, opposite, left, axis):
    half = own.shape[0] // 2
    low, high = shift(opposite[:half], axis, -1), shift(opposite[half:], axis, 1)
    right = jnp.concatenate([total(right[:half], low).astype(bf16), right[half:]], axis=0)
    left = jnp.concatenate([left[:half], total(left[half:], high).astype(bf16)], axis=0)
    return total(own, shift(right, axis, -1), shift(left, axis, 1)).astype(bf16)


def scatter_near(value, axis):
    return total(
        value[0], shift(value[1], axis, -1), shift(value[2], axis, 2), shift(value[3], axis, 1)
    ).astype(bf16)


def per_device(
    residual_in,
    query_latent,
    latent_cache,
    new_latent,
    context_lengths,
    value_up,
    out_proj,
    norm_gain,
    expert_ids,
    route_scores,
    expert_slots,
    expert_gate_up,
    expert_down,
):
    rows, model_width = residual_in.shape
    latent_width = value_up.shape[1]
    half = model_width // 2
    lanes = 128
    core = lax.axis_index("core")
    x_at = lax.axis_index("x")
    expert_at = lax.axis_index("y") * 4 + lax.axis_index("z")

    def mine(value, axis):
        return lax.dynamic_slice_in_dim(value, core * half, half, axis=axis)

    def others(value, axis):
        return lax.dynamic_slice_in_dim(value, (1 - core) * half, half, axis=axis)

    def whole(own, got):
        return jnp.where(
            core == 0,
            jnp.concatenate([own, got], axis=1),
            jnp.concatenate([got, own], axis=1),
        )

    gates = (route_scale * route_scores / jnp.sum(route_scores, axis=1, keepdims=True)).astype(bf16)
    table = combine_table(expert_ids, gates, expert_slots)
    slots = table.shape[1]

    latent_out = attend(query_latent, latent_cache, new_latent, context_lengths, latent_width)
    exchanged = lax.all_to_all(latent_out, ("x", "core"), split_axis=1, concat_axis=0, tiled=True)

    gate_up = expert_gate_up[0]
    down = expert_down[0]
    gate_up_own = mine(gate_up, 1)
    gate_up_got = swap(others(gate_up, 1))
    weight_in = jnp.concatenate(
        [gate_up_own[0], gate_up_own[1], gate_up_got[0], gate_up_got[1]], axis=1
    )
    weight_in = jnp.pad(weight_in, ((0, lanes), (0, 0)))
    weight_out = jnp.concatenate([mine(down, 1), swap(others(down, 1))], axis=0)

    residual_own, residual_got = mine(residual_in, 1), swap(others(residual_in, 1))
    residual_chip = jnp.where(
        core == 0,
        jnp.stack([residual_own, residual_got]),
        jnp.stack([residual_got, residual_own]),
    )
    group_table = lax.all_gather(table, ("x", "core"), axis=0, tiled=True)
    group_table = jnp.pad(group_table, ((0, 0), (0, lanes - slots))).reshape(4, 2, rows, lanes)

    values = jnp.einsum(
        "thl,hlv->thv", exchanged, value_up, preferred_element_type=f32
    ).astype(bf16)
    values = values.reshape(values.shape[0], values.shape[1] * values.shape[2])
    projected = jnp.dot(values, out_proj, preferred_element_type=f32)
    chip_sum = mine(projected, 1) + swap(others(projected, 1).astype(bf16)).astype(f32)
    chip_sum = chip_sum.reshape(4, 2, rows, half)
    own_place = (lax.broadcasted_iota(jnp.int32, (4, 1, 1), 0) == x_at)
    gain = mine(norm_gain, 0).astype(f32)

    attention_parts, gathered = [], []
    for part in range(2):
        part_sum = chip_sum[:, part]
        sent = (part_sum + jnp.where(own_place, residual_chip[part][None].astype(f32), 0.0)).astype(bf16)
        arrived = [shift(sent, "x", d) for d in (1, 2, -1)]
        own_rows = lambda v: lax.dynamic_index_in_dim(v, x_at, axis=0, keepdims=False)
        attention_parts.append(
            total(own_rows(part_sum), *[own_rows(v) for v in arrived]).astype(bf16)
        )
        residual_f32 = total(sent, *arrived).astype(bf16).astype(f32)
        squares = jnp.sum(residual_f32 * residual_f32, axis=2, keepdims=True)
        squares = squares + swap(squares)
        scaling = lax.rsqrt(squares / model_width + norm_eps)
        normed = (residual_f32 * scaling * gain[None, None, :]).astype(bf16)
        payload = jnp.concatenate([normed, group_table[:, part]], axis=2)
        gathered.append(payload.reshape(4 * rows, half + lanes))

    axes = (("y", "z"), ("z", "y"))
    near = [gather_near(gathered[p], axes[p][0]) for p in range(2)]
    far = [gather_far(near[p], axes[p][1]) for p in range(2)]

    back = []
    for part in range(2):
        blocks = far[part]
        products = [jnp.dot(b, weight_in, preferred_element_type=f32) for b in blocks]
        hidden = weight_in.shape[1] // 2
        got = swap(jnp.concatenate([p[:, hidden:].astype(bf16) for p in products], axis=0))
        product = jnp.concatenate([p[:, :hidden] for p in products], axis=0) + got.astype(f32)
        units = hidden // 2
        activated = (jax.nn.silu(product[:, :units]) * product[:, units:]).astype(bf16)
        activated = jnp.concatenate([activated, swap(activated)], axis=1)
        outs = []
        n = blocks[0].shape[0]
        for i, b in enumerate(blocks):
            weights = jnp.sum(
                jnp.where(
                    lax.broadcasted_iota(jnp.int32, (1, lanes), 1) == expert_at,
                    b[:, half:].astype(f32),
                    0.0,
                ),
                axis=1,
                keepdims=True,
            )
            out = jnp.dot(activated[i * n : (i + 1) * n], weight_out, preferred_element_type=f32)
            outs.append((out * weights).astype(bf16))
        back.append(outs)

    summed = [scatter_far(*back[p], axes[p][1]) for p in range(2)]
    summed = [scatter_near(summed[p].reshape(4, 4 * rows, half), axes[p][0]) for p in range(2)]
    to_x = jnp.stack([s.reshape(4, rows, half) for s in summed], axis=1)
    from_x = lax.all_to_all(to_x, "x", split_axis=0, concat_axis=0, tiled=True)
    chip_out = jnp.sum(from_x.astype(f32), axis=0)

    def to_tokens(own, other):
        return whole(own, swap(other))

    attention_out = to_tokens(
        jnp.where(core == 0, attention_parts[0], attention_parts[1]),
        jnp.where(core == 0, attention_parts[1], attention_parts[0]),
    )
    expert_sum = to_tokens(
        jnp.where(core == 0, chip_out[0], chip_out[1]).astype(bf16),
        jnp.where(core == 0, chip_out[1], chip_out[0]).astype(bf16),
    )
    residual_mid = total(residual_in, attention_out).astype(bf16)
    layer_output = total(residual_mid, expert_sum).astype(bf16)
    return (attention_out, layer_output)


def solution(mesh):
    torus = Mesh(mesh.devices.reshape(4, 4, 4, 2), ("y", "z", "x", "core"))
    dp, tp = ("y", "z"), ("x", "core")
    both = dp + tp
    placed = (
        P(both, None),
        P(both, None, None),
        P(both, None, None),
        P(both, None),
        P(both),
        P(tp, None, None),
        P(tp, None),
        P(),
        P(both, None),
        P(both, None),
        P(),
        P(dp, None, None, tp),
        P(dp, tp, None),
    )
    return jax.shard_map(
        per_device,
        mesh=torus,
        in_specs=placed,
        out_specs=(P(both, None), P(both, None)),
        check_vma=False,
    )
```

time: 634 us -> 235 us (0.37)
  waiting for transfers between devices: 308 us -> 78.3 us
  blocking collectives: 213 us -> 12.2 us
  starting transfers between devices: 5.37 us -> 88.2 us
  matrix products: 46.3 us -> 32.4 us
  between operations: 14.2 us -> 1.58 us
  other arithmetic: 22.5 us -> 10.1 us
  local copies, waits for them, and re-layouts: 22.3 us -> 11.8 us
    all_to_all x1 -> x2, waiting for transfers between devices: 255 us -> 0.01 us  [the longest x1 0.01 us: per_device(): lax.all_to_all(latent_out, ('x', 'core'), split_axis=1, concat_axis=0, ti...]
    all_to_all x2 -> x0, blocking collectives: 184 us -> none  [the longest x1 169 us: per_device(): lax.all_to_all(buffer, 'dp', split_axis=1, concat_axis=1, tiled=True)]
    ppermute x0 -> x46, starting transfers between devices: none -> 80.2 us  [the longest x34 45.3 us: shift(): lax.ppermute(value, axis, [((i + distance) % count, i) for i in range(cou...]
    ppermute x0 -> x46, waiting for transfers between devices: none -> 78.3 us  [the longest x34 74.3 us: shift(): lax.ppermute(value, axis, [((i + distance) % count, i) for i in range(cou...]
    reduce_scatter x2 -> x0, waiting for transfers between devices: 52.5 us -> none  [the longest x1 35.5 us: per_device(): lax.psum_scatter(weighted.astype(jnp.bfloat16), 'tp', scatter_dimension=0...]
    all_gather x2 -> x1, blocking collectives: 28.9 us -> 12.2 us  [per_device(): group_table = lax.all_gather(table, ('x', 'core'), axis=0, tiled=True)]
    convert_element_type x1, local copies, waits for them, and re-layouts: 16.7 us -> 0.06 us  [per_device(): others(projected, 1).astype(bf16)]
    dot_general x4 -> x18, matrix products: 37.8 us -> 26.7 us  [the longest x8 13.2 us: per_device(): jnp.dot(activated[i * n:(i + 1) * n], weight_out, preferred_element_type=...]
  transfers between devices with their start and end apart: 3 -> 48, of which waited for: 3 -> 26; matrix products, arithmetic and copies ran while one was open for 0% -> 21% of each run, Pallas kernels for 0% -> 0%
where the time goes in v1:
time: 235 us
  starting transfers between devices  88.2 us (38%)
  waiting for transfers between devices  78.3 us (33%)
  matrix products  32.4 us (14%)
  blocking collectives  12.2 us (5%)
  local copies, waits for them, and re-layouts  11.8 us (5%)
  other arithmetic  10.1 us (4%)
    ppermute x34, waiting for transfers between devices, shift(): lax.ppermute(value, axis, [((i + distance) % count, i) for i in range(cou...  74.3 us
    ppermute x34, starting transfers between devices, shift(): lax.ppermute(value, axis, [((i + distance) % count, i) for i in range(cou...  45.3 us
    ppermute x12, starting transfers between devices, swap(): return lax.ppermute(value, 'core', [(0, 1), (1, 0)])  35 us
    dot_general x8, matrix products, per_device(): jnp.dot(activated[i * n:(i + 1) * n], weight_out, preferred_element_type=...  13.2 us
    all_gather x1, blocking collectives, per_device(): group_table = lax.all_gather(table, ('x', 'core'), axis=0, tiled=True)  12.2 us
    dot_general x1, matrix products, per_device(): projected = jnp.dot(values, out_proj, preferred_element_type=f32)  7.91 us
    dot_general x8, matrix products, per_device(): jnp.dot(b, weight_in, preferred_element_type=f32)  5.37 us
  transfers between devices with their start and end apart: 48, of which 26 were waited for; matrix products, arithmetic and copies ran while one was open for 21% of the time, Pallas kernels for 0%

profile of v1, /device:TPU:1, one launch (start us, length us, event | category | flops | bytes accessed | tf_op | source)
XLA Modules:
  0.0 234.6 jit_solution(5797784961138988939)
XLA Ops:
  5.7 3.1 %fusion.95 = (f32[8,64]{1,0:T(8,128)S(1)}, f32[8,64,384]{2,1,0:T(8,128)S(1)}) fusion(bf16[8,64,576]{2,1,0:T(8,128)(2,1)} %param.14, bf16[8,384,576]{1,2,0:T(8,128)(2,1)} %param.15, s32[8]{0:T(128)} %param.17), kind=kOutput, calls=%fused_computation.208 | convolution fusion | flops 227278336 | bytes 4917280 | tf_op jit(solution)/shard_map/rhc,rtc->rht/dot_general | solution.py:15
  11.5 4.5 %all-to-all-start = ((bf16[8,64,512]{2,0,1:T(8,128)(2,1)}), bf16[8,64,512]{2,0,1:T(8,128)(2,1)S(1)}, u32[]{:S(2)}, u32[]{:S(2)}) async-start(bf16[8,64,512]{2,0,1:T(8,128)(2,1)} %copy.33), calls=%async_computation | async-start | bytes 1048576 | tf_op jit(solution)/shard_map/all_to_all | solution.py:133
  16.0 3.0 %dynamic-slice_bitcast_fusion = bf16[2,3584,128]{2,1,0:T(8,128)(2,1)} fusion(bf16[1,2,7168,128]{3,2,1,0:T(8,128)(2,1)} %param.24, s32[]{:T(128)S(6)} %select_n.119), kind=kLoop, calls=%fused_computation.35 | loop fusion | bytes 3670020 | tf_op jit(solution)/shard_map/dynamic_slice | solution.py:119
  22.2 12.2 %all_gather.3 = bf16[64,16]{1,0:T(8,128)(2,1)S(1)} all-gather(bf16[8,16]{1,0:T(8,128)(2,1)S(1)} %select_reduce_fusion.8), channel_id=1, replica_groups=mesh['y'=4,'z'=4,'x'=4,'core'=2] {'x','core'}, dimensions={0}, use_global_device_ids=true | all-gather | bytes 2304 | tf_op jit(solution)/shard_map/all_gather | solution.py:151
  38.5 7.9 %fusion.52 = f32[64,7168]{1,0:T(8,128)S(1)} fusion(bf16[1024,7168]{1,0:T(8,128)(2,1)} %param.19, bf16[8,8,8,128]{3,2,1,0:T(8,128)(2,1)S(1)} %fusion.32), kind=kOutput, calls=%fused_computation.118 | convolution fusion | flops 939524096 | bytes 16646144 | tf_op jit(solution)/shard_map/dot_general | solution.py:158
  46.8 1.6 collective-permute-done
  51.5 4.3 %collective-permute-done.2 = bf16[4,8,3584]{2,1,0:T(8,128)(2,1)S(1)} collective-permute-done((bf16[4,8,3584]{2,1,0:T(8,128)(2,1)S(1)}, bf16[4,8,3584]{2,1,0:T(8,128)(2,1)S(1)}, u32[]{:S(2)}, u32[]{:S(2)}) %collective-permute-start.2) | collective-permute-done | bytes 229408 | tf_op jit(solution)/shard_map/ppermute | solution.py:54
  55.8 3.0 %collective-permute-start.5 = (bf16[4,8,3584]{2,1,0:T(8,128)(2,1)S(1)}, bf16[4,8,3584]{2,1,0:T(8,128)(2,1)S(1)}, u32[]{:S(2)}, u32[]{:S(2)}) collective-permute-start(bf16[4,8,3584]{2,1,0:T(8,128)(2,1)S(1)} %get-tuple-element.25), channel_id=1, source_target_pairs={{2,0},{4,2},{6,4},{0,6},{3,1},{5,3},{7,5},{1,7},{10,8},{12,10},{14... | collective-permute-start | bytes 688136 | tf_op jit(solution)/shard_map/ppermute | solution.py:54
  59.7 5.3 %collective-permute-done.4 = bf16[4,8,3584]{2,1,0:T(8,128)(2,1)S(1)} collective-permute-done((bf16[4,8,3584]{2,1,0:T(8,128)(2,1)S(1)}, bf16[4,8,3584]{2,1,0:T(8,128)(2,1)S(1)}, u32[]{:S(2)}, u32[]{:S(2)}) %collective-permute-start.4) | collective-permute-done | bytes 229408 | tf_op jit(solution)/shard_map/ppermute | solution.py:54
  65.2 7.2 %collective-permute-start.9 = (f32[4,8,1]{1,0,2:T(4,128)S(1)}, f32[4,8,1]{1,0,2:T(4,128)S(1)}, u32[]{:S(2)}, u32[]{:S(2)}) collective-permute-start(f32[4,8,1]{1,0,2:T(4,128)S(1)} %bitcast.142), channel_id=1, source_target_pairs={{0,1},{1,0},{2,3},{3,2},{4,5},{5,4},{6,7},{7,6},{8,9},{9,8},{10,11... | collective-permute-start | bytes 392 | tf_op jit(solution)/shard_map/ppermute | solution.py:58
  72.4 3.1 %collective-permute-done.7 = bf16[4,8,3584]{2,1,0:T(8,128)(2,1)S(1)} collective-permute-done((bf16[4,8,3584]{2,1,0:T(8,128)(2,1)S(1)}, bf16[4,8,3584]{2,1,0:T(8,128)(2,1)S(1)}, u32[]{:S(2)}, u32[]{:S(2)}) %collective-permute-start.7) | collective-permute-done | bytes 229408 | tf_op jit(solution)/shard_map/ppermute | solution.py:54
  77.9 2.8 %collective-permute-start.10 = (bf16[32,3712]{1,0:T(8,128)(2,1)S(1)}, bf16[32,3712]{1,0:T(8,128)(2,1)S(1)}, u32[]{:S(2)}, u32[]{:S(2)}) collective-permute-start(bf16[32,3712]{1,0:T(8,128)(2,1)S(1)} %pad_maximum_fusion.10), channel_id=1, source_target_pairs={{32,0},{64,32},{96,64},{0,96},{33,1},{65,33},{97,65},{1,97},{34,2}... | collective-permute-start | bytes 712712 | tf_op jit(solution)/shard_map/ppermute | solution.py:54
  81.8 8.7 %collective-permute-done.10 = bf16[32,3712]{1,0:T(8,128)(2,1)S(1)} collective-permute-done((bf16[32,3712]{1,0:T(8,128)(2,1)S(1)}, bf16[32,3712]{1,0:T(8,128)(2,1)S(1)}, u32[]{:S(2)}, u32[]{:S(2)}) %collective-permute-start.10) | collective-permute-done | bytes 237600 | tf_op jit(solution)/shard_map/ppermute | solution.py:54
  90.5 3.8 %collective-permute-start.29 = (bf16[32,3712]{1,0:T(8,128)(2,1)S(1)}, bf16[32,3712]{1,0:T(8,128)(2,1)S(1)}, u32[]{:S(2)}, u32[]{:S(2)}) collective-permute-start(bf16[32,3712]{1,0:T(8,128)(2,1)S(1)} %pad_maximum_fusion.11), channel_id=1, source_target_pairs={{8,0},{16,8},{24,16},{0,24},{9,1},{17,9},{25,17},{1,25},{10,2},{18... | collective-permute-start | bytes 712712 | tf_op jit(solution)/shard_map/ppermute | solution.py:54
  95.0 1.6 collective-permute-start.31
  96.7 6.6 %collective-permute-done.29 = bf16[32,3712]{1,0:T(8,128)(2,1)S(1)} collective-permute-done((bf16[32,3712]{1,0:T(8,128)(2,1)S(1)}, bf16[32,3712]{1,0:T(8,128)(2,1)S(1)}, u32[]{:S(2)}, u32[]{:S(2)}) %collective-permute-start.29) | collective-permute-done | bytes 237600 | tf_op jit(solution)/shard_map/ppermute | solution.py:54
  103.4 3.6 %collective-permute-start.14 = (bf16[128,3712]{1,0:T(8,128)(2,1)S(1)}, bf16[128,3712]{1,0:T(8,128)(2,1)S(1)}, u32[]{:S(2)}, u32[]{:S(2)}) collective-permute-start(bf16[128,3712]{1,0:T(8,128)(2,1)S(1)} %pad_maximum_fusion.1), channel_id=1, source_target_pairs={{8,0},{16,8},{24,16},{0,24},{9,1},{17,9},{25,17},{1,25},{10,2},{18... | collective-permute-start | bytes 2850824 | tf_op jit(solution)/shard_map/ppermute | solution.py:54
  106.9 1.7 collective-permute-done.31
  108.7 3.2 %collective-permute-start.32 = (bf16[128,3712]{1,0:T(8,128)(2,1)S(1)}, bf16[128,3712]{1,0:T(8,128)(2,1)S(1)}, u32[]{:S(2)}, u32[]{:S(2)}) collective-permute-start(bf16[128,3712]{1,0:T(8,128)(2,1)S(1)} %pad_maximum_fusion.2), channel_id=1, source_target_pairs={{32,0},{64,32},{96,64},{0,96},{33,1},{65,33},{97,65},{1,97},{34,2}... | collective-permute-start | bytes 2850824 | tf_op jit(solution)/shard_map/ppermute | solution.py:54
  113.4 2.2 fusion.22
  117.0 8.4 %collective-permute-done.14 = bf16[128,3712]{1,0:T(8,128)(2,1)S(1)} collective-permute-done((bf16[128,3712]{1,0:T(8,128)(2,1)S(1)}, bf16[128,3712]{1,0:T(8,128)(2,1)S(1)}, u32[]{:S(2)}, u32[]{:S(2)}) %collective-permute-start.14) | collective-permute-done | bytes 950304 | tf_op jit(solution)/shard_map/ppermute | solution.py:54
  125.4 3.5 %collective-permute-start.15 = (bf16[64,3712]{1,0:T(8,128)(2,1)S(1)}, bf16[64,3712]{1,0:T(8,128)(2,1)S(1)}, u32[]{:S(2)}, u32[]{:S(2)}) collective-permute-start(bf16[64,3712]{1,0:T(8,128)(2,1)S(1)} %slice.325), channel_id=1, source_target_pairs={{8,0},{16,8},{24,16},{0,24},{9,1},{17,9},{25,17},{1,25},{10,2},{18... | collective-permute-start | bytes 1425416 | tf_op jit(solution)/shard_map/ppermute | solution.py:54
  131.9 2.4 %collective-permute-done.34 = bf16[128,3712]{1,0:T(8,128)(2,1)S(1)} collective-permute-done((bf16[128,3712]{1,0:T(8,128)(2,1)S(1)}, bf16[128,3712]{1,0:T(8,128)(2,1)S(1)}, u32[]{:S(2)}, u32[]{:S(2)}) %collective-permute-start.34) | collective-permute-done | bytes 950304 | tf_op jit(solution)/shard_map/ppermute | solution.py:54
  136.9 2.6 %collective-permute-done.17 = bf16[64,3712]{1,0:T(8,128)(2,1)S(1)} collective-permute-done((bf16[64,3712]{1,0:T(8,128)(2,1)S(1)}, bf16[64,3712]{1,0:T(8,128)(2,1)S(1)}, u32[]{:S(2)}, u32[]{:S(2)}) %collective-permute-start.17) | collective-permute-done | bytes 475168 | tf_op jit(solution)/shard_map/ppermute | solution.py:54
  140.3 4.1 %collective-permute-start.18 = (bf16[512,256]{1,0:T(8,128)(2,1)S(1)}, bf16[512,256]{1,0:T(8,128)(2,1)S(1)}, u32[]{:S(2)}, u32[]{:S(2)}) collective-permute-start(bf16[512,256]{1,0:T(8,128)(2,1)S(1)} %pad_maximum_fusion.8), channel_id=1, source_target_pairs={{0,1},{1,0},{2,3},{3,2},{4,5},{5,4},{6,7},{7,6},{8,9},{9,8},{10,11... | collective-permute-start | bytes 786440 | tf_op jit(solution)/shard_map/ppermute | solution.py:58
  145.6 1.7 collective-permute-done.35
  148.2 3.7 %collective-permute-start.36 = (bf16[512,256]{1,0:T(8,128)(2,1)S(1)}, bf16[512,256]{1,0:T(8,128)(2,1)S(1)}, u32[]{:S(2)}, u32[]{:S(2)}) collective-permute-start(bf16[512,256]{1,0:T(8,128)(2,1)S(1)} %pad_maximum_fusion.9), channel_id=1, source_target_pairs={{0,1},{1,0},{2,3},{3,2},{4,5},{5,4},{6,7},{7,6},{8,9},{9,8},{10,11... | collective-permute-start | bytes 786440 | tf_op jit(solution)/shard_map/ppermute | solution.py:58
  153.6 1.6 fusion.10
  155.4 1.6 fusion.9
  157.0 2.9 %collective-permute-start.23 = (bf16[64,3584]{1,0:T(8,128)(2,1)S(1)}, bf16[64,3584]{1,0:T(8,128)(2,1)S(1)}, u32[]{:S(2)}, u32[]{:S(2)}) collective-permute-start(bf16[64,3584]{1,0:T(8,128)(2,1)S(1)} %get-tuple-element.33), channel_id=1, source_target_pairs={{8,0},{16,8},{24,16},{0,24},{9,1},{17,9},{25,17},{1,25},{10,2},{18... | collective-permute-start | bytes 1376264 | tf_op jit(solution)/shard_map/ppermute | solution.py:54
  160.0 1.6 fusion.11
  161.7 1.6 fusion.18
  163.4 1.6 fusion.17
  165.1 2.7 %collective-permute-start.40 = (bf16[64,3584]{1,0:T(8,128)(2,1)S(1)}, bf16[64,3584]{1,0:T(8,128)(2,1)S(1)}, u32[]{:S(2)}, u32[]{:S(2)}) collective-permute-start(bf16[64,3584]{1,0:T(8,128)(2,1)S(1)} %get-tuple-element.38), channel_id=1, source_target_pairs={{32,0},{64,32},{96,64},{0,96},{33,1},{65,33},{97,65},{1,97},{34,2}... | collective-permute-start | bytes 1376264 | tf_op jit(solution)/shard_map/ppermute | solution.py:54
  167.8 1.6 fusion.19
  169.9 3.2 %collective-permute-start.24 = (bf16[128,3584]{1,0:T(8,128)(2,1)S(1)}, bf16[128,3584]{1,0:T(8,128)(2,1)S(1)}, u32[]{:S(2)}, u32[]{:S(2)}) collective-permute-start(bf16[128,3584]{1,0:T(8,128)(2,1)S(1)} %pad_maximum_fusion.4), channel_id=1, source_target_pairs={{8,0},{16,8},{24,16},{0,24},{9,1},{17,9},{25,17},{1,25},{10,2},{18... | collective-permute-start | bytes 2752520 | tf_op jit(solution)/shard_map/ppermute | solution.py:54
  173.1 2.8 %collective-permute-done.38 = bf16[64,3584]{1,0:T(8,128)(2,1)S(1)} collective-permute-done((bf16[64,3584]{1,0:T(8,128)(2,1)S(1)}, bf16[64,3584]{1,0:T(8,128)(2,1)S(1)}, u32[]{:S(2)}, u32[]{:S(2)}) %collective-permute-start.38) | collective-permute-done | bytes 458784 | tf_op jit(solution)/shard_map/ppermute | solution.py:54
  176.8 3.5 %collective-permute-start.41 = (bf16[128,3584]{1,0:T(8,128)(2,1)S(1)}, bf16[128,3584]{1,0:T(8,128)(2,1)S(1)}, u32[]{:S(2)}, u32[]{:S(2)}) collective-permute-start(bf16[128,3584]{1,0:T(8,128)(2,1)S(1)} %pad_maximum_fusion.6), channel_id=1, source_target_pairs={{32,0},{64,32},{96,64},{0,96},{33,1},{65,33},{97,65},{1,97},{34,2}... | collective-permute-start | bytes 2752520 | tf_op jit(solution)/shard_map/ppermute | solution.py:54
  180.3 11.2 %collective-permute-done.22 = bf16[128,3584]{1,0:T(8,128)(2,1)S(1)} collective-permute-done((bf16[128,3584]{1,0:T(8,128)(2,1)S(1)}, bf16[128,3584]{1,0:T(8,128)(2,1)S(1)}, u32[]{:S(2)}, u32[]{:S(2)}) %collective-permute-start.22) | collective-permute-done | bytes 917536 | tf_op jit(solution)/shard_map/ppermute | solution.py:54
  191.5 1.8 fusion.8
  196.1 1.6 collective-permute-done.39
  198.6 1.7 fusion.16
  200.5 2.0 collective-permute-start.43
  202.6 5.0 %collective-permute-done.25 = bf16[32,3584]{1,0:T(8,128)(2,1)S(1)} collective-permute-done((bf16[32,3584]{1,0:T(8,128)(2,1)S(1)}, bf16[32,3584]{1,0:T(8,128)(2,1)S(1)}, u32[]{:S(2)}, u32[]{:S(2)}) %collective-permute-start.25) | collective-permute-done | bytes 229408 | tf_op jit(solution)/shard_map/ppermute | solution.py:54
  209.4 3.0 %collective-permute-done.44 = bf16[32,3584]{1,0:T(8,128)(2,1)S(1)} collective-permute-done((bf16[32,3584]{1,0:T(8,128)(2,1)S(1)}, bf16[32,3584]{1,0:T(8,128)(2,1)S(1)}, u32[]{:S(2)}, u32[]{:S(2)}) %collective-permute-start.44) | collective-permute-done | bytes 229408 | tf_op jit(solution)/shard_map/ppermute | solution.py:54
  213.3 3.5 %all-to-all-start.1 = ((bf16[4,2,8,3584]{3,2,1,0:T(8,128)(2,1)}), bf16[4,2,8,3584]{3,2,1,0:T(8,128)(2,1)S(1)}, u32[]{:S(2)}, u32[]{:S(2)}) async-start(bf16[4,2,8,3584]{3,2,1,0:T(8,128)(2,1)} %pad_maximum_fusion.7), calls=%async_computation.1 | async-start | bytes 917504 | tf_op jit(solution)/shard_map/all_to_all | solution.py:214
  216.8 8.4 %collective-permute-start.8 = (bf16[8,3584]{1,0:T(8,128)(2,1)S(1)}, bf16[8,3584]{1,0:T(8,128)(2,1)S(1)}, u32[]{:S(2)}, u32[]{:S(2)}) collective-permute-start(bf16[8,3584]{1,0:T(8,128)(2,1)S(1)} %broadcast_select_fusion), channel_id=1, source_target_pairs={{0,1},{1,0},{2,3},{3,2},{4,5},{5,4},{6,7},{7,6},{8,9},{9,8},{10,11... | collective-permute-start | bytes 172040 | tf_op jit(solution)/shard_map/ppermute | solution.py:58
  225.3 7.7 %collective-permute-start.45 = (bf16[8,3584]{1,0:T(8,128)(2,1)S(1)}, bf16[8,3584]{1,0:T(8,128)(2,1)S(1)}, u32[]{:S(2)}, u32[]{:S(2)}) collective-permute-start(bf16[8,3584]{1,0:T(8,128)(2,1)S(1)} %get-tuple-element.40), channel_id=1, source_target_pairs={{0,1},{1,0},{2,3},{3,2},{4,5},{5,4},{6,7},{7,6},{8,9},{9,8},{10,11... | collective-permute-start | bytes 172040 | tf_op jit(solution)/shard_map/ppermute | solution.py:58
  (205 shorter events, 46.6 us)
Async XLA Ops:
  2.2 34.4 %collective-permute-start.1 = (bf16[8,3584]{1,0:T(8,128)(2,1)}, bf16[8,3584]{1,0:T(8,128)(2,1)S(1)}, u32[]{:S(2)}, u32[]{:S(2)}) collective-permute-start(bf16[8,3584]{1,0:T(8,128)(2,1)} %get-tuple-element.44), channel_id=1, source_target_pairs={{0,1},{1,0},{2,3},{3,2},{4,5},{5,4},{6,7},{7,6},{8,9},{9,8},{10,11... | collective-permute-start | bytes 172040 | tf_op jit(solution)/shard_map/ppermute | solution.py:58
  11.5 26.7 %all-to-all-start = ((bf16[8,64,512]{2,0,1:T(8,128)(2,1)}), bf16[8,64,512]{2,0,1:T(8,128)(2,1)S(1)}, u32[]{:S(2)}, u32[]{:S(2)}) async-start(bf16[8,64,512]{2,0,1:T(8,128)(2,1)} %copy.33), calls=%async_computation | async-start | bytes 1048576 | tf_op jit(solution)/shard_map/all_to_all | solution.py:133
  19.0 92.8 %collective-permute-start.13 = (bf16[2,3584,128]{2,1,0:T(8,128)(2,1)}, bf16[2,3584,128]{2,1,0:T(8,128)(2,1)}, u32[]{:S(2)}, u32[]{:S(2)}) collective-permute-start(bf16[2,3584,128]{2,1,0:T(8,128)(2,1)} %dynamic-slice_bitcast_fusion), channel_id=1, source_target_pairs={{0,1},{1,0},{2,3},{3,2},{4,5},{5,4},{6,7},{7,6},{8,9},{9,8},{10,11... | collective-permute-start | bytes 5505032 | tf_op jit(solution)/shard_map/ppermute | solution.py:58
  20.5 133.1 %collective-permute-start.20 = (bf16[128,3584]{1,0:T(8,128)(2,1)}, bf16[128,3584]{1,0:T(8,128)(2,1)}, u32[]{:S(2)}, u32[]{:S(2)}) collective-permute-start(bf16[128,3584]{1,0:T(8,128)(2,1)} %get-tuple-element.22), channel_id=1, source_target_pairs={{0,1},{1,0},{2,3},{3,2},{4,5},{5,4},{6,7},{7,6},{8,9},{9,8},{10,11... | collective-permute-start | bytes 2752520 | tf_op jit(solution)/shard_map/ppermute | solution.py:58
  46.5 1.9 collective-permute-start
  48.7 7.1 %collective-permute-start.2 = (bf16[4,8,3584]{2,1,0:T(8,128)(2,1)S(1)}, bf16[4,8,3584]{2,1,0:T(8,128)(2,1)S(1)}, u32[]{:S(2)}, u32[]{:S(2)}) collective-permute-start(bf16[4,8,3584]{2,1,0:T(8,128)(2,1)S(1)} %get-tuple-element.26), channel_id=1, source_target_pairs={{2,0},{4,2},{6,4},{0,6},{3,1},{5,3},{7,5},{1,7},{10,8},{12,10},{14... | collective-permute-start | bytes 688136 | tf_op jit(solution)/shard_map/ppermute | solution.py:54
  50.2 8.5 %collective-permute-start.3 = (bf16[4,8,3584]{2,1,0:T(8,128)(2,1)S(1)}, bf16[4,8,3584]{2,1,0:T(8,128)(2,1)S(1)}, u32[]{:S(2)}, u32[]{:S(2)}) collective-permute-start(bf16[4,8,3584]{2,1,0:T(8,128)(2,1)S(1)} %get-tuple-element.26), channel_id=1, source_target_pairs={{4,0},{6,2},{0,4},{2,6},{5,1},{7,3},{1,5},{3,7},{12,8},{14,10},{8,... | collective-permute-start | bytes 688136 | tf_op jit(solution)/shard_map/ppermute | solution.py:54
  51.4 13.5 %collective-permute-start.4 = (bf16[4,8,3584]{2,1,0:T(8,128)(2,1)S(1)}, bf16[4,8,3584]{2,1,0:T(8,128)(2,1)S(1)}, u32[]{:S(2)}, u32[]{:S(2)}) collective-permute-start(bf16[4,8,3584]{2,1,0:T(8,128)(2,1)S(1)} %get-tuple-element.26), channel_id=1, source_target_pairs={{6,0},{0,2},{2,4},{4,6},{7,1},{1,3},{3,5},{5,7},{14,8},{8,10},{10,... | collective-permute-start | bytes 688136 | tf_op jit(solution)/shard_map/ppermute | solution.py:54
  55.8 9.4 %collective-permute-start.5 = (bf16[4,8,3584]{2,1,0:T(8,128)(2,1)S(1)}, bf16[4,8,3584]{2,1,0:T(8,128)(2,1)S(1)}, u32[]{:S(2)}, u32[]{:S(2)}) collective-permute-start(bf16[4,8,3584]{2,1,0:T(8,128)(2,1)S(1)} %get-tuple-element.25), channel_id=1, source_target_pairs={{2,0},{4,2},{6,4},{0,6},{3,1},{5,3},{7,5},{1,7},{10,8},{12,10},{14... | collective-permute-start | bytes 688136 | tf_op jit(solution)/shard_map/ppermute | solution.py:54
  58.8 13.6 %collective-permute-start.6 = (bf16[4,8,3584]{2,1,0:T(8,128)(2,1)S(1)}, bf16[4,8,3584]{2,1,0:T(8,128)(2,1)S(1)}, u32[]{:S(2)}, u32[]{:S(2)}) collective-permute-start(bf16[4,8,3584]{2,1,0:T(8,128)(2,1)S(1)} %get-tuple-element.25), channel_id=1, source_target_pairs={{4,0},{6,2},{0,4},{2,6},{5,1},{7,3},{1,5},{3,7},{12,8},{14,10},{8,... | collective-permute-start | bytes 688136 | tf_op jit(solution)/shard_map/ppermute | solution.py:54
  65.0 10.5 %collective-permute-start.7 = (bf16[4,8,3584]{2,1,0:T(8,128)(2,1)S(1)}, bf16[4,8,3584]{2,1,0:T(8,128)(2,1)S(1)}, u32[]{:S(2)}, u32[]{:S(2)}) collective-permute-start(bf16[4,8,3584]{2,1,0:T(8,128)(2,1)S(1)} %get-tuple-element.25), channel_id=1, source_target_pairs={{6,0},{0,2},{2,4},{4,6},{7,1},{1,3},{3,5},{5,7},{14,8},{8,10},{10,... | collective-permute-start | bytes 688136 | tf_op jit(solution)/shard_map/ppermute | solution.py:54
  65.2 11.8 %collective-permute-start.9 = (f32[4,8,1]{1,0,2:T(4,128)S(1)}, f32[4,8,1]{1,0,2:T(4,128)S(1)}, u32[]{:S(2)}, u32[]{:S(2)}) collective-permute-start(f32[4,8,1]{1,0,2:T(4,128)S(1)} %bitcast.142), channel_id=1, source_target_pairs={{0,1},{1,0},{2,3},{3,2},{4,5},{5,4},{6,7},{7,6},{8,9},{9,8},{10,11... | collective-permute-start | bytes 392 | tf_op jit(solution)/shard_map/ppermute | solution.py:58
  75.7 2.0 collective-permute-start.28
  77.9 12.6 %collective-permute-start.10 = (bf16[32,3712]{1,0:T(8,128)(2,1)S(1)}, bf16[32,3712]{1,0:T(8,128)(2,1)S(1)}, u32[]{:S(2)}, u32[]{:S(2)}) collective-permute-start(bf16[32,3712]{1,0:T(8,128)(2,1)S(1)} %pad_maximum_fusion.10), channel_id=1, source_target_pairs={{32,0},{64,32},{96,64},{0,96},{33,1},{65,33},{97,65},{1,97},{34,2}... | collective-permute-start | bytes 712712 | tf_op jit(solution)/shard_map/ppermute | solution.py:54
  80.7 13.5 %collective-permute-start.11 = (bf16[32,3712]{1,0:T(8,128)(2,1)S(1)}, bf16[32,3712]{1,0:T(8,128)(2,1)S(1)}, u32[]{:S(2)}, u32[]{:S(2)}) collective-permute-start(bf16[32,3712]{1,0:T(8,128)(2,1)S(1)} %pad_maximum_fusion.10), channel_id=1, source_target_pairs={{64,0},{96,32},{0,64},{32,96},{65,1},{97,33},{1,65},{33,97},{66,2}... | collective-permute-start | bytes 712712 | tf_op jit(solution)/shard_map/ppermute | solution.py:54
  81.1 13.9 %collective-permute-start.12 = (bf16[32,3712]{1,0:T(8,128)(2,1)S(1)}, bf16[32,3712]{1,0:T(8,128)(2,1)S(1)}, u32[]{:S(2)}, u32[]{:S(2)}) collective-permute-start(bf16[32,3712]{1,0:T(8,128)(2,1)S(1)} %pad_maximum_fusion.10), channel_id=1, source_target_pairs={{96,0},{0,32},{32,64},{64,96},{97,1},{1,33},{33,65},{65,97},{98,2}... | collective-permute-start | bytes 712712 | tf_op jit(solution)/shard_map/ppermute | solution.py:54
  90.5 12.8 %collective-permute-start.29 = (bf16[32,3712]{1,0:T(8,128)(2,1)S(1)}, bf16[32,3712]{1,0:T(8,128)(2,1)S(1)}, u32[]{:S(2)}, u32[]{:S(2)}) collective-permute-start(bf16[32,3712]{1,0:T(8,128)(2,1)S(1)} %pad_maximum_fusion.11), channel_id=1, source_target_pairs={{8,0},{16,8},{24,16},{0,24},{9,1},{17,9},{25,17},{1,25},{10,2},{18... | collective-permute-start | bytes 712712 | tf_op jit(solution)/shard_map/ppermute | solution.py:54
  94.3 12.6 %collective-permute-start.30 = (bf16[32,3712]{1,0:T(8,128)(2,1)S(1)}, bf16[32,3712]{1,0:T(8,128)(2,1)S(1)}, u32[]{:S(2)}, u32[]{:S(2)}) collective-permute-start(bf16[32,3712]{1,0:T(8,128)(2,1)S(1)} %pad_maximum_fusion.11), channel_id=1, source_target_pairs={{16,0},{24,8},{0,16},{8,24},{17,1},{25,9},{1,17},{9,25},{18,2},{26... | collective-permute-start | bytes 712712 | tf_op jit(solution)/shard_map/ppermute | solution.py:54
  95.0 13.6 %collective-permute-start.31 = (bf16[32,3712]{1,0:T(8,128)(2,1)S(1)}, bf16[32,3712]{1,0:T(8,128)(2,1)S(1)}, u32[]{:S(2)}, u32[]{:S(2)}) collective-permute-start(bf16[32,3712]{1,0:T(8,128)(2,1)S(1)} %pad_maximum_fusion.11), channel_id=1, source_target_pairs={{24,0},{0,8},{8,16},{16,24},{25,1},{1,9},{9,17},{17,25},{26,2},{2,... | collective-permute-start | bytes 712712 | tf_op jit(solution)/shard_map/ppermute | solution.py:54
  103.4 22.0 %collective-permute-start.14 = (bf16[128,3712]{1,0:T(8,128)(2,1)S(1)}, bf16[128,3712]{1,0:T(8,128)(2,1)S(1)}, u32[]{:S(2)}, u32[]{:S(2)}) collective-permute-start(bf16[128,3712]{1,0:T(8,128)(2,1)S(1)} %pad_maximum_fusion.1), channel_id=1, source_target_pairs={{8,0},{16,8},{24,16},{0,24},{9,1},{17,9},{25,17},{1,25},{10,2},{18... | collective-permute-start | bytes 2850824 | tf_op jit(solution)/shard_map/ppermute | solution.py:54
  106.9 22.0 %collective-permute-start.16 = (bf16[128,3712]{1,0:T(8,128)(2,1)S(1)}, bf16[128,3712]{1,0:T(8,128)(2,1)S(1)}, u32[]{:S(2)}, u32[]{:S(2)}) collective-permute-start(bf16[128,3712]{1,0:T(8,128)(2,1)S(1)} %pad_maximum_fusion.1), channel_id=1, source_target_pairs={{24,0},{0,8},{8,16},{16,24},{25,1},{1,9},{9,17},{17,25},{26,2},{2,... | collective-permute-start | bytes 2850824 | tf_op jit(solution)/shard_map/ppermute | solution.py:54
  108.7 22.6 %collective-permute-start.32 = (bf16[128,3712]{1,0:T(8,128)(2,1)S(1)}, bf16[128,3712]{1,0:T(8,128)(2,1)S(1)}, u32[]{:S(2)}, u32[]{:S(2)}) collective-permute-start(bf16[128,3712]{1,0:T(8,128)(2,1)S(1)} %pad_maximum_fusion.2), channel_id=1, source_target_pairs={{32,0},{64,32},{96,64},{0,96},{33,1},{65,33},{97,65},{1,97},{34,2}... | collective-permute-start | bytes 2850824 | tf_op jit(solution)/shard_map/ppermute | solution.py:54
  111.8 22.5 %collective-permute-start.34 = (bf16[128,3712]{1,0:T(8,128)(2,1)S(1)}, bf16[128,3712]{1,0:T(8,128)(2,1)S(1)}, u32[]{:S(2)}, u32[]{:S(2)}) collective-permute-start(bf16[128,3712]{1,0:T(8,128)(2,1)S(1)} %pad_maximum_fusion.2), channel_id=1, source_target_pairs={{96,0},{0,32},{32,64},{64,96},{97,1},{1,33},{33,65},{65,97},{98,2}... | collective-permute-start | bytes 2850824 | tf_op jit(solution)/shard_map/ppermute | solution.py:54
  125.4 11.4 %collective-permute-start.15 = (bf16[64,3712]{1,0:T(8,128)(2,1)S(1)}, bf16[64,3712]{1,0:T(8,128)(2,1)S(1)}, u32[]{:S(2)}, u32[]{:S(2)}) collective-permute-start(bf16[64,3712]{1,0:T(8,128)(2,1)S(1)} %slice.325), channel_id=1, source_target_pairs={{8,0},{16,8},{24,16},{0,24},{9,1},{17,9},{25,17},{1,25},{10,2},{18... | collective-permute-start | bytes 1425416 | tf_op jit(solution)/shard_map/ppermute | solution.py:54
  129.0 10.6 %collective-permute-start.17 = (bf16[64,3712]{1,0:T(8,128)(2,1)S(1)}, bf16[64,3712]{1,0:T(8,128)(2,1)S(1)}, u32[]{:S(2)}, u32[]{:S(2)}) collective-permute-start(bf16[64,3712]{1,0:T(8,128)(2,1)S(1)} %slice.326), channel_id=1, source_target_pairs={{24,0},{0,8},{8,16},{16,24},{25,1},{1,9},{9,17},{17,25},{26,2},{2,... | collective-permute-start | bytes 1425416 | tf_op jit(solution)/shard_map/ppermute | solution.py:54
  135.2 10.3 %collective-permute-start.33 = (bf16[64,3712]{1,0:T(8,128)(2,1)S(1)}, bf16[64,3712]{1,0:T(8,128)(2,1)S(1)}, u32[]{:S(2)}, u32[]{:S(2)}) collective-permute-start(bf16[64,3712]{1,0:T(8,128)(2,1)S(1)} %slice.358), channel_id=1, source_target_pairs={{32,0},{64,32},{96,64},{0,96},{33,1},{65,33},{97,65},{1,97},{34,2}... | collective-permute-start | bytes 1425416 | tf_op jit(solution)/shard_map/ppermute | solution.py:54
  136.3 11.0 %collective-permute-start.35 = (bf16[64,3712]{1,0:T(8,128)(2,1)S(1)}, bf16[64,3712]{1,0:T(8,128)(2,1)S(1)}, u32[]{:S(2)}, u32[]{:S(2)}) collective-permute-start(bf16[64,3712]{1,0:T(8,128)(2,1)S(1)} %slice.359), channel_id=1, source_target_pairs={{96,0},{0,32},{32,64},{64,96},{97,1},{1,33},{33,65},{65,97},{98,2}... | collective-permute-start | bytes 1425416 | tf_op jit(solution)/shard_map/ppermute | solution.py:54
  140.3 11.7 %collective-permute-start.18 = (bf16[512,256]{1,0:T(8,128)(2,1)S(1)}, bf16[512,256]{1,0:T(8,128)(2,1)S(1)}, u32[]{:S(2)}, u32[]{:S(2)}) collective-permute-start(bf16[512,256]{1,0:T(8,128)(2,1)S(1)} %pad_maximum_fusion.8), channel_id=1, source_target_pairs={{0,1},{1,0},{2,3},{3,2},{4,5},{5,4},{6,7},{7,6},{8,9},{9,8},{10,11... | collective-permute-start | bytes 786440 | tf_op jit(solution)/shard_map/ppermute | solution.py:58
  148.2 4.8 %collective-permute-start.36 = (bf16[512,256]{1,0:T(8,128)(2,1)S(1)}, bf16[512,256]{1,0:T(8,128)(2,1)S(1)}, u32[]{:S(2)}, u32[]{:S(2)}) collective-permute-start(bf16[512,256]{1,0:T(8,128)(2,1)S(1)} %pad_maximum_fusion.9), channel_id=1, source_target_pairs={{0,1},{1,0},{2,3},{3,2},{4,5},{5,4},{6,7},{7,6},{8,9},{9,8},{10,11... | collective-permute-start | bytes 786440 | tf_op jit(solution)/shard_map/ppermute | solution.py:58
  152.2 1.4 collective-permute-start.19
  153.1 8.5 %collective-permute-start.37 = (bf16[512,128]{1,0:T(8,128)(2,1)S(1)}, bf16[512,128]{1,0:T(8,128)(2,1)S(1)}, u32[]{:S(2)}, u32[]{:S(2)}) collective-permute-start(bf16[512,128]{1,0:T(8,128)(2,1)S(1)} %fusion.46), channel_id=1, source_target_pairs={{0,1},{1,0},{2,3},{3,2},{4,5},{5,4},{6,7},{7,6},{8,9},{9,8},{10,11... | collective-permute-start | bytes 393224 | tf_op jit(solution)/shard_map/ppermute | solution.py:58
  155.3 14.2 %collective-permute-start.21 = (bf16[64,3584]{1,0:T(8,128)(2,1)S(1)}, bf16[64,3584]{1,0:T(8,128)(2,1)S(1)}, u32[]{:S(2)}, u32[]{:S(2)}) collective-permute-start(bf16[64,3584]{1,0:T(8,128)(2,1)S(1)} %get-tuple-element.32), channel_id=1, source_target_pairs={{24,0},{0,8},{8,16},{16,24},{25,1},{1,9},{9,17},{17,25},{26,2},{2,... | collective-permute-start | bytes 1376264 | tf_op jit(solution)/shard_map/ppermute | solution.py:54
  157.0 12.7 %collective-permute-start.23 = (bf16[64,3584]{1,0:T(8,128)(2,1)S(1)}, bf16[64,3584]{1,0:T(8,128)(2,1)S(1)}, u32[]{:S(2)}, u32[]{:S(2)}) collective-permute-start(bf16[64,3584]{1,0:T(8,128)(2,1)S(1)} %get-tuple-element.33), channel_id=1, source_target_pairs={{8,0},{16,8},{24,16},{0,24},{9,1},{17,9},{25,17},{1,25},{10,2},{18... | collective-permute-start | bytes 1376264 | tf_op jit(solution)/shard_map/ppermute | solution.py:54
  163.3 12.6 %collective-permute-start.38 = (bf16[64,3584]{1,0:T(8,128)(2,1)S(1)}, bf16[64,3584]{1,0:T(8,128)(2,1)S(1)}, u32[]{:S(2)}, u32[]{:S(2)}) collective-permute-start(bf16[64,3584]{1,0:T(8,128)(2,1)S(1)} %get-tuple-element.37), channel_id=1, source_target_pairs={{96,0},{0,32},{32,64},{64,96},{97,1},{1,33},{33,65},{65,97},{98,2}... | collective-permute-start | bytes 1376264 | tf_op jit(solution)/shard_map/ppermute | solution.py:54
  165.1 11.6 %collective-permute-start.40 = (bf16[64,3584]{1,0:T(8,128)(2,1)S(1)}, bf16[64,3584]{1,0:T(8,128)(2,1)S(1)}, u32[]{:S(2)}, u32[]{:S(2)}) collective-permute-start(bf16[64,3584]{1,0:T(8,128)(2,1)S(1)} %get-tuple-element.38), channel_id=1, source_target_pairs={{32,0},{64,32},{96,64},{0,96},{33,1},{65,33},{97,65},{1,97},{34,2}... | collective-permute-start | bytes 1376264 | tf_op jit(solution)/shard_map/ppermute | solution.py:54
  169.7 21.9 %collective-permute-start.22 = (bf16[128,3584]{1,0:T(8,128)(2,1)S(1)}, bf16[128,3584]{1,0:T(8,128)(2,1)S(1)}, u32[]{:S(2)}, u32[]{:S(2)}) collective-permute-start(bf16[128,3584]{1,0:T(8,128)(2,1)S(1)} %pad_maximum_fusion.3), channel_id=1, source_target_pairs={{24,0},{0,8},{8,16},{16,24},{25,1},{1,9},{9,17},{17,25},{26,2},{2,... | collective-permute-start | bytes 2752520 | tf_op jit(solution)/shard_map/ppermute | solution.py:54
  169.9 21.6 %collective-permute-start.24 = (bf16[128,3584]{1,0:T(8,128)(2,1)S(1)}, bf16[128,3584]{1,0:T(8,128)(2,1)S(1)}, u32[]{:S(2)}, u32[]{:S(2)}) collective-permute-start(bf16[128,3584]{1,0:T(8,128)(2,1)S(1)} %pad_maximum_fusion.4), channel_id=1, source_target_pairs={{8,0},{16,8},{24,16},{0,24},{9,1},{17,9},{25,17},{1,25},{10,2},{18... | collective-permute-start | bytes 2752520 | tf_op jit(solution)/shard_map/ppermute | solution.py:54
  176.2 21.5 %collective-permute-start.39 = (bf16[128,3584]{1,0:T(8,128)(2,1)S(1)}, bf16[128,3584]{1,0:T(8,128)(2,1)S(1)}, u32[]{:S(2)}, u32[]{:S(2)}) collective-permute-start(bf16[128,3584]{1,0:T(8,128)(2,1)S(1)} %pad_maximum_fusion.5), channel_id=1, source_target_pairs={{96,0},{0,32},{32,64},{64,96},{97,1},{1,33},{33,65},{65,97},{98,2}... | collective-permute-start | bytes 2752520 | tf_op jit(solution)/shard_map/ppermute | solution.py:54
  176.8 21.8 %collective-permute-start.41 = (bf16[128,3584]{1,0:T(8,128)(2,1)S(1)}, bf16[128,3584]{1,0:T(8,128)(2,1)S(1)}, u32[]{:S(2)}, u32[]{:S(2)}) collective-permute-start(bf16[128,3584]{1,0:T(8,128)(2,1)S(1)} %pad_maximum_fusion.6), channel_id=1, source_target_pairs={{32,0},{64,32},{96,64},{0,96},{33,1},{65,33},{97,65},{1,97},{34,2}... | collective-permute-start | bytes 2752520 | tf_op jit(solution)/shard_map/ppermute | solution.py:54
  193.3 14.2 %collective-permute-start.25 = (bf16[32,3584]{1,0:T(8,128)(2,1)S(1)}, bf16[32,3584]{1,0:T(8,128)(2,1)S(1)}, u32[]{:S(2)}, u32[]{:S(2)}) collective-permute-start(bf16[32,3584]{1,0:T(8,128)(2,1)S(1)} %get-tuple-element.29), channel_id=1, source_target_pairs={{96,0},{0,32},{32,64},{64,96},{97,1},{1,33},{33,65},{65,97},{98,2}... | collective-permute-start | bytes 688136 | tf_op jit(solution)/shard_map/ppermute | solution.py:54
  193.4 14.1 %collective-permute-start.26 = (bf16[32,3584]{1,0:T(8,128)(2,1)S(1)}, bf16[32,3584]{1,0:T(8,128)(2,1)S(1)}, u32[]{:S(2)}, u32[]{:S(2)}) collective-permute-start(bf16[32,3584]{1,0:T(8,128)(2,1)S(1)} %get-tuple-element.31), channel_id=1, source_target_pairs={{64,0},{96,32},{0,64},{32,96},{65,1},{97,33},{1,65},{33,97},{66,2}... | collective-permute-start | bytes 688136 | tf_op jit(solution)/shard_map/ppermute | solution.py:54
  194.9 13.0 %collective-permute-start.27 = (bf16[32,3584]{1,0:T(8,128)(2,1)S(1)}, bf16[32,3584]{1,0:T(8,128)(2,1)S(1)}, u32[]{:S(2)}, u32[]{:S(2)}) collective-permute-start(bf16[32,3584]{1,0:T(8,128)(2,1)S(1)} %get-tuple-element.30), channel_id=1, source_target_pairs={{32,0},{64,32},{96,64},{0,96},{33,1},{65,33},{97,65},{1,97},{34,2}... | collective-permute-start | bytes 688136 | tf_op jit(solution)/shard_map/ppermute | solution.py:54
  200.4 8.9 %collective-permute-start.42 = (bf16[32,3584]{1,0:T(8,128)(2,1)S(1)}, bf16[32,3584]{1,0:T(8,128)(2,1)S(1)}, u32[]{:S(2)}, u32[]{:S(2)}) collective-permute-start(bf16[32,3584]{1,0:T(8,128)(2,1)S(1)} %get-tuple-element.34), channel_id=1, source_target_pairs={{24,0},{0,8},{8,16},{16,24},{25,1},{1,9},{9,17},{17,25},{26,2},{2,... | collective-permute-start | bytes 688136 | tf_op jit(solution)/shard_map/ppermute | solution.py:54
  200.5 8.8 %collective-permute-start.43 = (bf16[32,3584]{1,0:T(8,128)(2,1)S(1)}, bf16[32,3584]{1,0:T(8,128)(2,1)S(1)}, u32[]{:S(2)}, u32[]{:S(2)}) collective-permute-start(bf16[32,3584]{1,0:T(8,128)(2,1)S(1)} %get-tuple-element.36), channel_id=1, source_target_pairs={{16,0},{24,8},{0,16},{8,24},{17,1},{25,9},{1,17},{9,25},{18,2},{26... | collective-permute-start | bytes 688136 | tf_op jit(solution)/shard_map/ppermute | solution.py:54
  207.5 4.9 %collective-permute-start.44 = (bf16[32,3584]{1,0:T(8,128)(2,1)S(1)}, bf16[32,3584]{1,0:T(8,128)(2,1)S(1)}, u32[]{:S(2)}, u32[]{:S(2)}) collective-permute-start(bf16[32,3584]{1,0:T(8,128)(2,1)S(1)} %get-tuple-element.35), channel_id=1, source_target_pairs={{8,0},{16,8},{24,16},{0,24},{9,1},{17,9},{25,17},{1,25},{10,2},{18... | collective-permute-start | bytes 688136 | tf_op jit(solution)/shard_map/ppermute | solution.py:54
  213.3 11.9 %all-to-all-start.1 = ((bf16[4,2,8,3584]{3,2,1,0:T(8,128)(2,1)}), bf16[4,2,8,3584]{3,2,1,0:T(8,128)(2,1)S(1)}, u32[]{:S(2)}, u32[]{:S(2)}) async-start(bf16[4,2,8,3584]{3,2,1,0:T(8,128)(2,1)} %pad_maximum_fusion.7), calls=%async_computation.1 | async-start | bytes 917504 | tf_op jit(solution)/shard_map/all_to_all | solution.py:214
  216.8 16.1 %collective-permute-start.8 = (bf16[8,3584]{1,0:T(8,128)(2,1)S(1)}, bf16[8,3584]{1,0:T(8,128)(2,1)S(1)}, u32[]{:S(2)}, u32[]{:S(2)}) collective-permute-start(bf16[8,3584]{1,0:T(8,128)(2,1)S(1)} %broadcast_select_fusion), channel_id=1, source_target_pairs={{0,1},{1,0},{2,3},{3,2},{4,5},{5,4},{6,7},{7,6},{8,9},{9,8},{10,11... | collective-permute-start | bytes 172040 | tf_op jit(solution)/shard_map/ppermute | solution.py:58
  225.3 8.6 %collective-permute-start.45 = (bf16[8,3584]{1,0:T(8,128)(2,1)S(1)}, bf16[8,3584]{1,0:T(8,128)(2,1)S(1)}, u32[]{:S(2)}, u32[]{:S(2)}) collective-permute-start(bf16[8,3584]{1,0:T(8,128)(2,1)S(1)} %get-tuple-element.40), channel_id=1, source_target_pairs={{0,1},{1,0},{2,3},{3,2},{4,5},{5,4},{6,7},{7,6},{8,9},{9,8},{10,11... | collective-permute-start | bytes 172040 | tf_op jit(solution)/shard_map/ppermute | solution.py:58
  (25 other events, 169.3 us)

commit v2 on v1

v2 whole, which is shorter than its diff:
```python
import jax
import jax.numpy as jnp
from jax import lax
from jax.sharding import Mesh, PartitionSpec as P

score_scale = 192.0 ** (-0.5)
route_scale = 2.5
norm_eps = 1e-06
f32 = jnp.float32
bf16 = jnp.bfloat16


def attend(query_rows, cache_rows, fresh_key, context_lengths, latent_width):
    scores = (
        jnp.einsum("rhc,rtc->rht", query_rows, cache_rows, preferred_element_type=jnp.float32)
        * score_scale
    )
    own_score = (
        jnp.einsum("rhc,rc->rh", query_rows, fresh_key, preferred_element_type=jnp.float32)
        * score_scale
    )
    positions = lax.broadcasted_iota(jnp.int32, scores.shape, 2)
    scores = jnp.where(positions < context_lengths[:, None, None], scores, -jnp.inf)
    row_max = jnp.maximum(jnp.max(scores, axis=2), own_score)
    cache_weights = jnp.exp(scores - row_max[:, :, None])
    own_weight = jnp.exp(own_score - row_max)
    denominator = jnp.sum(cache_weights, axis=2) + own_weight
    cache_weights = (cache_weights / denominator[:, :, None]).astype(jnp.bfloat16)
    own_weight = (own_weight / denominator).astype(jnp.bfloat16)
    own_weight = lax.optimization_barrier(own_weight).astype(jnp.float32)
    result = jnp.einsum(
        "rht,rtl->rhl",
        cache_weights,
        cache_rows[:, :, :latent_width],
        preferred_element_type=jnp.float32,
    )
    result = result + own_weight[:, :, None] * fresh_key[:, None, :latent_width].astype(jnp.float32)
    return result.astype(jnp.bfloat16)


def combine_table(expert_ids, gates, expert_slots):
    slot_count = expert_slots.shape[0]
    labels = lax.broadcasted_iota(jnp.int32, (1, 1, slot_count), 2)
    slot_of = jnp.sum(
        jnp.where(expert_ids[:, :, None] == labels, expert_slots[None, None, :], 0), axis=2
    )
    slot_hits = slot_of[:, :, None] == labels
    weight_table = jnp.sum(jnp.where(slot_hits, gates[:, :, None].astype(jnp.float32), 0.0), axis=1)
    return weight_table.astype(jnp.bfloat16)


near_axis = ("y", "z")
far_axis = ("z", "y")


def ring(axes, distance):
    pairs = []
    for y in range(4):
        for z in range(4):
            for core in range(2):
                if axes[core] == "y":
                    source = ((y + distance) % 4, z)
                else:
                    source = (y, (z + distance) % 4)
                pairs.append(((source[0] * 4 + source[1]) * 2 + core, (y * 4 + z) * 2 + core))
    return pairs


def shift(value, axes, distance):
    if axes == "x":
        return lax.ppermute(value, "x", [((i + distance) % 4, i) for i in range(4)])
    return lax.ppermute(value, ("y", "z", "core"), ring(axes, distance))


def swap(value):
    return lax.ppermute(value, "core", [(0, 1), (1, 0)])


def total(*terms):
    return sum(term.astype(f32) for term in terms)


def gather_near(block, axes):
    return jnp.stack([block, shift(block, axes, 1), shift(block, axes, 2), shift(block, axes, -1)])


def gather_far(block, axes):
    half = block.shape[0] // 2
    right, left = shift(block, axes, 1), shift(block, axes, -1)
    low, high = shift(right[:half], axes, 1), shift(left[half:], axes, -1)
    return [block, right, jnp.concatenate([low, high], axis=0), left]


def scatter_far(own, right, opposite, left, axes):
    half = own.shape[0] // 2
    low, high = shift(opposite[:half], axes, -1), shift(opposite[half:], axes, 1)
    right = jnp.concatenate([total(right[:half], low).astype(bf16), right[half:]], axis=0)
    left = jnp.concatenate([left[:half], total(left[half:], high).astype(bf16)], axis=0)
    return total(own, shift(right, axes, -1), shift(left, axes, 1)).astype(bf16)


def scatter_near(value, axes):
    return total(
        value[0], shift(value[1], axes, -1), shift(value[2], axes, 2), shift(value[3], axes, 1)
    )


def per_device(
    residual_in,
    query_latent,
    latent_cache,
    new_latent,
    context_lengths,
    value_up,
    out_proj,
    norm_gain,
    expert_ids,
    route_scores,
    expert_slots,
    expert_gate_up,
    expert_down,
):
    rows, model_width = residual_in.shape
    latent_width = value_up.shape[1]
    half = model_width // 2
    lanes = 128
    core = lax.axis_index("core")
    x_at = lax.axis_index("x")
    expert_at = lax.axis_index("y") * 4 + lax.axis_index("z")

    def mine(value, axis):
        return lax.dynamic_slice_in_dim(value, core * half, half, axis=axis)

    def others(value, axis):
        return lax.dynamic_slice_in_dim(value, (1 - core) * half, half, axis=axis)

    def by_core(own, got):
        return jnp.where(core == 0, jnp.stack([own, got]), jnp.stack([got, own]))

    def to_tokens(chip):
        own = jnp.where(core == 0, chip[0], chip[1])
        got = swap(jnp.where(core == 0, chip[1], chip[0]))
        return jnp.where(
            core == 0,
            jnp.concatenate([own, got], axis=1),
            jnp.concatenate([got, own], axis=1),
        )

    gates = (route_scale * route_scores / jnp.sum(route_scores, axis=1, keepdims=True)).astype(bf16)
    table = combine_table(expert_ids, gates, expert_slots)
    table = jnp.pad(table, ((0, 0), (0, lanes - table.shape[1])))

    latent_out = attend(query_latent, latent_cache, new_latent, context_lengths, latent_width)
    exchanged = lax.all_to_all(latent_out, ("x", "core"), split_axis=1, concat_axis=0, tiled=True)

    gate_up = expert_gate_up[0]
    down = expert_down[0]
    gate_up_own = mine(gate_up, 1)
    gate_up_got = swap(others(gate_up, 1))
    weight_in = jnp.concatenate(
        [gate_up_own[0], gate_up_own[1], gate_up_got[0], gate_up_got[1]], axis=1
    )
    weight_in = jnp.pad(weight_in, ((0, lanes), (0, 0)))
    weight_out = jnp.concatenate([mine(down, 1), swap(others(down, 1))], axis=0)

    chip_rows = by_core(
        jnp.concatenate([mine(residual_in, 1), table], axis=1),
        swap(jnp.concatenate([others(residual_in, 1), table], axis=1)),
    ).reshape(2 * rows, half + lanes)
    chip_residual, chip_table = chip_rows[:, :half], chip_rows[:, half:]

    values = jnp.einsum(
        "thl,hlv->thv", exchanged, value_up, preferred_element_type=f32
    ).astype(bf16)
    values = values.reshape(values.shape[0], values.shape[1] * values.shape[2])
    projected = jnp.dot(values, out_proj, preferred_element_type=f32)
    chip_sum = mine(projected, 1) + swap(others(projected, 1).astype(bf16)).astype(f32)
    chip_sum = chip_sum.reshape(4, 2 * rows, half)

    def for_chip(distance):
        place = lax.rem(x_at + distance, 4)
        return lax.dynamic_index_in_dim(chip_sum, place, axis=0, keepdims=False)

    attention = total(
        for_chip(0),
        shift(for_chip(1).astype(bf16), "x", -1),
        shift(for_chip(2).astype(bf16), "x", 2),
        shift(for_chip(3).astype(bf16), "x", 1),
    ).astype(bf16)
    residual_f32 = total(chip_residual, attention).astype(bf16).astype(f32)
    squares = jnp.sum(residual_f32 * residual_f32, axis=1, keepdims=True)
    squares = squares + swap(squares)
    scaling = lax.rsqrt(squares / model_width + norm_eps)
    gain = mine(norm_gain, 0).astype(f32)
    normed = (residual_f32 * scaling * gain[None, :]).astype(bf16)
    payload = jnp.concatenate([normed, chip_table], axis=1)

    width = half + lanes
    group = gather_near(payload, "x").reshape(8 * rows, width)
    near = gather_near(group, near_axis).reshape(4, 4, 2, rows, width)

    chunks = [near[:, :, c].reshape(16 * rows, width) for c in range(2)]
    hidden = weight_in.shape[1] // 2
    units = hidden // 2

    def crossed(value):
        value = value.reshape(4, 4, 4 * rows, value.shape[1])
        return value.transpose(1, 0, 2, 3).reshape(64 * rows, value.shape[3])

    sums = []
    for chunk in chunks:
        blocks = gather_far(chunk, far_axis)
        products = [jnp.dot(b, weight_in, preferred_element_type=f32) for b in blocks]
        got = swap(jnp.concatenate([p[:, hidden:].astype(bf16) for p in products], axis=0))
        product = jnp.concatenate([p[:, :hidden] for p in products], axis=0)
        product = product + crossed(got).astype(f32)
        activated = (jax.nn.silu(product[:, :units]) * product[:, units:]).astype(bf16)
        activated = jnp.concatenate([activated, crossed(swap(activated))], axis=1)
        outs = []
        n = 16 * rows
        for i, b in enumerate(blocks):
            weights = jnp.sum(
                jnp.where(
                    lax.broadcasted_iota(jnp.int32, (1, lanes), 1) == expert_at,
                    b[:, half:].astype(f32),
                    0.0,
                ),
                axis=1,
                keepdims=True,
            )
            out = jnp.dot(activated[i * n : (i + 1) * n], weight_out, preferred_element_type=f32)
            outs.append((out * weights).astype(bf16))
        back = scatter_far(*outs, far_axis).reshape(4, 4 * rows, half)
        sums.append(scatter_near(back, near_axis).astype(bf16))
    to_x = jnp.stack([s.reshape(4, rows, half) for s in sums], axis=1)
    chip_out = scatter_near(to_x, "x")

    attention_out = to_tokens(attention.reshape(2, rows, half))
    expert_sum = to_tokens(chip_out.astype(bf16))
    residual_mid = total(residual_in, attention_out).astype(bf16)
    layer_output = total(residual_mid, expert_sum).astype(bf16)
    return (attention_out, layer_output)


def solution(mesh):
    torus = Mesh(mesh.devices.reshape(4, 4, 4, 2), ("y", "z", "x", "core"))
    dp, tp = ("y", "z"), ("x", "core")
    both = dp + tp
    placed = (
        P(both, None),
        P(both, None, None),
        P(both, None, None),
        P(both, None),
        P(both),
        P(tp, None, None),
        P(tp, None),
        P(),
        P(both, None),
        P(both, None),
        P(),
        P(dp, None, None, tp),
        P(dp, tp, None),
    )
    return jax.shard_map(
        per_device,
        mesh=torus,
        in_specs=placed,
        out_specs=(P(both, None), P(both, None)),
        check_vma=False,
    )
```

time: 235 us -> 191 us (0.81)
  starting transfers between devices: 88.2 us -> 71.6 us
  blocking collectives: 12.2 us -> 0 us
  waiting for transfers between devices: 78.3 us -> 68.8 us
  local copies, waits for them, and re-layouts: 11.8 us -> 6.98 us
    ppermute x34, waiting for transfers between devices: 74.3 us -> 58.9 us  [the longest x25 47.5 us: shift(): return lax.ppermute(value, ('y', 'z', 'core'), ring(axes, distance))]
    all_gather x1 -> x0, blocking collectives: 12.2 us -> none  [per_device(): group_table = lax.all_gather(table, ('x', 'core'), axis=0, tiled=True)]
    ppermute x12 -> x11, starting transfers between devices: 35 us -> 23.6 us  [swap(): return lax.ppermute(value, 'core', [(0, 1), (1, 0)])]
    all_to_all x1, waiting for transfers between devices: 0.01 us -> 8.21 us  [per_device(): lax.all_to_all(latent_out, ('x', 'core'), split_axis=1, concat_axis=0, ti...]
    all_to_all x1 -> x0, starting transfers between devices: 3.46 us -> none  [per_device(): from_x = lax.all_to_all(to_x, 'x', split_axis=0, concat_axis=0, tiled=True)]
    ppermute x34, starting transfers between devices: 45.3 us -> 42.2 us  [the longest x25 33.7 us: shift(): return lax.ppermute(value, ('y', 'z', 'core'), ring(axes, distance))]
  transfers between devices with their start and end apart: 48 -> 46, of which waited for: 26 -> 20; matrix products, arithmetic and copies ran while one was open for 21% -> 21% of each run, Pallas kernels for 0% -> 0%
where the time goes in v2:
time: 191 us; the launch traced here: 190 us
  starting transfers between devices  71.6 us (37%)
  waiting for transfers between devices  68.8 us (36%)
  matrix products  32.6 us (17%)
  other arithmetic  8.74 us (5%)
  local copies, waits for them, and re-layouts  6.98 us (4%)
    ppermute x25, waiting for transfers between devices, shift(): return lax.ppermute(value, ('y', 'z', 'core'), ring(axes, distance))  47.5 us
    ppermute x25, starting transfers between devices, shift(): return lax.ppermute(value, ('y', 'z', 'core'), ring(axes, distance))  33.7 us
    ppermute x11, starting transfers between devices, swap(): return lax.ppermute(value, 'core', [(0, 1), (1, 0)])  23.6 us
    dot_general x8, matrix products, per_device(): jnp.dot(activated[i * n:(i + 1) * n], weight_out, preferred_element_type=...  13.2 us
    ppermute x9, waiting for transfers between devices, shift(): return lax.ppermute(value, 'x', [((i + distance) % 4, i) for i in range(4)])  11.4 us
    ppermute x9, starting transfers between devices, shift(): return lax.ppermute(value, 'x', [((i + distance) % 4, i) for i in range(4)])  8.46 us
    all_to_all x1, waiting for transfers between devices, per_device(): lax.all_to_all(latent_out, ('x', 'core'), split_axis=1, concat_axis=0, ti...  8.21 us
    dot_general x1, matrix products, per_device(): projected = jnp.dot(values, out_proj, preferred_element_type=f32)  8.06 us
  transfers between devices with their start and end apart: 46, of which 20 were waited for; matrix products, arithmetic and copies ran while one was open for 21% of the time, Pallas kernels for 0%

profile of v2, /device:TPU:1, one launch (start us, length us, event | category | flops | bytes accessed | tf_op | source)
XLA Modules:
  0.0 190.4 jit_solution(15586292045716440150)
XLA Ops:
  1.4 1.4 fusion.83
  2.8 3.1 %fusion.103 = (f32[8,64]{1,0:T(8,128)S(1)}, f32[8,64,384]{2,1,0:T(8,128)S(1)}) fusion(bf16[8,64,576]{2,1,0:T(8,128)(2,1)} %param.14, bf16[8,384,576]{1,2,0:T(8,128)(2,1)} %param.15, s32[8]{0:T(128)} %param.17), kind=kOutput, calls=%fused_computation.209 | convolution fusion | flops 227278336 | bytes 4917280 | tf_op jit(solution)/shard_map/rhc,rtc->rht/dot_general | solution.py:15
  8.6 5.8 %all-to-all-start = ((bf16[8,64,512]{2,0,1:T(8,128)(2,1)}), bf16[8,64,512]{2,0,1:T(8,128)(2,1)S(1)}, u32[]{:S(2)}, u32[]{:S(2)}) async-start(bf16[8,64,512]{2,0,1:T(8,128)(2,1)} %copy.43), calls=%async_computation | async-start | bytes 1048576 | tf_op jit(solution)/shard_map/all_to_all | solution.py:154
  15.7 8.2 %all-to-all-done = bf16[8,64,512]{2,0,1:T(8,128)(2,1)S(1)} async-done(((bf16[8,64,512]{2,0,1:T(8,128)(2,1)}), bf16[8,64,512]{2,0,1:T(8,128)(2,1)S(1)}, u32[]{:S(2)}, u32[]{:S(2)}) %all-to-all-start) | async-done | bytes 524320 | tf_op jit(solution)/shard_map/all_to_all | solution.py:154
  24.2 8.1 %fusion.51 = f32[64,7168]{1,0:T(8,128)S(1)} fusion(bf16[1024,7168]{1,0:T(8,128)(2,1)} %param.19, bf16[8,8,8,128]{3,2,1,0:T(8,128)(2,1)S(1)} %fusion.32), kind=kOutput, calls=%fused_computation.118 | convolution fusion | flops 939524096 | bytes 16646144 | tf_op jit(solution)/shard_map/dot_general | solution.py:176
  33.3 1.4 dynamic-slice_bitcast_fusion
  35.4 1.8 collective-permute-start.2
  38.8 2.4 %collective-permute-done.1 = bf16[16,3584]{1,0:T(8,128)(2,1)S(1)} collective-permute-done((bf16[16,3584]{1,0:T(8,128)(2,1)S(1)}, bf16[16,3584]{1,0:T(8,128)(2,1)S(1)}, u32[]{:S(2)}, u32[]{:S(2)}) %collective-permute-start.1) | collective-permute-done | bytes 114720 | tf_op jit(solution)/shard_map/ppermute | solution.py:71
  43.5 1.7 collective-permute-start.6
  46.1 2.2 %collective-permute-start.7 = (bf16[16,3712]{1,0:T(8,128)(2,1)S(1)}, bf16[16,3712]{1,0:T(8,128)(2,1)S(1)}, u32[]{:S(2)}, u32[]{:S(2)}) collective-permute-start(bf16[16,3712]{1,0:T(8,128)(2,1)S(1)} %get-tuple-element.40), channel_id=1, source_target_pairs={{2,0},{4,2},{6,4},{0,6},{3,1},{5,3},{7,5},{1,7},{10,8},{12,10},{14... | collective-permute-start | bytes 356360 | tf_op jit(solution)/shard_map/ppermute | solution.py:71
  51.1 3.0 %collective-permute-done.8 = bf16[16,3712]{1,0:T(8,128)(2,1)S(1)} collective-permute-done((bf16[16,3712]{1,0:T(8,128)(2,1)S(1)}, bf16[16,3712]{1,0:T(8,128)(2,1)S(1)}, u32[]{:S(2)}, u32[]{:S(2)}) %collective-permute-start.8) | collective-permute-done | bytes 118816 | tf_op jit(solution)/shard_map/ppermute | solution.py:71
  54.2 2.8 %collective-permute-done.9 = bf16[16,3712]{1,0:T(8,128)(2,1)S(1)} collective-permute-done((bf16[16,3712]{1,0:T(8,128)(2,1)S(1)}, bf16[16,3712]{1,0:T(8,128)(2,1)S(1)}, u32[]{:S(2)}, u32[]{:S(2)}) %collective-permute-start.9) | collective-permute-done | bytes 118816 | tf_op jit(solution)/shard_map/ppermute | solution.py:71
  57.1 3.8 %collective-permute-start.10 = (bf16[64,3712]{1,0:T(8,128)(2,1)S(1)}, bf16[64,3712]{1,0:T(8,128)(2,1)S(1)}, u32[]{:S(2)}, u32[]{:S(2)}) collective-permute-start(bf16[64,3712]{1,0:T(8,128)(2,1)S(1)} %bitcast.145), channel_id=1, source_target_pairs={{32,0},{9,1},{40,8},{17,9},{48,16},{25,17},{56,24},{1,25},{64,32},... | collective-permute-start | bytes 1425416 | tf_op jit(solution)/shard_map/ppermute | solution.py:72
  61.6 1.6 dynamic-slice_bitcast_fusion.2
  63.2 8.4 %collective-permute-done.10 = bf16[64,3712]{1,0:T(8,128)(2,1)S(1)} collective-permute-done((bf16[64,3712]{1,0:T(8,128)(2,1)S(1)}, bf16[64,3712]{1,0:T(8,128)(2,1)S(1)}, u32[]{:S(2)}, u32[]{:S(2)}) %collective-permute-start.10) | collective-permute-done | bytes 475168 | tf_op jit(solution)/shard_map/ppermute | solution.py:72
  71.6 3.4 %collective-permute-done.12 = bf16[64,3712]{1,0:T(8,128)(2,1)S(1)} collective-permute-done((bf16[64,3712]{1,0:T(8,128)(2,1)S(1)}, bf16[64,3712]{1,0:T(8,128)(2,1)S(1)}, u32[]{:S(2)}, u32[]{:S(2)}) %collective-permute-start.12) | collective-permute-done | bytes 475168 | tf_op jit(solution)/shard_map/ppermute | solution.py:72
  75.5 2.5 %collective-permute-start.28 = (bf16[128,3712]{1,0:T(8,128)(2,1)S(1)}, bf16[128,3712]{1,0:T(8,128)(2,1)S(1)}, u32[]{:S(2)}, u32[]{:S(2)}) collective-permute-start(bf16[128,3712]{1,0:T(8,128)(2,1)S(1)} %bitcast.134), channel_id=1, source_target_pairs={{8,0},{33,1},{16,8},{41,9},{24,16},{49,17},{0,24},{57,25},{40,32},... | collective-permute-start | bytes 2850824 | tf_op jit(solution)/shard_map/ppermute | solution.py:72
  78.0 2.7 %collective-permute-start.14 = (bf16[128,3712]{1,0:T(8,128)(2,1)S(1)}, bf16[128,3712]{1,0:T(8,128)(2,1)S(1)}, u32[]{:S(2)}, u32[]{:S(2)}) collective-permute-start(bf16[128,3712]{1,0:T(8,128)(2,1)S(1)} %bitcast.138), channel_id=1, source_target_pairs={{8,0},{33,1},{16,8},{41,9},{24,16},{49,17},{0,24},{57,25},{40,32},... | collective-permute-start | bytes 2850824 | tf_op jit(solution)/shard_map/ppermute | solution.py:72
  80.7 1.6 slice_bitcast_fusion.1
  82.2 2.2 %fusion.22 = bf16[3712,512]{1,0:T(8,128)(2,1)S(1)} fusion(bf16[3584,128]{1,0:T(8,128)(2,1)S(1)} %get-tuple-element.21, bf16[3584,128]{1,0:T(8,128)(2,1)S(1)} %get-tuple-element.20, bf16[3584,128]{1,0:T(8,128)(2,1)S(1)} %get-tuple-element.15, bf16[3584,128]{1,0:T(8,128)(2,1)S(1)} %get-tuple-element.14), kind=kLoop, calls=%fused_computation.31 | loop fusion | flops 24707072 | bytes 7471104 | tf_op jit(solution)/shard_map/concatenate | solution.py:160
  85.9 2.8 %collective-permute-done.28 = bf16[128,3712]{1,0:T(8,128)(2,1)S(1)} collective-permute-done((bf16[128,3712]{1,0:T(8,128)(2,1)S(1)}, bf16[128,3712]{1,0:T(8,128)(2,1)S(1)}, u32[]{:S(2)}, u32[]{:S(2)}) %collective-permute-start.28) | collective-permute-done | bytes 950304 | tf_op jit(solution)/shard_map/ppermute | solution.py:72
  88.7 3.5 %collective-permute-start.29 = (bf16[64,3712]{1,0:T(8,128)(2,1)S(1)}, bf16[64,3712]{1,0:T(8,128)(2,1)S(1)}, u32[]{:S(2)}, u32[]{:S(2)}) collective-permute-start(bf16[64,3712]{1,0:T(8,128)(2,1)S(1)} %slice.378), channel_id=1, source_target_pairs={{8,0},{33,1},{16,8},{41,9},{24,16},{49,17},{0,24},{57,25},{40,32},... | collective-permute-start | bytes 1425416 | tf_op jit(solution)/shard_map/ppermute | solution.py:72
  93.7 8.6 %collective-permute-done.16 = bf16[128,3712]{1,0:T(8,128)(2,1)S(1)} collective-permute-done((bf16[128,3712]{1,0:T(8,128)(2,1)S(1)}, bf16[128,3712]{1,0:T(8,128)(2,1)S(1)}, u32[]{:S(2)}, u32[]{:S(2)}) %collective-permute-start.16) | collective-permute-done | bytes 950304 | tf_op jit(solution)/shard_map/ppermute | solution.py:72
  103.9 1.5 collective-permute-start.17
  105.5 1.9 collective-permute-done.31
  108.1 3.7 %collective-permute-start.32 = (bf16[512,256]{1,0:T(8,128)(2,1)S(1)}, bf16[512,256]{1,0:T(8,128)(2,1)S(1)}, u32[]{:S(2)}, u32[]{:S(2)}) collective-permute-start(bf16[512,256]{1,0:T(8,128)(2,1)S(1)} %pad_maximum_fusion.8), channel_id=1, source_target_pairs={{0,1},{1,0},{2,3},{3,2},{4,5},{5,4},{6,7},{7,6},{8,9},{9,8},{10,11... | collective-permute-start | bytes 786440 | tf_op jit(solution)/shard_map/ppermute | solution.py:76
  113.8 4.6 %collective-permute-start.18 = (bf16[512,256]{1,0:T(8,128)(2,1)S(1)}, bf16[512,256]{1,0:T(8,128)(2,1)S(1)}, u32[]{:S(2)}, u32[]{:S(2)}) collective-permute-start(bf16[512,256]{1,0:T(8,128)(2,1)S(1)} %pad_maximum_fusion.7), channel_id=1, source_target_pairs={{0,1},{1,0},{2,3},{3,2},{4,5},{5,4},{6,7},{7,6},{8,9},{9,8},{10,11... | collective-permute-start | bytes 786440 | tf_op jit(solution)/shard_map/ppermute | solution.py:76
  120.9 1.6 fusion.18
  122.6 1.6 fusion.17
  124.3 2.7 %collective-permute-start.36 = (bf16[64,3584]{1,0:T(8,128)(2,1)S(1)}, bf16[64,3584]{1,0:T(8,128)(2,1)S(1)}, u32[]{:S(2)}, u32[]{:S(2)}) collective-permute-start(bf16[64,3584]{1,0:T(8,128)(2,1)S(1)} %get-tuple-element.31), channel_id=1, source_target_pairs={{8,0},{33,1},{16,8},{41,9},{24,16},{49,17},{0,24},{57,25},{40,32},... | collective-permute-start | bytes 1376264 | tf_op jit(solution)/shard_map/ppermute | solution.py:72
  127.0 1.6 fusion.19
  128.7 1.6 fusion.10
  130.7 1.6 fusion.9
  132.3 2.7 %collective-permute-start.23 = (bf16[64,3584]{1,0:T(8,128)(2,1)S(1)}, bf16[64,3584]{1,0:T(8,128)(2,1)S(1)}, u32[]{:S(2)}, u32[]{:S(2)}) collective-permute-start(bf16[64,3584]{1,0:T(8,128)(2,1)S(1)} %get-tuple-element.26), channel_id=1, source_target_pairs={{8,0},{33,1},{16,8},{41,9},{24,16},{49,17},{0,24},{57,25},{40,32},... | collective-permute-start | bytes 1376264 | tf_op jit(solution)/shard_map/ppermute | solution.py:72
  135.1 1.6 fusion.11
  137.2 2.7 %collective-permute-start.37 = (bf16[128,3584]{1,0:T(8,128)(2,1)S(1)}, bf16[128,3584]{1,0:T(8,128)(2,1)S(1)}, u32[]{:S(2)}, u32[]{:S(2)}) collective-permute-start(bf16[128,3584]{1,0:T(8,128)(2,1)S(1)} %pad_maximum_fusion.5), channel_id=1, source_target_pairs={{8,0},{33,1},{16,8},{41,9},{24,16},{49,17},{0,24},{57,25},{40,32},... | collective-permute-start | bytes 2752520 | tf_op jit(solution)/shard_map/ppermute | solution.py:72
  140.7 3.5 %collective-permute-start.24 = (bf16[128,3584]{1,0:T(8,128)(2,1)S(1)}, bf16[128,3584]{1,0:T(8,128)(2,1)S(1)}, u32[]{:S(2)}, u32[]{:S(2)}) collective-permute-start(bf16[128,3584]{1,0:T(8,128)(2,1)S(1)} %pad_maximum_fusion.3), channel_id=1, source_target_pairs={{8,0},{33,1},{16,8},{41,9},{24,16},{49,17},{0,24},{57,25},{40,32},... | collective-permute-start | bytes 2752520 | tf_op jit(solution)/shard_map/ppermute | solution.py:72
  144.1 6.6 %collective-permute-done.35 = bf16[128,3584]{1,0:T(8,128)(2,1)S(1)} collective-permute-done((bf16[128,3584]{1,0:T(8,128)(2,1)S(1)}, bf16[128,3584]{1,0:T(8,128)(2,1)S(1)}, u32[]{:S(2)}, u32[]{:S(2)}) %collective-permute-start.35) | collective-permute-done | bytes 917536 | tf_op jit(solution)/shard_map/ppermute | solution.py:72
  150.7 1.8 fusion.16
  153.5 1.9 collective-permute-start.40
  155.3 9.0 %collective-permute-done.22 = bf16[128,3584]{1,0:T(8,128)(2,1)S(1)} collective-permute-done((bf16[128,3584]{1,0:T(8,128)(2,1)S(1)}, bf16[128,3584]{1,0:T(8,128)(2,1)S(1)}, u32[]{:S(2)}, u32[]{:S(2)}) %collective-permute-start.22) | collective-permute-done | bytes 917536 | tf_op jit(solution)/shard_map/ppermute | solution.py:72
  164.3 1.8 fusion.8
  166.2 1.5 collective-permute-start.25
  167.6 2.5 %collective-permute-start.27 = (bf16[32,3584]{1,0:T(8,128)(2,1)S(1)}, bf16[32,3584]{1,0:T(8,128)(2,1)S(1)}, u32[]{:S(2)}, u32[]{:S(2)}) collective-permute-start(bf16[32,3584]{1,0:T(8,128)(2,1)S(1)} %get-tuple-element.23), channel_id=1, source_target_pairs={{32,0},{9,1},{40,8},{17,9},{48,16},{25,17},{56,24},{1,25},{64,32},... | collective-permute-start | bytes 688136 | tf_op jit(solution)/shard_map/ppermute | solution.py:72
  170.2 4.8 %collective-permute-done.25 = bf16[32,3584]{1,0:T(8,128)(2,1)S(1)} collective-permute-done((bf16[32,3584]{1,0:T(8,128)(2,1)S(1)}, bf16[32,3584]{1,0:T(8,128)(2,1)S(1)}, u32[]{:S(2)}, u32[]{:S(2)}) %collective-permute-start.25) | collective-permute-done | bytes 229408 | tf_op jit(solution)/shard_map/ppermute | solution.py:72
  175.9 1.8 collective-permute-start.42
  178.6 5.2 %collective-permute-start.4 = (bf16[8,3584]{1,0:T(8,128)(2,1)S(1)}, bf16[8,3584]{1,0:T(8,128)(2,1)S(1)}, u32[]{:S(2)}, u32[]{:S(2)}) collective-permute-start(bf16[8,3584]{1,0:T(8,128)(2,1)S(1)} %get-tuple-element.41), channel_id=1, source_target_pairs={{0,1},{1,0},{2,3},{3,2},{4,5},{5,4},{6,7},{7,6},{8,9},{9,8},{10,11... | collective-permute-start | bytes 172040 | tf_op jit(solution)/shard_map/ppermute | solution.py:76
  183.9 4.9 %collective-permute-start.44 = (bf16[8,3584]{1,0:T(8,128)(2,1)S(1)}, bf16[8,3584]{1,0:T(8,128)(2,1)S(1)}, u32[]{:S(2)}, u32[]{:S(2)}) collective-permute-start(bf16[8,3584]{1,0:T(8,128)(2,1)S(1)} %get-tuple-element.44), channel_id=1, source_target_pairs={{0,1},{1,0},{2,3},{3,2},{4,5},{5,4},{6,7},{7,6},{8,9},{9,8},{10,11... | collective-permute-start | bytes 172040 | tf_op jit(solution)/shard_map/ppermute | solution.py:76
  (199 shorter events, 31.3 us)
Async XLA Ops:
  0.6 23.3 %copy-start = (bf16[8,512,128]{2,1,0:T(8,128)(2,1)S(1)}, bf16[8,512,128]{2,1,0:T(8,128)(2,1)}, u32[]{:S(2)}) copy-start(bf16[8,512,128]{2,1,0:T(8,128)(2,1)} %param.18) | copy-start | bytes 3145732
  8.6 15.3 %all-to-all-start = ((bf16[8,64,512]{2,0,1:T(8,128)(2,1)}), bf16[8,64,512]{2,0,1:T(8,128)(2,1)S(1)}, u32[]{:S(2)}, u32[]{:S(2)}) async-start(bf16[8,64,512]{2,0,1:T(8,128)(2,1)} %copy.43), calls=%async_computation | async-start | bytes 1048576 | tf_op jit(solution)/shard_map/all_to_all | solution.py:154
  15.7 22.1 %collective-permute-start.5 = (bf16[8,3712]{1,0:T(8,128)(2,1)}, bf16[8,3712]{1,0:T(8,128)(2,1)}, u32[]{:S(2)}, u32[]{:S(2)}) collective-permute-start(bf16[8,3712]{1,0:T(8,128)(2,1)} %get-tuple-element.50), channel_id=1, source_target_pairs={{0,1},{1,0},{2,3},{3,2},{4,5},{5,4},{6,7},{7,6},{8,9},{9,8},{10,11... | collective-permute-start | bytes 178184 | tf_op jit(solution)/shard_map/ppermute | solution.py:76
  32.4 2.5 %collective-permute-start = (bf16[64,3584]{1,0:T(8,128)(2,1)S(1)}, bf16[64,3584]{1,0:T(8,128)(2,1)S(1)}, u32[]{:S(2)}, u32[]{:S(2)}) collective-permute-start(bf16[64,3584]{1,0:T(8,128)(2,1)S(1)} %dynamic-slice_convert_fusion), channel_id=1, source_target_pairs={{0,1},{1,0},{2,3},{3,2},{4,5},{5,4},{6,7},{7,6},{8,9},{9,8},{10,11... | collective-permute-start | bytes 1376264 | tf_op jit(solution)/shard_map/ppermute | solution.py:76
  34.7 45.9 %collective-permute-start.13 = (bf16[2,3584,128]{2,1,0:T(8,128)(2,1)}, bf16[2,3584,128]{2,1,0:T(8,128)(2,1)}, u32[]{:S(2)}, u32[]{:S(2)}) collective-permute-start(bf16[2,3584,128]{2,1,0:T(8,128)(2,1)} %dynamic-slice_bitcast_fusion), channel_id=1, source_target_pairs={{0,1},{1,0},{2,3},{3,2},{4,5},{5,4},{6,7},{7,6},{8,9},{9,8},{10,11... | collective-permute-start | bytes 5505032 | tf_op jit(solution)/shard_map/ppermute | solution.py:76
  35.0 6.1 %collective-permute-start.1 = (bf16[16,3584]{1,0:T(8,128)(2,1)S(1)}, bf16[16,3584]{1,0:T(8,128)(2,1)S(1)}, u32[]{:S(2)}, u32[]{:S(2)}) collective-permute-start(bf16[16,3584]{1,0:T(8,128)(2,1)S(1)} %get-tuple-element.32), channel_id=1, source_target_pairs={{6,0},{0,2},{2,4},{4,6},{7,1},{1,3},{3,5},{5,7},{14,8},{8,10},{10,... | collective-permute-start | bytes 344072 | tf_op jit(solution)/shard_map/ppermute | solution.py:71
  35.4 7.0 %collective-permute-start.2 = (bf16[16,3584]{1,0:T(8,128)(2,1)S(1)}, bf16[16,3584]{1,0:T(8,128)(2,1)S(1)}, u32[]{:S(2)}, u32[]{:S(2)}) collective-permute-start(bf16[16,3584]{1,0:T(8,128)(2,1)S(1)} %get-tuple-element.34), channel_id=1, source_target_pairs={{4,0},{6,2},{0,4},{2,6},{5,1},{7,3},{1,5},{3,7},{12,8},{14,10},{8,... | collective-permute-start | bytes 344072 | tf_op jit(solution)/shard_map/ppermute | solution.py:71
  37.1 6.2 %collective-permute-start.3 = (bf16[16,3584]{1,0:T(8,128)(2,1)S(1)}, bf16[16,3584]{1,0:T(8,128)(2,1)S(1)}, u32[]{:S(2)}, u32[]{:S(2)}) collective-permute-start(bf16[16,3584]{1,0:T(8,128)(2,1)S(1)} %get-tuple-element.33), channel_id=1, source_target_pairs={{2,0},{4,2},{6,4},{0,6},{3,1},{5,3},{7,5},{1,7},{10,8},{12,10},{14... | collective-permute-start | bytes 344072 | tf_op jit(solution)/shard_map/ppermute | solution.py:71
  43.5 2.5 %collective-permute-start.6 = (f32[16,1]{0,1:T(1,128)S(1)}, f32[16,1]{0,1:T(1,128)S(1)}, u32[]{:S(2)}, u32[]{:S(2)}) collective-permute-start(f32[16,1]{0,1:T(1,128)S(1)} %bitcast.172), channel_id=1, source_target_pairs={{0,1},{1,0},{2,3},{3,2},{4,5},{5,4},{6,7},{7,6},{8,9},{9,8},{10,11... | collective-permute-start | bytes 200 | tf_op jit(solution)/shard_map/ppermute | solution.py:76
  46.1 5.0 %collective-permute-start.7 = (bf16[16,3712]{1,0:T(8,128)(2,1)S(1)}, bf16[16,3712]{1,0:T(8,128)(2,1)S(1)}, u32[]{:S(2)}, u32[]{:S(2)}) collective-permute-start(bf16[16,3712]{1,0:T(8,128)(2,1)S(1)} %get-tuple-element.40), channel_id=1, source_target_pairs={{2,0},{4,2},{6,4},{0,6},{3,1},{5,3},{7,5},{1,7},{10,8},{12,10},{14... | collective-permute-start | bytes 356360 | tf_op jit(solution)/shard_map/ppermute | solution.py:71
  48.4 5.8 %collective-permute-start.8 = (bf16[16,3712]{1,0:T(8,128)(2,1)S(1)}, bf16[16,3712]{1,0:T(8,128)(2,1)S(1)}, u32[]{:S(2)}, u32[]{:S(2)}) collective-permute-start(bf16[16,3712]{1,0:T(8,128)(2,1)S(1)} %get-tuple-element.40), channel_id=1, source_target_pairs={{4,0},{6,2},{0,4},{2,6},{5,1},{7,3},{1,5},{3,7},{12,8},{14,10},{8,... | collective-permute-start | bytes 356360 | tf_op jit(solution)/shard_map/ppermute | solution.py:71
  48.4 8.6 %collective-permute-start.9 = (bf16[16,3712]{1,0:T(8,128)(2,1)S(1)}, bf16[16,3712]{1,0:T(8,128)(2,1)S(1)}, u32[]{:S(2)}, u32[]{:S(2)}) collective-permute-start(bf16[16,3712]{1,0:T(8,128)(2,1)S(1)} %get-tuple-element.40), channel_id=1, source_target_pairs={{6,0},{0,2},{2,4},{4,6},{7,1},{1,3},{3,5},{5,7},{14,8},{8,10},{10,... | collective-permute-start | bytes 356360 | tf_op jit(solution)/shard_map/ppermute | solution.py:71
  49.2 71.7 %collective-permute-start.20 = (bf16[128,3584]{1,0:T(8,128)(2,1)S(1)}, bf16[128,3584]{1,0:T(8,128)(2,1)}, u32[]{:S(2)}, u32[]{:S(2)}) collective-permute-start(bf16[128,3584]{1,0:T(8,128)(2,1)S(1)} %get-tuple-element.19), channel_id=1, source_target_pairs={{0,1},{1,0},{2,3},{3,2},{4,5},{5,4},{6,7},{7,6},{8,9},{9,8},{10,11... | collective-permute-start | bytes 2752520 | tf_op jit(solution)/shard_map/ppermute | solution.py:76
  57.1 14.5 %collective-permute-start.10 = (bf16[64,3712]{1,0:T(8,128)(2,1)S(1)}, bf16[64,3712]{1,0:T(8,128)(2,1)S(1)}, u32[]{:S(2)}, u32[]{:S(2)}) collective-permute-start(bf16[64,3712]{1,0:T(8,128)(2,1)S(1)} %bitcast.145), channel_id=1, source_target_pairs={{32,0},{9,1},{40,8},{17,9},{48,16},{25,17},{56,24},{1,25},{64,32},... | collective-permute-start | bytes 1425416 | tf_op jit(solution)/shard_map/ppermute | solution.py:72
  60.9 10.7 %collective-permute-start.11 = (bf16[64,3712]{1,0:T(8,128)(2,1)S(1)}, bf16[64,3712]{1,0:T(8,128)(2,1)S(1)}, u32[]{:S(2)}, u32[]{:S(2)}) collective-permute-start(bf16[64,3712]{1,0:T(8,128)(2,1)S(1)} %bitcast.146), channel_id=1, source_target_pairs={{64,0},{17,1},{72,8},{25,9},{80,16},{1,17},{88,24},{9,25},{96,32},... | collective-permute-start | bytes 1425416 | tf_op jit(solution)/shard_map/ppermute | solution.py:72
  60.9 14.1 %collective-permute-start.12 = (bf16[64,3712]{1,0:T(8,128)(2,1)S(1)}, bf16[64,3712]{1,0:T(8,128)(2,1)S(1)}, u32[]{:S(2)}, u32[]{:S(2)}) collective-permute-start(bf16[64,3712]{1,0:T(8,128)(2,1)S(1)} %bitcast.147), channel_id=1, source_target_pairs={{96,0},{25,1},{104,8},{1,9},{112,16},{9,17},{120,24},{17,25},{0,32... | collective-permute-start | bytes 1425416 | tf_op jit(solution)/shard_map/ppermute | solution.py:72
  75.5 13.2 %collective-permute-start.28 = (bf16[128,3712]{1,0:T(8,128)(2,1)S(1)}, bf16[128,3712]{1,0:T(8,128)(2,1)S(1)}, u32[]{:S(2)}, u32[]{:S(2)}) collective-permute-start(bf16[128,3712]{1,0:T(8,128)(2,1)S(1)} %bitcast.134), channel_id=1, source_target_pairs={{8,0},{33,1},{16,8},{41,9},{24,16},{49,17},{0,24},{57,25},{40,32},... | collective-permute-start | bytes 2850824 | tf_op jit(solution)/shard_map/ppermute | solution.py:72
  78.0 14.2 %collective-permute-start.30 = (bf16[128,3712]{1,0:T(8,128)(2,1)S(1)}, bf16[128,3712]{1,0:T(8,128)(2,1)S(1)}, u32[]{:S(2)}, u32[]{:S(2)}) collective-permute-start(bf16[128,3712]{1,0:T(8,128)(2,1)S(1)} %bitcast.135), channel_id=1, source_target_pairs={{24,0},{97,1},{0,8},{105,9},{8,16},{113,17},{16,24},{121,25},{56,3... | collective-permute-start | bytes 2850824 | tf_op jit(solution)/shard_map/ppermute | solution.py:72
  78.0 25.0 %collective-permute-start.14 = (bf16[128,3712]{1,0:T(8,128)(2,1)S(1)}, bf16[128,3712]{1,0:T(8,128)(2,1)S(1)}, u32[]{:S(2)}, u32[]{:S(2)}) collective-permute-start(bf16[128,3712]{1,0:T(8,128)(2,1)S(1)} %bitcast.138), channel_id=1, source_target_pairs={{8,0},{33,1},{16,8},{41,9},{24,16},{49,17},{0,24},{57,25},{40,32},... | collective-permute-start | bytes 2850824 | tf_op jit(solution)/shard_map/ppermute | solution.py:72
  80.7 21.6 %collective-permute-start.16 = (bf16[128,3712]{1,0:T(8,128)(2,1)S(1)}, bf16[128,3712]{1,0:T(8,128)(2,1)S(1)}, u32[]{:S(2)}, u32[]{:S(2)}) collective-permute-start(bf16[128,3712]{1,0:T(8,128)(2,1)S(1)} %bitcast.139), channel_id=1, source_target_pairs={{24,0},{97,1},{0,8},{105,9},{8,16},{113,17},{16,24},{121,25},{56,3... | collective-permute-start | bytes 2850824 | tf_op jit(solution)/shard_map/ppermute | solution.py:72
  88.7 16.7 %collective-permute-start.29 = (bf16[64,3712]{1,0:T(8,128)(2,1)S(1)}, bf16[64,3712]{1,0:T(8,128)(2,1)S(1)}, u32[]{:S(2)}, u32[]{:S(2)}) collective-permute-start(bf16[64,3712]{1,0:T(8,128)(2,1)S(1)} %slice.378), channel_id=1, source_target_pairs={{8,0},{33,1},{16,8},{41,9},{24,16},{49,17},{0,24},{57,25},{40,32},... | collective-permute-start | bytes 1425416 | tf_op jit(solution)/shard_map/ppermute | solution.py:72
  92.2 15.1 %collective-permute-start.31 = (bf16[64,3712]{1,0:T(8,128)(2,1)S(1)}, bf16[64,3712]{1,0:T(8,128)(2,1)S(1)}, u32[]{:S(2)}, u32[]{:S(2)}) collective-permute-start(bf16[64,3712]{1,0:T(8,128)(2,1)S(1)} %slice.379), channel_id=1, source_target_pairs={{24,0},{97,1},{0,8},{105,9},{8,16},{113,17},{16,24},{121,25},{56,3... | collective-permute-start | bytes 1425416 | tf_op jit(solution)/shard_map/ppermute | solution.py:72
  103.8 8.1 %collective-permute-start.15 = (bf16[64,3712]{1,0:T(8,128)(2,1)S(1)}, bf16[64,3712]{1,0:T(8,128)(2,1)S(1)}, u32[]{:S(2)}, u32[]{:S(2)}) collective-permute-start(bf16[64,3712]{1,0:T(8,128)(2,1)S(1)} %slice.345), channel_id=1, source_target_pairs={{8,0},{33,1},{16,8},{41,9},{24,16},{49,17},{0,24},{57,25},{40,32},... | collective-permute-start | bytes 1425416 | tf_op jit(solution)/shard_map/ppermute | solution.py:72
  103.9 9.1 %collective-permute-start.17 = (bf16[64,3712]{1,0:T(8,128)(2,1)S(1)}, bf16[64,3712]{1,0:T(8,128)(2,1)S(1)}, u32[]{:S(2)}, u32[]{:S(2)}) collective-permute-start(bf16[64,3712]{1,0:T(8,128)(2,1)S(1)} %slice.346), channel_id=1, source_target_pairs={{24,0},{97,1},{0,8},{105,9},{8,16},{113,17},{16,24},{121,25},{56,3... | collective-permute-start | bytes 1425416 | tf_op jit(solution)/shard_map/ppermute | solution.py:72
  108.1 10.4 %collective-permute-start.32 = (bf16[512,256]{1,0:T(8,128)(2,1)S(1)}, bf16[512,256]{1,0:T(8,128)(2,1)S(1)}, u32[]{:S(2)}, u32[]{:S(2)}) collective-permute-start(bf16[512,256]{1,0:T(8,128)(2,1)S(1)} %pad_maximum_fusion.8), channel_id=1, source_target_pairs={{0,1},{1,0},{2,3},{3,2},{4,5},{5,4},{6,7},{7,6},{8,9},{9,8},{10,11... | collective-permute-start | bytes 786440 | tf_op jit(solution)/shard_map/ppermute | solution.py:76
  113.8 5.9 %collective-permute-start.18 = (bf16[512,256]{1,0:T(8,128)(2,1)S(1)}, bf16[512,256]{1,0:T(8,128)(2,1)S(1)}, u32[]{:S(2)}, u32[]{:S(2)}) collective-permute-start(bf16[512,256]{1,0:T(8,128)(2,1)S(1)} %pad_maximum_fusion.7), channel_id=1, source_target_pairs={{0,1},{1,0},{2,3},{3,2},{4,5},{5,4},{6,7},{7,6},{8,9},{9,8},{10,11... | collective-permute-start | bytes 786440 | tf_op jit(solution)/shard_map/ppermute | solution.py:76
  118.9 1.9 %collective-permute-start.33 = (bf16[512,128]{1,0:T(8,128)(2,1)S(1)}, bf16[512,128]{1,0:T(8,128)(2,1)S(1)}, u32[]{:S(2)}, u32[]{:S(2)}) collective-permute-start(bf16[512,128]{1,0:T(8,128)(2,1)S(1)} %fusion.38), channel_id=1, source_target_pairs={{0,1},{1,0},{2,3},{3,2},{4,5},{5,4},{6,7},{7,6},{8,9},{9,8},{10,11... | collective-permute-start | bytes 393224 | tf_op jit(solution)/shard_map/ppermute | solution.py:76
  120.0 8.6 %collective-permute-start.19 = (bf16[512,128]{1,0:T(8,128)(2,1)S(1)}, bf16[512,128]{1,0:T(8,128)(2,1)S(1)}, u32[]{:S(2)}, u32[]{:S(2)}) collective-permute-start(bf16[512,128]{1,0:T(8,128)(2,1)S(1)} %fusion.39), channel_id=1, source_target_pairs={{0,1},{1,0},{2,3},{3,2},{4,5},{5,4},{6,7},{7,6},{8,9},{9,8},{10,11... | collective-permute-start | bytes 393224 | tf_op jit(solution)/shard_map/ppermute | solution.py:76
  122.5 14.2 %collective-permute-start.34 = (bf16[64,3584]{1,0:T(8,128)(2,1)S(1)}, bf16[64,3584]{1,0:T(8,128)(2,1)S(1)}, u32[]{:S(2)}, u32[]{:S(2)}) collective-permute-start(bf16[64,3584]{1,0:T(8,128)(2,1)S(1)} %get-tuple-element.30), channel_id=1, source_target_pairs={{24,0},{97,1},{0,8},{105,9},{8,16},{113,17},{16,24},{121,25},{56,3... | collective-permute-start | bytes 1376264 | tf_op jit(solution)/shard_map/ppermute | solution.py:72
  124.3 12.7 %collective-permute-start.36 = (bf16[64,3584]{1,0:T(8,128)(2,1)S(1)}, bf16[64,3584]{1,0:T(8,128)(2,1)S(1)}, u32[]{:S(2)}, u32[]{:S(2)}) collective-permute-start(bf16[64,3584]{1,0:T(8,128)(2,1)S(1)} %get-tuple-element.31), channel_id=1, source_target_pairs={{8,0},{33,1},{16,8},{41,9},{24,16},{49,17},{0,24},{57,25},{40,32},... | collective-permute-start | bytes 1376264 | tf_op jit(solution)/shard_map/ppermute | solution.py:72
  130.4 9.6 %collective-permute-start.21 = (bf16[64,3584]{1,0:T(8,128)(2,1)S(1)}, bf16[64,3584]{1,0:T(8,128)(2,1)S(1)}, u32[]{:S(2)}, u32[]{:S(2)}) collective-permute-start(bf16[64,3584]{1,0:T(8,128)(2,1)S(1)} %get-tuple-element.25), channel_id=1, source_target_pairs={{24,0},{97,1},{0,8},{105,9},{8,16},{113,17},{16,24},{121,25},{56,3... | collective-permute-start | bytes 1376264 | tf_op jit(solution)/shard_map/ppermute | solution.py:72
  132.3 8.2 %collective-permute-start.23 = (bf16[64,3584]{1,0:T(8,128)(2,1)S(1)}, bf16[64,3584]{1,0:T(8,128)(2,1)S(1)}, u32[]{:S(2)}, u32[]{:S(2)}) collective-permute-start(bf16[64,3584]{1,0:T(8,128)(2,1)S(1)} %get-tuple-element.26), channel_id=1, source_target_pairs={{8,0},{33,1},{16,8},{41,9},{24,16},{49,17},{0,24},{57,25},{40,32},... | collective-permute-start | bytes 1376264 | tf_op jit(solution)/shard_map/ppermute | solution.py:72
  136.9 13.8 %collective-permute-start.35 = (bf16[128,3584]{1,0:T(8,128)(2,1)S(1)}, bf16[128,3584]{1,0:T(8,128)(2,1)S(1)}, u32[]{:S(2)}, u32[]{:S(2)}) collective-permute-start(bf16[128,3584]{1,0:T(8,128)(2,1)S(1)} %pad_maximum_fusion.4), channel_id=1, source_target_pairs={{24,0},{97,1},{0,8},{105,9},{8,16},{113,17},{16,24},{121,25},{56,3... | collective-permute-start | bytes 2752520 | tf_op jit(solution)/shard_map/ppermute | solution.py:72
  137.2 13.5 %collective-permute-start.37 = (bf16[128,3584]{1,0:T(8,128)(2,1)S(1)}, bf16[128,3584]{1,0:T(8,128)(2,1)S(1)}, u32[]{:S(2)}, u32[]{:S(2)}) collective-permute-start(bf16[128,3584]{1,0:T(8,128)(2,1)S(1)} %pad_maximum_fusion.5), channel_id=1, source_target_pairs={{8,0},{33,1},{16,8},{41,9},{24,16},{49,17},{0,24},{57,25},{40,32},... | collective-permute-start | bytes 2752520 | tf_op jit(solution)/shard_map/ppermute | solution.py:72
  140.1 24.2 %collective-permute-start.22 = (bf16[128,3584]{1,0:T(8,128)(2,1)S(1)}, bf16[128,3584]{1,0:T(8,128)(2,1)S(1)}, u32[]{:S(2)}, u32[]{:S(2)}) collective-permute-start(bf16[128,3584]{1,0:T(8,128)(2,1)S(1)} %pad_maximum_fusion.2), channel_id=1, source_target_pairs={{24,0},{97,1},{0,8},{105,9},{8,16},{113,17},{16,24},{121,25},{56,3... | collective-permute-start | bytes 2752520 | tf_op jit(solution)/shard_map/ppermute | solution.py:72
  140.7 23.6 %collective-permute-start.24 = (bf16[128,3584]{1,0:T(8,128)(2,1)S(1)}, bf16[128,3584]{1,0:T(8,128)(2,1)S(1)}, u32[]{:S(2)}, u32[]{:S(2)}) collective-permute-start(bf16[128,3584]{1,0:T(8,128)(2,1)S(1)} %pad_maximum_fusion.3), channel_id=1, source_target_pairs={{8,0},{33,1},{16,8},{41,9},{24,16},{49,17},{0,24},{57,25},{40,32},... | collective-permute-start | bytes 2752520 | tf_op jit(solution)/shard_map/ppermute | solution.py:72
  152.6 15.0 %collective-permute-start.38 = (bf16[32,3584]{1,0:T(8,128)(2,1)S(1)}, bf16[32,3584]{1,0:T(8,128)(2,1)S(1)}, u32[]{:S(2)}, u32[]{:S(2)}) collective-permute-start(bf16[32,3584]{1,0:T(8,128)(2,1)S(1)} %get-tuple-element.27), channel_id=1, source_target_pairs={{96,0},{25,1},{104,8},{1,9},{112,16},{9,17},{120,24},{17,25},{0,32... | collective-permute-start | bytes 688136 | tf_op jit(solution)/shard_map/ppermute | solution.py:72
  152.8 17.3 %collective-permute-start.39 = (bf16[32,3584]{1,0:T(8,128)(2,1)S(1)}, bf16[32,3584]{1,0:T(8,128)(2,1)S(1)}, u32[]{:S(2)}, u32[]{:S(2)}) collective-permute-start(bf16[32,3584]{1,0:T(8,128)(2,1)S(1)} %get-tuple-element.29), channel_id=1, source_target_pairs={{64,0},{17,1},{72,8},{25,9},{80,16},{1,17},{88,24},{9,25},{96,32},... | collective-permute-start | bytes 688136 | tf_op jit(solution)/shard_map/ppermute | solution.py:72
  153.5 16.6 %collective-permute-start.40 = (bf16[32,3584]{1,0:T(8,128)(2,1)S(1)}, bf16[32,3584]{1,0:T(8,128)(2,1)S(1)}, u32[]{:S(2)}, u32[]{:S(2)}) collective-permute-start(bf16[32,3584]{1,0:T(8,128)(2,1)S(1)} %get-tuple-element.28), channel_id=1, source_target_pairs={{32,0},{9,1},{40,8},{17,9},{48,16},{25,17},{56,24},{1,25},{64,32},... | collective-permute-start | bytes 688136 | tf_op jit(solution)/shard_map/ppermute | solution.py:72
  166.2 8.9 %collective-permute-start.25 = (bf16[32,3584]{1,0:T(8,128)(2,1)S(1)}, bf16[32,3584]{1,0:T(8,128)(2,1)S(1)}, u32[]{:S(2)}, u32[]{:S(2)}) collective-permute-start(bf16[32,3584]{1,0:T(8,128)(2,1)S(1)} %get-tuple-element.22), channel_id=1, source_target_pairs={{96,0},{25,1},{104,8},{1,9},{112,16},{9,17},{120,24},{17,25},{0,32... | collective-permute-start | bytes 688136 | tf_op jit(solution)/shard_map/ppermute | solution.py:72
  167.6 7.5 %collective-permute-start.26 = (bf16[32,3584]{1,0:T(8,128)(2,1)S(1)}, bf16[32,3584]{1,0:T(8,128)(2,1)S(1)}, u32[]{:S(2)}, u32[]{:S(2)}) collective-permute-start(bf16[32,3584]{1,0:T(8,128)(2,1)S(1)} %get-tuple-element.24), channel_id=1, source_target_pairs={{64,0},{17,1},{72,8},{25,9},{80,16},{1,17},{88,24},{9,25},{96,32},... | collective-permute-start | bytes 688136 | tf_op jit(solution)/shard_map/ppermute | solution.py:72
  167.6 8.0 %collective-permute-start.27 = (bf16[32,3584]{1,0:T(8,128)(2,1)S(1)}, bf16[32,3584]{1,0:T(8,128)(2,1)S(1)}, u32[]{:S(2)}, u32[]{:S(2)}) collective-permute-start(bf16[32,3584]{1,0:T(8,128)(2,1)S(1)} %get-tuple-element.23), channel_id=1, source_target_pairs={{32,0},{9,1},{40,8},{17,9},{48,16},{25,17},{56,24},{1,25},{64,32},... | collective-permute-start | bytes 688136 | tf_op jit(solution)/shard_map/ppermute | solution.py:72
  170.1 20.3 %copy-start.1 = (bf16[8,512,128]{2,1,0:T(8,128)(2,1)S(1)}, bf16[8,512,128]{2,1,0:T(8,128)(2,1)}, u32[]{:S(2)}) copy-start(bf16[8,512,128]{2,1,0:T(8,128)(2,1)} %param.18) | copy-start | bytes 3145732
  175.8 8.0 %collective-permute-start.41 = (bf16[2,8,3584]{2,1,0:T(8,128)(2,1)S(1)}, bf16[2,8,3584]{2,1,0:T(8,128)(2,1)S(1)}, u32[]{:S(2)}, u32[]{:S(2)}) collective-permute-start(bf16[2,8,3584]{2,1,0:T(8,128)(2,1)S(1)} %get-tuple-element.35), channel_id=1, source_target_pairs={{6,0},{0,2},{2,4},{4,6},{7,1},{1,3},{3,5},{5,7},{14,8},{8,10},{10,... | collective-permute-start | bytes 344072 | tf_op jit(solution)/shard_map/ppermute | solution.py:71
  175.9 7.9 %collective-permute-start.42 = (bf16[2,8,3584]{2,1,0:T(8,128)(2,1)S(1)}, bf16[2,8,3584]{2,1,0:T(8,128)(2,1)S(1)}, u32[]{:S(2)}, u32[]{:S(2)}) collective-permute-start(bf16[2,8,3584]{2,1,0:T(8,128)(2,1)S(1)} %get-tuple-element.37), channel_id=1, source_target_pairs={{4,0},{6,2},{0,4},{2,6},{5,1},{7,3},{1,5},{3,7},{12,8},{14,10},{8,... | collective-permute-start | bytes 344072 | tf_op jit(solution)/shard_map/ppermute | solution.py:71
  177.7 6.1 %collective-permute-start.43 = (bf16[2,8,3584]{2,1,0:T(8,128)(2,1)S(1)}, bf16[2,8,3584]{2,1,0:T(8,128)(2,1)S(1)}, u32[]{:S(2)}, u32[]{:S(2)}) collective-permute-start(bf16[2,8,3584]{2,1,0:T(8,128)(2,1)S(1)} %get-tuple-element.36), channel_id=1, source_target_pairs={{2,0},{4,2},{6,4},{0,6},{3,1},{5,3},{7,5},{1,7},{10,8},{12,10},{14... | collective-permute-start | bytes 344072 | tf_op jit(solution)/shard_map/ppermute | solution.py:71
  178.6 10.2 %collective-permute-start.4 = (bf16[8,3584]{1,0:T(8,128)(2,1)S(1)}, bf16[8,3584]{1,0:T(8,128)(2,1)S(1)}, u32[]{:S(2)}, u32[]{:S(2)}) collective-permute-start(bf16[8,3584]{1,0:T(8,128)(2,1)S(1)} %get-tuple-element.41), channel_id=1, source_target_pairs={{0,1},{1,0},{2,3},{3,2},{4,5},{5,4},{6,7},{7,6},{8,9},{9,8},{10,11... | collective-permute-start | bytes 172040 | tf_op jit(solution)/shard_map/ppermute | solution.py:76
  183.9 5.8 %collective-permute-start.44 = (bf16[8,3584]{1,0:T(8,128)(2,1)S(1)}, bf16[8,3584]{1,0:T(8,128)(2,1)S(1)}, u32[]{:S(2)}, u32[]{:S(2)}) collective-permute-start(bf16[8,3584]{1,0:T(8,128)(2,1)S(1)} %get-tuple-element.44), channel_id=1, source_target_pairs={{0,1},{1,0},{2,3},{3,2},{4,5},{5,4},{6,7},{7,6},{8,9},{9,8},{10,11... | collective-permute-start | bytes 172040 | tf_op jit(solution)/shard_map/ppermute | solution.py:76
  (24 other events, 123.7 us)

commit v3 on v2

--- a/solution.py
+++ b/solution.py
@@ -197,42 +197,61 @@
 
     width = half + lanes
     group = gather_near(payload, "x").reshape(8 * rows, width)
-    near = gather_near(group, near_axis).reshape(4, 4, 2, rows, width)
-
-    chunks = [near[:, :, c].reshape(16 * rows, width) for c in range(2)]
+    count = 8 * rows
+
+    far_own = gather_far(group, far_axis)
+    right, left, opposite = (shift(group, near_axis, d) for d in (1, -1, 2))
+    far_sides = gather_far(jnp.concatenate([right, left], axis=0), far_axis)
+    far_opposite = gather_far(opposite, far_axis)
+
     hidden = weight_in.shape[1] // 2
     units = hidden // 2
 
     def crossed(value):
-        value = value.reshape(4, 4, 4 * rows, value.shape[1])
-        return value.transpose(1, 0, 2, 3).reshape(64 * rows, value.shape[3])
-
-    sums = []
-    for chunk in chunks:
-        blocks = gather_far(chunk, far_axis)
-        products = [jnp.dot(b, weight_in, preferred_element_type=f32) for b in blocks]
-        got = swap(jnp.concatenate([p[:, hidden:].astype(bf16) for p in products], axis=0))
-        product = jnp.concatenate([p[:, :hidden] for p in products], axis=0)
-        product = product + crossed(got).astype(f32)
-        activated = (jax.nn.silu(product[:, :units]) * product[:, units:]).astype(bf16)
-        activated = jnp.concatenate([activated, crossed(swap(activated))], axis=1)
-        outs = []
-        n = 16 * rows
-        for i, b in enumerate(blocks):
-            weights = jnp.sum(
-                jnp.where(
-                    lax.broadcasted_iota(jnp.int32, (1, lanes), 1) == expert_at,
-                    b[:, half:].astype(f32),
-                    0.0,
-                ),
-                axis=1,
-                keepdims=True,
+        value = value.reshape(4, 4, count, value.shape[1])
+        return value.transpose(1, 0, 2, 3).reshape(16 * count, value.shape[3])
+
+    def into(blocks):
+        return [jnp.dot(b, weight_in, preferred_element_type=f32) for b in blocks]
+
+    def table_of(blocks):
+        labels = lax.broadcasted_iota(jnp.int32, (1, lanes), 1)
+        return [
+            jnp.sum(
+                jnp.where(labels == expert_at, b[:, half:].astype(f32), 0.0), axis=1, keepdims=True
             )
-            out = jnp.dot(activated[i * n : (i + 1) * n], weight_out, preferred_element_type=f32)
-            outs.append((out * weights).astype(bf16))
-        back = scatter_far(*outs, far_axis).reshape(4, 4 * rows, half)
-        sums.append(scatter_near(back, near_axis).astype(bf16))
-    to_x = jnp.stack([s.reshape(4, rows, half) for s in sums], axis=1)
+            for b in blocks
+        ]
+
+    def by_near(own, sides, opposite):
+        return jnp.concatenate(
+            own + [v[:count] for v in sides] + opposite + [v[count:] for v in sides], axis=0
+        )
+
+    product = by_near(into(far_own), into(far_sides), into(far_opposite))
+    weights = by_near(table_of(far_own), table_of(far_sides), table_of(far_opposite))
+    got = swap(product[:, hidden:].astype(bf16))
+    product = product[:, :hidden] + crossed(got).astype(f32)
+    activated = (jax.nn.silu(product[:, :units]) * product[:, units:]).astype(bf16)
+    activated = jnp.concatenate([activated, crossed(swap(activated))], axis=1)
+
+    def out_of(near):
+        rows_of = slice(near * 4 * count, (near + 1) * 4 * count)
+        out = jnp.dot(activated[rows_of], weight_out, preferred_element_type=f32)
+        out = (out * weights[rows_of]).astype(bf16)
+        return [out[i * count : (i + 1) * count] for i in range(4)]
+
+    back_opposite = scatter_far(*out_of(2), far_axis)
+    sides = [jnp.concatenate(pair, axis=0) for pair in zip(out_of(1), out_of(3))]
+    back_sides = scatter_far(*sides, far_axis)
+    back_own = scatter_far(*out_of(0), far_axis)
+    summed = total(
+        back_own,
+        shift(back_sides[:count], near_axis, -1),
+        shift(back_opposite, near_axis, 2),
+        shift(back_sides[count:], near_axis, 1),
+    ).astype(bf16)
+    to_x = summed.reshape(4, 2, rows, half)
     chip_out = scatter_near(to_x, "x")
 
     attention_out = to_tokens(attention.reshape(2, rows, half))

time: 191 us -> 213 us (1.12)
  waiting for transfers between devices: 68.8 us -> 92.7 us
  matrix products: 32.6 us -> 30.1 us
    ppermute x25 -> x30, waiting for transfers between devices: 47.5 us -> 70.3 us  [shift(): return lax.ppermute(value, ('y', 'z', 'core'), ring(axes, distance))]
    dot_general x16, matrix products: 18.6 us -> 16.1 us  [the longest x12 8.79 us: into(): return [jnp.dot(b, weight_in, preferred_element_type=f32) for b in blocks]]
    ppermute x11 -> x9, starting transfers between devices: 23.6 us -> 24.5 us  [swap(): return lax.ppermute(value, 'core', [(0, 1), (1, 0)])]
    ppermute x25 -> x30, starting transfers between devices: 33.7 us -> 33.7 us  [shift(): return lax.ppermute(value, ('y', 'z', 'core'), ring(axes, distance))]
  transfers between devices with their start and end apart: 46 -> 49, of which waited for: 20 -> 31; matrix products, arithmetic and copies ran while one was open for 21% -> 17% of each run, Pallas kernels for 0% -> 0%
where the time goes in v3:
time: 213 us; the launch traced here: 212 us
  waiting for transfers between devices  92.7 us (44%)
  starting transfers between devices  71.5 us (34%)
  matrix products  30.1 us (14%)
  other arithmetic  9.48 us (4%)
  local copies, waits for them, and re-layouts  7.11 us (3%)
    ppermute x30, waiting for transfers between devices, shift(): return lax.ppermute(value, ('y', 'z', 'core'), ring(axes, distance))  70.3 us
    ppermute x30, starting transfers between devices, shift(): return lax.ppermute(value, ('y', 'z', 'core'), ring(axes, distance))  33.7 us
    ppermute x9, starting transfers between devices, swap(): return lax.ppermute(value, 'core', [(0, 1), (1, 0)])  24.5 us
    ppermute x9, waiting for transfers between devices, shift(): return lax.ppermute(value, 'x', [((i + distance) % 4, i) for i in range(4)])  10.3 us
    dot_general x12, matrix products, into(): return [jnp.dot(b, weight_in, preferred_element_type=f32) for b in blocks]  8.79 us
    all_to_all x1, waiting for transfers between devices, per_device(): lax.all_to_all(latent_out, ('x', 'core'), split_axis=1, concat_axis=0, ti...  8.21 us
    dot_general x1, matrix products, per_device(): projected = jnp.dot(values, out_proj, preferred_element_type=f32)  8.06 us
    ppermute x9, starting transfers between devices, shift(): return lax.ppermute(value, 'x', [((i + distance) % 4, i) for i in range(4)])  7.58 us
  transfers between devices with their start and end apart: 49, of which 31 were waited for; matrix products, arithmetic and copies ran while one was open for 17% of the time, Pallas kernels for 0%

profile of v3, /device:TPU:1, one launch (start us, length us, event | category | flops | bytes accessed | tf_op | source)
XLA Modules:
  0.0 212.3 jit_solution(6374594171183890242)
XLA Ops:
  1.4 1.4 fusion.54
  2.8 3.1 %fusion.69 = (f32[8,64]{1,0:T(8,128)S(1)}, f32[8,64,384]{2,1,0:T(8,128)S(1)}) fusion(bf16[8,64,576]{2,1,0:T(8,128)(2,1)} %param.14, bf16[8,384,576]{1,2,0:T(8,128)(2,1)} %param.15, s32[8]{0:T(128)} %param.17), kind=kOutput, calls=%fused_computation.194 | convolution fusion | flops 227278336 | bytes 4917280 | tf_op jit(solution)/shard_map/rhc,rtc->rht/dot_general | solution.py:15
  8.6 5.8 %all-to-all-start = ((bf16[8,64,512]{2,0,1:T(8,128)(2,1)}), bf16[8,64,512]{2,0,1:T(8,128)(2,1)S(1)}, u32[]{:S(2)}, u32[]{:S(2)}) async-start(bf16[8,64,512]{2,0,1:T(8,128)(2,1)} %copy.31), calls=%async_computation | async-start | bytes 1048576 | tf_op jit(solution)/shard_map/all_to_all | solution.py:154
  15.7 8.2 %all-to-all-done = bf16[8,64,512]{2,0,1:T(8,128)(2,1)S(1)} async-done(((bf16[8,64,512]{2,0,1:T(8,128)(2,1)}), bf16[8,64,512]{2,0,1:T(8,128)(2,1)S(1)}, u32[]{:S(2)}, u32[]{:S(2)}) %all-to-all-start) | async-done | bytes 524320 | tf_op jit(solution)/shard_map/all_to_all | solution.py:154
  24.2 8.1 %fusion.42 = f32[64,7168]{1,0:T(8,128)S(1)} fusion(bf16[1024,7168]{1,0:T(8,128)(2,1)} %param.19, bf16[8,8,8,128]{3,2,1,0:T(8,128)(2,1)S(1)} %fusion.20), kind=kOutput, calls=%fused_computation.100 | convolution fusion | flops 939524096 | bytes 16646144 | tf_op jit(solution)/shard_map/dot_general | solution.py:176
  33.3 1.4 dynamic-slice_bitcast_fusion
  39.3 1.8 collective-permute-done.2
  41.1 3.3 %collective-permute-done.1 = bf16[16,3584]{1,0:T(8,128)(2,1)S(1)} collective-permute-done((bf16[16,3584]{1,0:T(8,128)(2,1)S(1)}, bf16[16,3584]{1,0:T(8,128)(2,1)S(1)}, u32[]{:S(2)}, u32[]{:S(2)}) %collective-permute-start.1) | collective-permute-done | bytes 114720 | tf_op jit(solution)/shard_map/ppermute | solution.py:71
  46.8 1.5 collective-permute-start.8
  48.2 1.8 collective-permute-start.7
  51.3 3.8 %collective-permute-done.9 = bf16[16,3712]{1,0:T(8,128)(2,1)S(1)} collective-permute-done((bf16[16,3712]{1,0:T(8,128)(2,1)S(1)}, bf16[16,3712]{1,0:T(8,128)(2,1)S(1)}, u32[]{:S(2)}, u32[]{:S(2)}) %collective-permute-start.9) | collective-permute-done | bytes 118816 | tf_op jit(solution)/shard_map/ppermute | solution.py:71
  55.4 3.8 %collective-permute-start.15 = (bf16[64,3712]{1,0:T(8,128)(2,1)S(1)}, bf16[64,3712]{1,0:T(8,128)(2,1)S(1)}, u32[]{:S(2)}, u32[]{:S(2)}) collective-permute-start(bf16[64,3712]{1,0:T(8,128)(2,1)S(1)} %bitcast.145), channel_id=1, source_target_pairs={{32,0},{9,1},{40,8},{17,9},{48,16},{25,17},{56,24},{1,25},{64,32},... | collective-permute-start | bytes 1425416 | tf_op jit(solution)/shard_map/ppermute | solution.py:72
  59.2 1.6 dynamic-slice_bitcast_fusion.2
  60.9 2.8 %collective-permute-start.11 = (bf16[64,3712]{1,0:T(8,128)(2,1)S(1)}, bf16[64,3712]{1,0:T(8,128)(2,1)S(1)}, u32[]{:S(2)}, u32[]{:S(2)}) collective-permute-start(bf16[64,3712]{1,0:T(8,128)(2,1)S(1)} %bitcast.147), channel_id=1, source_target_pairs={{8,0},{33,1},{16,8},{41,9},{24,16},{49,17},{0,24},{57,25},{40,32},... | collective-permute-start | bytes 1425416 | tf_op jit(solution)/shard_map/ppermute | solution.py:72
  66.1 3.7 %collective-permute-done.16 = bf16[64,3712]{1,0:T(8,128)(2,1)S(1)} collective-permute-done((bf16[64,3712]{1,0:T(8,128)(2,1)S(1)}, bf16[64,3712]{1,0:T(8,128)(2,1)S(1)}, u32[]{:S(2)}, u32[]{:S(2)}) %collective-permute-start.16) | collective-permute-done | bytes 475168 | tf_op jit(solution)/shard_map/ppermute | solution.py:72
  70.8 3.1 %collective-permute-start.17 = (bf16[128,3712]{1,0:T(8,128)(2,1)S(1)}, bf16[128,3712]{1,0:T(8,128)(2,1)S(1)}, u32[]{:S(2)}, u32[]{:S(2)}) collective-permute-start(bf16[128,3712]{1,0:T(8,128)(2,1)S(1)} %constant_dynamic-update-slice_fusion.2), channel_id=1, source_target_pairs={{8,0},{33,1},{16,8},{41,9},{24,16},{49,17},{0,24},{57,25},{40,32},... | collective-permute-start | bytes 2850824 | tf_op jit(solution)/shard_map/ppermute | solution.py:72
  73.9 2.2 %collective-permute-done.13 = bf16[64,3712]{1,0:T(8,128)(2,1)S(1)} collective-permute-done((bf16[64,3712]{1,0:T(8,128)(2,1)S(1)}, bf16[64,3712]{1,0:T(8,128)(2,1)S(1)}, u32[]{:S(2)}, u32[]{:S(2)}) %collective-permute-start.13) | collective-permute-done | bytes 475168 | tf_op jit(solution)/shard_map/ppermute | solution.py:72
  76.1 2.7 %collective-permute-start.12 = (bf16[32,3712]{1,0:T(8,128)(2,1)S(1)}, bf16[32,3712]{1,0:T(8,128)(2,1)S(1)}, u32[]{:S(2)}, u32[]{:S(2)}) collective-permute-start(bf16[32,3712]{1,0:T(8,128)(2,1)S(1)} %slice.405), channel_id=1, source_target_pairs={{8,0},{33,1},{16,8},{41,9},{24,16},{49,17},{0,24},{57,25},{40,32},... | collective-permute-start | bytes 712712 | tf_op jit(solution)/shard_map/ppermute | solution.py:72
  78.9 1.6 slice_bitcast_fusion.1
  80.4 2.2 %fusion.10 = bf16[3712,512]{1,0:T(8,128)(2,1)S(1)} fusion(bf16[3584,128]{1,0:T(8,128)(2,1)S(1)} %get-tuple-element.41, bf16[3584,128]{1,0:T(8,128)(2,1)S(1)} %get-tuple-element.40, bf16[3584,128]{1,0:T(8,128)(2,1)S(1)} %get-tuple-element.19, bf16[3584,128]{1,0:T(8,128)(2,1)S(1)} %get-tuple-element.18), kind=kLoop, calls=%fused_computation.15 | loop fusion | flops 24707072 | bytes 7471104 | tf_op jit(solution)/shard_map/concatenate | solution.py:160
  85.0 7.2 %collective-permute-done.12 = bf16[32,3712]{1,0:T(8,128)(2,1)S(1)} collective-permute-done((bf16[32,3712]{1,0:T(8,128)(2,1)S(1)}, bf16[32,3712]{1,0:T(8,128)(2,1)S(1)}, u32[]{:S(2)}, u32[]{:S(2)}) %collective-permute-start.12) | collective-permute-done | bytes 237600 | tf_op jit(solution)/shard_map/ppermute | solution.py:72
  92.2 3.4 %collective-permute-start.22 = (bf16[64,3712]{1,0:T(8,128)(2,1)S(1)}, bf16[64,3712]{1,0:T(8,128)(2,1)S(1)}, u32[]{:S(2)}, u32[]{:S(2)}) collective-permute-start(bf16[64,3712]{1,0:T(8,128)(2,1)S(1)} %collective-permute-done.21), channel_id=1, source_target_pairs={{8,0},{33,1},{16,8},{41,9},{24,16},{49,17},{0,24},{57,25},{40,32},... | collective-permute-start | bytes 1425416 | tf_op jit(solution)/shard_map/ppermute | solution.py:72
  97.7 3.5 %collective-permute-done.22 = bf16[64,3712]{1,0:T(8,128)(2,1)S(1)} collective-permute-done((bf16[64,3712]{1,0:T(8,128)(2,1)S(1)}, bf16[64,3712]{1,0:T(8,128)(2,1)S(1)}, u32[]{:S(2)}, u32[]{:S(2)}) %collective-permute-start.22) | collective-permute-done | bytes 475168 | tf_op jit(solution)/shard_map/ppermute | solution.py:72
  101.2 3.2 %collective-permute-start.23 = (bf16[32,3712]{1,0:T(8,128)(2,1)S(1)}, bf16[32,3712]{1,0:T(8,128)(2,1)S(1)}, u32[]{:S(2)}, u32[]{:S(2)}) collective-permute-start(bf16[32,3712]{1,0:T(8,128)(2,1)S(1)} %slice.413), channel_id=1, source_target_pairs={{8,0},{33,1},{16,8},{41,9},{24,16},{49,17},{0,24},{57,25},{40,32},... | collective-permute-start | bytes 712712 | tf_op jit(solution)/shard_map/ppermute | solution.py:72
  105.7 1.7 collective-permute-done.23
  107.5 4.4 %collective-permute-done.25 = bf16[32,3712]{1,0:T(8,128)(2,1)S(1)} collective-permute-done((bf16[32,3712]{1,0:T(8,128)(2,1)S(1)}, bf16[32,3712]{1,0:T(8,128)(2,1)S(1)}, u32[]{:S(2)}, u32[]{:S(2)}) %collective-permute-start.25) | collective-permute-done | bytes 237600 | tf_op jit(solution)/shard_map/ppermute | solution.py:72
  112.3 1.5 collective-permute-start.20
  115.1 4.6 %collective-permute-done.18 = bf16[64,3712]{1,0:T(8,128)(2,1)S(1)} collective-permute-done((bf16[64,3712]{1,0:T(8,128)(2,1)S(1)}, bf16[64,3712]{1,0:T(8,128)(2,1)S(1)}, u32[]{:S(2)}, u32[]{:S(2)}) %collective-permute-start.18) | collective-permute-done | bytes 475168 | tf_op jit(solution)/shard_map/ppermute | solution.py:72
  119.7 1.3 collective-permute-done.20
  125.0 8.5 %collective-permute-start.26 = (bf16[1024,256]{1,0:T(8,128)(2,1)S(1)}, bf16[1024,256]{1,0:T(8,128)(2,1)S(1)}, u32[]{:S(2)}, u32[]{:S(2)}) collective-permute-start(bf16[1024,256]{1,0:T(8,128)(2,1)S(1)} %slice.565), channel_id=1, source_target_pairs={{0,1},{1,0},{2,3},{3,2},{4,5},{5,4},{6,7},{7,6},{8,9},{9,8},{10,11... | collective-permute-start | bytes 1572872 | tf_op jit(solution)/shard_map/ppermute | solution.py:76
  137.4 1.8 fusion.6
  139.3 2.9 %collective-permute-start.35 = (bf16[64,3584]{1,0:T(8,128)(2,1)S(1)}, bf16[64,3584]{1,0:T(8,128)(2,1)S(1)}, u32[]{:S(2)}, u32[]{:S(2)}) collective-permute-start(bf16[64,3584]{1,0:T(8,128)(2,1)S(1)} %get-tuple-element.36), channel_id=1, source_target_pairs={{8,0},{33,1},{16,8},{41,9},{24,16},{49,17},{0,24},{57,25},{40,32},... | collective-permute-start | bytes 1376264 | tf_op jit(solution)/shard_map/ppermute | solution.py:72
  142.2 1.8 fusion.5
  144.3 1.8 fusion.7
  146.2 2.7 %collective-permute-start.40 = (bf16[32,3584]{1,0:T(8,128)(2,1)S(1)}, bf16[32,3584]{1,0:T(8,128)(2,1)S(1)}, u32[]{:S(2)}, u32[]{:S(2)}) collective-permute-start(bf16[32,3584]{1,0:T(8,128)(2,1)S(1)} %get-tuple-element.29), channel_id=1, source_target_pairs={{8,0},{33,1},{16,8},{41,9},{24,16},{49,17},{0,24},{57,25},{40,32},... | collective-permute-start | bytes 688136 | tf_op jit(solution)/shard_map/ppermute | solution.py:72
  149.0 1.8 fusion.4
  151.0 4.3 %collective-permute-done.38 = bf16[32,3584]{1,0:T(8,128)(2,1)S(1)} collective-permute-done((bf16[32,3584]{1,0:T(8,128)(2,1)S(1)}, bf16[32,3584]{1,0:T(8,128)(2,1)S(1)}, u32[]{:S(2)}, u32[]{:S(2)}) %collective-permute-start.38) | collective-permute-done | bytes 229408 | tf_op jit(solution)/shard_map/ppermute | solution.py:72
  155.6 2.4 %collective-permute-done.29 = bf16[32,3584]{1,0:T(8,128)(2,1)S(1)} collective-permute-done((bf16[32,3584]{1,0:T(8,128)(2,1)S(1)}, bf16[32,3584]{1,0:T(8,128)(2,1)S(1)}, u32[]{:S(2)}, u32[]{:S(2)}) %collective-permute-start.29) | collective-permute-done | bytes 229408 | tf_op jit(solution)/shard_map/ppermute | solution.py:72
  158.0 2.4 %collective-permute-done.31 = bf16[32,3584]{1,0:T(8,128)(2,1)S(1)} collective-permute-done((bf16[32,3584]{1,0:T(8,128)(2,1)S(1)}, bf16[32,3584]{1,0:T(8,128)(2,1)S(1)}, u32[]{:S(2)}, u32[]{:S(2)}) %collective-permute-start.31) | collective-permute-done | bytes 229408 | tf_op jit(solution)/shard_map/ppermute | solution.py:72
  162.4 2.2 %collective-permute-start.36 = (bf16[128,3584]{1,0:T(8,128)(2,1)S(1)}, bf16[128,3584]{1,0:T(8,128)(2,1)S(1)}, u32[]{:S(2)}, u32[]{:S(2)}) collective-permute-start(bf16[128,3584]{1,0:T(8,128)(2,1)S(1)} %pad_maximum_fusion.2), channel_id=1, source_target_pairs={{8,0},{33,1},{16,8},{41,9},{24,16},{49,17},{0,24},{57,25},{40,32},... | collective-permute-start | bytes 2752520 | tf_op jit(solution)/shard_map/ppermute | solution.py:72
  165.3 1.5 collective-permute-done.39
  167.1 17.9 %collective-permute-done.36 = bf16[128,3584]{1,0:T(8,128)(2,1)S(1)} collective-permute-done((bf16[128,3584]{1,0:T(8,128)(2,1)S(1)}, bf16[128,3584]{1,0:T(8,128)(2,1)S(1)}, u32[]{:S(2)}, u32[]{:S(2)}) %collective-permute-start.36) | collective-permute-done | bytes 917536 | tf_op jit(solution)/shard_map/ppermute | solution.py:72
  185.0 1.5 collective-permute-done.34
  187.0 1.4 collective-permute-start.37
  188.4 6.1 %collective-permute-done.43 = bf16[64,3584]{1,0:T(8,128)(2,1)S(1)} collective-permute-done((bf16[64,3584]{1,0:T(8,128)(2,1)S(1)}, bf16[64,3584]{1,0:T(8,128)(2,1)S(1)}, u32[]{:S(2)}, u32[]{:S(2)}) %collective-permute-start.43) | collective-permute-done | bytes 458784 | tf_op jit(solution)/shard_map/ppermute | solution.py:72
  194.6 1.3 collective-permute-done.37
  198.4 6.0 %collective-permute-start.4 = (bf16[8,3584]{1,0:T(8,128)(2,1)S(1)}, bf16[8,3584]{1,0:T(8,128)(2,1)S(1)}, u32[]{:S(2)}, u32[]{:S(2)}) collective-permute-start(bf16[8,3584]{1,0:T(8,128)(2,1)S(1)} %get-tuple-element.52), channel_id=1, source_target_pairs={{0,1},{1,0},{2,3},{3,2},{4,5},{5,4},{6,7},{7,6},{8,9},{9,8},{10,11... | collective-permute-start | bytes 172040 | tf_op jit(solution)/shard_map/ppermute | solution.py:76
  204.5 6.1 %collective-permute-start.47 = (bf16[8,3584]{1,0:T(8,128)(2,1)S(1)}, bf16[8,3584]{1,0:T(8,128)(2,1)S(1)}, u32[]{:S(2)}, u32[]{:S(2)}) collective-permute-start(bf16[8,3584]{1,0:T(8,128)(2,1)S(1)} %get-tuple-element.55), channel_id=1, source_target_pairs={{0,1},{1,0},{2,3},{3,2},{4,5},{5,4},{6,7},{7,6},{8,9},{9,8},{10,11... | collective-permute-start | bytes 172040 | tf_op jit(solution)/shard_map/ppermute | solution.py:76
  (179 shorter events, 41.5 us)
Async XLA Ops:
  8.6 15.3 %all-to-all-start = ((bf16[8,64,512]{2,0,1:T(8,128)(2,1)}), bf16[8,64,512]{2,0,1:T(8,128)(2,1)S(1)}, u32[]{:S(2)}, u32[]{:S(2)}) async-start(bf16[8,64,512]{2,0,1:T(8,128)(2,1)} %copy.31), calls=%async_computation | async-start | bytes 1048576 | tf_op jit(solution)/shard_map/all_to_all | solution.py:154
  15.7 21.4 %collective-permute-start.5 = (bf16[8,3712]{1,0:T(8,128)(2,1)}, bf16[8,3712]{1,0:T(8,128)(2,1)}, u32[]{:S(2)}, u32[]{:S(2)}) collective-permute-start(bf16[8,3712]{1,0:T(8,128)(2,1)} %get-tuple-element.61), channel_id=1, source_target_pairs={{0,1},{1,0},{2,3},{3,2},{4,5},{5,4},{6,7},{7,6},{8,9},{9,8},{10,11... | collective-permute-start | bytes 178184 | tf_op jit(solution)/shard_map/ppermute | solution.py:76
  32.4 2.5 %collective-permute-start = (bf16[64,3584]{1,0:T(8,128)(2,1)S(1)}, bf16[64,3584]{1,0:T(8,128)(2,1)S(1)}, u32[]{:S(2)}, u32[]{:S(2)}) collective-permute-start(bf16[64,3584]{1,0:T(8,128)(2,1)S(1)} %dynamic-slice_convert_fusion), channel_id=1, source_target_pairs={{0,1},{1,0},{2,3},{3,2},{4,5},{5,4},{6,7},{7,6},{8,9},{9,8},{10,11... | collective-permute-start | bytes 1376264 | tf_op jit(solution)/shard_map/ppermute | solution.py:76
  34.7 41.4 %collective-permute-start.10 = (bf16[2,3584,128]{2,1,0:T(8,128)(2,1)}, bf16[2,3584,128]{2,1,0:T(8,128)(2,1)}, u32[]{:S(2)}, u32[]{:S(2)}) collective-permute-start(bf16[2,3584,128]{2,1,0:T(8,128)(2,1)} %dynamic-slice_bitcast_fusion), channel_id=1, source_target_pairs={{0,1},{1,0},{2,3},{3,2},{4,5},{5,4},{6,7},{7,6},{8,9},{9,8},{10,11... | collective-permute-start | bytes 5505032 | tf_op jit(solution)/shard_map/ppermute | solution.py:76
  35.0 4.3 %collective-permute-start.3 = (bf16[16,3584]{1,0:T(8,128)(2,1)S(1)}, bf16[16,3584]{1,0:T(8,128)(2,1)S(1)}, u32[]{:S(2)}, u32[]{:S(2)}) collective-permute-start(bf16[16,3584]{1,0:T(8,128)(2,1)S(1)} %get-tuple-element.45), channel_id=1, source_target_pairs={{2,0},{4,2},{6,4},{0,6},{3,1},{5,3},{7,5},{1,7},{10,8},{12,10},{14... | collective-permute-start | bytes 344072 | tf_op jit(solution)/shard_map/ppermute | solution.py:71
  35.9 5.2 %collective-permute-start.2 = (bf16[16,3584]{1,0:T(8,128)(2,1)S(1)}, bf16[16,3584]{1,0:T(8,128)(2,1)S(1)}, u32[]{:S(2)}, u32[]{:S(2)}) collective-permute-start(bf16[16,3584]{1,0:T(8,128)(2,1)S(1)} %get-tuple-element.46), channel_id=1, source_target_pairs={{4,0},{6,2},{0,4},{2,6},{5,1},{7,3},{1,5},{3,7},{12,8},{14,10},{8,... | collective-permute-start | bytes 344072 | tf_op jit(solution)/shard_map/ppermute | solution.py:71
  37.1 7.3 %collective-permute-start.1 = (bf16[16,3584]{1,0:T(8,128)(2,1)S(1)}, bf16[16,3584]{1,0:T(8,128)(2,1)S(1)}, u32[]{:S(2)}, u32[]{:S(2)}) collective-permute-start(bf16[16,3584]{1,0:T(8,128)(2,1)S(1)} %get-tuple-element.44), channel_id=1, source_target_pairs={{6,0},{0,2},{2,4},{4,6},{7,1},{1,3},{3,5},{5,7},{14,8},{8,10},{10,... | collective-permute-start | bytes 344072 | tf_op jit(solution)/shard_map/ppermute | solution.py:71
  44.6 1.9 collective-permute-start.6
  46.7 8.4 %collective-permute-start.9 = (bf16[16,3712]{1,0:T(8,128)(2,1)S(1)}, bf16[16,3712]{1,0:T(8,128)(2,1)S(1)}, u32[]{:S(2)}, u32[]{:S(2)}) collective-permute-start(bf16[16,3712]{1,0:T(8,128)(2,1)S(1)} %get-tuple-element.51), channel_id=1, source_target_pairs={{6,0},{0,2},{2,4},{4,6},{7,1},{1,3},{3,5},{5,7},{14,8},{8,10},{10,... | collective-permute-start | bytes 356360 | tf_op jit(solution)/shard_map/ppermute | solution.py:71
  46.8 8.3 %collective-permute-start.8 = (bf16[16,3712]{1,0:T(8,128)(2,1)S(1)}, bf16[16,3712]{1,0:T(8,128)(2,1)S(1)}, u32[]{:S(2)}, u32[]{:S(2)}) collective-permute-start(bf16[16,3712]{1,0:T(8,128)(2,1)S(1)} %get-tuple-element.51), channel_id=1, source_target_pairs={{4,0},{6,2},{0,4},{2,6},{5,1},{7,3},{1,5},{3,7},{12,8},{14,10},{8,... | collective-permute-start | bytes 356360 | tf_op jit(solution)/shard_map/ppermute | solution.py:71
  48.2 7.1 %collective-permute-start.7 = (bf16[16,3712]{1,0:T(8,128)(2,1)S(1)}, bf16[16,3712]{1,0:T(8,128)(2,1)S(1)}, u32[]{:S(2)}, u32[]{:S(2)}) collective-permute-start(bf16[16,3712]{1,0:T(8,128)(2,1)S(1)} %get-tuple-element.51), channel_id=1, source_target_pairs={{2,0},{4,2},{6,4},{0,6},{3,1},{5,3},{7,5},{1,7},{10,8},{12,10},{14... | collective-permute-start | bytes 356360 | tf_op jit(solution)/shard_map/ppermute | solution.py:71
  50.1 87.2 %collective-permute-start.28 = (bf16[128,3584]{1,0:T(8,128)(2,1)S(1)}, bf16[128,3584]{1,0:T(8,128)(2,1)}, u32[]{:S(2)}, u32[]{:S(2)}) collective-permute-start(bf16[128,3584]{1,0:T(8,128)(2,1)S(1)} %get-tuple-element.39), channel_id=1, source_target_pairs={{0,1},{1,0},{2,3},{3,2},{4,5},{5,4},{6,7},{7,6},{8,9},{9,8},{10,11... | collective-permute-start | bytes 2752520 | tf_op jit(solution)/shard_map/ppermute | solution.py:76
  55.4 9.4 %collective-permute-start.15 = (bf16[64,3712]{1,0:T(8,128)(2,1)S(1)}, bf16[64,3712]{1,0:T(8,128)(2,1)S(1)}, u32[]{:S(2)}, u32[]{:S(2)}) collective-permute-start(bf16[64,3712]{1,0:T(8,128)(2,1)S(1)} %bitcast.145), channel_id=1, source_target_pairs={{32,0},{9,1},{40,8},{17,9},{48,16},{25,17},{56,24},{1,25},{64,32},... | collective-permute-start | bytes 1425416 | tf_op jit(solution)/shard_map/ppermute | solution.py:72
  60.8 9.1 %collective-permute-start.16 = (bf16[64,3712]{1,0:T(8,128)(2,1)S(1)}, bf16[64,3712]{1,0:T(8,128)(2,1)S(1)}, u32[]{:S(2)}, u32[]{:S(2)}) collective-permute-start(bf16[64,3712]{1,0:T(8,128)(2,1)S(1)} %bitcast.146), channel_id=1, source_target_pairs={{96,0},{25,1},{104,8},{1,9},{112,16},{9,17},{120,24},{17,25},{0,32... | collective-permute-start | bytes 1425416 | tf_op jit(solution)/shard_map/ppermute | solution.py:72
  60.9 9.9 %collective-permute-start.11 = (bf16[64,3712]{1,0:T(8,128)(2,1)S(1)}, bf16[64,3712]{1,0:T(8,128)(2,1)S(1)}, u32[]{:S(2)}, u32[]{:S(2)}) collective-permute-start(bf16[64,3712]{1,0:T(8,128)(2,1)S(1)} %bitcast.147), channel_id=1, source_target_pairs={{8,0},{33,1},{16,8},{41,9},{24,16},{49,17},{0,24},{57,25},{40,32},... | collective-permute-start | bytes 1425416 | tf_op jit(solution)/shard_map/ppermute | solution.py:72
  64.8 11.3 %collective-permute-start.13 = (bf16[64,3712]{1,0:T(8,128)(2,1)S(1)}, bf16[64,3712]{1,0:T(8,128)(2,1)S(1)}, u32[]{:S(2)}, u32[]{:S(2)}) collective-permute-start(bf16[64,3712]{1,0:T(8,128)(2,1)S(1)} %bitcast.148), channel_id=1, source_target_pairs={{24,0},{97,1},{0,8},{105,9},{8,16},{113,17},{16,24},{121,25},{56,3... | collective-permute-start | bytes 1425416 | tf_op jit(solution)/shard_map/ppermute | solution.py:72
  69.8 15.0 %collective-permute-start.21 = (bf16[64,3712]{1,0:T(8,128)(2,1)S(1)}, bf16[64,3712]{1,0:T(8,128)(2,1)S(1)}, u32[]{:S(2)}, u32[]{:S(2)}) collective-permute-start(bf16[64,3712]{1,0:T(8,128)(2,1)S(1)} %bitcast.149), channel_id=1, source_target_pairs={{64,0},{17,1},{72,8},{25,9},{80,16},{1,17},{88,24},{9,25},{96,32},... | collective-permute-start | bytes 1425416 | tf_op jit(solution)/shard_map/ppermute | solution.py:72
  70.8 41.3 %collective-permute-start.17 = (bf16[128,3712]{1,0:T(8,128)(2,1)S(1)}, bf16[128,3712]{1,0:T(8,128)(2,1)S(1)}, u32[]{:S(2)}, u32[]{:S(2)}) collective-permute-start(bf16[128,3712]{1,0:T(8,128)(2,1)S(1)} %constant_dynamic-update-slice_fusion.2), channel_id=1, source_target_pairs={{8,0},{33,1},{16,8},{41,9},{24,16},{49,17},{0,24},{57,25},{40,32},... | collective-permute-start | bytes 2850824 | tf_op jit(solution)/shard_map/ppermute | solution.py:72
  76.1 36.1 %collective-permute-start.19 = (bf16[128,3712]{1,0:T(8,128)(2,1)S(1)}, bf16[128,3712]{1,0:T(8,128)(2,1)S(1)}, u32[]{:S(2)}, u32[]{:S(2)}) collective-permute-start(bf16[128,3712]{1,0:T(8,128)(2,1)S(1)} %constant_dynamic-update-slice_fusion.2), channel_id=1, source_target_pairs={{24,0},{97,1},{0,8},{105,9},{8,16},{113,17},{16,24},{121,25},{56,3... | collective-permute-start | bytes 2850824 | tf_op jit(solution)/shard_map/ppermute | solution.py:72
  76.1 16.1 %collective-permute-start.12 = (bf16[32,3712]{1,0:T(8,128)(2,1)S(1)}, bf16[32,3712]{1,0:T(8,128)(2,1)S(1)}, u32[]{:S(2)}, u32[]{:S(2)}) collective-permute-start(bf16[32,3712]{1,0:T(8,128)(2,1)S(1)} %slice.405), channel_id=1, source_target_pairs={{8,0},{33,1},{16,8},{41,9},{24,16},{49,17},{0,24},{57,25},{40,32},... | collective-permute-start | bytes 712712 | tf_op jit(solution)/shard_map/ppermute | solution.py:72
  84.9 12.0 %collective-permute-start.14 = (bf16[32,3712]{1,0:T(8,128)(2,1)S(1)}, bf16[32,3712]{1,0:T(8,128)(2,1)S(1)}, u32[]{:S(2)}, u32[]{:S(2)}) collective-permute-start(bf16[32,3712]{1,0:T(8,128)(2,1)S(1)} %slice.406), channel_id=1, source_target_pairs={{24,0},{97,1},{0,8},{105,9},{8,16},{113,17},{16,24},{121,25},{56,3... | collective-permute-start | bytes 712712 | tf_op jit(solution)/shard_map/ppermute | solution.py:72
  92.2 9.0 %collective-permute-start.22 = (bf16[64,3712]{1,0:T(8,128)(2,1)S(1)}, bf16[64,3712]{1,0:T(8,128)(2,1)S(1)}, u32[]{:S(2)}, u32[]{:S(2)}) collective-permute-start(bf16[64,3712]{1,0:T(8,128)(2,1)S(1)} %collective-permute-done.21), channel_id=1, source_target_pairs={{8,0},{33,1},{16,8},{41,9},{24,16},{49,17},{0,24},{57,25},{40,32},... | collective-permute-start | bytes 1425416 | tf_op jit(solution)/shard_map/ppermute | solution.py:72
  96.9 8.7 %collective-permute-start.24 = (bf16[64,3712]{1,0:T(8,128)(2,1)S(1)}, bf16[64,3712]{1,0:T(8,128)(2,1)S(1)}, u32[]{:S(2)}, u32[]{:S(2)}) collective-permute-start(bf16[64,3712]{1,0:T(8,128)(2,1)S(1)} %collective-permute-done.21), channel_id=1, source_target_pairs={{24,0},{97,1},{0,8},{105,9},{8,16},{113,17},{16,24},{121,25},{56,3... | collective-permute-start | bytes 1425416 | tf_op jit(solution)/shard_map/ppermute | solution.py:72
  101.2 6.2 %collective-permute-start.23 = (bf16[32,3712]{1,0:T(8,128)(2,1)S(1)}, bf16[32,3712]{1,0:T(8,128)(2,1)S(1)}, u32[]{:S(2)}, u32[]{:S(2)}) collective-permute-start(bf16[32,3712]{1,0:T(8,128)(2,1)S(1)} %slice.413), channel_id=1, source_target_pairs={{8,0},{33,1},{16,8},{41,9},{24,16},{49,17},{0,24},{57,25},{40,32},... | collective-permute-start | bytes 712712 | tf_op jit(solution)/shard_map/ppermute | solution.py:72
  105.6 6.2 %collective-permute-start.25 = (bf16[32,3712]{1,0:T(8,128)(2,1)S(1)}, bf16[32,3712]{1,0:T(8,128)(2,1)S(1)}, u32[]{:S(2)}, u32[]{:S(2)}) collective-permute-start(bf16[32,3712]{1,0:T(8,128)(2,1)S(1)} %slice.414), channel_id=1, source_target_pairs={{24,0},{97,1},{0,8},{105,9},{8,16},{113,17},{16,24},{121,25},{56,3... | collective-permute-start | bytes 712712 | tf_op jit(solution)/shard_map/ppermute | solution.py:72
  112.1 7.6 %collective-permute-start.18 = (bf16[64,3712]{1,0:T(8,128)(2,1)S(1)}, bf16[64,3712]{1,0:T(8,128)(2,1)S(1)}, u32[]{:S(2)}, u32[]{:S(2)}) collective-permute-start(bf16[64,3712]{1,0:T(8,128)(2,1)S(1)} %slice.409), channel_id=1, source_target_pairs={{8,0},{33,1},{16,8},{41,9},{24,16},{49,17},{0,24},{57,25},{40,32},... | collective-permute-start | bytes 1425416 | tf_op jit(solution)/shard_map/ppermute | solution.py:72
  112.3 8.8 %collective-permute-start.20 = (bf16[64,3712]{1,0:T(8,128)(2,1)S(1)}, bf16[64,3712]{1,0:T(8,128)(2,1)S(1)}, u32[]{:S(2)}, u32[]{:S(2)}) collective-permute-start(bf16[64,3712]{1,0:T(8,128)(2,1)S(1)} %slice.410), channel_id=1, source_target_pairs={{24,0},{97,1},{0,8},{105,9},{8,16},{113,17},{16,24},{121,25},{56,3... | collective-permute-start | bytes 1425416 | tf_op jit(solution)/shard_map/ppermute | solution.py:72
  125.0 10.1 %collective-permute-start.26 = (bf16[1024,256]{1,0:T(8,128)(2,1)S(1)}, bf16[1024,256]{1,0:T(8,128)(2,1)S(1)}, u32[]{:S(2)}, u32[]{:S(2)}) collective-permute-start(bf16[1024,256]{1,0:T(8,128)(2,1)S(1)} %slice.565), channel_id=1, source_target_pairs={{0,1},{1,0},{2,3},{3,2},{4,5},{5,4},{6,7},{7,6},{8,9},{9,8},{10,11... | collective-permute-start | bytes 1572872 | tf_op jit(solution)/shard_map/ppermute | solution.py:76
  139.3 22.3 %collective-permute-start.35 = (bf16[64,3584]{1,0:T(8,128)(2,1)S(1)}, bf16[64,3584]{1,0:T(8,128)(2,1)S(1)}, u32[]{:S(2)}, u32[]{:S(2)}) collective-permute-start(bf16[64,3584]{1,0:T(8,128)(2,1)S(1)} %get-tuple-element.36), channel_id=1, source_target_pairs={{8,0},{33,1},{16,8},{41,9},{24,16},{49,17},{0,24},{57,25},{40,32},... | collective-permute-start | bytes 1376264 | tf_op jit(solution)/shard_map/ppermute | solution.py:72
  144.2 18.2 %collective-permute-start.33 = (bf16[64,3584]{1,0:T(8,128)(2,1)S(1)}, bf16[64,3584]{1,0:T(8,128)(2,1)S(1)}, u32[]{:S(2)}, u32[]{:S(2)}) collective-permute-start(bf16[64,3584]{1,0:T(8,128)(2,1)S(1)} %get-tuple-element.34), channel_id=1, source_target_pairs={{24,0},{97,1},{0,8},{105,9},{8,16},{113,17},{16,24},{121,25},{56,3... | collective-permute-start | bytes 1376264 | tf_op jit(solution)/shard_map/ppermute | solution.py:72
  146.2 9.1 %collective-permute-start.38 = (bf16[32,3584]{1,0:T(8,128)(2,1)S(1)}, bf16[32,3584]{1,0:T(8,128)(2,1)S(1)}, u32[]{:S(2)}, u32[]{:S(2)}) collective-permute-start(bf16[32,3584]{1,0:T(8,128)(2,1)S(1)} %get-tuple-element.28), channel_id=1, source_target_pairs={{24,0},{97,1},{0,8},{105,9},{8,16},{113,17},{16,24},{121,25},{56,3... | collective-permute-start | bytes 688136 | tf_op jit(solution)/shard_map/ppermute | solution.py:72
  146.2 9.0 %collective-permute-start.40 = (bf16[32,3584]{1,0:T(8,128)(2,1)S(1)}, bf16[32,3584]{1,0:T(8,128)(2,1)S(1)}, u32[]{:S(2)}, u32[]{:S(2)}) collective-permute-start(bf16[32,3584]{1,0:T(8,128)(2,1)S(1)} %get-tuple-element.29), channel_id=1, source_target_pairs={{8,0},{33,1},{16,8},{41,9},{24,16},{49,17},{0,24},{57,25},{40,32},... | collective-permute-start | bytes 688136 | tf_op jit(solution)/shard_map/ppermute | solution.py:72
  150.9 7.1 %collective-permute-start.29 = (bf16[32,3584]{1,0:T(8,128)(2,1)S(1)}, bf16[32,3584]{1,0:T(8,128)(2,1)S(1)}, u32[]{:S(2)}, u32[]{:S(2)}) collective-permute-start(bf16[32,3584]{1,0:T(8,128)(2,1)S(1)} %get-tuple-element.22), channel_id=1, source_target_pairs={{24,0},{97,1},{0,8},{105,9},{8,16},{113,17},{16,24},{121,25},{56,3... | collective-permute-start | bytes 688136 | tf_op jit(solution)/shard_map/ppermute | solution.py:72
  155.2 5.2 %collective-permute-start.31 = (bf16[32,3584]{1,0:T(8,128)(2,1)S(1)}, bf16[32,3584]{1,0:T(8,128)(2,1)S(1)}, u32[]{:S(2)}, u32[]{:S(2)}) collective-permute-start(bf16[32,3584]{1,0:T(8,128)(2,1)S(1)} %get-tuple-element.23), channel_id=1, source_target_pairs={{8,0},{33,1},{16,8},{41,9},{24,16},{49,17},{0,24},{57,25},{40,32},... | collective-permute-start | bytes 688136 | tf_op jit(solution)/shard_map/ppermute | solution.py:72
  155.4 9.9 %collective-permute-start.41 = (bf16[64,3584]{1,0:T(8,128)(2,1)S(1)}, bf16[64,3584]{1,0:T(8,128)(2,1)S(1)}, u32[]{:S(2)}, u32[]{:S(2)}) collective-permute-start(bf16[64,3584]{1,0:T(8,128)(2,1)S(1)} %pad_maximum_fusion.7), channel_id=1, source_target_pairs={{8,0},{33,1},{16,8},{41,9},{24,16},{49,17},{0,24},{57,25},{40,32},... | collective-permute-start | bytes 1376264 | tf_op jit(solution)/shard_map/ppermute | solution.py:72
  158.0 8.8 %collective-permute-start.39 = (bf16[64,3584]{1,0:T(8,128)(2,1)S(1)}, bf16[64,3584]{1,0:T(8,128)(2,1)S(1)}, u32[]{:S(2)}, u32[]{:S(2)}) collective-permute-start(bf16[64,3584]{1,0:T(8,128)(2,1)S(1)} %pad_maximum_fusion.6), channel_id=1, source_target_pairs={{24,0},{97,1},{0,8},{105,9},{8,16},{113,17},{16,24},{121,25},{56,3... | collective-permute-start | bytes 1376264 | tf_op jit(solution)/shard_map/ppermute | solution.py:72
  160.6 27.9 %collective-permute-start.32 = (bf16[64,3584]{1,0:T(8,128)(2,1)S(1)}, bf16[64,3584]{1,0:T(8,128)(2,1)S(1)}, u32[]{:S(2)}, u32[]{:S(2)}) collective-permute-start(bf16[64,3584]{1,0:T(8,128)(2,1)S(1)} %pad_maximum_fusion.5), channel_id=1, source_target_pairs={{8,0},{33,1},{16,8},{41,9},{24,16},{49,17},{0,24},{57,25},{40,32},... | collective-permute-start | bytes 1376264 | tf_op jit(solution)/shard_map/ppermute | solution.py:72
  161.6 26.8 %collective-permute-start.30 = (bf16[64,3584]{1,0:T(8,128)(2,1)S(1)}, bf16[64,3584]{1,0:T(8,128)(2,1)S(1)}, u32[]{:S(2)}, u32[]{:S(2)}) collective-permute-start(bf16[64,3584]{1,0:T(8,128)(2,1)S(1)} %pad_maximum_fusion.4), channel_id=1, source_target_pairs={{24,0},{97,1},{0,8},{105,9},{8,16},{113,17},{16,24},{121,25},{56,3... | collective-permute-start | bytes 1376264 | tf_op jit(solution)/shard_map/ppermute | solution.py:72
  162.4 22.6 %collective-permute-start.36 = (bf16[128,3584]{1,0:T(8,128)(2,1)S(1)}, bf16[128,3584]{1,0:T(8,128)(2,1)S(1)}, u32[]{:S(2)}, u32[]{:S(2)}) collective-permute-start(bf16[128,3584]{1,0:T(8,128)(2,1)S(1)} %pad_maximum_fusion.2), channel_id=1, source_target_pairs={{8,0},{33,1},{16,8},{41,9},{24,16},{49,17},{0,24},{57,25},{40,32},... | collective-permute-start | bytes 2752520 | tf_op jit(solution)/shard_map/ppermute | solution.py:72
  165.3 21.2 %collective-permute-start.34 = (bf16[128,3584]{1,0:T(8,128)(2,1)S(1)}, bf16[128,3584]{1,0:T(8,128)(2,1)S(1)}, u32[]{:S(2)}, u32[]{:S(2)}) collective-permute-start(bf16[128,3584]{1,0:T(8,128)(2,1)S(1)} %pad_maximum_fusion.1), channel_id=1, source_target_pairs={{24,0},{97,1},{0,8},{105,9},{8,16},{113,17},{16,24},{121,25},{56,3... | collective-permute-start | bytes 2752520 | tf_op jit(solution)/shard_map/ppermute | solution.py:72
  167.0 21.4 %collective-permute-start.42 = (bf16[64,3584]{1,0:T(8,128)(2,1)S(1)}, bf16[64,3584]{1,0:T(8,128)(2,1)S(1)}, u32[]{:S(2)}, u32[]{:S(2)}) collective-permute-start(bf16[64,3584]{1,0:T(8,128)(2,1)S(1)} %add_convert_fusion.2), channel_id=1, source_target_pairs={{64,0},{17,1},{72,8},{25,9},{80,16},{1,17},{88,24},{9,25},{96,32},... | collective-permute-start | bytes 1376264 | tf_op jit(solution)/shard_map/ppermute | solution.py:72
  186.9 7.7 %collective-permute-start.43 = (bf16[64,3584]{1,0:T(8,128)(2,1)S(1)}, bf16[64,3584]{1,0:T(8,128)(2,1)S(1)}, u32[]{:S(2)}, u32[]{:S(2)}) collective-permute-start(bf16[64,3584]{1,0:T(8,128)(2,1)S(1)} %get-tuple-element.43), channel_id=1, source_target_pairs={{32,0},{9,1},{40,8},{17,9},{48,16},{25,17},{56,24},{1,25},{64,32},... | collective-permute-start | bytes 1376264 | tf_op jit(solution)/shard_map/ppermute | solution.py:72
  187.0 8.9 %collective-permute-start.37 = (bf16[64,3584]{1,0:T(8,128)(2,1)S(1)}, bf16[64,3584]{1,0:T(8,128)(2,1)S(1)}, u32[]{:S(2)}, u32[]{:S(2)}) collective-permute-start(bf16[64,3584]{1,0:T(8,128)(2,1)S(1)} %get-tuple-element.42), channel_id=1, source_target_pairs={{96,0},{25,1},{104,8},{1,9},{112,16},{9,17},{120,24},{17,25},{0,32... | collective-permute-start | bytes 1376264 | tf_op jit(solution)/shard_map/ppermute | solution.py:72
  196.3 8.2 %collective-permute-start.46 = (bf16[2,8,3584]{2,1,0:T(8,128)(2,1)S(1)}, bf16[2,8,3584]{2,1,0:T(8,128)(2,1)S(1)}, u32[]{:S(2)}, u32[]{:S(2)}) collective-permute-start(bf16[2,8,3584]{2,1,0:T(8,128)(2,1)S(1)} %get-tuple-element.48), channel_id=1, source_target_pairs={{2,0},{4,2},{6,4},{0,6},{3,1},{5,3},{7,5},{1,7},{10,8},{12,10},{14... | collective-permute-start | bytes 344072 | tf_op jit(solution)/shard_map/ppermute | solution.py:71
  196.8 7.6 %collective-permute-start.45 = (bf16[2,8,3584]{2,1,0:T(8,128)(2,1)S(1)}, bf16[2,8,3584]{2,1,0:T(8,128)(2,1)S(1)}, u32[]{:S(2)}, u32[]{:S(2)}) collective-permute-start(bf16[2,8,3584]{2,1,0:T(8,128)(2,1)S(1)} %get-tuple-element.49), channel_id=1, source_target_pairs={{4,0},{6,2},{0,4},{2,6},{5,1},{7,3},{1,5},{3,7},{12,8},{14,10},{8,... | collective-permute-start | bytes 344072 | tf_op jit(solution)/shard_map/ppermute | solution.py:71
  197.9 6.5 %collective-permute-start.44 = (bf16[2,8,3584]{2,1,0:T(8,128)(2,1)S(1)}, bf16[2,8,3584]{2,1,0:T(8,128)(2,1)S(1)}, u32[]{:S(2)}, u32[]{:S(2)}) collective-permute-start(bf16[2,8,3584]{2,1,0:T(8,128)(2,1)S(1)} %get-tuple-element.47), channel_id=1, source_target_pairs={{6,0},{0,2},{2,4},{4,6},{7,1},{1,3},{3,5},{5,7},{14,8},{8,10},{10,... | collective-permute-start | bytes 344072 | tf_op jit(solution)/shard_map/ppermute | solution.py:71
  198.4 12.2 %collective-permute-start.4 = (bf16[8,3584]{1,0:T(8,128)(2,1)S(1)}, bf16[8,3584]{1,0:T(8,128)(2,1)S(1)}, u32[]{:S(2)}, u32[]{:S(2)}) collective-permute-start(bf16[8,3584]{1,0:T(8,128)(2,1)S(1)} %get-tuple-element.52), channel_id=1, source_target_pairs={{0,1},{1,0},{2,3},{3,2},{4,5},{5,4},{6,7},{7,6},{8,9},{9,8},{10,11... | collective-permute-start | bytes 172040 | tf_op jit(solution)/shard_map/ppermute | solution.py:76
  204.5 7.0 %collective-permute-start.47 = (bf16[8,3584]{1,0:T(8,128)(2,1)S(1)}, bf16[8,3584]{1,0:T(8,128)(2,1)S(1)}, u32[]{:S(2)}, u32[]{:S(2)}) collective-permute-start(bf16[8,3584]{1,0:T(8,128)(2,1)S(1)} %get-tuple-element.55), channel_id=1, source_target_pairs={{0,1},{1,0},{2,3},{3,2},{4,5},{5,4},{6,7},{7,6},{8,9},{9,8},{10,11... | collective-permute-start | bytes 172040 | tf_op jit(solution)/shard_map/ppermute | solution.py:76
  (11 other events, 109.0 us)

commit v4 on v3

--- a/solution.py
+++ b/solution.py
@@ -1,6 +1,8 @@
 import jax
 import jax.numpy as jnp
 from jax import lax
+from jax.experimental import pallas as pl
+from jax.experimental.pallas import tpu as pltpu
 from jax.sharding import Mesh, PartitionSpec as P
 
 score_scale = 192.0 ** (-0.5)
@@ -47,6 +49,36 @@
     slot_hits = slot_of[:, :, None] == labels
     weight_table = jnp.sum(jnp.where(slot_hits, gates[:, :, None].astype(jnp.float32), 0.0), axis=1)
     return weight_table.astype(jnp.bfloat16)
+
+
+def project_block(first_ref, values_ref, weight_ref, out_ref):
+    out_ref[...] = jnp.dot(values_ref[...], weight_ref[...], preferred_element_type=f32)
+
+
+def project(values, weight, core):
+    rows, depth = values.shape
+    width = weight.shape[1]
+    block = 512
+    blocks = width // block
+    first = ((1 - core) * (blocks // 2)).astype(jnp.int32).reshape(1)
+    return pl.pallas_call(
+        project_block,
+        out_shape=jax.ShapeDtypeStruct((rows, width), f32),
+        grid_spec=pltpu.PrefetchScalarGridSpec(
+            num_scalar_prefetch=1,
+            grid=(blocks,),
+            in_specs=[
+                pl.BlockSpec((rows, depth), lambda i, first: (0, 0)),
+                pl.BlockSpec((depth, block), lambda i, first: (0, lax.rem(i + first[0], blocks))),
+            ],
+            out_specs=pl.BlockSpec((rows, block), lambda i, first: (0, i)),
+        ),
+        compiler_params=pltpu.CompilerParams(vmem_limit_bytes=16 * 1024 * 1024),
+        cost_estimate=pl.CostEstimate(
+            flops=2 * rows * depth * width, bytes_accessed=2 * depth * width, transcendentals=0
+        ),
+        name="project",
+    )(first, values, weight)
 
 
 near_axis = ("y", "z")
@@ -173,8 +205,8 @@
         "thl,hlv->thv", exchanged, value_up, preferred_element_type=f32
     ).astype(bf16)
     values = values.reshape(values.shape[0], values.shape[1] * values.shape[2])
-    projected = jnp.dot(values, out_proj, preferred_element_type=f32)
-    chip_sum = mine(projected, 1) + swap(others(projected, 1).astype(bf16)).astype(f32)
+    projected = project(values, out_proj, core)
+    chip_sum = projected[:, half:] + swap(projected[:, :half].astype(bf16)).astype(f32)
     chip_sum = chip_sum.reshape(4, 2 * rows, half)
 
     def for_chip(distance):
@@ -200,9 +232,12 @@
     count = 8 * rows
 
     far_own = gather_far(group, far_axis)
-    right, left, opposite = (shift(group, near_axis, d) for d in (1, -1, 2))
-    far_sides = gather_far(jnp.concatenate([right, left], axis=0), far_axis)
-    far_opposite = gather_far(opposite, far_axis)
+    near = [shift(group, near_axis, d) for d in (1, 2, -1)]
+    part = count // 2
+    rest = [
+        gather_far(jnp.concatenate([v[c * part : (c + 1) * part] for v in near], axis=0), far_axis)
+        for c in range(2)
+    ]
 
     hidden = weight_in.shape[1] // 2
     units = hidden // 2
@@ -223,33 +258,47 @@
             for b in blocks
         ]
 
-    def by_near(own, sides, opposite):
+    def in_order(own, rest):
+        return jnp.concatenate(own + rest[0] + rest[1], axis=0)
+
+    def by_near(value):
+        cut = 4 * count
+        own = value[:cut].reshape(1, 4, 2, part, value.shape[1])
+        others = value[cut:].reshape(2, 4, 3, part, value.shape[1]).transpose(2, 1, 0, 3, 4)
+        return jnp.concatenate([own, others], axis=0).reshape(16 * count, value.shape[1])
+
+    def by_chunk(value):
+        value = value.reshape(4, 4, 2, part, value.shape[1])
+        own, others = value[:1], value[1:].transpose(2, 1, 0, 3, 4)
         return jnp.concatenate(
-            own + [v[:count] for v in sides] + opposite + [v[count:] for v in sides], axis=0
+            [own.reshape(4 * count, value.shape[4]), others.reshape(12 * count, value.shape[4])],
+            axis=0,
         )
 
-    product = by_near(into(far_own), into(far_sides), into(far_opposite))
-    weights = by_near(table_of(far_own), table_of(far_sides), table_of(far_opposite))
+    product = in_order(into(far_own), [into(r) for r in rest])
+    weights = in_order(table_of(far_own), [table_of(r) for r in rest])
     got = swap(product[:, hidden:].astype(bf16))
-    product = product[:, :hidden] + crossed(got).astype(f32)
+    product = product[:, :hidden] + by_chunk(crossed(by_near(got))).astype(f32)
     activated = (jax.nn.silu(product[:, :units]) * product[:, units:]).astype(bf16)
-    activated = jnp.concatenate([activated, crossed(swap(activated))], axis=1)
-
-    def out_of(near):
-        rows_of = slice(near * 4 * count, (near + 1) * 4 * count)
+    activated = jnp.concatenate([activated, by_chunk(crossed(by_near(swap(activated))))], axis=1)
+
+    def out_of(start, size):
+        rows_of = slice(start, start + 4 * size)
         out = jnp.dot(activated[rows_of], weight_out, preferred_element_type=f32)
         out = (out * weights[rows_of]).astype(bf16)
-        return [out[i * count : (i + 1) * count] for i in range(4)]
-
-    back_opposite = scatter_far(*out_of(2), far_axis)
-    sides = [jnp.concatenate(pair, axis=0) for pair in zip(out_of(1), out_of(3))]
-    back_sides = scatter_far(*sides, far_axis)
-    back_own = scatter_far(*out_of(0), far_axis)
+        return [out[i * size : (i + 1) * size] for i in range(4)]
+
+    cut = 4 * count
+    back = [scatter_far(*out_of(cut + c * 12 * part, 3 * part), far_axis) for c in range(2)]
+    back_own = scatter_far(*out_of(0, count), far_axis)
+    sent = [
+        jnp.concatenate([b[n * part : (n + 1) * part] for b in back], axis=0) for n in range(3)
+    ]
     summed = total(
         back_own,
-        shift(back_sides[:count], near_axis, -1),
-        shift(back_opposite, near_axis, 2),
-        shift(back_sides[count:], near_axis, 1),
+        shift(sent[0], near_axis, -1),
+        shift(sent[1], near_axis, 2),
+        shift(sent[2], near_axis, 1),
     ).astype(bf16)
     to_x = summed.reshape(4, 2, rows, half)
     chip_out = scatter_near(to_x, "x")

time: 213 us -> 222 us (1.042)
  matrix products: 30.1 us -> 20.9 us
  local copies, waits for them, and re-layouts: 7.11 us -> 14.2 us
  Pallas kernels: 0 us -> 5.66 us
  waiting for transfers between devices: 92.7 us -> 97.4 us
    dot_general x1 -> x0, matrix products: 8.06 us -> none  [per_device(): projected = jnp.dot(values, out_proj, preferred_element_type=f32)]
    unnamed x31 -> x47, local copies, waits for them, and re-layouts: 0.24 us -> 6.72 us
    pallas_call x0 -> x1, Pallas kernels: none -> 5.66 us  [project(): pl.pallas_call(project_block, out_shape=jax.ShapeDtypeStruct((rows, width...]
    ppermute x30, waiting for transfers between devices: 70.3 us -> 73.8 us  [shift(): return lax.ppermute(value, ('y', 'z', 'core'), ring(axes, distance))]
    ppermute x9, starting transfers between devices: 24.5 us -> 21.1 us  [swap(): return lax.ppermute(value, 'core', [(0, 1), (1, 0)])]
    dot_general x4 -> x3, matrix products: 7.29 us -> 5.98 us  [out_of(): out = jnp.dot(activated[rows_of], weight_out, preferred_element_type=f32)]
  transfers between devices with their start and end apart: 49 -> 49, of which waited for: 31 -> 24; matrix products, arithmetic and copies ran while one was open for 17% -> 11% of each run, Pallas kernels for 0% -> 0%
where the time goes in v4:
time: 222 us
  waiting for transfers between devices  97.4 us (44%)
  starting transfers between devices  71 us (32%)
  matrix products  20.9 us (9%)
  local copies, waits for them, and re-layouts  14.2 us (6%)
  other arithmetic  10.7 us (5%)
  Pallas kernels  5.66 us (3%)
    ppermute x30, waiting for transfers between devices, shift(): return lax.ppermute(value, ('y', 'z', 'core'), ring(axes, distance))  73.8 us
    ppermute x30, starting transfers between devices, shift(): return lax.ppermute(value, ('y', 'z', 'core'), ring(axes, distance))  35.7 us
    ppermute x9, starting transfers between devices, swap(): return lax.ppermute(value, 'core', [(0, 1), (1, 0)])  21.1 us
    ppermute x9, waiting for transfers between devices, shift(): return lax.ppermute(value, 'x', [((i + distance) % 4, i) for i in range(4)])  11.3 us
    dot_general x12, matrix products, into(): return [jnp.dot(b, weight_in, preferred_element_type=f32) for b in blocks]  8.96 us
    all_to_all x1, waiting for transfers between devices, per_device(): lax.all_to_all(latent_out, ('x', 'core'), split_axis=1, concat_axis=0, ti...  8.84 us
    ppermute x9, starting transfers between devices, shift(): return lax.ppermute(value, 'x', [((i + distance) % 4, i) for i in range(4)])  8.46 us
    unnamed x47, local copies, waits for them, and re-layouts  6.72 us
  transfers between devices with their start and end apart: 49, of which 24 were waited for; matrix products, arithmetic and copies ran while one was open for 11% of the time, Pallas kernels for 0%

profile of v4, /device:TPU:1, one launch (start us, length us, event | category | flops | bytes accessed | tf_op | source)
XLA Modules:
  0.0 221.6 jit_solution(1394979683335975853)
XLA Ops:
  1.4 1.4 fusion.54
  2.8 3.1 %fusion.71 = (f32[8,64]{1,0:T(8,128)S(1)}, f32[8,64,384]{2,1,0:T(8,128)S(1)}) fusion(bf16[8,64,576]{2,1,0:T(8,128)(2,1)} %param.14, bf16[8,384,576]{1,2,0:T(8,128)(2,1)} %param.15, s32[8]{0:T(128)} %param.17), kind=kOutput, calls=%fused_computation.185 | convolution fusion | flops 227278336 | bytes 4917280 | tf_op jit(solution)/shard_map/rhc,rtc->rht/dot_general | solution.py:17
  8.6 5.8 %all-to-all-start = ((bf16[8,64,512]{2,0,1:T(8,128)(2,1)}), bf16[8,64,512]{2,0,1:T(8,128)(2,1)S(1)}, u32[]{:S(2)}, u32[]{:S(2)}) async-start(bf16[8,64,512]{2,0,1:T(8,128)(2,1)} %copy.41), calls=%async_computation | async-start | bytes 1048576 | tf_op jit(solution)/shard_map/all_to_all | solution.py:186
  15.1 8.8 %all-to-all-done = bf16[8,64,512]{2,0,1:T(8,128)(2,1)S(1)} async-done(((bf16[8,64,512]{2,0,1:T(8,128)(2,1)}), bf16[8,64,512]{2,0,1:T(8,128)(2,1)S(1)}, u32[]{:S(2)}, u32[]{:S(2)}) %all-to-all-start) | async-done | bytes 524320 | tf_op jit(solution)/shard_map/all_to_all | solution.py:186
  24.3 5.2 %copy-done.2 = bf16[1024,7168]{1,0:T(8,128)(2,1)S(1)} copy-done((bf16[1024,7168]{1,0:T(8,128)(2,1)S(1)}, bf16[1024,7168]{1,0:T(8,128)(2,1)}, u32[]{:S(2)}) %copy-start.2) | copy-done | bytes 14680088
  29.4 5.7 %project.1 = f32[64,7168]{1,0:T(8,128)S(1)} custom-call(s32[1]{0:T(128)} %bitcast.first_ref, bf16[64,1024]{1,0:T(8,128)(2,1)S(1)} %bitcast.141, bf16[1024,7168]{1,0:T(8,128)(2,1)S(1)} %copy-done.2), custom_call_target="tpu_custom_call" | custom-call | flops 939524096 | bytes 14680064 | tf_op jit(solution)/shard_map/project/pallas_call | solution.py:64
  36.3 1.3 collective-permute-done
  39.2 1.8 collective-permute-start.2
  41.7 3.4 %collective-permute-done.1 = bf16[16,3584]{1,0:T(8,128)(2,1)S(1)} collective-permute-done((bf16[16,3584]{1,0:T(8,128)(2,1)S(1)}, bf16[16,3584]{1,0:T(8,128)(2,1)S(1)}, u32[]{:S(2)}, u32[]{:S(2)}) %collective-permute-start.1) | collective-permute-done | bytes 114720 | tf_op jit(solution)/shard_map/ppermute | solution.py:103
  45.1 1.3 collective-permute-done.2
  47.5 1.5 collective-permute-start.6
  50.0 2.2 collective-permute-start.7
  52.9 1.4 dynamic-slice_bitcast_fusion
  55.1 2.9 %collective-permute-done.8 = bf16[16,3712]{1,0:T(8,128)(2,1)S(1)} collective-permute-done((bf16[16,3712]{1,0:T(8,128)(2,1)S(1)}, bf16[16,3712]{1,0:T(8,128)(2,1)S(1)}, u32[]{:S(2)}, u32[]{:S(2)}) %collective-permute-start.8) | collective-permute-done | bytes 118816 | tf_op jit(solution)/shard_map/ppermute | solution.py:103
  58.0 2.8 %collective-permute-done.9 = bf16[16,3712]{1,0:T(8,128)(2,1)S(1)} collective-permute-done((bf16[16,3712]{1,0:T(8,128)(2,1)S(1)}, bf16[16,3712]{1,0:T(8,128)(2,1)S(1)}, u32[]{:S(2)}, u32[]{:S(2)}) %collective-permute-start.9) | collective-permute-done | bytes 118816 | tf_op jit(solution)/shard_map/ppermute | solution.py:103
  60.9 3.8 %collective-permute-start.15 = (bf16[64,3712]{1,0:T(8,128)(2,1)S(1)}, bf16[64,3712]{1,0:T(8,128)(2,1)S(1)}, u32[]{:S(2)}, u32[]{:S(2)}) collective-permute-start(bf16[64,3712]{1,0:T(8,128)(2,1)S(1)} %bitcast.145), channel_id=1, source_target_pairs={{32,0},{9,1},{40,8},{17,9},{48,16},{25,17},{56,24},{1,25},{64,32},... | collective-permute-start | bytes 1425416 | tf_op jit(solution)/shard_map/ppermute | solution.py:104
  64.7 1.6 dynamic-slice_bitcast_fusion.2
  66.3 2.8 %collective-permute-start.11 = (bf16[64,3712]{1,0:T(8,128)(2,1)S(1)}, bf16[64,3712]{1,0:T(8,128)(2,1)S(1)}, u32[]{:S(2)}, u32[]{:S(2)}) collective-permute-start(bf16[64,3712]{1,0:T(8,128)(2,1)S(1)} %bitcast.146), channel_id=1, source_target_pairs={{8,0},{33,1},{16,8},{41,9},{24,16},{49,17},{0,24},{57,25},{40,32},... | collective-permute-start | bytes 1425416 | tf_op jit(solution)/shard_map/ppermute | solution.py:104
  69.1 1.3 collective-permute-done.15
  70.6 12.4 %collective-permute-done.16 = bf16[64,3712]{1,0:T(8,128)(2,1)S(1)} collective-permute-done((bf16[64,3712]{1,0:T(8,128)(2,1)S(1)}, bf16[64,3712]{1,0:T(8,128)(2,1)S(1)}, u32[]{:S(2)}, u32[]{:S(2)}) %collective-permute-start.16) | collective-permute-done | bytes 475168 | tf_op jit(solution)/shard_map/ppermute | solution.py:104
  83.1 6.1 %collective-permute-done.17 = bf16[64,3712]{1,0:T(8,128)(2,1)S(1)} collective-permute-done((bf16[64,3712]{1,0:T(8,128)(2,1)S(1)}, bf16[64,3712]{1,0:T(8,128)(2,1)S(1)}, u32[]{:S(2)}, u32[]{:S(2)}) %collective-permute-start.17) | collective-permute-done | bytes 475168 | tf_op jit(solution)/shard_map/ppermute | solution.py:104
  90.9 2.3 %collective-permute-start.22 = (bf16[96,3712]{1,0:T(8,128)(2,1)S(1)}, bf16[96,3712]{1,0:T(8,128)(2,1)S(1)}, u32[]{:S(2)}, u32[]{:S(2)}) collective-permute-start(bf16[96,3712]{1,0:T(8,128)(2,1)S(1)} %pad_maximum_fusion.2), channel_id=1, source_target_pairs={{8,0},{33,1},{16,8},{41,9},{24,16},{49,17},{0,24},{57,25},{40,32},... | collective-permute-start | bytes 2138120 | tf_op jit(solution)/shard_map/ppermute | solution.py:104
  93.4 2.9 %collective-permute-start.12 = (bf16[32,3712]{1,0:T(8,128)(2,1)S(1)}, bf16[32,3712]{1,0:T(8,128)(2,1)S(1)}, u32[]{:S(2)}, u32[]{:S(2)}) collective-permute-start(bf16[32,3712]{1,0:T(8,128)(2,1)S(1)} %slice.401), channel_id=1, source_target_pairs={{8,0},{33,1},{16,8},{41,9},{24,16},{49,17},{0,24},{57,25},{40,32},... | collective-permute-start | bytes 712712 | tf_op jit(solution)/shard_map/ppermute | solution.py:104
  96.5 2.2 fusion.9
  100.2 9.7 %collective-permute-done.12 = bf16[32,3712]{1,0:T(8,128)(2,1)S(1)} collective-permute-done((bf16[32,3712]{1,0:T(8,128)(2,1)S(1)}, bf16[32,3712]{1,0:T(8,128)(2,1)S(1)}, u32[]{:S(2)}, u32[]{:S(2)}) %collective-permute-start.12) | collective-permute-done | bytes 237600 | tf_op jit(solution)/shard_map/ppermute | solution.py:104
  109.9 6.1 %collective-permute-done.14 = bf16[32,3712]{1,0:T(8,128)(2,1)S(1)} collective-permute-done((bf16[32,3712]{1,0:T(8,128)(2,1)S(1)}, bf16[32,3712]{1,0:T(8,128)(2,1)S(1)}, u32[]{:S(2)}, u32[]{:S(2)}) %collective-permute-start.14) | collective-permute-done | bytes 237600 | tf_op jit(solution)/shard_map/ppermute | solution.py:104
  117.7 1.4 collective-permute-start.19
  120.2 2.6 %collective-permute-start.23 = (bf16[48,3712]{1,0:T(8,128)(2,1)S(1)}, bf16[48,3712]{1,0:T(8,128)(2,1)S(1)}, u32[]{:S(2)}, u32[]{:S(2)}) collective-permute-start(bf16[48,3712]{1,0:T(8,128)(2,1)S(1)} %slice.411), channel_id=1, source_target_pairs={{8,0},{33,1},{16,8},{41,9},{24,16},{49,17},{0,24},{57,25},{40,32},... | collective-permute-start | bytes 1069064 | tf_op jit(solution)/shard_map/ppermute | solution.py:104
  124.1 3.4 %collective-permute-done.21 = bf16[48,3712]{1,0:T(8,128)(2,1)S(1)} collective-permute-done((bf16[48,3712]{1,0:T(8,128)(2,1)S(1)}, bf16[48,3712]{1,0:T(8,128)(2,1)S(1)}, u32[]{:S(2)}, u32[]{:S(2)}) %collective-permute-start.21) | collective-permute-done | bytes 356384 | tf_op jit(solution)/shard_map/ppermute | solution.py:104
  134.1 7.7 %collective-permute-start.26 = (bf16[1024,256]{1,0:T(8,128)(2,1)}, bf16[1024,256]{1,0:T(8,128)(2,1)S(1)}, u32[]{:S(2)}, u32[]{:S(2)}) collective-permute-start(bf16[1024,256]{1,0:T(8,128)(2,1)} %slice.527), channel_id=1, source_target_pairs={{0,1},{1,0},{2,3},{3,2},{4,5},{5,4},{6,7},{7,6},{8,9},{9,8},{10,11... | collective-permute-start | bytes 1572872 | tf_op jit(solution)/shard_map/ppermute | solution.py:108
  141.8 1.3 dynamic-slice_bitcast_fusion.4
  143.8 1.4 copy-done.11
  148.3 1.8 fusion.6
  150.2 4.9 %collective-permute-start.31 = (bf16[32,3584]{1,0:T(8,128)(2,1)S(1)}, bf16[32,3584]{1,0:T(8,128)(2,1)S(1)}, u32[]{:S(2)}, u32[]{:S(2)}) collective-permute-start(bf16[32,3584]{1,0:T(8,128)(2,1)S(1)} %get-tuple-element.35), channel_id=1, source_target_pairs={{8,0},{33,1},{16,8},{41,9},{24,16},{49,17},{0,24},{57,25},{40,32},... | collective-permute-start | bytes 688136 | tf_op jit(solution)/shard_map/ppermute | solution.py:104
  155.1 2.1 fusion.4
  157.4 2.7 %collective-permute-start.35 = (bf16[48,3584]{1,0:T(8,128)(2,1)S(1)}, bf16[48,3584]{1,0:T(8,128)(2,1)S(1)}, u32[]{:S(2)}, u32[]{:S(2)}) collective-permute-start(bf16[48,3584]{1,0:T(8,128)(2,1)S(1)} %get-tuple-element.23), channel_id=1, source_target_pairs={{8,0},{33,1},{16,8},{41,9},{24,16},{49,17},{0,24},{57,25},{40,32},... | collective-permute-start | bytes 1032200 | tf_op jit(solution)/shard_map/ppermute | solution.py:104
  160.1 2.1 fusion.5
  162.3 2.7 %collective-permute-start.39 = (bf16[48,3584]{1,0:T(8,128)(2,1)S(1)}, bf16[48,3584]{1,0:T(8,128)(2,1)S(1)}, u32[]{:S(2)}, u32[]{:S(2)}) collective-permute-start(bf16[48,3584]{1,0:T(8,128)(2,1)S(1)} %get-tuple-element.29), channel_id=1, source_target_pairs={{8,0},{33,1},{16,8},{41,9},{24,16},{49,17},{0,24},{57,25},{40,32},... | collective-permute-start | bytes 1032200 | tf_op jit(solution)/shard_map/ppermute | solution.py:104
  165.3 2.7 %collective-permute-start.32 = (bf16[64,3584]{1,0:T(8,128)(2,1)S(1)}, bf16[64,3584]{1,0:T(8,128)(2,1)S(1)}, u32[]{:S(2)}, u32[]{:S(2)}) collective-permute-start(bf16[64,3584]{1,0:T(8,128)(2,1)S(1)} %pad_maximum_fusion.12), channel_id=1, source_target_pairs={{8,0},{33,1},{16,8},{41,9},{24,16},{49,17},{0,24},{57,25},{40,32},... | collective-permute-start | bytes 1376264 | tf_op jit(solution)/shard_map/ppermute | solution.py:104
  168.4 1.6 collective-permute-done.37
  171.8 10.4 %collective-permute-done.34 = bf16[96,3584]{1,0:T(8,128)(2,1)S(1)} collective-permute-done((bf16[96,3584]{1,0:T(8,128)(2,1)S(1)}, bf16[96,3584]{1,0:T(8,128)(2,1)S(1)}, u32[]{:S(2)}, u32[]{:S(2)}) %collective-permute-start.34) | collective-permute-done | bytes 688160 | tf_op jit(solution)/shard_map/ppermute | solution.py:104
  182.6 6.7 %collective-permute-done.38 = bf16[96,3584]{1,0:T(8,128)(2,1)S(1)} collective-permute-done((bf16[96,3584]{1,0:T(8,128)(2,1)S(1)}, bf16[96,3584]{1,0:T(8,128)(2,1)S(1)}, u32[]{:S(2)}, u32[]{:S(2)}) %collective-permute-start.38) | collective-permute-done | bytes 688160 | tf_op jit(solution)/shard_map/ppermute | solution.py:104
  189.3 3.0 %collective-permute-done.40 = bf16[96,3584]{1,0:T(8,128)(2,1)S(1)} collective-permute-done((bf16[96,3584]{1,0:T(8,128)(2,1)S(1)}, bf16[96,3584]{1,0:T(8,128)(2,1)S(1)}, u32[]{:S(2)}, u32[]{:S(2)}) %collective-permute-start.40) | collective-permute-done | bytes 688160 | tf_op jit(solution)/shard_map/ppermute | solution.py:104
  192.8 2.0 collective-permute-start.42
  195.7 10.8 %collective-permute-done.41 = bf16[64,3584]{1,0:T(8,128)(2,1)S(1)} collective-permute-done((bf16[64,3584]{1,0:T(8,128)(2,1)S(1)}, bf16[64,3584]{1,0:T(8,128)(2,1)S(1)}, u32[]{:S(2)}, u32[]{:S(2)}) %collective-permute-start.41) | collective-permute-done | bytes 458784 | tf_op jit(solution)/shard_map/ppermute | solution.py:104
  207.7 2.5 %collective-permute-start.45 = (bf16[2,8,3584]{2,1,0:T(8,128)(2,1)S(1)}, bf16[2,8,3584]{2,1,0:T(8,128)(2,1)S(1)}, u32[]{:S(2)}, u32[]{:S(2)}) collective-permute-start(bf16[2,8,3584]{2,1,0:T(8,128)(2,1)S(1)} %get-tuple-element.59), channel_id=1, source_target_pairs={{4,0},{6,2},{0,4},{2,6},{5,1},{7,3},{1,5},{3,7},{12,8},{14,10},{8,... | collective-permute-start | bytes 344072 | tf_op jit(solution)/shard_map/ppermute | solution.py:103
  210.4 4.9 %collective-permute-start.4 = (bf16[8,3584]{1,0:T(8,128)(2,1)S(1)}, bf16[8,3584]{1,0:T(8,128)(2,1)S(1)}, u32[]{:S(2)}, u32[]{:S(2)}) collective-permute-start(bf16[8,3584]{1,0:T(8,128)(2,1)S(1)} %get-tuple-element.62), channel_id=1, source_target_pairs={{0,1},{1,0},{2,3},{3,2},{4,5},{5,4},{6,7},{7,6},{8,9},{9,8},{10,11... | collective-permute-start | bytes 172040 | tf_op jit(solution)/shard_map/ppermute | solution.py:108
  215.4 4.6 %collective-permute-start.47 = (bf16[8,3584]{1,0:T(8,128)(2,1)S(1)}, bf16[8,3584]{1,0:T(8,128)(2,1)S(1)}, u32[]{:S(2)}, u32[]{:S(2)}) collective-permute-start(bf16[8,3584]{1,0:T(8,128)(2,1)S(1)} %get-tuple-element.65), channel_id=1, source_target_pairs={{0,1},{1,0},{2,3},{3,2},{4,5},{5,4},{6,7},{7,6},{8,9},{9,8},{10,11... | collective-permute-start | bytes 172040 | tf_op jit(solution)/shard_map/ppermute | solution.py:108
  (208 shorter events, 36.8 us)
Async XLA Ops:
  8.6 15.3 %all-to-all-start = ((bf16[8,64,512]{2,0,1:T(8,128)(2,1)}), bf16[8,64,512]{2,0,1:T(8,128)(2,1)S(1)}, u32[]{:S(2)}, u32[]{:S(2)}) async-start(bf16[8,64,512]{2,0,1:T(8,128)(2,1)} %copy.41), calls=%async_computation | async-start | bytes 1048576 | tf_op jit(solution)/shard_map/all_to_all | solution.py:186
  35.1 2.5 %collective-permute-start = (bf16[64,3584]{1,0:T(8,128)(2,1)S(1)}, bf16[64,3584]{1,0:T(8,128)(2,1)}, u32[]{:S(2)}, u32[]{:S(2)}) collective-permute-start(bf16[64,3584]{1,0:T(8,128)(2,1)S(1)} %slice.528), channel_id=1, source_target_pairs={{0,1},{1,0},{2,3},{3,2},{4,5},{5,4},{6,7},{7,6},{8,9},{9,8},{10,11... | collective-permute-start | bytes 1376264 | tf_op jit(solution)/shard_map/ppermute | solution.py:108
  36.1 5.6 %collective-permute-start.5 = (bf16[8,3712]{1,0:T(8,128)(2,1)S(1)}, bf16[8,3712]{1,0:T(8,128)(2,1)S(1)}, u32[]{:S(2)}, u32[]{:S(2)}) collective-permute-start(bf16[8,3712]{1,0:T(8,128)(2,1)S(1)} %get-tuple-element.71), channel_id=1, source_target_pairs={{0,1},{1,0},{2,3},{3,2},{4,5},{5,4},{6,7},{7,6},{8,9},{9,8},{10,11... | collective-permute-start | bytes 178184 | tf_op jit(solution)/shard_map/ppermute | solution.py:108
  38.8 6.2 %collective-permute-start.1 = (bf16[16,3584]{1,0:T(8,128)(2,1)S(1)}, bf16[16,3584]{1,0:T(8,128)(2,1)S(1)}, u32[]{:S(2)}, u32[]{:S(2)}) collective-permute-start(bf16[16,3584]{1,0:T(8,128)(2,1)S(1)} %get-tuple-element.42), channel_id=1, source_target_pairs={{6,0},{0,2},{2,4},{4,6},{7,1},{1,3},{3,5},{5,7},{14,8},{8,10},{10,... | collective-permute-start | bytes 344072 | tf_op jit(solution)/shard_map/ppermute | solution.py:103
  39.2 7.1 %collective-permute-start.2 = (bf16[16,3584]{1,0:T(8,128)(2,1)S(1)}, bf16[16,3584]{1,0:T(8,128)(2,1)S(1)}, u32[]{:S(2)}, u32[]{:S(2)}) collective-permute-start(bf16[16,3584]{1,0:T(8,128)(2,1)S(1)} %get-tuple-element.44), channel_id=1, source_target_pairs={{4,0},{6,2},{0,4},{2,6},{5,1},{7,3},{1,5},{3,7},{12,8},{14,10},{8,... | collective-permute-start | bytes 344072 | tf_op jit(solution)/shard_map/ppermute | solution.py:103
  41.0 6.3 %collective-permute-start.3 = (bf16[16,3584]{1,0:T(8,128)(2,1)S(1)}, bf16[16,3584]{1,0:T(8,128)(2,1)S(1)}, u32[]{:S(2)}, u32[]{:S(2)}) collective-permute-start(bf16[16,3584]{1,0:T(8,128)(2,1)S(1)} %get-tuple-element.43), channel_id=1, source_target_pairs={{2,0},{4,2},{6,4},{0,6},{3,1},{5,3},{7,5},{1,7},{10,8},{12,10},{14... | collective-permute-start | bytes 344072 | tf_op jit(solution)/shard_map/ppermute | solution.py:103
  50.0 5.1 %collective-permute-start.7 = (bf16[16,3712]{1,0:T(8,128)(2,1)S(1)}, bf16[16,3712]{1,0:T(8,128)(2,1)S(1)}, u32[]{:S(2)}, u32[]{:S(2)}) collective-permute-start(bf16[16,3712]{1,0:T(8,128)(2,1)S(1)} %get-tuple-element.61), channel_id=1, source_target_pairs={{2,0},{4,2},{6,4},{0,6},{3,1},{5,3},{7,5},{1,7},{10,8},{12,10},{14... | collective-permute-start | bytes 356360 | tf_op jit(solution)/shard_map/ppermute | solution.py:103
  52.2 5.8 %collective-permute-start.8 = (bf16[16,3712]{1,0:T(8,128)(2,1)S(1)}, bf16[16,3712]{1,0:T(8,128)(2,1)S(1)}, u32[]{:S(2)}, u32[]{:S(2)}) collective-permute-start(bf16[16,3712]{1,0:T(8,128)(2,1)S(1)} %get-tuple-element.61), channel_id=1, source_target_pairs={{4,0},{6,2},{0,4},{2,6},{5,1},{7,3},{1,5},{3,7},{12,8},{14,10},{8,... | collective-permute-start | bytes 356360 | tf_op jit(solution)/shard_map/ppermute | solution.py:103
  52.2 8.6 %collective-permute-start.9 = (bf16[16,3712]{1,0:T(8,128)(2,1)S(1)}, bf16[16,3712]{1,0:T(8,128)(2,1)S(1)}, u32[]{:S(2)}, u32[]{:S(2)}) collective-permute-start(bf16[16,3712]{1,0:T(8,128)(2,1)S(1)} %get-tuple-element.61), channel_id=1, source_target_pairs={{6,0},{0,2},{2,4},{4,6},{7,1},{1,3},{3,5},{5,7},{14,8},{8,10},{10,... | collective-permute-start | bytes 356360 | tf_op jit(solution)/shard_map/ppermute | solution.py:103
  54.2 39.2 %collective-permute-start.10 = (bf16[2,3584,128]{2,1,0:T(8,128)(2,1)}, bf16[2,3584,128]{2,1,0:T(8,128)(2,1)S(1)}, u32[]{:S(2)}, u32[]{:S(2)}) collective-permute-start(bf16[2,3584,128]{2,1,0:T(8,128)(2,1)} %dynamic-slice_bitcast_fusion), channel_id=1, source_target_pairs={{0,1},{1,0},{2,3},{3,2},{4,5},{5,4},{6,7},{7,6},{8,9},{9,8},{10,11... | collective-permute-start | bytes 5505032 | tf_op jit(solution)/shard_map/ppermute | solution.py:108
  60.9 9.5 %collective-permute-start.15 = (bf16[64,3712]{1,0:T(8,128)(2,1)S(1)}, bf16[64,3712]{1,0:T(8,128)(2,1)S(1)}, u32[]{:S(2)}, u32[]{:S(2)}) collective-permute-start(bf16[64,3712]{1,0:T(8,128)(2,1)S(1)} %bitcast.145), channel_id=1, source_target_pairs={{32,0},{9,1},{40,8},{17,9},{48,16},{25,17},{56,24},{1,25},{64,32},... | collective-permute-start | bytes 1425416 | tf_op jit(solution)/shard_map/ppermute | solution.py:104
  66.3 24.6 %collective-permute-start.11 = (bf16[64,3712]{1,0:T(8,128)(2,1)S(1)}, bf16[64,3712]{1,0:T(8,128)(2,1)S(1)}, u32[]{:S(2)}, u32[]{:S(2)}) collective-permute-start(bf16[64,3712]{1,0:T(8,128)(2,1)S(1)} %bitcast.146), channel_id=1, source_target_pairs={{8,0},{33,1},{16,8},{41,9},{24,16},{49,17},{0,24},{57,25},{40,32},... | collective-permute-start | bytes 1425416 | tf_op jit(solution)/shard_map/ppermute | solution.py:104
  69.1 24.2 %collective-permute-start.13 = (bf16[64,3712]{1,0:T(8,128)(2,1)S(1)}, bf16[64,3712]{1,0:T(8,128)(2,1)S(1)}, u32[]{:S(2)}, u32[]{:S(2)}) collective-permute-start(bf16[64,3712]{1,0:T(8,128)(2,1)S(1)} %bitcast.147), channel_id=1, source_target_pairs={{24,0},{97,1},{0,8},{105,9},{8,16},{113,17},{16,24},{121,25},{56,3... | collective-permute-start | bytes 1425416 | tf_op jit(solution)/shard_map/ppermute | solution.py:104
  69.1 14.0 %collective-permute-start.16 = (bf16[64,3712]{1,0:T(8,128)(2,1)S(1)}, bf16[64,3712]{1,0:T(8,128)(2,1)S(1)}, u32[]{:S(2)}, u32[]{:S(2)}) collective-permute-start(bf16[64,3712]{1,0:T(8,128)(2,1)S(1)} %bitcast.148), channel_id=1, source_target_pairs={{64,0},{17,1},{72,8},{25,9},{80,16},{1,17},{88,24},{9,25},{96,32},... | collective-permute-start | bytes 1425416 | tf_op jit(solution)/shard_map/ppermute | solution.py:104
  70.4 18.8 %collective-permute-start.17 = (bf16[64,3712]{1,0:T(8,128)(2,1)S(1)}, bf16[64,3712]{1,0:T(8,128)(2,1)S(1)}, u32[]{:S(2)}, u32[]{:S(2)}) collective-permute-start(bf16[64,3712]{1,0:T(8,128)(2,1)S(1)} %bitcast.149), channel_id=1, source_target_pairs={{96,0},{25,1},{104,8},{1,9},{112,16},{9,17},{120,24},{17,25},{0,32... | collective-permute-start | bytes 1425416 | tf_op jit(solution)/shard_map/ppermute | solution.py:104
  89.3 28.3 %collective-permute-start.18 = (bf16[96,3712]{1,0:T(8,128)(2,1)S(1)}, bf16[96,3712]{1,0:T(8,128)(2,1)S(1)}, u32[]{:S(2)}, u32[]{:S(2)}) collective-permute-start(bf16[96,3712]{1,0:T(8,128)(2,1)S(1)} %pad_maximum_fusion.1), channel_id=1, source_target_pairs={{8,0},{33,1},{16,8},{41,9},{24,16},{49,17},{0,24},{57,25},{40,32},... | collective-permute-start | bytes 2138120 | tf_op jit(solution)/shard_map/ppermute | solution.py:104
  90.4 29.4 %collective-permute-start.20 = (bf16[96,3712]{1,0:T(8,128)(2,1)S(1)}, bf16[96,3712]{1,0:T(8,128)(2,1)S(1)}, u32[]{:S(2)}, u32[]{:S(2)}) collective-permute-start(bf16[96,3712]{1,0:T(8,128)(2,1)S(1)} %pad_maximum_fusion.1), channel_id=1, source_target_pairs={{24,0},{97,1},{0,8},{105,9},{8,16},{113,17},{16,24},{121,25},{56,3... | collective-permute-start | bytes 2138120 | tf_op jit(solution)/shard_map/ppermute | solution.py:104
  90.9 29.2 %collective-permute-start.22 = (bf16[96,3712]{1,0:T(8,128)(2,1)S(1)}, bf16[96,3712]{1,0:T(8,128)(2,1)S(1)}, u32[]{:S(2)}, u32[]{:S(2)}) collective-permute-start(bf16[96,3712]{1,0:T(8,128)(2,1)S(1)} %pad_maximum_fusion.2), channel_id=1, source_target_pairs={{8,0},{33,1},{16,8},{41,9},{24,16},{49,17},{0,24},{57,25},{40,32},... | collective-permute-start | bytes 2138120 | tf_op jit(solution)/shard_map/ppermute | solution.py:104
  93.3 29.5 %collective-permute-start.24 = (bf16[96,3712]{1,0:T(8,128)(2,1)S(1)}, bf16[96,3712]{1,0:T(8,128)(2,1)S(1)}, u32[]{:S(2)}, u32[]{:S(2)}) collective-permute-start(bf16[96,3712]{1,0:T(8,128)(2,1)S(1)} %pad_maximum_fusion.2), channel_id=1, source_target_pairs={{24,0},{97,1},{0,8},{105,9},{8,16},{113,17},{16,24},{121,25},{56,3... | collective-permute-start | bytes 2138120 | tf_op jit(solution)/shard_map/ppermute | solution.py:104
  93.4 16.5 %collective-permute-start.12 = (bf16[32,3712]{1,0:T(8,128)(2,1)S(1)}, bf16[32,3712]{1,0:T(8,128)(2,1)S(1)}, u32[]{:S(2)}, u32[]{:S(2)}) collective-permute-start(bf16[32,3712]{1,0:T(8,128)(2,1)S(1)} %slice.401), channel_id=1, source_target_pairs={{8,0},{33,1},{16,8},{41,9},{24,16},{49,17},{0,24},{57,25},{40,32},... | collective-permute-start | bytes 712712 | tf_op jit(solution)/shard_map/ppermute | solution.py:104
  109.9 6.2 %collective-permute-start.14 = (bf16[32,3712]{1,0:T(8,128)(2,1)S(1)}, bf16[32,3712]{1,0:T(8,128)(2,1)S(1)}, u32[]{:S(2)}, u32[]{:S(2)}) collective-permute-start(bf16[32,3712]{1,0:T(8,128)(2,1)S(1)} %slice.402), channel_id=1, source_target_pairs={{24,0},{97,1},{0,8},{105,9},{8,16},{113,17},{16,24},{121,25},{56,3... | collective-permute-start | bytes 712712 | tf_op jit(solution)/shard_map/ppermute | solution.py:104
  117.7 6.3 %collective-permute-start.19 = (bf16[48,3712]{1,0:T(8,128)(2,1)S(1)}, bf16[48,3712]{1,0:T(8,128)(2,1)S(1)}, u32[]{:S(2)}, u32[]{:S(2)}) collective-permute-start(bf16[48,3712]{1,0:T(8,128)(2,1)S(1)} %slice.406), channel_id=1, source_target_pairs={{8,0},{33,1},{16,8},{41,9},{24,16},{49,17},{0,24},{57,25},{40,32},... | collective-permute-start | bytes 1069064 | tf_op jit(solution)/shard_map/ppermute | solution.py:104
  119.9 7.5 %collective-permute-start.21 = (bf16[48,3712]{1,0:T(8,128)(2,1)S(1)}, bf16[48,3712]{1,0:T(8,128)(2,1)S(1)}, u32[]{:S(2)}, u32[]{:S(2)}) collective-permute-start(bf16[48,3712]{1,0:T(8,128)(2,1)S(1)} %slice.407), channel_id=1, source_target_pairs={{24,0},{97,1},{0,8},{105,9},{8,16},{113,17},{16,24},{121,25},{56,3... | collective-permute-start | bytes 1069064 | tf_op jit(solution)/shard_map/ppermute | solution.py:104
  120.2 8.8 %collective-permute-start.23 = (bf16[48,3712]{1,0:T(8,128)(2,1)S(1)}, bf16[48,3712]{1,0:T(8,128)(2,1)S(1)}, u32[]{:S(2)}, u32[]{:S(2)}) collective-permute-start(bf16[48,3712]{1,0:T(8,128)(2,1)S(1)} %slice.411), channel_id=1, source_target_pairs={{8,0},{33,1},{16,8},{41,9},{24,16},{49,17},{0,24},{57,25},{40,32},... | collective-permute-start | bytes 1069064 | tf_op jit(solution)/shard_map/ppermute | solution.py:104
  122.8 8.7 %collective-permute-start.25 = (bf16[48,3712]{1,0:T(8,128)(2,1)S(1)}, bf16[48,3712]{1,0:T(8,128)(2,1)S(1)}, u32[]{:S(2)}, u32[]{:S(2)}) collective-permute-start(bf16[48,3712]{1,0:T(8,128)(2,1)S(1)} %slice.412), channel_id=1, source_target_pairs={{24,0},{97,1},{0,8},{105,9},{8,16},{113,17},{16,24},{121,25},{56,3... | collective-permute-start | bytes 1069064 | tf_op jit(solution)/shard_map/ppermute | solution.py:104
  134.1 9.4 %collective-permute-start.26 = (bf16[1024,256]{1,0:T(8,128)(2,1)}, bf16[1024,256]{1,0:T(8,128)(2,1)S(1)}, u32[]{:S(2)}, u32[]{:S(2)}) collective-permute-start(bf16[1024,256]{1,0:T(8,128)(2,1)} %slice.527), channel_id=1, source_target_pairs={{0,1},{1,0},{2,3},{3,2},{4,5},{5,4},{6,7},{7,6},{8,9},{9,8},{10,11... | collective-permute-start | bytes 1572872 | tf_op jit(solution)/shard_map/ppermute | solution.py:108
  143.1 5.1 %collective-permute-start.28 = (bf16[128,3584]{1,0:T(8,128)(2,1)}, bf16[128,3584]{1,0:T(8,128)(2,1)}, u32[]{:S(2)}, u32[]{:S(2)}) collective-permute-start(bf16[128,3584]{1,0:T(8,128)(2,1)} %get-tuple-element.41), channel_id=1, source_target_pairs={{0,1},{1,0},{2,3},{3,2},{4,5},{5,4},{6,7},{7,6},{8,9},{9,8},{10,11... | collective-permute-start | bytes 2752520 | tf_op jit(solution)/shard_map/ppermute | solution.py:108
  145.5 2.6 %collective-permute-start.27 = (bf16[1024,128]{1,0:T(8,128)(2,1)S(1)}, bf16[1024,128]{1,0:T(8,128)(2,1)S(1)}, u32[]{:S(2)}, u32[]{:S(2)}) collective-permute-start(bf16[1024,128]{1,0:T(8,128)(2,1)S(1)} %fusion.21), channel_id=1, source_target_pairs={{0,1},{1,0},{2,3},{3,2},{4,5},{5,4},{6,7},{7,6},{8,9},{9,8},{10,11... | collective-permute-start | bytes 786440 | tf_op jit(solution)/shard_map/ppermute | solution.py:108
  150.2 12.2 %collective-permute-start.29 = (bf16[32,3584]{1,0:T(8,128)(2,1)S(1)}, bf16[32,3584]{1,0:T(8,128)(2,1)S(1)}, u32[]{:S(2)}, u32[]{:S(2)}) collective-permute-start(bf16[32,3584]{1,0:T(8,128)(2,1)S(1)} %get-tuple-element.34), channel_id=1, source_target_pairs={{24,0},{97,1},{0,8},{105,9},{8,16},{113,17},{16,24},{121,25},{56,3... | collective-permute-start | bytes 688136 | tf_op jit(solution)/shard_map/ppermute | solution.py:104
  150.2 14.8 %collective-permute-start.31 = (bf16[32,3584]{1,0:T(8,128)(2,1)S(1)}, bf16[32,3584]{1,0:T(8,128)(2,1)S(1)}, u32[]{:S(2)}, u32[]{:S(2)}) collective-permute-start(bf16[32,3584]{1,0:T(8,128)(2,1)S(1)} %get-tuple-element.35), channel_id=1, source_target_pairs={{8,0},{33,1},{16,8},{41,9},{24,16},{49,17},{0,24},{57,25},{40,32},... | collective-permute-start | bytes 688136 | tf_op jit(solution)/shard_map/ppermute | solution.py:104
  157.3 8.0 %collective-permute-start.33 = (bf16[48,3584]{1,0:T(8,128)(2,1)S(1)}, bf16[48,3584]{1,0:T(8,128)(2,1)S(1)}, u32[]{:S(2)}, u32[]{:S(2)}) collective-permute-start(bf16[48,3584]{1,0:T(8,128)(2,1)S(1)} %get-tuple-element.22), channel_id=1, source_target_pairs={{24,0},{97,1},{0,8},{105,9},{8,16},{113,17},{16,24},{121,25},{56,3... | collective-permute-start | bytes 1032200 | tf_op jit(solution)/shard_map/ppermute | solution.py:104
  157.4 10.6 %collective-permute-start.35 = (bf16[48,3584]{1,0:T(8,128)(2,1)S(1)}, bf16[48,3584]{1,0:T(8,128)(2,1)S(1)}, u32[]{:S(2)}, u32[]{:S(2)}) collective-permute-start(bf16[48,3584]{1,0:T(8,128)(2,1)S(1)} %get-tuple-element.23), channel_id=1, source_target_pairs={{8,0},{33,1},{16,8},{41,9},{24,16},{49,17},{0,24},{57,25},{40,32},... | collective-permute-start | bytes 1032200 | tf_op jit(solution)/shard_map/ppermute | solution.py:104
  162.3 7.7 %collective-permute-start.37 = (bf16[48,3584]{1,0:T(8,128)(2,1)S(1)}, bf16[48,3584]{1,0:T(8,128)(2,1)S(1)}, u32[]{:S(2)}, u32[]{:S(2)}) collective-permute-start(bf16[48,3584]{1,0:T(8,128)(2,1)S(1)} %get-tuple-element.28), channel_id=1, source_target_pairs={{24,0},{97,1},{0,8},{105,9},{8,16},{113,17},{16,24},{121,25},{56,3... | collective-permute-start | bytes 1032200 | tf_op jit(solution)/shard_map/ppermute | solution.py:104
  162.3 8.8 %collective-permute-start.39 = (bf16[48,3584]{1,0:T(8,128)(2,1)S(1)}, bf16[48,3584]{1,0:T(8,128)(2,1)S(1)}, u32[]{:S(2)}, u32[]{:S(2)}) collective-permute-start(bf16[48,3584]{1,0:T(8,128)(2,1)S(1)} %get-tuple-element.29), channel_id=1, source_target_pairs={{8,0},{33,1},{16,8},{41,9},{24,16},{49,17},{0,24},{57,25},{40,32},... | collective-permute-start | bytes 1032200 | tf_op jit(solution)/shard_map/ppermute | solution.py:104
  165.2 30.5 %collective-permute-start.30 = (bf16[64,3584]{1,0:T(8,128)(2,1)S(1)}, bf16[64,3584]{1,0:T(8,128)(2,1)S(1)}, u32[]{:S(2)}, u32[]{:S(2)}) collective-permute-start(bf16[64,3584]{1,0:T(8,128)(2,1)S(1)} %pad_maximum_fusion.11), channel_id=1, source_target_pairs={{24,0},{97,1},{0,8},{105,9},{8,16},{113,17},{16,24},{121,25},{56,3... | collective-permute-start | bytes 1376264 | tf_op jit(solution)/shard_map/ppermute | solution.py:104
  165.3 30.4 %collective-permute-start.32 = (bf16[64,3584]{1,0:T(8,128)(2,1)S(1)}, bf16[64,3584]{1,0:T(8,128)(2,1)S(1)}, u32[]{:S(2)}, u32[]{:S(2)}) collective-permute-start(bf16[64,3584]{1,0:T(8,128)(2,1)S(1)} %pad_maximum_fusion.12), channel_id=1, source_target_pairs={{8,0},{33,1},{16,8},{41,9},{24,16},{49,17},{0,24},{57,25},{40,32},... | collective-permute-start | bytes 1376264 | tf_op jit(solution)/shard_map/ppermute | solution.py:104
  168.2 14.0 %collective-permute-start.34 = (bf16[96,3584]{1,0:T(8,128)(2,1)S(1)}, bf16[96,3584]{1,0:T(8,128)(2,1)S(1)}, u32[]{:S(2)}, u32[]{:S(2)}) collective-permute-start(bf16[96,3584]{1,0:T(8,128)(2,1)S(1)} %pad_maximum_fusion.3), channel_id=1, source_target_pairs={{24,0},{97,1},{0,8},{105,9},{8,16},{113,17},{16,24},{121,25},{56,3... | collective-permute-start | bytes 2064392 | tf_op jit(solution)/shard_map/ppermute | solution.py:104
  169.9 12.3 %collective-permute-start.36 = (bf16[96,3584]{1,0:T(8,128)(2,1)S(1)}, bf16[96,3584]{1,0:T(8,128)(2,1)S(1)}, u32[]{:S(2)}, u32[]{:S(2)}) collective-permute-start(bf16[96,3584]{1,0:T(8,128)(2,1)S(1)} %pad_maximum_fusion.4), channel_id=1, source_target_pairs={{8,0},{33,1},{16,8},{41,9},{24,16},{49,17},{0,24},{57,25},{40,32},... | collective-permute-start | bytes 2064392 | tf_op jit(solution)/shard_map/ppermute | solution.py:104
  171.4 17.9 %collective-permute-start.38 = (bf16[96,3584]{1,0:T(8,128)(2,1)S(1)}, bf16[96,3584]{1,0:T(8,128)(2,1)S(1)}, u32[]{:S(2)}, u32[]{:S(2)}) collective-permute-start(bf16[96,3584]{1,0:T(8,128)(2,1)S(1)} %pad_maximum_fusion.5), channel_id=1, source_target_pairs={{24,0},{97,1},{0,8},{105,9},{8,16},{113,17},{16,24},{121,25},{56,3... | collective-permute-start | bytes 2064392 | tf_op jit(solution)/shard_map/ppermute | solution.py:104
  182.2 10.1 %collective-permute-start.40 = (bf16[96,3584]{1,0:T(8,128)(2,1)S(1)}, bf16[96,3584]{1,0:T(8,128)(2,1)S(1)}, u32[]{:S(2)}, u32[]{:S(2)}) collective-permute-start(bf16[96,3584]{1,0:T(8,128)(2,1)S(1)} %pad_maximum_fusion.6), channel_id=1, source_target_pairs={{8,0},{33,1},{16,8},{41,9},{24,16},{49,17},{0,24},{57,25},{40,32},... | collective-permute-start | bytes 2064392 | tf_op jit(solution)/shard_map/ppermute | solution.py:104
  192.7 13.8 %collective-permute-start.41 = (bf16[64,3584]{1,0:T(8,128)(2,1)S(1)}, bf16[64,3584]{1,0:T(8,128)(2,1)S(1)}, u32[]{:S(2)}, u32[]{:S(2)}) collective-permute-start(bf16[64,3584]{1,0:T(8,128)(2,1)S(1)} %pad_maximum_fusion.13), channel_id=1, source_target_pairs={{96,0},{25,1},{104,8},{1,9},{112,16},{9,17},{120,24},{17,25},{0,32... | collective-permute-start | bytes 1376264 | tf_op jit(solution)/shard_map/ppermute | solution.py:104
  192.8 13.7 %collective-permute-start.42 = (bf16[64,3584]{1,0:T(8,128)(2,1)S(1)}, bf16[64,3584]{1,0:T(8,128)(2,1)S(1)}, u32[]{:S(2)}, u32[]{:S(2)}) collective-permute-start(bf16[64,3584]{1,0:T(8,128)(2,1)S(1)} %pad_maximum_fusion.14), channel_id=1, source_target_pairs={{64,0},{17,1},{72,8},{25,9},{80,16},{1,17},{88,24},{9,25},{96,32},... | collective-permute-start | bytes 1376264 | tf_op jit(solution)/shard_map/ppermute | solution.py:104
  194.9 12.4 %collective-permute-start.43 = (bf16[64,3584]{1,0:T(8,128)(2,1)S(1)}, bf16[64,3584]{1,0:T(8,128)(2,1)S(1)}, u32[]{:S(2)}, u32[]{:S(2)}) collective-permute-start(bf16[64,3584]{1,0:T(8,128)(2,1)S(1)} %pad_maximum_fusion.15), channel_id=1, source_target_pairs={{32,0},{9,1},{40,8},{17,9},{48,16},{25,17},{56,24},{1,25},{64,32},... | collective-permute-start | bytes 1376264 | tf_op jit(solution)/shard_map/ppermute | solution.py:104
  207.6 7.6 %collective-permute-start.44 = (bf16[2,8,3584]{2,1,0:T(8,128)(2,1)S(1)}, bf16[2,8,3584]{2,1,0:T(8,128)(2,1)S(1)}, u32[]{:S(2)}, u32[]{:S(2)}) collective-permute-start(bf16[2,8,3584]{2,1,0:T(8,128)(2,1)S(1)} %get-tuple-element.57), channel_id=1, source_target_pairs={{6,0},{0,2},{2,4},{4,6},{7,1},{1,3},{3,5},{5,7},{14,8},{8,10},{10,... | collective-permute-start | bytes 344072 | tf_op jit(solution)/shard_map/ppermute | solution.py:103
  207.7 7.6 %collective-permute-start.45 = (bf16[2,8,3584]{2,1,0:T(8,128)(2,1)S(1)}, bf16[2,8,3584]{2,1,0:T(8,128)(2,1)S(1)}, u32[]{:S(2)}, u32[]{:S(2)}) collective-permute-start(bf16[2,8,3584]{2,1,0:T(8,128)(2,1)S(1)} %get-tuple-element.59), channel_id=1, source_target_pairs={{4,0},{6,2},{0,4},{2,6},{5,1},{7,3},{1,5},{3,7},{12,8},{14,10},{8,... | collective-permute-start | bytes 344072 | tf_op jit(solution)/shard_map/ppermute | solution.py:103
  210.2 5.1 %collective-permute-start.46 = (bf16[2,8,3584]{2,1,0:T(8,128)(2,1)S(1)}, bf16[2,8,3584]{2,1,0:T(8,128)(2,1)S(1)}, u32[]{:S(2)}, u32[]{:S(2)}) collective-permute-start(bf16[2,8,3584]{2,1,0:T(8,128)(2,1)S(1)} %get-tuple-element.58), channel_id=1, source_target_pairs={{2,0},{4,2},{6,4},{0,6},{3,1},{5,3},{7,5},{1,7},{10,8},{12,10},{14... | collective-permute-start | bytes 344072 | tf_op jit(solution)/shard_map/ppermute | solution.py:103
  210.4 9.6 %collective-permute-start.4 = (bf16[8,3584]{1,0:T(8,128)(2,1)S(1)}, bf16[8,3584]{1,0:T(8,128)(2,1)S(1)}, u32[]{:S(2)}, u32[]{:S(2)}) collective-permute-start(bf16[8,3584]{1,0:T(8,128)(2,1)S(1)} %get-tuple-element.62), channel_id=1, source_target_pairs={{0,1},{1,0},{2,3},{3,2},{4,5},{5,4},{6,7},{7,6},{8,9},{9,8},{10,11... | collective-permute-start | bytes 172040 | tf_op jit(solution)/shard_map/ppermute | solution.py:108
  215.4 5.5 %collective-permute-start.47 = (bf16[8,3584]{1,0:T(8,128)(2,1)S(1)}, bf16[8,3584]{1,0:T(8,128)(2,1)S(1)}, u32[]{:S(2)}, u32[]{:S(2)}) collective-permute-start(bf16[8,3584]{1,0:T(8,128)(2,1)S(1)} %get-tuple-element.65), channel_id=1, source_target_pairs={{0,1},{1,0},{2,3},{3,2},{4,5},{5,4},{6,7},{7,6},{8,9},{9,8},{10,11... | collective-permute-start | bytes 172040 | tf_op jit(solution)/shard_map/ppermute | solution.py:108
  (23 other events, 214.7 us)

commit v5 on v2

--- a/solution.py
+++ b/solution.py
@@ -216,20 +216,22 @@
         product = product + crossed(got).astype(f32)
         activated = (jax.nn.silu(product[:, :units]) * product[:, units:]).astype(bf16)
         activated = jnp.concatenate([activated, crossed(swap(activated))], axis=1)
-        outs = []
+        labels = lax.broadcasted_iota(jnp.int32, (1, lanes), 1)
+        weights = jnp.concatenate(
+            [
+                jnp.sum(
+                    jnp.where(labels == expert_at, b[:, half:].astype(f32), 0.0),
+                    axis=1,
+                    keepdims=True,
+                )
+                for b in blocks
+            ],
+            axis=0,
+        )
+        out = jnp.dot(activated, weight_out, preferred_element_type=f32)
+        out = (out * weights).astype(bf16)
         n = 16 * rows
-        for i, b in enumerate(blocks):
-            weights = jnp.sum(
-                jnp.where(
-                    lax.broadcasted_iota(jnp.int32, (1, lanes), 1) == expert_at,
-                    b[:, half:].astype(f32),
-                    0.0,
-                ),
-                axis=1,
-                keepdims=True,
-            )
-            out = jnp.dot(activated[i * n : (i + 1) * n], weight_out, preferred_element_type=f32)
-            outs.append((out * weights).astype(bf16))
+        outs = [out[i * n : (i + 1) * n] for i in range(4)]
         back = scatter_far(*outs, far_axis).reshape(4, 4 * rows, half)
         sums.append(scatter_near(back, near_axis).astype(bf16))
     to_x = jnp.stack([s.reshape(4, rows, half) for s in sums], axis=1)

time: 191 us -> 186 us (0.974)
  waiting for transfers between devices: 68.8 us -> 79.2 us
  matrix products: 32.6 us -> 24.1 us
  starting transfers between devices: 71.6 us -> 64.6 us
    ppermute x25, waiting for transfers between devices: 47.5 us -> 56.5 us  [shift(): return lax.ppermute(value, ('y', 'z', 'core'), ring(axes, distance))]
    dot_general x8 -> x2, matrix products: 13.2 us -> 4.61 us  [per_device(): out = jnp.dot(activated, weight_out, preferred_element_type=f32)]
    ppermute x11, starting transfers between devices: 23.6 us -> 17.9 us  [swap(): return lax.ppermute(value, 'core', [(0, 1), (1, 0)])]
  transfers between devices with their start and end apart: 46 -> 46, of which waited for: 20 -> 24; matrix products, arithmetic and copies ran while one was open for 21% -> 17% of each run, Pallas kernels for 0% -> 0%
where the time goes in v5:
time: 186 us
  waiting for transfers between devices  79.2 us (43%)
  starting transfers between devices  64.6 us (35%)
  matrix products  24.1 us (13%)
  other arithmetic  9.46 us (5%)
  local copies, waits for them, and re-layouts  6.98 us (4%)
    ppermute x25, waiting for transfers between devices, shift(): return lax.ppermute(value, ('y', 'z', 'core'), ring(axes, distance))  56.5 us
    ppermute x25, starting transfers between devices, shift(): return lax.ppermute(value, ('y', 'z', 'core'), ring(axes, distance))  32.3 us
    ppermute x11, starting transfers between devices, swap(): return lax.ppermute(value, 'core', [(0, 1), (1, 0)])  17.9 us
    ppermute x9, waiting for transfers between devices, shift(): return lax.ppermute(value, 'x', [((i + distance) % 4, i) for i in range(4)])  11.4 us
    ppermute x9, starting transfers between devices, shift(): return lax.ppermute(value, 'x', [((i + distance) % 4, i) for i in range(4)])  8.46 us
    all_to_all x1, waiting for transfers between devices, per_device(): lax.all_to_all(latent_out, ('x', 'core'), split_axis=1, concat_axis=0, ti...  8.21 us
    dot_general x1, matrix products, per_device(): projected = jnp.dot(values, out_proj, preferred_element_type=f32)  8.06 us
    all_to_all x1, starting transfers between devices, per_device(): lax.all_to_all(latent_out, ('x', 'core'), split_axis=1, concat_axis=0, ti...  5.8 us
  transfers between devices with their start and end apart: 46, of which 24 were waited for; matrix products, arithmetic and copies ran while one was open for 17% of the time, Pallas kernels for 0%

profile of v5, /device:TPU:1, one launch (start us, length us, event | category | flops | bytes accessed | tf_op | source)
XLA Modules:
  0.0 185.9 jit_solution(16979813775042532301)
XLA Ops:
  1.5 1.7 fusion.59
  3.2 3.0 %fusion.73 = (f32[8,64]{1,0:T(8,128)S(1)}, f32[8,64,384]{2,1,0:T(8,128)S(1)}) fusion(bf16[8,64,576]{2,1,0:T(8,128)(2,1)} %param.14, bf16[8,384,576]{1,2,0:T(8,128)(2,1)} %param.15, s32[8]{0:T(128)} %param.17), kind=kOutput, calls=%fused_computation.169 | convolution fusion | flops 227278336 | bytes 4917280 | tf_op jit(solution)/shard_map/rhc,rtc->rht/dot_general | solution.py:15
  6.6 1.1 fusion.12
  7.7 1.1 copy.43
  8.8 5.8 %all-to-all-start = ((bf16[8,64,512]{2,0,1:T(8,128)(2,1)}), bf16[8,64,512]{2,0,1:T(8,128)(2,1)S(1)}, u32[]{:S(2)}, u32[]{:S(2)}) async-start(bf16[8,64,512]{2,0,1:T(8,128)(2,1)} %copy.43), calls=%async_computation | async-start | bytes 1048576 | tf_op jit(solution)/shard_map/all_to_all | solution.py:154
  15.9 8.2 %all-to-all-done = bf16[8,64,512]{2,0,1:T(8,128)(2,1)S(1)} async-done(((bf16[8,64,512]{2,0,1:T(8,128)(2,1)}), bf16[8,64,512]{2,0,1:T(8,128)(2,1)S(1)}, u32[]{:S(2)}, u32[]{:S(2)}) %all-to-all-start) | async-done | bytes 524320 | tf_op jit(solution)/shard_map/all_to_all | solution.py:154
  24.4 8.1 %fusion.41 = f32[64,7168]{1,0:T(8,128)S(1)} fusion(bf16[1024,7168]{1,0:T(8,128)(2,1)} %param.19, bf16[8,8,8,128]{3,2,1,0:T(8,128)(2,1)S(1)} %fusion.16), kind=kOutput, calls=%fused_computation.92 | convolution fusion | flops 939524096 | bytes 16646144 | tf_op jit(solution)/shard_map/dot_general | solution.py:176
  33.5 1.4 dynamic-slice_bitcast_fusion
  35.5 1.8 collective-permute-start.2
  39.0 2.4 %collective-permute-done.1 = bf16[16,3584]{1,0:T(8,128)(2,1)S(1)} collective-permute-done((bf16[16,3584]{1,0:T(8,128)(2,1)S(1)}, bf16[16,3584]{1,0:T(8,128)(2,1)S(1)}, u32[]{:S(2)}, u32[]{:S(2)}) %collective-permute-start.1) | collective-permute-done | bytes 114720 | tf_op jit(solution)/shard_map/ppermute | solution.py:71
  41.3 1.2 collective-permute-done.2
  42.6 1.0 collective-permute-done.3
  43.7 1.7 collective-permute-start.6
  46.3 2.2 %collective-permute-start.7 = (bf16[16,3712]{1,0:T(8,128)(2,1)S(1)}, bf16[16,3712]{1,0:T(8,128)(2,1)S(1)}, u32[]{:S(2)}, u32[]{:S(2)}) collective-permute-start(bf16[16,3712]{1,0:T(8,128)(2,1)S(1)} %get-tuple-element.48), channel_id=1, source_target_pairs={{2,0},{4,2},{6,4},{0,6},{3,1},{5,3},{7,5},{1,7},{10,8},{12,10},{14... | collective-permute-start | bytes 356360 | tf_op jit(solution)/shard_map/ppermute | solution.py:71
  50.3 1.0 collective-permute-done.7
  51.3 3.0 %collective-permute-done.8 = bf16[16,3712]{1,0:T(8,128)(2,1)S(1)} collective-permute-done((bf16[16,3712]{1,0:T(8,128)(2,1)S(1)}, bf16[16,3712]{1,0:T(8,128)(2,1)S(1)}, u32[]{:S(2)}, u32[]{:S(2)}) %collective-permute-start.8) | collective-permute-done | bytes 118816 | tf_op jit(solution)/shard_map/ppermute | solution.py:71
  54.3 2.8 %collective-permute-done.9 = bf16[16,3712]{1,0:T(8,128)(2,1)S(1)} collective-permute-done((bf16[16,3712]{1,0:T(8,128)(2,1)S(1)}, bf16[16,3712]{1,0:T(8,128)(2,1)S(1)}, u32[]{:S(2)}, u32[]{:S(2)}) %collective-permute-start.9) | collective-permute-done | bytes 118816 | tf_op jit(solution)/shard_map/ppermute | solution.py:71
  57.2 3.8 %collective-permute-start.10 = (bf16[64,3712]{1,0:T(8,128)(2,1)S(1)}, bf16[64,3712]{1,0:T(8,128)(2,1)S(1)}, u32[]{:S(2)}, u32[]{:S(2)}) collective-permute-start(bf16[64,3712]{1,0:T(8,128)(2,1)S(1)} %bitcast.155), channel_id=1, source_target_pairs={{32,0},{9,1},{40,8},{17,9},{48,16},{25,17},{56,24},{1,25},{64,32},... | collective-permute-start | bytes 1425416 | tf_op jit(solution)/shard_map/ppermute | solution.py:72
  61.8 1.6 dynamic-slice_bitcast_fusion.2
  63.4 8.4 %collective-permute-done.10 = bf16[64,3712]{1,0:T(8,128)(2,1)S(1)} collective-permute-done((bf16[64,3712]{1,0:T(8,128)(2,1)S(1)}, bf16[64,3712]{1,0:T(8,128)(2,1)S(1)}, u32[]{:S(2)}, u32[]{:S(2)}) %collective-permute-start.10) | collective-permute-done | bytes 475168 | tf_op jit(solution)/shard_map/ppermute | solution.py:72
  71.8 3.4 %collective-permute-done.12 = bf16[64,3712]{1,0:T(8,128)(2,1)S(1)} collective-permute-done((bf16[64,3712]{1,0:T(8,128)(2,1)S(1)}, bf16[64,3712]{1,0:T(8,128)(2,1)S(1)}, u32[]{:S(2)}, u32[]{:S(2)}) %collective-permute-start.12) | collective-permute-done | bytes 475168 | tf_op jit(solution)/shard_map/ppermute | solution.py:72
  75.7 2.5 %collective-permute-start.28 = (bf16[128,3712]{1,0:T(8,128)(2,1)S(1)}, bf16[128,3712]{1,0:T(8,128)(2,1)S(1)}, u32[]{:S(2)}, u32[]{:S(2)}) collective-permute-start(bf16[128,3712]{1,0:T(8,128)(2,1)S(1)} %bitcast.144), channel_id=1, source_target_pairs={{8,0},{33,1},{16,8},{41,9},{24,16},{49,17},{0,24},{57,25},{40,32},... | collective-permute-start | bytes 2850824 | tf_op jit(solution)/shard_map/ppermute | solution.py:72
  78.2 2.7 %collective-permute-start.14 = (bf16[128,3712]{1,0:T(8,128)(2,1)S(1)}, bf16[128,3712]{1,0:T(8,128)(2,1)S(1)}, u32[]{:S(2)}, u32[]{:S(2)}) collective-permute-start(bf16[128,3712]{1,0:T(8,128)(2,1)S(1)} %bitcast.148), channel_id=1, source_target_pairs={{8,0},{33,1},{16,8},{41,9},{24,16},{49,17},{0,24},{57,25},{40,32},... | collective-permute-start | bytes 2850824 | tf_op jit(solution)/shard_map/ppermute | solution.py:72
  80.9 1.6 slice_bitcast_fusion.1
  82.4 2.2 %fusion.6 = bf16[3712,512]{1,0:T(8,128)(2,1)S(1)} fusion(bf16[3584,128]{1,0:T(8,128)(2,1)S(1)} %get-tuple-element.31, bf16[3584,128]{1,0:T(8,128)(2,1)S(1)} %get-tuple-element.30, bf16[3584,128]{1,0:T(8,128)(2,1)S(1)} %get-tuple-element.27, bf16[3584,128]{1,0:T(8,128)(2,1)S(1)} %get-tuple-element.26), kind=kLoop, calls=%fused_computation.9 | loop fusion | flops 24707072 | bytes 7471104 | tf_op jit(solution)/shard_map/concatenate | solution.py:160
  86.1 2.8 %collective-permute-done.28 = bf16[128,3712]{1,0:T(8,128)(2,1)S(1)} collective-permute-done((bf16[128,3712]{1,0:T(8,128)(2,1)S(1)}, bf16[128,3712]{1,0:T(8,128)(2,1)S(1)}, u32[]{:S(2)}, u32[]{:S(2)}) %collective-permute-start.28) | collective-permute-done | bytes 950304 | tf_op jit(solution)/shard_map/ppermute | solution.py:72
  88.9 3.5 %collective-permute-start.29 = (bf16[64,3712]{1,0:T(8,128)(2,1)S(1)}, bf16[64,3712]{1,0:T(8,128)(2,1)S(1)}, u32[]{:S(2)}, u32[]{:S(2)}) collective-permute-start(bf16[64,3712]{1,0:T(8,128)(2,1)S(1)} %slice.367), channel_id=1, source_target_pairs={{8,0},{33,1},{16,8},{41,9},{24,16},{49,17},{0,24},{57,25},{40,32},... | collective-permute-start | bytes 1425416 | tf_op jit(solution)/shard_map/ppermute | solution.py:72
  93.9 8.6 %collective-permute-done.16 = bf16[128,3712]{1,0:T(8,128)(2,1)S(1)} collective-permute-done((bf16[128,3712]{1,0:T(8,128)(2,1)S(1)}, bf16[128,3712]{1,0:T(8,128)(2,1)S(1)}, u32[]{:S(2)}, u32[]{:S(2)}) %collective-permute-start.16) | collective-permute-done | bytes 950304 | tf_op jit(solution)/shard_map/ppermute | solution.py:72
  104.1 1.5 collective-permute-start.17
  105.7 1.9 %collective-permute-done.31 = bf16[64,3712]{1,0:T(8,128)(2,1)S(1)} collective-permute-done((bf16[64,3712]{1,0:T(8,128)(2,1)S(1)}, bf16[64,3712]{1,0:T(8,128)(2,1)S(1)}, u32[]{:S(2)}, u32[]{:S(2)}) %collective-permute-start.31) | collective-permute-done | bytes 475168 | tf_op jit(solution)/shard_map/ppermute | solution.py:72
  108.3 3.6 %collective-permute-done.15 = bf16[64,3712]{1,0:T(8,128)(2,1)S(1)} collective-permute-done((bf16[64,3712]{1,0:T(8,128)(2,1)S(1)}, bf16[64,3712]{1,0:T(8,128)(2,1)S(1)}, u32[]{:S(2)}, u32[]{:S(2)}) %collective-permute-start.15) | collective-permute-done | bytes 475168 | tf_op jit(solution)/shard_map/ppermute | solution.py:72
  111.9 1.3 collective-permute-done.17
  114.1 4.6 %collective-permute-start.32 = (bf16[512,256]{1,0:T(8,128)(2,1)S(1)}, bf16[512,256]{1,0:T(8,128)(2,1)S(1)}, u32[]{:S(2)}, u32[]{:S(2)}) collective-permute-start(bf16[512,256]{1,0:T(8,128)(2,1)S(1)} %pad_maximum_fusion.10), channel_id=1, source_target_pairs={{0,1},{1,0},{2,3},{3,2},{4,5},{5,4},{6,7},{7,6},{8,9},{9,8},{10,11... | collective-permute-start | bytes 786440 | tf_op jit(solution)/shard_map/ppermute | solution.py:76
  121.5 2.3 %multiply_convert_fusion = bf16[512,3584]{1,0:T(8,128)(2,1)S(1)} fusion(f32[512]{0:T(512)S(1)} %bitcast.185, bf16[128,3584]{1,0:T(8,128)(2,1)} %collective-permute-done.20, bf16[128,3584]{1,0:T(8,128)(2,1)S(1)} %get-tuple-element.32, bf16[512,128]{1,0:T(8,128)(2,1)S(1)} %bitcast.171, bf16[512,128]{1,0:T(8,128)(2,1)S(1)} %fusion.22), kind=kOutput, calls=%fused_computation.5 | convolution fusion | flops 947388416 | bytes 5769216 | tf_op jit(solution)/shard_map/dot_general | solution.py:231
  124.1 2.7 %collective-permute-start.36 = (bf16[64,3584]{1,0:T(8,128)(2,1)S(1)}, bf16[64,3584]{1,0:T(8,128)(2,1)S(1)}, u32[]{:S(2)}, u32[]{:S(2)}) collective-permute-start(bf16[64,3584]{1,0:T(8,128)(2,1)S(1)} %get-tuple-element.23), channel_id=1, source_target_pairs={{8,0},{33,1},{16,8},{41,9},{24,16},{49,17},{0,24},{57,25},{40,32},... | collective-permute-start | bytes 1376264 | tf_op jit(solution)/shard_map/ppermute | solution.py:72
  126.7 2.3 %multiply_convert_fusion.1 = bf16[512,3584]{1,0:T(8,128)(2,1)S(1)} fusion(f32[512]{0:T(512)S(1)} %bitcast.184, bf16[128,3584]{1,0:T(8,128)(2,1)} %collective-permute-done.20, bf16[128,3584]{1,0:T(8,128)(2,1)S(1)} %get-tuple-element.32, bf16[512,128]{1,0:T(8,128)(2,1)S(1)} %bitcast.172, bf16[512,128]{1,0:T(8,128)(2,1)S(1)} %fusion.23), kind=kOutput, calls=%fused_computation.6 | convolution fusion | flops 947388416 | bytes 5769216 | tf_op jit(solution)/shard_map/dot_general | solution.py:231
  129.5 2.7 %collective-permute-start.23 = (bf16[64,3584]{1,0:T(8,128)(2,1)S(1)}, bf16[64,3584]{1,0:T(8,128)(2,1)S(1)}, u32[]{:S(2)}, u32[]{:S(2)}) collective-permute-start(bf16[64,3584]{1,0:T(8,128)(2,1)S(1)} %get-tuple-element.17), channel_id=1, source_target_pairs={{8,0},{33,1},{16,8},{41,9},{24,16},{49,17},{0,24},{57,25},{40,32},... | collective-permute-start | bytes 1376264 | tf_op jit(solution)/shard_map/ppermute | solution.py:72
  133.3 2.7 %collective-permute-start.37 = (bf16[128,3584]{1,0:T(8,128)(2,1)S(1)}, bf16[128,3584]{1,0:T(8,128)(2,1)S(1)}, u32[]{:S(2)}, u32[]{:S(2)}) collective-permute-start(bf16[128,3584]{1,0:T(8,128)(2,1)S(1)} %pad_maximum_fusion.7), channel_id=1, source_target_pairs={{8,0},{33,1},{16,8},{41,9},{24,16},{49,17},{0,24},{57,25},{40,32},... | collective-permute-start | bytes 2752520 | tf_op jit(solution)/shard_map/ppermute | solution.py:72
  136.1 2.2 %collective-permute-done.21 = bf16[64,3584]{1,0:T(8,128)(2,1)S(1)} collective-permute-done((bf16[64,3584]{1,0:T(8,128)(2,1)S(1)}, bf16[64,3584]{1,0:T(8,128)(2,1)S(1)}, u32[]{:S(2)}, u32[]{:S(2)}) %collective-permute-start.21) | collective-permute-done | bytes 458784 | tf_op jit(solution)/shard_map/ppermute | solution.py:72
  138.8 2.7 %collective-permute-start.24 = (bf16[128,3584]{1,0:T(8,128)(2,1)S(1)}, bf16[128,3584]{1,0:T(8,128)(2,1)S(1)}, u32[]{:S(2)}, u32[]{:S(2)}) collective-permute-start(bf16[128,3584]{1,0:T(8,128)(2,1)S(1)} %pad_maximum_fusion.5), channel_id=1, source_target_pairs={{8,0},{33,1},{16,8},{41,9},{24,16},{49,17},{0,24},{57,25},{40,32},... | collective-permute-start | bytes 2752520 | tf_op jit(solution)/shard_map/ppermute | solution.py:72
  141.5 6.6 %collective-permute-done.35 = bf16[128,3584]{1,0:T(8,128)(2,1)S(1)} collective-permute-done((bf16[128,3584]{1,0:T(8,128)(2,1)S(1)}, bf16[128,3584]{1,0:T(8,128)(2,1)S(1)}, u32[]{:S(2)}, u32[]{:S(2)}) %collective-permute-start.35) | collective-permute-done | bytes 917536 | tf_op jit(solution)/shard_map/ppermute | solution.py:72
  149.4 1.9 %collective-permute-start.40 = (bf16[32,3584]{1,0:T(8,128)(2,1)S(1)}, bf16[32,3584]{1,0:T(8,128)(2,1)S(1)}, u32[]{:S(2)}, u32[]{:S(2)}) collective-permute-start(bf16[32,3584]{1,0:T(8,128)(2,1)S(1)} %get-tuple-element.38), channel_id=1, source_target_pairs={{32,0},{9,1},{40,8},{17,9},{48,16},{25,17},{56,24},{1,25},{64,32},... | collective-permute-start | bytes 688136 | tf_op jit(solution)/shard_map/ppermute | solution.py:72
  151.3 11.0 %collective-permute-done.22 = bf16[128,3584]{1,0:T(8,128)(2,1)S(1)} collective-permute-done((bf16[128,3584]{1,0:T(8,128)(2,1)S(1)}, bf16[128,3584]{1,0:T(8,128)(2,1)S(1)}, u32[]{:S(2)}, u32[]{:S(2)}) %collective-permute-start.22) | collective-permute-done | bytes 917536 | tf_op jit(solution)/shard_map/ppermute | solution.py:72
  163.6 2.5 %collective-permute-start.27 = (bf16[32,3584]{1,0:T(8,128)(2,1)S(1)}, bf16[32,3584]{1,0:T(8,128)(2,1)S(1)}, u32[]{:S(2)}, u32[]{:S(2)}) collective-permute-start(bf16[32,3584]{1,0:T(8,128)(2,1)S(1)} %get-tuple-element.35), channel_id=1, source_target_pairs={{32,0},{9,1},{40,8},{17,9},{48,16},{25,17},{56,24},{1,25},{64,32},... | collective-permute-start | bytes 688136 | tf_op jit(solution)/shard_map/ppermute | solution.py:72
  166.2 5.4 %collective-permute-done.25 = bf16[32,3584]{1,0:T(8,128)(2,1)S(1)} collective-permute-done((bf16[32,3584]{1,0:T(8,128)(2,1)S(1)}, bf16[32,3584]{1,0:T(8,128)(2,1)S(1)}, u32[]{:S(2)}, u32[]{:S(2)}) %collective-permute-start.25) | collective-permute-done | bytes 229408 | tf_op jit(solution)/shard_map/ppermute | solution.py:72
  172.5 1.8 collective-permute-start.42
  175.1 4.1 %collective-permute-start.4 = (bf16[8,3584]{1,0:T(8,128)(2,1)S(1)}, bf16[8,3584]{1,0:T(8,128)(2,1)S(1)}, u32[]{:S(2)}, u32[]{:S(2)}) collective-permute-start(bf16[8,3584]{1,0:T(8,128)(2,1)S(1)} %get-tuple-element.49), channel_id=1, source_target_pairs={{0,1},{1,0},{2,3},{3,2},{4,5},{5,4},{6,7},{7,6},{8,9},{9,8},{10,11... | collective-permute-start | bytes 172040 | tf_op jit(solution)/shard_map/ppermute | solution.py:76
  179.4 4.9 %collective-permute-start.44 = (bf16[8,3584]{1,0:T(8,128)(2,1)S(1)}, bf16[8,3584]{1,0:T(8,128)(2,1)S(1)}, u32[]{:S(2)}, u32[]{:S(2)}) collective-permute-start(bf16[8,3584]{1,0:T(8,128)(2,1)S(1)} %get-tuple-element.52), channel_id=1, source_target_pairs={{0,1},{1,0},{2,3},{3,2},{4,5},{5,4},{6,7},{7,6},{8,9},{9,8},{10,11... | collective-permute-start | bytes 172040 | tf_op jit(solution)/shard_map/ppermute | solution.py:76
  (185 shorter events, 27.3 us)
Async XLA Ops:
  0.6 23.5 %copy-start = (bf16[8,512,128]{2,1,0:T(8,128)(2,1)S(1)}, bf16[8,512,128]{2,1,0:T(8,128)(2,1)}, u32[]{:S(2)}) copy-start(bf16[8,512,128]{2,1,0:T(8,128)(2,1)} %param.18) | copy-start | bytes 3145732
  8.8 15.3 %all-to-all-start = ((bf16[8,64,512]{2,0,1:T(8,128)(2,1)}), bf16[8,64,512]{2,0,1:T(8,128)(2,1)S(1)}, u32[]{:S(2)}, u32[]{:S(2)}) async-start(bf16[8,64,512]{2,0,1:T(8,128)(2,1)} %copy.43), calls=%async_computation | async-start | bytes 1048576 | tf_op jit(solution)/shard_map/all_to_all | solution.py:154
  15.9 22.2 %collective-permute-start.5 = (bf16[8,3712]{1,0:T(8,128)(2,1)}, bf16[8,3712]{1,0:T(8,128)(2,1)}, u32[]{:S(2)}, u32[]{:S(2)}) collective-permute-start(bf16[8,3712]{1,0:T(8,128)(2,1)} %get-tuple-element.58), channel_id=1, source_target_pairs={{0,1},{1,0},{2,3},{3,2},{4,5},{5,4},{6,7},{7,6},{8,9},{9,8},{10,11... | collective-permute-start | bytes 178184 | tf_op jit(solution)/shard_map/ppermute | solution.py:76
  32.6 2.5 %collective-permute-start = (bf16[64,3584]{1,0:T(8,128)(2,1)S(1)}, bf16[64,3584]{1,0:T(8,128)(2,1)S(1)}, u32[]{:S(2)}, u32[]{:S(2)}) collective-permute-start(bf16[64,3584]{1,0:T(8,128)(2,1)S(1)} %dynamic-slice_convert_fusion), channel_id=1, source_target_pairs={{0,1},{1,0},{2,3},{3,2},{4,5},{5,4},{6,7},{7,6},{8,9},{9,8},{10,11... | collective-permute-start | bytes 1376264 | tf_op jit(solution)/shard_map/ppermute | solution.py:76
  34.9 45.9 %collective-permute-start.13 = (bf16[2,3584,128]{2,1,0:T(8,128)(2,1)}, bf16[2,3584,128]{2,1,0:T(8,128)(2,1)}, u32[]{:S(2)}, u32[]{:S(2)}) collective-permute-start(bf16[2,3584,128]{2,1,0:T(8,128)(2,1)} %dynamic-slice_bitcast_fusion), channel_id=1, source_target_pairs={{0,1},{1,0},{2,3},{3,2},{4,5},{5,4},{6,7},{7,6},{8,9},{9,8},{10,11... | collective-permute-start | bytes 5505032 | tf_op jit(solution)/shard_map/ppermute | solution.py:76
  35.2 6.1 %collective-permute-start.1 = (bf16[16,3584]{1,0:T(8,128)(2,1)S(1)}, bf16[16,3584]{1,0:T(8,128)(2,1)S(1)}, u32[]{:S(2)}, u32[]{:S(2)}) collective-permute-start(bf16[16,3584]{1,0:T(8,128)(2,1)S(1)} %get-tuple-element.40), channel_id=1, source_target_pairs={{6,0},{0,2},{2,4},{4,6},{7,1},{1,3},{3,5},{5,7},{14,8},{8,10},{10,... | collective-permute-start | bytes 344072 | tf_op jit(solution)/shard_map/ppermute | solution.py:71
  35.5 7.0 %collective-permute-start.2 = (bf16[16,3584]{1,0:T(8,128)(2,1)S(1)}, bf16[16,3584]{1,0:T(8,128)(2,1)S(1)}, u32[]{:S(2)}, u32[]{:S(2)}) collective-permute-start(bf16[16,3584]{1,0:T(8,128)(2,1)S(1)} %get-tuple-element.42), channel_id=1, source_target_pairs={{4,0},{6,2},{0,4},{2,6},{5,1},{7,3},{1,5},{3,7},{12,8},{14,10},{8,... | collective-permute-start | bytes 344072 | tf_op jit(solution)/shard_map/ppermute | solution.py:71
  37.3 6.2 %collective-permute-start.3 = (bf16[16,3584]{1,0:T(8,128)(2,1)S(1)}, bf16[16,3584]{1,0:T(8,128)(2,1)S(1)}, u32[]{:S(2)}, u32[]{:S(2)}) collective-permute-start(bf16[16,3584]{1,0:T(8,128)(2,1)S(1)} %get-tuple-element.41), channel_id=1, source_target_pairs={{2,0},{4,2},{6,4},{0,6},{3,1},{5,3},{7,5},{1,7},{10,8},{12,10},{14... | collective-permute-start | bytes 344072 | tf_op jit(solution)/shard_map/ppermute | solution.py:71
  43.7 2.5 %collective-permute-start.6 = (f32[16,1]{0,1:T(1,128)S(1)}, f32[16,1]{0,1:T(1,128)S(1)}, u32[]{:S(2)}, u32[]{:S(2)}) collective-permute-start(f32[16,1]{0,1:T(1,128)S(1)} %bitcast.186), channel_id=1, source_target_pairs={{0,1},{1,0},{2,3},{3,2},{4,5},{5,4},{6,7},{7,6},{8,9},{9,8},{10,11... | collective-permute-start | bytes 200 | tf_op jit(solution)/shard_map/ppermute | solution.py:76
  46.3 5.0 %collective-permute-start.7 = (bf16[16,3712]{1,0:T(8,128)(2,1)S(1)}, bf16[16,3712]{1,0:T(8,128)(2,1)S(1)}, u32[]{:S(2)}, u32[]{:S(2)}) collective-permute-start(bf16[16,3712]{1,0:T(8,128)(2,1)S(1)} %get-tuple-element.48), channel_id=1, source_target_pairs={{2,0},{4,2},{6,4},{0,6},{3,1},{5,3},{7,5},{1,7},{10,8},{12,10},{14... | collective-permute-start | bytes 356360 | tf_op jit(solution)/shard_map/ppermute | solution.py:71
  48.6 5.8 %collective-permute-start.8 = (bf16[16,3712]{1,0:T(8,128)(2,1)S(1)}, bf16[16,3712]{1,0:T(8,128)(2,1)S(1)}, u32[]{:S(2)}, u32[]{:S(2)}) collective-permute-start(bf16[16,3712]{1,0:T(8,128)(2,1)S(1)} %get-tuple-element.48), channel_id=1, source_target_pairs={{4,0},{6,2},{0,4},{2,6},{5,1},{7,3},{1,5},{3,7},{12,8},{14,10},{8,... | collective-permute-start | bytes 356360 | tf_op jit(solution)/shard_map/ppermute | solution.py:71
  48.6 8.6 %collective-permute-start.9 = (bf16[16,3712]{1,0:T(8,128)(2,1)S(1)}, bf16[16,3712]{1,0:T(8,128)(2,1)S(1)}, u32[]{:S(2)}, u32[]{:S(2)}) collective-permute-start(bf16[16,3712]{1,0:T(8,128)(2,1)S(1)} %get-tuple-element.48), channel_id=1, source_target_pairs={{6,0},{0,2},{2,4},{4,6},{7,1},{1,3},{3,5},{5,7},{14,8},{8,10},{10,... | collective-permute-start | bytes 356360 | tf_op jit(solution)/shard_map/ppermute | solution.py:71
  49.4 72.2 %collective-permute-start.20 = (bf16[128,3584]{1,0:T(8,128)(2,1)S(1)}, bf16[128,3584]{1,0:T(8,128)(2,1)}, u32[]{:S(2)}, u32[]{:S(2)}) collective-permute-start(bf16[128,3584]{1,0:T(8,128)(2,1)S(1)} %get-tuple-element.33), channel_id=1, source_target_pairs={{0,1},{1,0},{2,3},{3,2},{4,5},{5,4},{6,7},{7,6},{8,9},{9,8},{10,11... | collective-permute-start | bytes 2752520 | tf_op jit(solution)/shard_map/ppermute | solution.py:76
  57.2 14.5 %collective-permute-start.10 = (bf16[64,3712]{1,0:T(8,128)(2,1)S(1)}, bf16[64,3712]{1,0:T(8,128)(2,1)S(1)}, u32[]{:S(2)}, u32[]{:S(2)}) collective-permute-start(bf16[64,3712]{1,0:T(8,128)(2,1)S(1)} %bitcast.155), channel_id=1, source_target_pairs={{32,0},{9,1},{40,8},{17,9},{48,16},{25,17},{56,24},{1,25},{64,32},... | collective-permute-start | bytes 1425416 | tf_op jit(solution)/shard_map/ppermute | solution.py:72
  61.1 10.7 %collective-permute-start.11 = (bf16[64,3712]{1,0:T(8,128)(2,1)S(1)}, bf16[64,3712]{1,0:T(8,128)(2,1)S(1)}, u32[]{:S(2)}, u32[]{:S(2)}) collective-permute-start(bf16[64,3712]{1,0:T(8,128)(2,1)S(1)} %bitcast.156), channel_id=1, source_target_pairs={{64,0},{17,1},{72,8},{25,9},{80,16},{1,17},{88,24},{9,25},{96,32},... | collective-permute-start | bytes 1425416 | tf_op jit(solution)/shard_map/ppermute | solution.py:72
  61.1 14.1 %collective-permute-start.12 = (bf16[64,3712]{1,0:T(8,128)(2,1)S(1)}, bf16[64,3712]{1,0:T(8,128)(2,1)S(1)}, u32[]{:S(2)}, u32[]{:S(2)}) collective-permute-start(bf16[64,3712]{1,0:T(8,128)(2,1)S(1)} %bitcast.157), channel_id=1, source_target_pairs={{96,0},{25,1},{104,8},{1,9},{112,16},{9,17},{120,24},{17,25},{0,32... | collective-permute-start | bytes 1425416 | tf_op jit(solution)/shard_map/ppermute | solution.py:72
  75.7 13.2 %collective-permute-start.28 = (bf16[128,3712]{1,0:T(8,128)(2,1)S(1)}, bf16[128,3712]{1,0:T(8,128)(2,1)S(1)}, u32[]{:S(2)}, u32[]{:S(2)}) collective-permute-start(bf16[128,3712]{1,0:T(8,128)(2,1)S(1)} %bitcast.144), channel_id=1, source_target_pairs={{8,0},{33,1},{16,8},{41,9},{24,16},{49,17},{0,24},{57,25},{40,32},... | collective-permute-start | bytes 2850824 | tf_op jit(solution)/shard_map/ppermute | solution.py:72
  78.2 14.2 %collective-permute-start.30 = (bf16[128,3712]{1,0:T(8,128)(2,1)S(1)}, bf16[128,3712]{1,0:T(8,128)(2,1)S(1)}, u32[]{:S(2)}, u32[]{:S(2)}) collective-permute-start(bf16[128,3712]{1,0:T(8,128)(2,1)S(1)} %bitcast.145), channel_id=1, source_target_pairs={{24,0},{97,1},{0,8},{105,9},{8,16},{113,17},{16,24},{121,25},{56,3... | collective-permute-start | bytes 2850824 | tf_op jit(solution)/shard_map/ppermute | solution.py:72
  78.2 25.0 %collective-permute-start.14 = (bf16[128,3712]{1,0:T(8,128)(2,1)S(1)}, bf16[128,3712]{1,0:T(8,128)(2,1)S(1)}, u32[]{:S(2)}, u32[]{:S(2)}) collective-permute-start(bf16[128,3712]{1,0:T(8,128)(2,1)S(1)} %bitcast.148), channel_id=1, source_target_pairs={{8,0},{33,1},{16,8},{41,9},{24,16},{49,17},{0,24},{57,25},{40,32},... | collective-permute-start | bytes 2850824 | tf_op jit(solution)/shard_map/ppermute | solution.py:72
  80.9 21.6 %collective-permute-start.16 = (bf16[128,3712]{1,0:T(8,128)(2,1)S(1)}, bf16[128,3712]{1,0:T(8,128)(2,1)S(1)}, u32[]{:S(2)}, u32[]{:S(2)}) collective-permute-start(bf16[128,3712]{1,0:T(8,128)(2,1)S(1)} %bitcast.149), channel_id=1, source_target_pairs={{24,0},{97,1},{0,8},{105,9},{8,16},{113,17},{16,24},{121,25},{56,3... | collective-permute-start | bytes 2850824 | tf_op jit(solution)/shard_map/ppermute | solution.py:72
  88.9 16.7 %collective-permute-start.29 = (bf16[64,3712]{1,0:T(8,128)(2,1)S(1)}, bf16[64,3712]{1,0:T(8,128)(2,1)S(1)}, u32[]{:S(2)}, u32[]{:S(2)}) collective-permute-start(bf16[64,3712]{1,0:T(8,128)(2,1)S(1)} %slice.367), channel_id=1, source_target_pairs={{8,0},{33,1},{16,8},{41,9},{24,16},{49,17},{0,24},{57,25},{40,32},... | collective-permute-start | bytes 1425416 | tf_op jit(solution)/shard_map/ppermute | solution.py:72
  92.4 15.1 %collective-permute-start.31 = (bf16[64,3712]{1,0:T(8,128)(2,1)S(1)}, bf16[64,3712]{1,0:T(8,128)(2,1)S(1)}, u32[]{:S(2)}, u32[]{:S(2)}) collective-permute-start(bf16[64,3712]{1,0:T(8,128)(2,1)S(1)} %slice.368), channel_id=1, source_target_pairs={{24,0},{97,1},{0,8},{105,9},{8,16},{113,17},{16,24},{121,25},{56,3... | collective-permute-start | bytes 1425416 | tf_op jit(solution)/shard_map/ppermute | solution.py:72
  104.0 7.9 %collective-permute-start.15 = (bf16[64,3712]{1,0:T(8,128)(2,1)S(1)}, bf16[64,3712]{1,0:T(8,128)(2,1)S(1)}, u32[]{:S(2)}, u32[]{:S(2)}) collective-permute-start(bf16[64,3712]{1,0:T(8,128)(2,1)S(1)} %slice.339), channel_id=1, source_target_pairs={{8,0},{33,1},{16,8},{41,9},{24,16},{49,17},{0,24},{57,25},{40,32},... | collective-permute-start | bytes 1425416 | tf_op jit(solution)/shard_map/ppermute | solution.py:72
  104.1 9.1 %collective-permute-start.17 = (bf16[64,3712]{1,0:T(8,128)(2,1)S(1)}, bf16[64,3712]{1,0:T(8,128)(2,1)S(1)}, u32[]{:S(2)}, u32[]{:S(2)}) collective-permute-start(bf16[64,3712]{1,0:T(8,128)(2,1)S(1)} %slice.340), channel_id=1, source_target_pairs={{24,0},{97,1},{0,8},{105,9},{8,16},{113,17},{16,24},{121,25},{56,3... | collective-permute-start | bytes 1425416 | tf_op jit(solution)/shard_map/ppermute | solution.py:72
  114.1 5.7 %collective-permute-start.32 = (bf16[512,256]{1,0:T(8,128)(2,1)S(1)}, bf16[512,256]{1,0:T(8,128)(2,1)S(1)}, u32[]{:S(2)}, u32[]{:S(2)}) collective-permute-start(bf16[512,256]{1,0:T(8,128)(2,1)S(1)} %pad_maximum_fusion.10), channel_id=1, source_target_pairs={{0,1},{1,0},{2,3},{3,2},{4,5},{5,4},{6,7},{7,6},{8,9},{9,8},{10,11... | collective-permute-start | bytes 786440 | tf_op jit(solution)/shard_map/ppermute | solution.py:76
  118.6 1.9 %collective-permute-start.18 = (bf16[512,256]{1,0:T(8,128)(2,1)S(1)}, bf16[512,256]{1,0:T(8,128)(2,1)S(1)}, u32[]{:S(2)}, u32[]{:S(2)}) collective-permute-start(bf16[512,256]{1,0:T(8,128)(2,1)S(1)} %pad_maximum_fusion.9), channel_id=1, source_target_pairs={{0,1},{1,0},{2,3},{3,2},{4,5},{5,4},{6,7},{7,6},{8,9},{9,8},{10,11... | collective-permute-start | bytes 786440 | tf_op jit(solution)/shard_map/ppermute | solution.py:76
  120.1 1.4 collective-permute-start.33
  120.8 5.9 %collective-permute-start.19 = (bf16[512,128]{1,0:T(8,128)(2,1)S(1)}, bf16[512,128]{1,0:T(8,128)(2,1)S(1)}, u32[]{:S(2)}, u32[]{:S(2)}) collective-permute-start(bf16[512,128]{1,0:T(8,128)(2,1)S(1)} %fusion.23), channel_id=1, source_target_pairs={{0,1},{1,0},{2,3},{3,2},{4,5},{5,4},{6,7},{7,6},{8,9},{9,8},{10,11... | collective-permute-start | bytes 393224 | tf_op jit(solution)/shard_map/ppermute | solution.py:76
  124.0 8.9 %collective-permute-start.34 = (bf16[64,3584]{1,0:T(8,128)(2,1)S(1)}, bf16[64,3584]{1,0:T(8,128)(2,1)S(1)}, u32[]{:S(2)}, u32[]{:S(2)}) collective-permute-start(bf16[64,3584]{1,0:T(8,128)(2,1)S(1)} %get-tuple-element.22), channel_id=1, source_target_pairs={{24,0},{97,1},{0,8},{105,9},{8,16},{113,17},{16,24},{121,25},{56,3... | collective-permute-start | bytes 1376264 | tf_op jit(solution)/shard_map/ppermute | solution.py:72
  124.1 8.8 %collective-permute-start.36 = (bf16[64,3584]{1,0:T(8,128)(2,1)S(1)}, bf16[64,3584]{1,0:T(8,128)(2,1)S(1)}, u32[]{:S(2)}, u32[]{:S(2)}) collective-permute-start(bf16[64,3584]{1,0:T(8,128)(2,1)S(1)} %get-tuple-element.23), channel_id=1, source_target_pairs={{8,0},{33,1},{16,8},{41,9},{24,16},{49,17},{0,24},{57,25},{40,32},... | collective-permute-start | bytes 1376264 | tf_op jit(solution)/shard_map/ppermute | solution.py:72
  129.2 9.1 %collective-permute-start.21 = (bf16[64,3584]{1,0:T(8,128)(2,1)S(1)}, bf16[64,3584]{1,0:T(8,128)(2,1)S(1)}, u32[]{:S(2)}, u32[]{:S(2)}) collective-permute-start(bf16[64,3584]{1,0:T(8,128)(2,1)S(1)} %get-tuple-element.16), channel_id=1, source_target_pairs={{24,0},{97,1},{0,8},{105,9},{8,16},{113,17},{16,24},{121,25},{56,3... | collective-permute-start | bytes 1376264 | tf_op jit(solution)/shard_map/ppermute | solution.py:72
  129.5 8.8 %collective-permute-start.23 = (bf16[64,3584]{1,0:T(8,128)(2,1)S(1)}, bf16[64,3584]{1,0:T(8,128)(2,1)S(1)}, u32[]{:S(2)}, u32[]{:S(2)}) collective-permute-start(bf16[64,3584]{1,0:T(8,128)(2,1)S(1)} %get-tuple-element.17), channel_id=1, source_target_pairs={{8,0},{33,1},{16,8},{41,9},{24,16},{49,17},{0,24},{57,25},{40,32},... | collective-permute-start | bytes 1376264 | tf_op jit(solution)/shard_map/ppermute | solution.py:72
  133.2 15.0 %collective-permute-start.35 = (bf16[128,3584]{1,0:T(8,128)(2,1)S(1)}, bf16[128,3584]{1,0:T(8,128)(2,1)S(1)}, u32[]{:S(2)}, u32[]{:S(2)}) collective-permute-start(bf16[128,3584]{1,0:T(8,128)(2,1)S(1)} %pad_maximum_fusion.6), channel_id=1, source_target_pairs={{24,0},{97,1},{0,8},{105,9},{8,16},{113,17},{16,24},{121,25},{56,3... | collective-permute-start | bytes 2752520 | tf_op jit(solution)/shard_map/ppermute | solution.py:72
  133.3 14.8 %collective-permute-start.37 = (bf16[128,3584]{1,0:T(8,128)(2,1)S(1)}, bf16[128,3584]{1,0:T(8,128)(2,1)S(1)}, u32[]{:S(2)}, u32[]{:S(2)}) collective-permute-start(bf16[128,3584]{1,0:T(8,128)(2,1)S(1)} %pad_maximum_fusion.7), channel_id=1, source_target_pairs={{8,0},{33,1},{16,8},{41,9},{24,16},{49,17},{0,24},{57,25},{40,32},... | collective-permute-start | bytes 2752520 | tf_op jit(solution)/shard_map/ppermute | solution.py:72
  138.6 23.7 %collective-permute-start.22 = (bf16[128,3584]{1,0:T(8,128)(2,1)S(1)}, bf16[128,3584]{1,0:T(8,128)(2,1)S(1)}, u32[]{:S(2)}, u32[]{:S(2)}) collective-permute-start(bf16[128,3584]{1,0:T(8,128)(2,1)S(1)} %pad_maximum_fusion.4), channel_id=1, source_target_pairs={{24,0},{97,1},{0,8},{105,9},{8,16},{113,17},{16,24},{121,25},{56,3... | collective-permute-start | bytes 2752520 | tf_op jit(solution)/shard_map/ppermute | solution.py:72
  138.8 23.5 %collective-permute-start.24 = (bf16[128,3584]{1,0:T(8,128)(2,1)S(1)}, bf16[128,3584]{1,0:T(8,128)(2,1)S(1)}, u32[]{:S(2)}, u32[]{:S(2)}) collective-permute-start(bf16[128,3584]{1,0:T(8,128)(2,1)S(1)} %pad_maximum_fusion.5), channel_id=1, source_target_pairs={{8,0},{33,1},{16,8},{41,9},{24,16},{49,17},{0,24},{57,25},{40,32},... | collective-permute-start | bytes 2752520 | tf_op jit(solution)/shard_map/ppermute | solution.py:72
  148.5 15.1 %collective-permute-start.38 = (bf16[32,3584]{1,0:T(8,128)(2,1)S(1)}, bf16[32,3584]{1,0:T(8,128)(2,1)S(1)}, u32[]{:S(2)}, u32[]{:S(2)}) collective-permute-start(bf16[32,3584]{1,0:T(8,128)(2,1)S(1)} %get-tuple-element.37), channel_id=1, source_target_pairs={{96,0},{25,1},{104,8},{1,9},{112,16},{9,17},{120,24},{17,25},{0,32... | collective-permute-start | bytes 688136 | tf_op jit(solution)/shard_map/ppermute | solution.py:72
  148.8 17.3 %collective-permute-start.39 = (bf16[32,3584]{1,0:T(8,128)(2,1)S(1)}, bf16[32,3584]{1,0:T(8,128)(2,1)S(1)}, u32[]{:S(2)}, u32[]{:S(2)}) collective-permute-start(bf16[32,3584]{1,0:T(8,128)(2,1)S(1)} %get-tuple-element.39), channel_id=1, source_target_pairs={{64,0},{17,1},{72,8},{25,9},{80,16},{1,17},{88,24},{9,25},{96,32},... | collective-permute-start | bytes 688136 | tf_op jit(solution)/shard_map/ppermute | solution.py:72
  149.4 16.6 %collective-permute-start.40 = (bf16[32,3584]{1,0:T(8,128)(2,1)S(1)}, bf16[32,3584]{1,0:T(8,128)(2,1)S(1)}, u32[]{:S(2)}, u32[]{:S(2)}) collective-permute-start(bf16[32,3584]{1,0:T(8,128)(2,1)S(1)} %get-tuple-element.38), channel_id=1, source_target_pairs={{32,0},{9,1},{40,8},{17,9},{48,16},{25,17},{56,24},{1,25},{64,32},... | collective-permute-start | bytes 688136 | tf_op jit(solution)/shard_map/ppermute | solution.py:72
  162.3 23.6 %copy-start.1 = (bf16[8,512,128]{2,1,0:T(8,128)(2,1)S(1)}, bf16[8,512,128]{2,1,0:T(8,128)(2,1)}, u32[]{:S(2)}) copy-start(bf16[8,512,128]{2,1,0:T(8,128)(2,1)} %param.18) | copy-start | bytes 3145732
  162.7 8.9 %collective-permute-start.25 = (bf16[32,3584]{1,0:T(8,128)(2,1)S(1)}, bf16[32,3584]{1,0:T(8,128)(2,1)S(1)}, u32[]{:S(2)}, u32[]{:S(2)}) collective-permute-start(bf16[32,3584]{1,0:T(8,128)(2,1)S(1)} %get-tuple-element.34), channel_id=1, source_target_pairs={{96,0},{25,1},{104,8},{1,9},{112,16},{9,17},{120,24},{17,25},{0,32... | collective-permute-start | bytes 688136 | tf_op jit(solution)/shard_map/ppermute | solution.py:72
  163.6 8.0 %collective-permute-start.26 = (bf16[32,3584]{1,0:T(8,128)(2,1)S(1)}, bf16[32,3584]{1,0:T(8,128)(2,1)S(1)}, u32[]{:S(2)}, u32[]{:S(2)}) collective-permute-start(bf16[32,3584]{1,0:T(8,128)(2,1)S(1)} %get-tuple-element.36), channel_id=1, source_target_pairs={{64,0},{17,1},{72,8},{25,9},{80,16},{1,17},{88,24},{9,25},{96,32},... | collective-permute-start | bytes 688136 | tf_op jit(solution)/shard_map/ppermute | solution.py:72
  163.6 8.6 %collective-permute-start.27 = (bf16[32,3584]{1,0:T(8,128)(2,1)S(1)}, bf16[32,3584]{1,0:T(8,128)(2,1)S(1)}, u32[]{:S(2)}, u32[]{:S(2)}) collective-permute-start(bf16[32,3584]{1,0:T(8,128)(2,1)S(1)} %get-tuple-element.35), channel_id=1, source_target_pairs={{32,0},{9,1},{40,8},{17,9},{48,16},{25,17},{56,24},{1,25},{64,32},... | collective-permute-start | bytes 688136 | tf_op jit(solution)/shard_map/ppermute | solution.py:72
  172.4 6.9 %collective-permute-start.41 = (bf16[2,8,3584]{2,1,0:T(8,128)(2,1)S(1)}, bf16[2,8,3584]{2,1,0:T(8,128)(2,1)S(1)}, u32[]{:S(2)}, u32[]{:S(2)}) collective-permute-start(bf16[2,8,3584]{2,1,0:T(8,128)(2,1)S(1)} %get-tuple-element.43), channel_id=1, source_target_pairs={{6,0},{0,2},{2,4},{4,6},{7,1},{1,3},{3,5},{5,7},{14,8},{8,10},{10,... | collective-permute-start | bytes 344072 | tf_op jit(solution)/shard_map/ppermute | solution.py:71
  172.5 6.8 %collective-permute-start.42 = (bf16[2,8,3584]{2,1,0:T(8,128)(2,1)S(1)}, bf16[2,8,3584]{2,1,0:T(8,128)(2,1)S(1)}, u32[]{:S(2)}, u32[]{:S(2)}) collective-permute-start(bf16[2,8,3584]{2,1,0:T(8,128)(2,1)S(1)} %get-tuple-element.45), channel_id=1, source_target_pairs={{4,0},{6,2},{0,4},{2,6},{5,1},{7,3},{1,5},{3,7},{12,8},{14,10},{8,... | collective-permute-start | bytes 344072 | tf_op jit(solution)/shard_map/ppermute | solution.py:71
  174.2 5.1 %collective-permute-start.43 = (bf16[2,8,3584]{2,1,0:T(8,128)(2,1)S(1)}, bf16[2,8,3584]{2,1,0:T(8,128)(2,1)S(1)}, u32[]{:S(2)}, u32[]{:S(2)}) collective-permute-start(bf16[2,8,3584]{2,1,0:T(8,128)(2,1)S(1)} %get-tuple-element.44), channel_id=1, source_target_pairs={{2,0},{4,2},{6,4},{0,6},{3,1},{5,3},{7,5},{1,7},{10,8},{12,10},{14... | collective-permute-start | bytes 344072 | tf_op jit(solution)/shard_map/ppermute | solution.py:71
  175.1 9.1 %collective-permute-start.4 = (bf16[8,3584]{1,0:T(8,128)(2,1)S(1)}, bf16[8,3584]{1,0:T(8,128)(2,1)S(1)}, u32[]{:S(2)}, u32[]{:S(2)}) collective-permute-start(bf16[8,3584]{1,0:T(8,128)(2,1)S(1)} %get-tuple-element.49), channel_id=1, source_target_pairs={{0,1},{1,0},{2,3},{3,2},{4,5},{5,4},{6,7},{7,6},{8,9},{9,8},{10,11... | collective-permute-start | bytes 172040 | tf_op jit(solution)/shard_map/ppermute | solution.py:76
  179.4 5.8 %collective-permute-start.44 = (bf16[8,3584]{1,0:T(8,128)(2,1)S(1)}, bf16[8,3584]{1,0:T(8,128)(2,1)S(1)}, u32[]{:S(2)}, u32[]{:S(2)}) collective-permute-start(bf16[8,3584]{1,0:T(8,128)(2,1)S(1)} %get-tuple-element.52), channel_id=1, source_target_pairs={{0,1},{1,0},{2,3},{3,2},{4,5},{5,4},{6,7},{7,6},{8,9},{9,8},{10,11... | collective-permute-start | bytes 172040 | tf_op jit(solution)/shard_map/ppermute | solution.py:76
  (20 other events, 145.5 us)

commit v6 on v5

--- a/solution.py
+++ b/solution.py
@@ -49,27 +49,23 @@
     return weight_table.astype(jnp.bfloat16)
 
 
-near_axis = ("y", "z")
+first_axis = ("x", "z")
+near_axis = ("y", "x")
 far_axis = ("z", "y")
 
 
 def ring(axes, distance):
     pairs = []
-    for y in range(4):
-        for z in range(4):
-            for core in range(2):
-                if axes[core] == "y":
-                    source = ((y + distance) % 4, z)
-                else:
-                    source = (y, (z + distance) % 4)
-                pairs.append(((source[0] * 4 + source[1]) * 2 + core, (y * 4 + z) * 2 + core))
+    for target in range(128):
+        core, place = target % 2, {"x": target // 2 % 4, "z": target // 8 % 4, "y": target // 32}
+        place[axes[core]] = (place[axes[core]] + distance) % 4
+        source = ((place["y"] * 4 + place["z"]) * 4 + place["x"]) * 2 + core
+        pairs.append((source, target))
     return pairs
 
 
 def shift(value, axes, distance):
-    if axes == "x":
-        return lax.ppermute(value, "x", [((i + distance) % 4, i) for i in range(4)])
-    return lax.ppermute(value, ("y", "z", "core"), ring(axes, distance))
+    return lax.ppermute(value, ("y", "z", "x", "core"), ring(axes, distance))
 
 
 def swap(value):
@@ -183,9 +179,9 @@
 
     attention = total(
         for_chip(0),
-        shift(for_chip(1).astype(bf16), "x", -1),
-        shift(for_chip(2).astype(bf16), "x", 2),
-        shift(for_chip(3).astype(bf16), "x", 1),
+        shift(for_chip(1).astype(bf16), ("x", "x"), -1),
+        shift(for_chip(2).astype(bf16), ("x", "x"), 2),
+        shift(for_chip(3).astype(bf16), ("x", "x"), 1),
     ).astype(bf16)
     residual_f32 = total(chip_residual, attention).astype(bf16).astype(f32)
     squares = jnp.sum(residual_f32 * residual_f32, axis=1, keepdims=True)
@@ -196,7 +192,7 @@
     payload = jnp.concatenate([normed, chip_table], axis=1)
 
     width = half + lanes
-    group = gather_near(payload, "x").reshape(8 * rows, width)
+    group = gather_near(payload, first_axis).reshape(8 * rows, width)
     near = gather_near(group, near_axis).reshape(4, 4, 2, rows, width)
 
     chunks = [near[:, :, c].reshape(16 * rows, width) for c in range(2)]
@@ -204,8 +200,11 @@
     units = hidden // 2
 
     def crossed(value):
-        value = value.reshape(4, 4, 4 * rows, value.shape[1])
-        return value.transpose(1, 0, 2, 3).reshape(64 * rows, value.shape[3])
+        value = value.reshape(4, 4, 4, rows, value.shape[1])
+        value = jnp.where(
+            core == 0, value.transpose(2, 0, 1, 3, 4), value.transpose(1, 2, 0, 3, 4)
+        )
+        return value.reshape(64 * rows, value.shape[4])
 
     sums = []
     for chunk in chunks:
@@ -235,7 +234,7 @@
         back = scatter_far(*outs, far_axis).reshape(4, 4 * rows, half)
         sums.append(scatter_near(back, near_axis).astype(bf16))
     to_x = jnp.stack([s.reshape(4, rows, half) for s in sums], axis=1)
-    chip_out = scatter_near(to_x, "x")
+    chip_out = scatter_near(to_x, first_axis)
 
     attention_out = to_tokens(attention.reshape(2, rows, half))
     expert_sum = to_tokens(chip_out.astype(bf16))

time: 186 us -> 180 us (0.968)
  starting transfers between devices: 64.6 us -> 60.2 us
  waiting for transfers between devices: 79.2 us -> 76.9 us
    ppermute x11, starting transfers between devices: 17.9 us -> 14 us  [swap(): return lax.ppermute(value, 'core', [(0, 1), (1, 0)])]
    ppermute x34, waiting for transfers between devices: 68 us -> 65.5 us  [shift(): return lax.ppermute(value, ('y', 'z', 'x', 'core'), ring(axes, distance))]
  transfers between devices with their start and end apart: 46 -> 46, of which waited for: 24 -> 25; matrix products, arithmetic and copies ran while one was open for 17% -> 18% of each run, Pallas kernels for 0% -> 0%
where the time goes in v6:
time: 180 us; the launch traced here: 179 us
  waiting for transfers between devices  76.9 us (43%)
  starting transfers between devices  60.2 us (33%)
  matrix products  24.1 us (13%)
  other arithmetic  9.53 us (5%)
  local copies, waits for them, and re-layouts  7 us (4%)
    ppermute x34, waiting for transfers between devices, shift(): return lax.ppermute(value, ('y', 'z', 'x', 'core'), ring(axes, distance))  65.5 us
    ppermute x34, starting transfers between devices, shift(): return lax.ppermute(value, ('y', 'z', 'x', 'core'), ring(axes, distance))  40.4 us
    ppermute x11, starting transfers between devices, swap(): return lax.ppermute(value, 'core', [(0, 1), (1, 0)])  14 us
    all_to_all x1, waiting for transfers between devices, per_device(): lax.all_to_all(latent_out, ('x', 'core'), split_axis=1, concat_axis=0, ti...  8.21 us
    dot_general x1, matrix products, per_device(): projected = jnp.dot(values, out_proj, preferred_element_type=f32)  8.06 us
    all_to_all x1, starting transfers between devices, per_device(): lax.all_to_all(latent_out, ('x', 'core'), split_axis=1, concat_axis=0, ti...  5.8 us
    dot_general x8, matrix products, per_device(): jnp.dot(b, weight_in, preferred_element_type=f32)  5.37 us
    dot_general x2, matrix products, per_device(): out = jnp.dot(activated, weight_out, preferred_element_type=f32)  4.61 us
  transfers between devices with their start and end apart: 46, of which 25 were waited for; matrix products, arithmetic and copies ran while one was open for 18% of the time, Pallas kernels for 0%

profile of v6, /device:TPU:1, one launch (start us, length us, event | category | flops | bytes accessed | tf_op | source)
XLA Modules:
  0.0 179.4 jit_solution(1927889451963105152)
XLA Ops:
  1.5 1.7 fusion.61
  3.2 3.0 %fusion.75 = (f32[8,64]{1,0:T(8,128)S(1)}, f32[8,64,384]{2,1,0:T(8,128)S(1)}) fusion(bf16[8,64,576]{2,1,0:T(8,128)(2,1)} %param.14, bf16[8,384,576]{1,2,0:T(8,128)(2,1)} %param.15, s32[8]{0:T(128)} %param.17), kind=kOutput, calls=%fused_computation.174 | convolution fusion | flops 227278336 | bytes 4917280 | tf_op jit(solution)/shard_map/rhc,rtc->rht/dot_general | solution.py:15
  6.6 1.1 fusion.12
  7.7 1.1 copy.55
  8.8 5.8 %all-to-all-start = ((bf16[8,64,512]{2,0,1:T(8,128)(2,1)}), bf16[8,64,512]{2,0,1:T(8,128)(2,1)S(1)}, u32[]{:S(2)}, u32[]{:S(2)}) async-start(bf16[8,64,512]{2,0,1:T(8,128)(2,1)} %copy.55), calls=%async_computation | async-start | bytes 1048576 | tf_op jit(solution)/shard_map/all_to_all | solution.py:150
  15.9 8.2 %all-to-all-done = bf16[8,64,512]{2,0,1:T(8,128)(2,1)S(1)} async-done(((bf16[8,64,512]{2,0,1:T(8,128)(2,1)}), bf16[8,64,512]{2,0,1:T(8,128)(2,1)S(1)}, u32[]{:S(2)}, u32[]{:S(2)}) %all-to-all-start) | async-done | bytes 524320 | tf_op jit(solution)/shard_map/all_to_all | solution.py:150
  24.4 8.1 %fusion.43 = f32[64,7168]{1,0:T(8,128)S(1)} fusion(bf16[1024,7168]{1,0:T(8,128)(2,1)} %param.19, bf16[8,8,8,128]{3,2,1,0:T(8,128)(2,1)S(1)} %fusion.16), kind=kOutput, calls=%fused_computation.95 | convolution fusion | flops 939524096 | bytes 16646144 | tf_op jit(solution)/shard_map/dot_general | solution.py:172
  33.5 1.4 dynamic-slice_bitcast_fusion
  35.6 1.8 collective-permute-start.2
  39.0 2.4 %collective-permute-done.1 = bf16[16,3584]{1,0:T(8,128)(2,1)S(1)} collective-permute-done((bf16[16,3584]{1,0:T(8,128)(2,1)S(1)}, bf16[16,3584]{1,0:T(8,128)(2,1)S(1)}, u32[]{:S(2)}, u32[]{:S(2)}) %collective-permute-start.1) | collective-permute-done | bytes 114720 | tf_op jit(solution)/shard_map/ppermute | solution.py:68
  41.3 1.2 collective-permute-done.2
  42.6 1.0 collective-permute-done.3
  43.7 1.7 collective-permute-start.6
  46.4 3.8 %collective-permute-start.7 = (bf16[16,3712]{1,0:T(8,128)(2,1)S(1)}, bf16[16,3712]{1,0:T(8,128)(2,1)S(1)}, u32[]{:S(2)}, u32[]{:S(2)}) collective-permute-start(bf16[16,3712]{1,0:T(8,128)(2,1)S(1)} %get-tuple-element.48), channel_id=1, source_target_pairs={{2,0},{9,1},{4,2},{11,3},{6,4},{13,5},{0,6},{15,7},{10,8},{17,9},{... | collective-permute-start | bytes 356360 | tf_op jit(solution)/shard_map/ppermute | solution.py:68
  51.1 2.1 %collective-permute-done.7 = bf16[16,3712]{1,0:T(8,128)(2,1)S(1)} collective-permute-done((bf16[16,3712]{1,0:T(8,128)(2,1)S(1)}, bf16[16,3712]{1,0:T(8,128)(2,1)S(1)}, u32[]{:S(2)}, u32[]{:S(2)}) %collective-permute-start.7) | collective-permute-done | bytes 118816 | tf_op jit(solution)/shard_map/ppermute | solution.py:68
  53.2 2.2 %collective-permute-done.8 = bf16[16,3712]{1,0:T(8,128)(2,1)S(1)} collective-permute-done((bf16[16,3712]{1,0:T(8,128)(2,1)S(1)}, bf16[16,3712]{1,0:T(8,128)(2,1)S(1)}, u32[]{:S(2)}, u32[]{:S(2)}) %collective-permute-start.8) | collective-permute-done | bytes 118816 | tf_op jit(solution)/shard_map/ppermute | solution.py:68
  56.4 2.2 %collective-permute-start.10 = (bf16[64,3712]{1,0:T(8,128)(2,1)S(1)}, bf16[64,3712]{1,0:T(8,128)(2,1)S(1)}, u32[]{:S(2)}, u32[]{:S(2)}) collective-permute-start(bf16[64,3712]{1,0:T(8,128)(2,1)S(1)} %bitcast.167), channel_id=1, source_target_pairs={{32,0},{3,1},{34,2},{5,3},{36,4},{7,5},{38,6},{1,7},{40,8},{11,9},... | collective-permute-start | bytes 1425416 | tf_op jit(solution)/shard_map/ppermute | solution.py:68
  59.3 1.6 dynamic-slice_bitcast_fusion.2
  60.9 8.4 %collective-permute-done.10 = bf16[64,3712]{1,0:T(8,128)(2,1)S(1)} collective-permute-done((bf16[64,3712]{1,0:T(8,128)(2,1)S(1)}, bf16[64,3712]{1,0:T(8,128)(2,1)S(1)}, u32[]{:S(2)}, u32[]{:S(2)}) %collective-permute-start.10) | collective-permute-done | bytes 475168 | tf_op jit(solution)/shard_map/ppermute | solution.py:68
  69.3 3.4 %collective-permute-done.12 = bf16[64,3712]{1,0:T(8,128)(2,1)S(1)} collective-permute-done((bf16[64,3712]{1,0:T(8,128)(2,1)S(1)}, bf16[64,3712]{1,0:T(8,128)(2,1)S(1)}, u32[]{:S(2)}, u32[]{:S(2)}) %collective-permute-start.12) | collective-permute-done | bytes 475168 | tf_op jit(solution)/shard_map/ppermute | solution.py:68
  73.2 2.5 %collective-permute-start.28 = (bf16[128,3712]{1,0:T(8,128)(2,1)S(1)}, bf16[128,3712]{1,0:T(8,128)(2,1)S(1)}, u32[]{:S(2)}, u32[]{:S(2)}) collective-permute-start(bf16[128,3712]{1,0:T(8,128)(2,1)S(1)} %bitcast.152), channel_id=1, source_target_pairs={{8,0},{33,1},{10,2},{35,3},{12,4},{37,5},{14,6},{39,7},{16,8},{41,... | collective-permute-start | bytes 2850824 | tf_op jit(solution)/shard_map/ppermute | solution.py:68
  75.7 2.7 %collective-permute-start.14 = (bf16[128,3712]{1,0:T(8,128)(2,1)S(1)}, bf16[128,3712]{1,0:T(8,128)(2,1)S(1)}, u32[]{:S(2)}, u32[]{:S(2)}) collective-permute-start(bf16[128,3712]{1,0:T(8,128)(2,1)S(1)} %bitcast.156), channel_id=1, source_target_pairs={{8,0},{33,1},{10,2},{35,3},{12,4},{37,5},{14,6},{39,7},{16,8},{41,... | collective-permute-start | bytes 2850824 | tf_op jit(solution)/shard_map/ppermute | solution.py:68
  78.4 1.6 slice_bitcast_fusion.1
  80.0 2.2 %fusion.6 = bf16[3712,512]{1,0:T(8,128)(2,1)S(1)} fusion(bf16[3584,128]{1,0:T(8,128)(2,1)S(1)} %get-tuple-element.31, bf16[3584,128]{1,0:T(8,128)(2,1)S(1)} %get-tuple-element.30, bf16[3584,128]{1,0:T(8,128)(2,1)S(1)} %get-tuple-element.27, bf16[3584,128]{1,0:T(8,128)(2,1)S(1)} %get-tuple-element.26), kind=kLoop, calls=%fused_computation.9 | loop fusion | flops 24707072 | bytes 7471104 | tf_op jit(solution)/shard_map/concatenate | solution.py:156
  83.6 2.8 %collective-permute-done.28 = bf16[128,3712]{1,0:T(8,128)(2,1)S(1)} collective-permute-done((bf16[128,3712]{1,0:T(8,128)(2,1)S(1)}, bf16[128,3712]{1,0:T(8,128)(2,1)S(1)}, u32[]{:S(2)}, u32[]{:S(2)}) %collective-permute-start.28) | collective-permute-done | bytes 950304 | tf_op jit(solution)/shard_map/ppermute | solution.py:68
  86.5 3.5 %collective-permute-start.29 = (bf16[64,3712]{1,0:T(8,128)(2,1)S(1)}, bf16[64,3712]{1,0:T(8,128)(2,1)S(1)}, u32[]{:S(2)}, u32[]{:S(2)}) collective-permute-start(bf16[64,3712]{1,0:T(8,128)(2,1)S(1)} %slice.367), channel_id=1, source_target_pairs={{8,0},{33,1},{10,2},{35,3},{12,4},{37,5},{14,6},{39,7},{16,8},{41,... | collective-permute-start | bytes 1425416 | tf_op jit(solution)/shard_map/ppermute | solution.py:68
  91.5 8.6 %collective-permute-done.16 = bf16[128,3712]{1,0:T(8,128)(2,1)S(1)} collective-permute-done((bf16[128,3712]{1,0:T(8,128)(2,1)S(1)}, bf16[128,3712]{1,0:T(8,128)(2,1)S(1)}, u32[]{:S(2)}, u32[]{:S(2)}) %collective-permute-start.16) | collective-permute-done | bytes 950304 | tf_op jit(solution)/shard_map/ppermute | solution.py:68
  101.7 1.5 collective-permute-start.17
  103.2 1.9 %collective-permute-done.31 = bf16[64,3712]{1,0:T(8,128)(2,1)S(1)} collective-permute-done((bf16[64,3712]{1,0:T(8,128)(2,1)S(1)}, bf16[64,3712]{1,0:T(8,128)(2,1)S(1)}, u32[]{:S(2)}, u32[]{:S(2)}) %collective-permute-start.31) | collective-permute-done | bytes 475168 | tf_op jit(solution)/shard_map/ppermute | solution.py:68
  105.9 4.7 %collective-permute-start.32 = (bf16[512,256]{1,0:T(8,128)(2,1)S(1)}, bf16[512,256]{1,0:T(8,128)(2,1)S(1)}, u32[]{:S(2)}, u32[]{:S(2)}) collective-permute-start(bf16[512,256]{1,0:T(8,128)(2,1)S(1)} %pad_maximum_fusion.10), channel_id=1, source_target_pairs={{0,1},{1,0},{2,3},{3,2},{4,5},{5,4},{6,7},{7,6},{8,9},{9,8},{10,11... | collective-permute-start | bytes 786440 | tf_op jit(solution)/shard_map/ppermute | solution.py:72
  111.6 5.5 %collective-permute-start.18 = (bf16[512,256]{1,0:T(8,128)(2,1)S(1)}, bf16[512,256]{1,0:T(8,128)(2,1)S(1)}, u32[]{:S(2)}, u32[]{:S(2)}) collective-permute-start(bf16[512,256]{1,0:T(8,128)(2,1)S(1)} %pad_maximum_fusion.9), channel_id=1, source_target_pairs={{0,1},{1,0},{2,3},{3,2},{4,5},{5,4},{6,7},{7,6},{8,9},{9,8},{10,11... | collective-permute-start | bytes 786440 | tf_op jit(solution)/shard_map/ppermute | solution.py:72
  120.1 2.3 %multiply_convert_fusion = bf16[512,3584]{1,0:T(8,128)(2,1)S(1)} fusion(f32[512]{0:T(512)S(1)} %bitcast.195, bf16[128,3584]{1,0:T(8,128)(2,1)} %collective-permute-done.20, bf16[128,3584]{1,0:T(8,128)(2,1)S(1)} %get-tuple-element.32, bf16[512,128]{1,0:T(8,128)(2,1)S(1)} %bitcast.181, bf16[512,128]{1,0:T(8,128)(2,1)S(1)} %fusion.22), kind=kOutput, calls=%fused_computation.5 | convolution fusion | flops 947388416 | bytes 5769216 | tf_op jit(solution)/shard_map/dot_general | solution.py:230
  122.7 2.7 %collective-permute-start.36 = (bf16[64,3584]{1,0:T(8,128)(2,1)S(1)}, bf16[64,3584]{1,0:T(8,128)(2,1)S(1)}, u32[]{:S(2)}, u32[]{:S(2)}) collective-permute-start(bf16[64,3584]{1,0:T(8,128)(2,1)S(1)} %get-tuple-element.23), channel_id=1, source_target_pairs={{8,0},{33,1},{10,2},{35,3},{12,4},{37,5},{14,6},{39,7},{16,8},{41,... | collective-permute-start | bytes 1376264 | tf_op jit(solution)/shard_map/ppermute | solution.py:68
  125.4 2.3 %multiply_convert_fusion.1 = bf16[512,3584]{1,0:T(8,128)(2,1)S(1)} fusion(f32[512]{0:T(512)S(1)} %bitcast.194, bf16[128,3584]{1,0:T(8,128)(2,1)} %collective-permute-done.20, bf16[128,3584]{1,0:T(8,128)(2,1)S(1)} %get-tuple-element.32, bf16[512,128]{1,0:T(8,128)(2,1)S(1)} %bitcast.182, bf16[512,128]{1,0:T(8,128)(2,1)S(1)} %fusion.23), kind=kOutput, calls=%fused_computation.6 | convolution fusion | flops 947388416 | bytes 5769216 | tf_op jit(solution)/shard_map/dot_general | solution.py:230
  127.9 2.7 %collective-permute-start.23 = (bf16[64,3584]{1,0:T(8,128)(2,1)S(1)}, bf16[64,3584]{1,0:T(8,128)(2,1)S(1)}, u32[]{:S(2)}, u32[]{:S(2)}) collective-permute-start(bf16[64,3584]{1,0:T(8,128)(2,1)S(1)} %get-tuple-element.17), channel_id=1, source_target_pairs={{8,0},{33,1},{10,2},{35,3},{12,4},{37,5},{14,6},{39,7},{16,8},{41,... | collective-permute-start | bytes 1376264 | tf_op jit(solution)/shard_map/ppermute | solution.py:68
  131.9 2.7 %collective-permute-start.37 = (bf16[128,3584]{1,0:T(8,128)(2,1)S(1)}, bf16[128,3584]{1,0:T(8,128)(2,1)S(1)}, u32[]{:S(2)}, u32[]{:S(2)}) collective-permute-start(bf16[128,3584]{1,0:T(8,128)(2,1)S(1)} %pad_maximum_fusion.7), channel_id=1, source_target_pairs={{8,0},{33,1},{10,2},{35,3},{12,4},{37,5},{14,6},{39,7},{16,8},{41,... | collective-permute-start | bytes 2752520 | tf_op jit(solution)/shard_map/ppermute | solution.py:68
  134.7 2.0 %collective-permute-done.21 = bf16[64,3584]{1,0:T(8,128)(2,1)S(1)} collective-permute-done((bf16[64,3584]{1,0:T(8,128)(2,1)S(1)}, bf16[64,3584]{1,0:T(8,128)(2,1)S(1)}, u32[]{:S(2)}, u32[]{:S(2)}) %collective-permute-start.21) | collective-permute-done | bytes 458784 | tf_op jit(solution)/shard_map/ppermute | solution.py:68
  137.1 2.7 %collective-permute-start.24 = (bf16[128,3584]{1,0:T(8,128)(2,1)S(1)}, bf16[128,3584]{1,0:T(8,128)(2,1)S(1)}, u32[]{:S(2)}, u32[]{:S(2)}) collective-permute-start(bf16[128,3584]{1,0:T(8,128)(2,1)S(1)} %pad_maximum_fusion.5), channel_id=1, source_target_pairs={{8,0},{33,1},{10,2},{35,3},{12,4},{37,5},{14,6},{39,7},{16,8},{41,... | collective-permute-start | bytes 2752520 | tf_op jit(solution)/shard_map/ppermute | solution.py:68
  139.9 6.6 %collective-permute-done.35 = bf16[128,3584]{1,0:T(8,128)(2,1)S(1)} collective-permute-done((bf16[128,3584]{1,0:T(8,128)(2,1)S(1)}, bf16[128,3584]{1,0:T(8,128)(2,1)S(1)}, u32[]{:S(2)}, u32[]{:S(2)}) %collective-permute-start.35) | collective-permute-done | bytes 917536 | tf_op jit(solution)/shard_map/ppermute | solution.py:68
  147.0 1.8 collective-permute-start.39
  148.8 1.0 collective-permute-start.40
  149.8 10.9 %collective-permute-done.22 = bf16[128,3584]{1,0:T(8,128)(2,1)S(1)} collective-permute-done((bf16[128,3584]{1,0:T(8,128)(2,1)S(1)}, bf16[128,3584]{1,0:T(8,128)(2,1)S(1)}, u32[]{:S(2)}, u32[]{:S(2)}) %collective-permute-start.22) | collective-permute-done | bytes 917536 | tf_op jit(solution)/shard_map/ppermute | solution.py:68
  161.2 1.8 collective-permute-start.26
  162.9 1.0 collective-permute-start.27
  164.1 5.6 %collective-permute-done.25 = bf16[32,3584]{1,0:T(8,128)(2,1)S(1)} collective-permute-done((bf16[32,3584]{1,0:T(8,128)(2,1)S(1)}, bf16[32,3584]{1,0:T(8,128)(2,1)S(1)}, u32[]{:S(2)}, u32[]{:S(2)}) %collective-permute-start.25) | collective-permute-done | bytes 229408 | tf_op jit(solution)/shard_map/ppermute | solution.py:68
  170.9 2.5 %collective-permute-start.43 = (bf16[2,8,3584]{2,1,0:T(8,128)(2,1)S(1)}, bf16[2,8,3584]{2,1,0:T(8,128)(2,1)S(1)}, u32[]{:S(2)}, u32[]{:S(2)}) collective-permute-start(bf16[2,8,3584]{2,1,0:T(8,128)(2,1)S(1)} %get-tuple-element.44), channel_id=1, source_target_pairs={{2,0},{9,1},{4,2},{11,3},{6,4},{13,5},{0,6},{15,7},{10,8},{17,9},{... | collective-permute-start | bytes 344072 | tf_op jit(solution)/shard_map/ppermute | solution.py:68
  173.5 3.1 %collective-permute-done.41 = bf16[2,8,3584]{2,1,0:T(8,128)(2,1)S(1)} collective-permute-done((bf16[2,8,3584]{2,1,0:T(8,128)(2,1)S(1)}, bf16[2,8,3584]{2,1,0:T(8,128)(2,1)S(1)}, u32[]{:S(2)}, u32[]{:S(2)}) %collective-permute-start.41) | collective-permute-done | bytes 114720 | tf_op jit(solution)/shard_map/ppermute | solution.py:68
  177.7 1.0 collective-permute-done.44
  (185 shorter events, 25.6 us)
Async XLA Ops:
  0.6 23.5 %copy-start = (bf16[8,512,128]{2,1,0:T(8,128)(2,1)S(1)}, bf16[8,512,128]{2,1,0:T(8,128)(2,1)}, u32[]{:S(2)}) copy-start(bf16[8,512,128]{2,1,0:T(8,128)(2,1)} %param.18) | copy-start | bytes 3145732
  8.8 15.3 %all-to-all-start = ((bf16[8,64,512]{2,0,1:T(8,128)(2,1)}), bf16[8,64,512]{2,0,1:T(8,128)(2,1)S(1)}, u32[]{:S(2)}, u32[]{:S(2)}) async-start(bf16[8,64,512]{2,0,1:T(8,128)(2,1)} %copy.55), calls=%async_computation | async-start | bytes 1048576 | tf_op jit(solution)/shard_map/all_to_all | solution.py:150
  15.9 22.2 %collective-permute-start.5 = (bf16[8,3712]{1,0:T(8,128)(2,1)}, bf16[8,3712]{1,0:T(8,128)(2,1)}, u32[]{:S(2)}, u32[]{:S(2)}) collective-permute-start(bf16[8,3712]{1,0:T(8,128)(2,1)} %get-tuple-element.58), channel_id=1, source_target_pairs={{0,1},{1,0},{2,3},{3,2},{4,5},{5,4},{6,7},{7,6},{8,9},{9,8},{10,11... | collective-permute-start | bytes 178184 | tf_op jit(solution)/shard_map/ppermute | solution.py:72
  32.6 2.5 %collective-permute-start = (bf16[64,3584]{1,0:T(8,128)(2,1)S(1)}, bf16[64,3584]{1,0:T(8,128)(2,1)S(1)}, u32[]{:S(2)}, u32[]{:S(2)}) collective-permute-start(bf16[64,3584]{1,0:T(8,128)(2,1)S(1)} %dynamic-slice_convert_fusion), channel_id=1, source_target_pairs={{0,1},{1,0},{2,3},{3,2},{4,5},{5,4},{6,7},{7,6},{8,9},{9,8},{10,11... | collective-permute-start | bytes 1376264 | tf_op jit(solution)/shard_map/ppermute | solution.py:72
  34.9 43.5 %collective-permute-start.13 = (bf16[2,3584,128]{2,1,0:T(8,128)(2,1)}, bf16[2,3584,128]{2,1,0:T(8,128)(2,1)}, u32[]{:S(2)}, u32[]{:S(2)}) collective-permute-start(bf16[2,3584,128]{2,1,0:T(8,128)(2,1)} %dynamic-slice_bitcast_fusion), channel_id=1, source_target_pairs={{0,1},{1,0},{2,3},{3,2},{4,5},{5,4},{6,7},{7,6},{8,9},{9,8},{10,11... | collective-permute-start | bytes 5505032 | tf_op jit(solution)/shard_map/ppermute | solution.py:72
  35.2 6.1 %collective-permute-start.1 = (bf16[16,3584]{1,0:T(8,128)(2,1)S(1)}, bf16[16,3584]{1,0:T(8,128)(2,1)S(1)}, u32[]{:S(2)}, u32[]{:S(2)}) collective-permute-start(bf16[16,3584]{1,0:T(8,128)(2,1)S(1)} %get-tuple-element.40), channel_id=1, source_target_pairs={{6,0},{7,1},{0,2},{1,3},{2,4},{3,5},{4,6},{5,7},{14,8},{15,9},{8,1... | collective-permute-start | bytes 344072 | tf_op jit(solution)/shard_map/ppermute | solution.py:68
  35.6 7.0 %collective-permute-start.2 = (bf16[16,3584]{1,0:T(8,128)(2,1)S(1)}, bf16[16,3584]{1,0:T(8,128)(2,1)S(1)}, u32[]{:S(2)}, u32[]{:S(2)}) collective-permute-start(bf16[16,3584]{1,0:T(8,128)(2,1)S(1)} %get-tuple-element.42), channel_id=1, source_target_pairs={{4,0},{5,1},{6,2},{7,3},{0,4},{1,5},{2,6},{3,7},{12,8},{13,9},{14,... | collective-permute-start | bytes 344072 | tf_op jit(solution)/shard_map/ppermute | solution.py:68
  37.3 6.2 %collective-permute-start.3 = (bf16[16,3584]{1,0:T(8,128)(2,1)S(1)}, bf16[16,3584]{1,0:T(8,128)(2,1)S(1)}, u32[]{:S(2)}, u32[]{:S(2)}) collective-permute-start(bf16[16,3584]{1,0:T(8,128)(2,1)S(1)} %get-tuple-element.41), channel_id=1, source_target_pairs={{2,0},{3,1},{4,2},{5,3},{6,4},{7,5},{0,6},{1,7},{10,8},{11,9},{12,... | collective-permute-start | bytes 344072 | tf_op jit(solution)/shard_map/ppermute | solution.py:68
  43.7 2.5 %collective-permute-start.6 = (f32[16,1]{0,1:T(1,128)S(1)}, f32[16,1]{0,1:T(1,128)S(1)}, u32[]{:S(2)}, u32[]{:S(2)}) collective-permute-start(f32[16,1]{0,1:T(1,128)S(1)} %bitcast.196), channel_id=1, source_target_pairs={{0,1},{1,0},{2,3},{3,2},{4,5},{5,4},{6,7},{7,6},{8,9},{9,8},{10,11... | collective-permute-start | bytes 200 | tf_op jit(solution)/shard_map/ppermute | solution.py:72
  46.4 6.9 %collective-permute-start.7 = (bf16[16,3712]{1,0:T(8,128)(2,1)S(1)}, bf16[16,3712]{1,0:T(8,128)(2,1)S(1)}, u32[]{:S(2)}, u32[]{:S(2)}) collective-permute-start(bf16[16,3712]{1,0:T(8,128)(2,1)S(1)} %get-tuple-element.48), channel_id=1, source_target_pairs={{2,0},{9,1},{4,2},{11,3},{6,4},{13,5},{0,6},{15,7},{10,8},{17,9},{... | collective-permute-start | bytes 356360 | tf_op jit(solution)/shard_map/ppermute | solution.py:68
  50.2 5.3 %collective-permute-start.8 = (bf16[16,3712]{1,0:T(8,128)(2,1)S(1)}, bf16[16,3712]{1,0:T(8,128)(2,1)S(1)}, u32[]{:S(2)}, u32[]{:S(2)}) collective-permute-start(bf16[16,3712]{1,0:T(8,128)(2,1)S(1)} %get-tuple-element.48), channel_id=1, source_target_pairs={{4,0},{17,1},{6,2},{19,3},{0,4},{21,5},{2,6},{23,7},{12,8},{25,9},... | collective-permute-start | bytes 356360 | tf_op jit(solution)/shard_map/ppermute | solution.py:68
  50.2 6.2 %collective-permute-start.9 = (bf16[16,3712]{1,0:T(8,128)(2,1)S(1)}, bf16[16,3712]{1,0:T(8,128)(2,1)S(1)}, u32[]{:S(2)}, u32[]{:S(2)}) collective-permute-start(bf16[16,3712]{1,0:T(8,128)(2,1)S(1)} %get-tuple-element.48), channel_id=1, source_target_pairs={{6,0},{25,1},{0,2},{27,3},{2,4},{29,5},{4,6},{31,7},{14,8},{1,9},{... | collective-permute-start | bytes 356360 | tf_op jit(solution)/shard_map/ppermute | solution.py:68
  51.0 69.1 %collective-permute-start.20 = (bf16[128,3584]{1,0:T(8,128)(2,1)S(1)}, bf16[128,3584]{1,0:T(8,128)(2,1)}, u32[]{:S(2)}, u32[]{:S(2)}) collective-permute-start(bf16[128,3584]{1,0:T(8,128)(2,1)S(1)} %get-tuple-element.33), channel_id=1, source_target_pairs={{0,1},{1,0},{2,3},{3,2},{4,5},{5,4},{6,7},{7,6},{8,9},{9,8},{10,11... | collective-permute-start | bytes 2752520 | tf_op jit(solution)/shard_map/ppermute | solution.py:72
  56.4 12.9 %collective-permute-start.10 = (bf16[64,3712]{1,0:T(8,128)(2,1)S(1)}, bf16[64,3712]{1,0:T(8,128)(2,1)S(1)}, u32[]{:S(2)}, u32[]{:S(2)}) collective-permute-start(bf16[64,3712]{1,0:T(8,128)(2,1)S(1)} %bitcast.167), channel_id=1, source_target_pairs={{32,0},{3,1},{34,2},{5,3},{36,4},{7,5},{38,6},{1,7},{40,8},{11,9},... | collective-permute-start | bytes 1425416 | tf_op jit(solution)/shard_map/ppermute | solution.py:68
  58.6 10.7 %collective-permute-start.11 = (bf16[64,3712]{1,0:T(8,128)(2,1)S(1)}, bf16[64,3712]{1,0:T(8,128)(2,1)S(1)}, u32[]{:S(2)}, u32[]{:S(2)}) collective-permute-start(bf16[64,3712]{1,0:T(8,128)(2,1)S(1)} %bitcast.168), channel_id=1, source_target_pairs={{64,0},{5,1},{66,2},{7,3},{68,4},{1,5},{70,6},{3,7},{72,8},{13,9},... | collective-permute-start | bytes 1425416 | tf_op jit(solution)/shard_map/ppermute | solution.py:68
  58.7 14.1 %collective-permute-start.12 = (bf16[64,3712]{1,0:T(8,128)(2,1)S(1)}, bf16[64,3712]{1,0:T(8,128)(2,1)S(1)}, u32[]{:S(2)}, u32[]{:S(2)}) collective-permute-start(bf16[64,3712]{1,0:T(8,128)(2,1)S(1)} %bitcast.169), channel_id=1, source_target_pairs={{96,0},{7,1},{98,2},{1,3},{100,4},{3,5},{102,6},{5,7},{104,8},{15,... | collective-permute-start | bytes 1425416 | tf_op jit(solution)/shard_map/ppermute | solution.py:68
  73.2 13.2 %collective-permute-start.28 = (bf16[128,3712]{1,0:T(8,128)(2,1)S(1)}, bf16[128,3712]{1,0:T(8,128)(2,1)S(1)}, u32[]{:S(2)}, u32[]{:S(2)}) collective-permute-start(bf16[128,3712]{1,0:T(8,128)(2,1)S(1)} %bitcast.152), channel_id=1, source_target_pairs={{8,0},{33,1},{10,2},{35,3},{12,4},{37,5},{14,6},{39,7},{16,8},{41,... | collective-permute-start | bytes 2850824 | tf_op jit(solution)/shard_map/ppermute | solution.py:68
  75.7 14.2 %collective-permute-start.30 = (bf16[128,3712]{1,0:T(8,128)(2,1)S(1)}, bf16[128,3712]{1,0:T(8,128)(2,1)S(1)}, u32[]{:S(2)}, u32[]{:S(2)}) collective-permute-start(bf16[128,3712]{1,0:T(8,128)(2,1)S(1)} %bitcast.153), channel_id=1, source_target_pairs={{24,0},{97,1},{26,2},{99,3},{28,4},{101,5},{30,6},{103,7},{0,8},{1... | collective-permute-start | bytes 2850824 | tf_op jit(solution)/shard_map/ppermute | solution.py:68
  75.7 25.0 %collective-permute-start.14 = (bf16[128,3712]{1,0:T(8,128)(2,1)S(1)}, bf16[128,3712]{1,0:T(8,128)(2,1)S(1)}, u32[]{:S(2)}, u32[]{:S(2)}) collective-permute-start(bf16[128,3712]{1,0:T(8,128)(2,1)S(1)} %bitcast.156), channel_id=1, source_target_pairs={{8,0},{33,1},{10,2},{35,3},{12,4},{37,5},{14,6},{39,7},{16,8},{41,... | collective-permute-start | bytes 2850824 | tf_op jit(solution)/shard_map/ppermute | solution.py:68
  78.4 21.6 %collective-permute-start.16 = (bf16[128,3712]{1,0:T(8,128)(2,1)S(1)}, bf16[128,3712]{1,0:T(8,128)(2,1)S(1)}, u32[]{:S(2)}, u32[]{:S(2)}) collective-permute-start(bf16[128,3712]{1,0:T(8,128)(2,1)S(1)} %bitcast.157), channel_id=1, source_target_pairs={{24,0},{97,1},{26,2},{99,3},{28,4},{101,5},{30,6},{103,7},{0,8},{1... | collective-permute-start | bytes 2850824 | tf_op jit(solution)/shard_map/ppermute | solution.py:68
  86.5 16.7 %collective-permute-start.29 = (bf16[64,3712]{1,0:T(8,128)(2,1)S(1)}, bf16[64,3712]{1,0:T(8,128)(2,1)S(1)}, u32[]{:S(2)}, u32[]{:S(2)}) collective-permute-start(bf16[64,3712]{1,0:T(8,128)(2,1)S(1)} %slice.367), channel_id=1, source_target_pairs={{8,0},{33,1},{10,2},{35,3},{12,4},{37,5},{14,6},{39,7},{16,8},{41,... | collective-permute-start | bytes 1425416 | tf_op jit(solution)/shard_map/ppermute | solution.py:68
  90.0 15.1 %collective-permute-start.31 = (bf16[64,3712]{1,0:T(8,128)(2,1)S(1)}, bf16[64,3712]{1,0:T(8,128)(2,1)S(1)}, u32[]{:S(2)}, u32[]{:S(2)}) collective-permute-start(bf16[64,3712]{1,0:T(8,128)(2,1)S(1)} %slice.368), channel_id=1, source_target_pairs={{24,0},{97,1},{26,2},{99,3},{28,4},{101,5},{30,6},{103,7},{0,8},{1... | collective-permute-start | bytes 1425416 | tf_op jit(solution)/shard_map/ppermute | solution.py:68
  101.6 9.0 %collective-permute-start.15 = (bf16[64,3712]{1,0:T(8,128)(2,1)S(1)}, bf16[64,3712]{1,0:T(8,128)(2,1)S(1)}, u32[]{:S(2)}, u32[]{:S(2)}) collective-permute-start(bf16[64,3712]{1,0:T(8,128)(2,1)S(1)} %slice.339), channel_id=1, source_target_pairs={{8,0},{33,1},{10,2},{35,3},{12,4},{37,5},{14,6},{39,7},{16,8},{41,... | collective-permute-start | bytes 1425416 | tf_op jit(solution)/shard_map/ppermute | solution.py:68
  101.7 9.1 %collective-permute-start.17 = (bf16[64,3712]{1,0:T(8,128)(2,1)S(1)}, bf16[64,3712]{1,0:T(8,128)(2,1)S(1)}, u32[]{:S(2)}, u32[]{:S(2)}) collective-permute-start(bf16[64,3712]{1,0:T(8,128)(2,1)S(1)} %slice.340), channel_id=1, source_target_pairs={{24,0},{97,1},{26,2},{99,3},{28,4},{101,5},{30,6},{103,7},{0,8},{1... | collective-permute-start | bytes 1425416 | tf_op jit(solution)/shard_map/ppermute | solution.py:68
  105.9 11.4 %collective-permute-start.32 = (bf16[512,256]{1,0:T(8,128)(2,1)S(1)}, bf16[512,256]{1,0:T(8,128)(2,1)S(1)}, u32[]{:S(2)}, u32[]{:S(2)}) collective-permute-start(bf16[512,256]{1,0:T(8,128)(2,1)S(1)} %pad_maximum_fusion.10), channel_id=1, source_target_pairs={{0,1},{1,0},{2,3},{3,2},{4,5},{5,4},{6,7},{7,6},{8,9},{9,8},{10,11... | collective-permute-start | bytes 786440 | tf_op jit(solution)/shard_map/ppermute | solution.py:72
  111.6 6.7 %collective-permute-start.18 = (bf16[512,256]{1,0:T(8,128)(2,1)S(1)}, bf16[512,256]{1,0:T(8,128)(2,1)S(1)}, u32[]{:S(2)}, u32[]{:S(2)}) collective-permute-start(bf16[512,256]{1,0:T(8,128)(2,1)S(1)} %pad_maximum_fusion.9), channel_id=1, source_target_pairs={{0,1},{1,0},{2,3},{3,2},{4,5},{5,4},{6,7},{7,6},{8,9},{9,8},{10,11... | collective-permute-start | bytes 786440 | tf_op jit(solution)/shard_map/ppermute | solution.py:72
  118.6 1.4 collective-permute-start.33
  119.4 6.0 %collective-permute-start.19 = (bf16[512,128]{1,0:T(8,128)(2,1)S(1)}, bf16[512,128]{1,0:T(8,128)(2,1)S(1)}, u32[]{:S(2)}, u32[]{:S(2)}) collective-permute-start(bf16[512,128]{1,0:T(8,128)(2,1)S(1)} %fusion.23), channel_id=1, source_target_pairs={{0,1},{1,0},{2,3},{3,2},{4,5},{5,4},{6,7},{7,6},{8,9},{9,8},{10,11... | collective-permute-start | bytes 393224 | tf_op jit(solution)/shard_map/ppermute | solution.py:72
  122.6 8.9 %collective-permute-start.34 = (bf16[64,3584]{1,0:T(8,128)(2,1)S(1)}, bf16[64,3584]{1,0:T(8,128)(2,1)S(1)}, u32[]{:S(2)}, u32[]{:S(2)}) collective-permute-start(bf16[64,3584]{1,0:T(8,128)(2,1)S(1)} %get-tuple-element.22), channel_id=1, source_target_pairs={{24,0},{97,1},{26,2},{99,3},{28,4},{101,5},{30,6},{103,7},{0,8},{1... | collective-permute-start | bytes 1376264 | tf_op jit(solution)/shard_map/ppermute | solution.py:68
  122.7 8.8 %collective-permute-start.36 = (bf16[64,3584]{1,0:T(8,128)(2,1)S(1)}, bf16[64,3584]{1,0:T(8,128)(2,1)S(1)}, u32[]{:S(2)}, u32[]{:S(2)}) collective-permute-start(bf16[64,3584]{1,0:T(8,128)(2,1)S(1)} %get-tuple-element.23), channel_id=1, source_target_pairs={{8,0},{33,1},{10,2},{35,3},{12,4},{37,5},{14,6},{39,7},{16,8},{41,... | collective-permute-start | bytes 1376264 | tf_op jit(solution)/shard_map/ppermute | solution.py:68
  127.8 8.9 %collective-permute-start.21 = (bf16[64,3584]{1,0:T(8,128)(2,1)S(1)}, bf16[64,3584]{1,0:T(8,128)(2,1)S(1)}, u32[]{:S(2)}, u32[]{:S(2)}) collective-permute-start(bf16[64,3584]{1,0:T(8,128)(2,1)S(1)} %get-tuple-element.16), channel_id=1, source_target_pairs={{24,0},{97,1},{26,2},{99,3},{28,4},{101,5},{30,6},{103,7},{0,8},{1... | collective-permute-start | bytes 1376264 | tf_op jit(solution)/shard_map/ppermute | solution.py:68
  127.9 8.8 %collective-permute-start.23 = (bf16[64,3584]{1,0:T(8,128)(2,1)S(1)}, bf16[64,3584]{1,0:T(8,128)(2,1)S(1)}, u32[]{:S(2)}, u32[]{:S(2)}) collective-permute-start(bf16[64,3584]{1,0:T(8,128)(2,1)S(1)} %get-tuple-element.17), channel_id=1, source_target_pairs={{8,0},{33,1},{10,2},{35,3},{12,4},{37,5},{14,6},{39,7},{16,8},{41,... | collective-permute-start | bytes 1376264 | tf_op jit(solution)/shard_map/ppermute | solution.py:68
  131.8 14.8 %collective-permute-start.35 = (bf16[128,3584]{1,0:T(8,128)(2,1)S(1)}, bf16[128,3584]{1,0:T(8,128)(2,1)S(1)}, u32[]{:S(2)}, u32[]{:S(2)}) collective-permute-start(bf16[128,3584]{1,0:T(8,128)(2,1)S(1)} %pad_maximum_fusion.6), channel_id=1, source_target_pairs={{24,0},{97,1},{26,2},{99,3},{28,4},{101,5},{30,6},{103,7},{0,8},{1... | collective-permute-start | bytes 2752520 | tf_op jit(solution)/shard_map/ppermute | solution.py:68
  131.9 14.6 %collective-permute-start.37 = (bf16[128,3584]{1,0:T(8,128)(2,1)S(1)}, bf16[128,3584]{1,0:T(8,128)(2,1)S(1)}, u32[]{:S(2)}, u32[]{:S(2)}) collective-permute-start(bf16[128,3584]{1,0:T(8,128)(2,1)S(1)} %pad_maximum_fusion.7), channel_id=1, source_target_pairs={{8,0},{33,1},{10,2},{35,3},{12,4},{37,5},{14,6},{39,7},{16,8},{41,... | collective-permute-start | bytes 2752520 | tf_op jit(solution)/shard_map/ppermute | solution.py:68
  137.0 23.7 %collective-permute-start.22 = (bf16[128,3584]{1,0:T(8,128)(2,1)S(1)}, bf16[128,3584]{1,0:T(8,128)(2,1)S(1)}, u32[]{:S(2)}, u32[]{:S(2)}) collective-permute-start(bf16[128,3584]{1,0:T(8,128)(2,1)S(1)} %pad_maximum_fusion.4), channel_id=1, source_target_pairs={{24,0},{97,1},{26,2},{99,3},{28,4},{101,5},{30,6},{103,7},{0,8},{1... | collective-permute-start | bytes 2752520 | tf_op jit(solution)/shard_map/ppermute | solution.py:68
  137.1 23.5 %collective-permute-start.24 = (bf16[128,3584]{1,0:T(8,128)(2,1)S(1)}, bf16[128,3584]{1,0:T(8,128)(2,1)S(1)}, u32[]{:S(2)}, u32[]{:S(2)}) collective-permute-start(bf16[128,3584]{1,0:T(8,128)(2,1)S(1)} %pad_maximum_fusion.5), channel_id=1, source_target_pairs={{8,0},{33,1},{10,2},{35,3},{12,4},{37,5},{14,6},{39,7},{16,8},{41,... | collective-permute-start | bytes 2752520 | tf_op jit(solution)/shard_map/ppermute | solution.py:68
  146.9 16.0 %collective-permute-start.38 = (bf16[32,3584]{1,0:T(8,128)(2,1)S(1)}, bf16[32,3584]{1,0:T(8,128)(2,1)S(1)}, u32[]{:S(2)}, u32[]{:S(2)}) collective-permute-start(bf16[32,3584]{1,0:T(8,128)(2,1)S(1)} %get-tuple-element.37), channel_id=1, source_target_pairs={{96,0},{7,1},{98,2},{1,3},{100,4},{3,5},{102,6},{5,7},{104,8},{15,... | collective-permute-start | bytes 688136 | tf_op jit(solution)/shard_map/ppermute | solution.py:68
  147.0 17.0 %collective-permute-start.39 = (bf16[32,3584]{1,0:T(8,128)(2,1)S(1)}, bf16[32,3584]{1,0:T(8,128)(2,1)S(1)}, u32[]{:S(2)}, u32[]{:S(2)}) collective-permute-start(bf16[32,3584]{1,0:T(8,128)(2,1)S(1)} %get-tuple-element.39), channel_id=1, source_target_pairs={{64,0},{5,1},{66,2},{7,3},{68,4},{1,5},{70,6},{3,7},{72,8},{13,9},... | collective-permute-start | bytes 688136 | tf_op jit(solution)/shard_map/ppermute | solution.py:68
  148.8 15.2 %collective-permute-start.40 = (bf16[32,3584]{1,0:T(8,128)(2,1)S(1)}, bf16[32,3584]{1,0:T(8,128)(2,1)S(1)}, u32[]{:S(2)}, u32[]{:S(2)}) collective-permute-start(bf16[32,3584]{1,0:T(8,128)(2,1)S(1)} %get-tuple-element.38), channel_id=1, source_target_pairs={{32,0},{3,1},{34,2},{5,3},{36,4},{7,5},{38,6},{1,7},{40,8},{11,9},... | collective-permute-start | bytes 688136 | tf_op jit(solution)/shard_map/ppermute | solution.py:68
  160.7 18.7 %copy-start.1 = (bf16[8,512,128]{2,1,0:T(8,128)(2,1)S(1)}, bf16[8,512,128]{2,1,0:T(8,128)(2,1)}, u32[]{:S(2)}) copy-start(bf16[8,512,128]{2,1,0:T(8,128)(2,1)} %param.18) | copy-start | bytes 3145732
  161.1 8.6 %collective-permute-start.25 = (bf16[32,3584]{1,0:T(8,128)(2,1)S(1)}, bf16[32,3584]{1,0:T(8,128)(2,1)S(1)}, u32[]{:S(2)}, u32[]{:S(2)}) collective-permute-start(bf16[32,3584]{1,0:T(8,128)(2,1)S(1)} %get-tuple-element.34), channel_id=1, source_target_pairs={{96,0},{7,1},{98,2},{1,3},{100,4},{3,5},{102,6},{5,7},{104,8},{15,... | collective-permute-start | bytes 688136 | tf_op jit(solution)/shard_map/ppermute | solution.py:68
  161.2 8.5 %collective-permute-start.26 = (bf16[32,3584]{1,0:T(8,128)(2,1)S(1)}, bf16[32,3584]{1,0:T(8,128)(2,1)S(1)}, u32[]{:S(2)}, u32[]{:S(2)}) collective-permute-start(bf16[32,3584]{1,0:T(8,128)(2,1)S(1)} %get-tuple-element.36), channel_id=1, source_target_pairs={{64,0},{5,1},{66,2},{7,3},{68,4},{1,5},{70,6},{3,7},{72,8},{13,9},... | collective-permute-start | bytes 688136 | tf_op jit(solution)/shard_map/ppermute | solution.py:68
  162.9 7.4 %collective-permute-start.27 = (bf16[32,3584]{1,0:T(8,128)(2,1)S(1)}, bf16[32,3584]{1,0:T(8,128)(2,1)S(1)}, u32[]{:S(2)}, u32[]{:S(2)}) collective-permute-start(bf16[32,3584]{1,0:T(8,128)(2,1)S(1)} %get-tuple-element.35), channel_id=1, source_target_pairs={{32,0},{3,1},{34,2},{5,3},{36,4},{7,5},{38,6},{1,7},{40,8},{11,9},... | collective-permute-start | bytes 688136 | tf_op jit(solution)/shard_map/ppermute | solution.py:68
  170.5 6.2 %collective-permute-start.41 = (bf16[2,8,3584]{2,1,0:T(8,128)(2,1)S(1)}, bf16[2,8,3584]{2,1,0:T(8,128)(2,1)S(1)}, u32[]{:S(2)}, u32[]{:S(2)}) collective-permute-start(bf16[2,8,3584]{2,1,0:T(8,128)(2,1)S(1)} %get-tuple-element.43), channel_id=1, source_target_pairs={{6,0},{25,1},{0,2},{27,3},{2,4},{29,5},{4,6},{31,7},{14,8},{1,9},{... | collective-permute-start | bytes 344072 | tf_op jit(solution)/shard_map/ppermute | solution.py:68
  170.9 5.7 %collective-permute-start.42 = (bf16[2,8,3584]{2,1,0:T(8,128)(2,1)S(1)}, bf16[2,8,3584]{2,1,0:T(8,128)(2,1)S(1)}, u32[]{:S(2)}, u32[]{:S(2)}) collective-permute-start(bf16[2,8,3584]{2,1,0:T(8,128)(2,1)S(1)} %get-tuple-element.45), channel_id=1, source_target_pairs={{4,0},{17,1},{6,2},{19,3},{0,4},{21,5},{2,6},{23,7},{12,8},{25,9},... | collective-permute-start | bytes 344072 | tf_op jit(solution)/shard_map/ppermute | solution.py:68
  170.9 6.3 %collective-permute-start.43 = (bf16[2,8,3584]{2,1,0:T(8,128)(2,1)S(1)}, bf16[2,8,3584]{2,1,0:T(8,128)(2,1)S(1)}, u32[]{:S(2)}, u32[]{:S(2)}) collective-permute-start(bf16[2,8,3584]{2,1,0:T(8,128)(2,1)S(1)} %get-tuple-element.44), channel_id=1, source_target_pairs={{2,0},{9,1},{4,2},{11,3},{6,4},{13,5},{0,6},{15,7},{10,8},{17,9},{... | collective-permute-start | bytes 344072 | tf_op jit(solution)/shard_map/ppermute | solution.py:68
  173.4 4.3 %collective-permute-start.4 = (bf16[8,3584]{1,0:T(8,128)(2,1)S(1)}, bf16[8,3584]{1,0:T(8,128)(2,1)S(1)}, u32[]{:S(2)}, u32[]{:S(2)}) collective-permute-start(bf16[8,3584]{1,0:T(8,128)(2,1)S(1)} %get-tuple-element.49), channel_id=1, source_target_pairs={{0,1},{1,0},{2,3},{3,2},{4,5},{5,4},{6,7},{7,6},{8,9},{9,8},{10,11... | collective-permute-start | bytes 172040 | tf_op jit(solution)/shard_map/ppermute | solution.py:72
  177.3 1.3 collective-permute-start.44
  (20 other events, 153.0 us)

commit v7 on v6

--- a/solution.py
+++ b/solution.py
@@ -149,6 +149,9 @@
     latent_out = attend(query_latent, latent_cache, new_latent, context_lengths, latent_width)
     exchanged = lax.all_to_all(latent_out, ("x", "core"), split_axis=1, concat_axis=0, tiled=True)
 
+    exchanged, expert_gate_up, expert_down = lax.optimization_barrier(
+        (exchanged, expert_gate_up, expert_down)
+    )
     gate_up = expert_gate_up[0]
     down = expert_down[0]
     gate_up_own = mine(gate_up, 1)

time: 180 us -> 178 us (0.989)
  waiting for transfers between devices: 76.9 us -> 81.2 us
  local copies, waits for them, and re-layouts: 7 us -> 4.34 us
  matrix products: 24.1 us -> 21.7 us
    ppermute x34, waiting for transfers between devices: 65.5 us -> 69.2 us  [shift(): return lax.ppermute(value, ('y', 'z', 'x', 'core'), ring(axes, distance))]
    dot_general x2, matrix products: 4.61 us -> 2.27 us  [per_device(): out = jnp.dot(activated, weight_out, preferred_element_type=f32)]
  transfers between devices with their start and end apart: 46 -> 46, of which waited for: 25 -> 27; matrix products, arithmetic and copies ran while one was open for 18% -> 15% of each run, Pallas kernels for 0% -> 0%
where the time goes in v7:
time: 178 us
  waiting for transfers between devices  81.2 us (46%)
  starting transfers between devices  59.7 us (34%)
  matrix products  21.7 us (12%)
  other arithmetic  9.54 us (5%)
  local copies, waits for them, and re-layouts  4.34 us (2%)
    ppermute x34, waiting for transfers between devices, shift(): return lax.ppermute(value, ('y', 'z', 'x', 'core'), ring(axes, distance))  69.2 us
    ppermute x34, starting transfers between devices, shift(): return lax.ppermute(value, ('y', 'z', 'x', 'core'), ring(axes, distance))  40.2 us
    ppermute x11, starting transfers between devices, swap(): return lax.ppermute(value, 'core', [(0, 1), (1, 0)])  13.7 us
    all_to_all x1, waiting for transfers between devices, per_device(): lax.all_to_all(latent_out, ('x', 'core'), split_axis=1, concat_axis=0, ti...  8.12 us
    dot_general x1, matrix products, per_device(): projected = jnp.dot(values, out_proj, preferred_element_type=f32)  7.91 us
    all_to_all x1, starting transfers between devices, per_device(): lax.all_to_all(latent_out, ('x', 'core'), split_axis=1, concat_axis=0, ti...  5.8 us
    dot_general x8, matrix products, per_device(): jnp.dot(b, weight_in, preferred_element_type=f32)  5.37 us
    ppermute x11, waiting for transfers between devices, swap(): return lax.ppermute(value, 'core', [(0, 1), (1, 0)])  3.87 us
  transfers between devices with their start and end apart: 46, of which 27 were waited for; matrix products, arithmetic and copies ran while one was open for 15% of the time, Pallas kernels for 0%

profile of v7, /device:TPU:1, one launch (start us, length us, event | category | flops | bytes accessed | tf_op | source)
XLA Modules:
  0.0 178.1 jit_solution(1104365167539345401)
XLA Ops:
  1.5 1.7 fusion.59
  3.2 3.0 %fusion.73 = (f32[8,64]{1,0:T(8,128)S(1)}, f32[8,64,384]{2,1,0:T(8,128)S(1)}) fusion(bf16[8,64,576]{2,1,0:T(8,128)(2,1)} %param.14, bf16[8,384,576]{1,2,0:T(8,128)(2,1)} %param.15, s32[8]{0:T(128)} %param.17), kind=kOutput, calls=%fused_computation.173 | convolution fusion | flops 227278336 | bytes 4917280 | tf_op jit(solution)/shard_map/rhc,rtc->rht/dot_general | solution.py:15
  6.6 1.1 fusion.12
  7.7 1.1 copy.55
  8.8 5.8 %all-to-all-start = ((bf16[8,64,512]{2,0,1:T(8,128)(2,1)}), bf16[8,64,512]{2,0,1:T(8,128)(2,1)S(1)}, u32[]{:S(2)}, u32[]{:S(2)}) async-start(bf16[8,64,512]{2,0,1:T(8,128)(2,1)} %copy.55), calls=%async_computation | async-start | bytes 1048576 | tf_op jit(solution)/shard_map/all_to_all | solution.py:150
  16.0 8.1 %all-to-all-done = bf16[8,64,512]{2,0,1:T(8,128)(2,1)S(1)} async-done(((bf16[8,64,512]{2,0,1:T(8,128)(2,1)}), bf16[8,64,512]{2,0,1:T(8,128)(2,1)S(1)}, u32[]{:S(2)}, u32[]{:S(2)}) %all-to-all-start) | async-done | bytes 524320 | tf_op jit(solution)/shard_map/all_to_all | solution.py:150
  24.5 7.9 %fusion.41 = f32[64,7168]{1,0:T(8,128)S(1)} fusion(bf16[1024,7168]{1,0:T(8,128)(2,1)} %param.19, bf16[8,8,8,128]{3,2,1,0:T(8,128)(2,1)S(1)} %fusion.16), kind=kOutput, calls=%fused_computation.94 | convolution fusion | flops 939524096 | bytes 16646144 | tf_op jit(solution)/shard_map/dot_general | solution.py:175
  32.5 1.0 collective-permute-start
  35.4 1.8 %collective-permute-start.2 = (bf16[16,3584]{1,0:T(8,128)(2,1)S(1)}, bf16[16,3584]{1,0:T(8,128)(2,1)S(1)}, u32[]{:S(2)}, u32[]{:S(2)}) collective-permute-start(bf16[16,3584]{1,0:T(8,128)(2,1)S(1)} %get-tuple-element.48), channel_id=1, source_target_pairs={{4,0},{5,1},{6,2},{7,3},{0,4},{1,5},{2,6},{3,7},{12,8},{13,9},{14,... | collective-permute-start | bytes 344072 | tf_op jit(solution)/shard_map/ppermute | solution.py:68
  37.9 1.6 dynamic-slice_bitcast_fusion
  39.5 1.8 collective-permute-done.1
  41.3 1.3 collective-permute-done.2
  42.5 1.0 collective-permute-done.3
  43.7 1.5 collective-permute-start.6
  46.2 3.8 %collective-permute-start.7 = (bf16[16,3712]{1,0:T(8,128)(2,1)S(1)}, bf16[16,3712]{1,0:T(8,128)(2,1)S(1)}, u32[]{:S(2)}, u32[]{:S(2)}) collective-permute-start(bf16[16,3712]{1,0:T(8,128)(2,1)S(1)} %get-tuple-element.54), channel_id=1, source_target_pairs={{2,0},{9,1},{4,2},{11,3},{6,4},{13,5},{0,6},{15,7},{10,8},{17,9},{... | collective-permute-start | bytes 356360 | tf_op jit(solution)/shard_map/ppermute | solution.py:68
  50.9 2.1 %collective-permute-done.7 = bf16[16,3712]{1,0:T(8,128)(2,1)S(1)} collective-permute-done((bf16[16,3712]{1,0:T(8,128)(2,1)S(1)}, bf16[16,3712]{1,0:T(8,128)(2,1)S(1)}, u32[]{:S(2)}, u32[]{:S(2)}) %collective-permute-start.7) | collective-permute-done | bytes 118816 | tf_op jit(solution)/shard_map/ppermute | solution.py:68
  53.1 2.2 %collective-permute-done.8 = bf16[16,3712]{1,0:T(8,128)(2,1)S(1)} collective-permute-done((bf16[16,3712]{1,0:T(8,128)(2,1)S(1)}, bf16[16,3712]{1,0:T(8,128)(2,1)S(1)}, u32[]{:S(2)}, u32[]{:S(2)}) %collective-permute-start.8) | collective-permute-done | bytes 118816 | tf_op jit(solution)/shard_map/ppermute | solution.py:68
  56.3 2.2 %collective-permute-start.10 = (bf16[64,3712]{1,0:T(8,128)(2,1)S(1)}, bf16[64,3712]{1,0:T(8,128)(2,1)S(1)}, u32[]{:S(2)}, u32[]{:S(2)}) collective-permute-start(bf16[64,3712]{1,0:T(8,128)(2,1)S(1)} %bitcast.169), channel_id=1, source_target_pairs={{32,0},{3,1},{34,2},{5,3},{36,4},{7,5},{38,6},{1,7},{40,8},{11,9},... | collective-permute-start | bytes 1425416 | tf_op jit(solution)/shard_map/ppermute | solution.py:68
  59.3 9.9 %collective-permute-done.10 = bf16[64,3712]{1,0:T(8,128)(2,1)S(1)} collective-permute-done((bf16[64,3712]{1,0:T(8,128)(2,1)S(1)}, bf16[64,3712]{1,0:T(8,128)(2,1)S(1)}, u32[]{:S(2)}, u32[]{:S(2)}) %collective-permute-start.10) | collective-permute-done | bytes 475168 | tf_op jit(solution)/shard_map/ppermute | solution.py:68
  69.2 3.4 %collective-permute-done.12 = bf16[64,3712]{1,0:T(8,128)(2,1)S(1)} collective-permute-done((bf16[64,3712]{1,0:T(8,128)(2,1)S(1)}, bf16[64,3712]{1,0:T(8,128)(2,1)S(1)}, u32[]{:S(2)}, u32[]{:S(2)}) %collective-permute-start.12) | collective-permute-done | bytes 475168 | tf_op jit(solution)/shard_map/ppermute | solution.py:68
  73.1 2.5 %collective-permute-start.28 = (bf16[128,3712]{1,0:T(8,128)(2,1)S(1)}, bf16[128,3712]{1,0:T(8,128)(2,1)S(1)}, u32[]{:S(2)}, u32[]{:S(2)}) collective-permute-start(bf16[128,3712]{1,0:T(8,128)(2,1)S(1)} %bitcast.153), channel_id=1, source_target_pairs={{8,0},{33,1},{10,2},{35,3},{12,4},{37,5},{14,6},{39,7},{16,8},{41,... | collective-permute-start | bytes 2850824 | tf_op jit(solution)/shard_map/ppermute | solution.py:68
  75.6 2.7 %collective-permute-start.14 = (bf16[128,3712]{1,0:T(8,128)(2,1)S(1)}, bf16[128,3712]{1,0:T(8,128)(2,1)S(1)}, u32[]{:S(2)}, u32[]{:S(2)}) collective-permute-start(bf16[128,3712]{1,0:T(8,128)(2,1)S(1)} %bitcast.157), channel_id=1, source_target_pairs={{8,0},{33,1},{10,2},{35,3},{12,4},{37,5},{14,6},{39,7},{16,8},{41,... | collective-permute-start | bytes 2850824 | tf_op jit(solution)/shard_map/ppermute | solution.py:68
  78.4 2.2 %fusion.6 = bf16[3712,512]{1,0:T(8,128)(2,1)S(1)} fusion(bf16[3584,128]{1,0:T(8,128)(2,1)S(1)} %get-tuple-element.37, bf16[3584,128]{1,0:T(8,128)(2,1)S(1)} %get-tuple-element.36, bf16[3584,128]{1,0:T(8,128)(2,1)S(1)} %get-tuple-element.33, bf16[3584,128]{1,0:T(8,128)(2,1)S(1)} %get-tuple-element.32), kind=kLoop, calls=%fused_computation.9 | loop fusion | flops 24707072 | bytes 7471104 | tf_op jit(solution)/shard_map/concatenate | solution.py:159
  82.0 4.3 %collective-permute-done.28 = bf16[128,3712]{1,0:T(8,128)(2,1)S(1)} collective-permute-done((bf16[128,3712]{1,0:T(8,128)(2,1)S(1)}, bf16[128,3712]{1,0:T(8,128)(2,1)S(1)}, u32[]{:S(2)}, u32[]{:S(2)}) %collective-permute-start.28) | collective-permute-done | bytes 950304 | tf_op jit(solution)/shard_map/ppermute | solution.py:68
  86.3 3.5 %collective-permute-start.29 = (bf16[64,3712]{1,0:T(8,128)(2,1)S(1)}, bf16[64,3712]{1,0:T(8,128)(2,1)S(1)}, u32[]{:S(2)}, u32[]{:S(2)}) collective-permute-start(bf16[64,3712]{1,0:T(8,128)(2,1)S(1)} %slice.367), channel_id=1, source_target_pairs={{8,0},{33,1},{10,2},{35,3},{12,4},{37,5},{14,6},{39,7},{16,8},{41,... | collective-permute-start | bytes 1425416 | tf_op jit(solution)/shard_map/ppermute | solution.py:68
  91.3 5.1 %collective-permute-done.14 = bf16[128,3712]{1,0:T(8,128)(2,1)S(1)} collective-permute-done((bf16[128,3712]{1,0:T(8,128)(2,1)S(1)}, bf16[128,3712]{1,0:T(8,128)(2,1)S(1)}, u32[]{:S(2)}, u32[]{:S(2)}) %collective-permute-start.14) | collective-permute-done | bytes 950304 | tf_op jit(solution)/shard_map/ppermute | solution.py:68
  97.1 2.7 %collective-permute-done.16 = bf16[128,3712]{1,0:T(8,128)(2,1)S(1)} collective-permute-done((bf16[128,3712]{1,0:T(8,128)(2,1)S(1)}, bf16[128,3712]{1,0:T(8,128)(2,1)S(1)}, u32[]{:S(2)}, u32[]{:S(2)}) %collective-permute-start.16) | collective-permute-done | bytes 950304 | tf_op jit(solution)/shard_map/ppermute | solution.py:68
  102.4 2.6 %collective-permute-done.31 = bf16[64,3712]{1,0:T(8,128)(2,1)S(1)} collective-permute-done((bf16[64,3712]{1,0:T(8,128)(2,1)S(1)}, bf16[64,3712]{1,0:T(8,128)(2,1)S(1)}, u32[]{:S(2)}, u32[]{:S(2)}) %collective-permute-start.31) | collective-permute-done | bytes 475168 | tf_op jit(solution)/shard_map/ppermute | solution.py:68
  105.7 4.7 %collective-permute-start.32 = (bf16[512,256]{1,0:T(8,128)(2,1)S(1)}, bf16[512,256]{1,0:T(8,128)(2,1)S(1)}, u32[]{:S(2)}, u32[]{:S(2)}) collective-permute-start(bf16[512,256]{1,0:T(8,128)(2,1)S(1)} %pad_maximum_fusion.10), channel_id=1, source_target_pairs={{0,1},{1,0},{2,3},{3,2},{4,5},{5,4},{6,7},{7,6},{8,9},{9,8},{10,11... | collective-permute-start | bytes 786440 | tf_op jit(solution)/shard_map/ppermute | solution.py:72
  111.4 5.5 %collective-permute-start.18 = (bf16[512,256]{1,0:T(8,128)(2,1)S(1)}, bf16[512,256]{1,0:T(8,128)(2,1)S(1)}, u32[]{:S(2)}, u32[]{:S(2)}) collective-permute-start(bf16[512,256]{1,0:T(8,128)(2,1)S(1)} %pad_maximum_fusion.9), channel_id=1, source_target_pairs={{0,1},{1,0},{2,3},{3,2},{4,5},{5,4},{6,7},{7,6},{8,9},{9,8},{10,11... | collective-permute-start | bytes 786440 | tf_op jit(solution)/shard_map/ppermute | solution.py:72
  119.9 1.1 multiply_convert_fusion
  121.3 2.7 %collective-permute-start.36 = (bf16[64,3584]{1,0:T(8,128)(2,1)S(1)}, bf16[64,3584]{1,0:T(8,128)(2,1)S(1)}, u32[]{:S(2)}, u32[]{:S(2)}) collective-permute-start(bf16[64,3584]{1,0:T(8,128)(2,1)S(1)} %get-tuple-element.29), channel_id=1, source_target_pairs={{8,0},{33,1},{10,2},{35,3},{12,4},{37,5},{14,6},{39,7},{16,8},{41,... | collective-permute-start | bytes 1376264 | tf_op jit(solution)/shard_map/ppermute | solution.py:68
  124.0 1.1 multiply_convert_fusion.1
  125.3 2.7 %collective-permute-start.23 = (bf16[64,3584]{1,0:T(8,128)(2,1)S(1)}, bf16[64,3584]{1,0:T(8,128)(2,1)S(1)}, u32[]{:S(2)}, u32[]{:S(2)}) collective-permute-start(bf16[64,3584]{1,0:T(8,128)(2,1)S(1)} %get-tuple-element.23), channel_id=1, source_target_pairs={{8,0},{33,1},{10,2},{35,3},{12,4},{37,5},{14,6},{39,7},{16,8},{41,... | collective-permute-start | bytes 1376264 | tf_op jit(solution)/shard_map/ppermute | solution.py:68
  128.0 2.1 %collective-permute-done.34 = bf16[64,3584]{1,0:T(8,128)(2,1)S(1)} collective-permute-done((bf16[64,3584]{1,0:T(8,128)(2,1)S(1)}, bf16[64,3584]{1,0:T(8,128)(2,1)S(1)}, u32[]{:S(2)}, u32[]{:S(2)}) %collective-permute-start.34) | collective-permute-done | bytes 458784 | tf_op jit(solution)/shard_map/ppermute | solution.py:68
  130.6 2.7 %collective-permute-start.37 = (bf16[128,3584]{1,0:T(8,128)(2,1)S(1)}, bf16[128,3584]{1,0:T(8,128)(2,1)S(1)}, u32[]{:S(2)}, u32[]{:S(2)}) collective-permute-start(bf16[128,3584]{1,0:T(8,128)(2,1)S(1)} %pad_maximum_fusion.7), channel_id=1, source_target_pairs={{8,0},{33,1},{10,2},{35,3},{12,4},{37,5},{14,6},{39,7},{16,8},{41,... | collective-permute-start | bytes 2752520 | tf_op jit(solution)/shard_map/ppermute | solution.py:68
  133.3 1.7 collective-permute-done.21
  135.5 2.7 %collective-permute-start.24 = (bf16[128,3584]{1,0:T(8,128)(2,1)S(1)}, bf16[128,3584]{1,0:T(8,128)(2,1)S(1)}, u32[]{:S(2)}, u32[]{:S(2)}) collective-permute-start(bf16[128,3584]{1,0:T(8,128)(2,1)S(1)} %pad_maximum_fusion.5), channel_id=1, source_target_pairs={{8,0},{33,1},{10,2},{35,3},{12,4},{37,5},{14,6},{39,7},{16,8},{41,... | collective-permute-start | bytes 2752520 | tf_op jit(solution)/shard_map/ppermute | solution.py:68
  138.2 6.6 %collective-permute-done.35 = bf16[128,3584]{1,0:T(8,128)(2,1)S(1)} collective-permute-done((bf16[128,3584]{1,0:T(8,128)(2,1)S(1)}, bf16[128,3584]{1,0:T(8,128)(2,1)S(1)}, u32[]{:S(2)}, u32[]{:S(2)}) %collective-permute-start.35) | collective-permute-done | bytes 917536 | tf_op jit(solution)/shard_map/ppermute | solution.py:68
  145.3 1.8 %collective-permute-start.39 = (bf16[32,3584]{1,0:T(8,128)(2,1)S(1)}, bf16[32,3584]{1,0:T(8,128)(2,1)S(1)}, u32[]{:S(2)}, u32[]{:S(2)}) collective-permute-start(bf16[32,3584]{1,0:T(8,128)(2,1)S(1)} %get-tuple-element.45), channel_id=1, source_target_pairs={{64,0},{5,1},{66,2},{7,3},{68,4},{1,5},{70,6},{3,7},{72,8},{13,9},... | collective-permute-start | bytes 688136 | tf_op jit(solution)/shard_map/ppermute | solution.py:68
  147.1 1.0 collective-permute-start.40
  148.2 11.2 %collective-permute-done.22 = bf16[128,3584]{1,0:T(8,128)(2,1)S(1)} collective-permute-done((bf16[128,3584]{1,0:T(8,128)(2,1)S(1)}, bf16[128,3584]{1,0:T(8,128)(2,1)S(1)}, u32[]{:S(2)}, u32[]{:S(2)}) %collective-permute-start.22) | collective-permute-done | bytes 917536 | tf_op jit(solution)/shard_map/ppermute | solution.py:68
  159.8 1.8 %collective-permute-start.26 = (bf16[32,3584]{1,0:T(8,128)(2,1)S(1)}, bf16[32,3584]{1,0:T(8,128)(2,1)S(1)}, u32[]{:S(2)}, u32[]{:S(2)}) collective-permute-start(bf16[32,3584]{1,0:T(8,128)(2,1)S(1)} %get-tuple-element.42), channel_id=1, source_target_pairs={{64,0},{5,1},{66,2},{7,3},{68,4},{1,5},{70,6},{3,7},{72,8},{13,9},... | collective-permute-start | bytes 688136 | tf_op jit(solution)/shard_map/ppermute | solution.py:68
  161.6 1.0 collective-permute-start.27
  162.8 5.6 %collective-permute-done.25 = bf16[32,3584]{1,0:T(8,128)(2,1)S(1)} collective-permute-done((bf16[32,3584]{1,0:T(8,128)(2,1)S(1)}, bf16[32,3584]{1,0:T(8,128)(2,1)S(1)}, u32[]{:S(2)}, u32[]{:S(2)}) %collective-permute-start.25) | collective-permute-done | bytes 229408 | tf_op jit(solution)/shard_map/ppermute | solution.py:68
  169.3 2.6 %collective-permute-start.43 = (bf16[2,8,3584]{2,1,0:T(8,128)(2,1)S(1)}, bf16[2,8,3584]{2,1,0:T(8,128)(2,1)S(1)}, u32[]{:S(2)}, u32[]{:S(2)}) collective-permute-start(bf16[2,8,3584]{2,1,0:T(8,128)(2,1)S(1)} %get-tuple-element.50), channel_id=1, source_target_pairs={{2,0},{9,1},{4,2},{11,3},{6,4},{13,5},{0,6},{15,7},{10,8},{17,9},{... | collective-permute-start | bytes 344072 | tf_op jit(solution)/shard_map/ppermute | solution.py:68
  172.0 3.3 %collective-permute-done.41 = bf16[2,8,3584]{2,1,0:T(8,128)(2,1)S(1)} collective-permute-done((bf16[2,8,3584]{2,1,0:T(8,128)(2,1)S(1)}, bf16[2,8,3584]{2,1,0:T(8,128)(2,1)S(1)}, u32[]{:S(2)}, u32[]{:S(2)}) %collective-permute-start.41) | collective-permute-done | bytes 114720 | tf_op jit(solution)/shard_map/ppermute | solution.py:68
  176.1 1.2 collective-permute-done.44
  (186 shorter events, 25.4 us)
Async XLA Ops:
  0.6 23.5 %copy-start = (bf16[8,512,128]{2,1,0:T(8,128)(2,1)S(1)}, bf16[8,512,128]{2,1,0:T(8,128)(2,1)}, u32[]{:S(2)}) copy-start(bf16[8,512,128]{2,1,0:T(8,128)(2,1)} %param.18) | copy-start | bytes 3145732
  8.8 15.3 %all-to-all-start = ((bf16[8,64,512]{2,0,1:T(8,128)(2,1)}), bf16[8,64,512]{2,0,1:T(8,128)(2,1)S(1)}, u32[]{:S(2)}, u32[]{:S(2)}) async-start(bf16[8,64,512]{2,0,1:T(8,128)(2,1)} %copy.55), calls=%async_computation | async-start | bytes 1048576 | tf_op jit(solution)/shard_map/all_to_all | solution.py:150
  15.9 17.5 %collective-permute-start.5 = (bf16[8,3712]{1,0:T(8,128)(2,1)}, bf16[8,3712]{1,0:T(8,128)(2,1)}, u32[]{:S(2)}, u32[]{:S(2)}) collective-permute-start(bf16[8,3712]{1,0:T(8,128)(2,1)} %get-tuple-element.64), channel_id=1, source_target_pairs={{0,1},{1,0},{2,3},{3,2},{4,5},{5,4},{6,7},{7,6},{8,9},{9,8},{10,11... | collective-permute-start | bytes 178184 | tf_op jit(solution)/shard_map/ppermute | solution.py:72
  32.5 2.4 %collective-permute-start = (bf16[64,3584]{1,0:T(8,128)(2,1)S(1)}, bf16[64,3584]{1,0:T(8,128)(2,1)S(1)}, u32[]{:S(2)}, u32[]{:S(2)}) collective-permute-start(bf16[64,3584]{1,0:T(8,128)(2,1)S(1)} %dynamic-slice_convert_fusion), channel_id=1, source_target_pairs={{0,1},{1,0},{2,3},{3,2},{4,5},{5,4},{6,7},{7,6},{8,9},{9,8},{10,11... | collective-permute-start | bytes 1376264 | tf_op jit(solution)/shard_map/ppermute | solution.py:72
  35.0 6.2 %collective-permute-start.1 = (bf16[16,3584]{1,0:T(8,128)(2,1)S(1)}, bf16[16,3584]{1,0:T(8,128)(2,1)S(1)}, u32[]{:S(2)}, u32[]{:S(2)}) collective-permute-start(bf16[16,3584]{1,0:T(8,128)(2,1)S(1)} %get-tuple-element.46), channel_id=1, source_target_pairs={{6,0},{7,1},{0,2},{1,3},{2,4},{3,5},{4,6},{5,7},{14,8},{15,9},{8,1... | collective-permute-start | bytes 344072 | tf_op jit(solution)/shard_map/ppermute | solution.py:68
  35.4 7.1 %collective-permute-start.2 = (bf16[16,3584]{1,0:T(8,128)(2,1)S(1)}, bf16[16,3584]{1,0:T(8,128)(2,1)S(1)}, u32[]{:S(2)}, u32[]{:S(2)}) collective-permute-start(bf16[16,3584]{1,0:T(8,128)(2,1)S(1)} %get-tuple-element.48), channel_id=1, source_target_pairs={{4,0},{5,1},{6,2},{7,3},{0,4},{1,5},{2,6},{3,7},{12,8},{13,9},{14,... | collective-permute-start | bytes 344072 | tf_op jit(solution)/shard_map/ppermute | solution.py:68
  37.2 6.3 %collective-permute-start.3 = (bf16[16,3584]{1,0:T(8,128)(2,1)S(1)}, bf16[16,3584]{1,0:T(8,128)(2,1)S(1)}, u32[]{:S(2)}, u32[]{:S(2)}) collective-permute-start(bf16[16,3584]{1,0:T(8,128)(2,1)S(1)} %get-tuple-element.47), channel_id=1, source_target_pairs={{2,0},{3,1},{4,2},{5,3},{6,4},{7,5},{0,6},{1,7},{10,8},{11,9},{12,... | collective-permute-start | bytes 344072 | tf_op jit(solution)/shard_map/ppermute | solution.py:68
  39.5 19.7 %copy-start.2 = (bf16[1,2,7168,128]{3,2,1,0:T(8,128)(2,1)S(1)}, bf16[1,2,7168,128]{3,2,1,0:T(8,128)(2,1)}, u32[]{:S(2)}) copy-start(bf16[1,2,7168,128]{3,2,1,0:T(8,128)(2,1)} %param.24) | copy-start | bytes 11010052
  43.7 2.4 %collective-permute-start.6 = (f32[16,1]{0,1:T(1,128)S(1)}, f32[16,1]{0,1:T(1,128)S(1)}, u32[]{:S(2)}, u32[]{:S(2)}) collective-permute-start(f32[16,1]{0,1:T(1,128)S(1)} %bitcast.198), channel_id=1, source_target_pairs={{0,1},{1,0},{2,3},{3,2},{4,5},{5,4},{6,7},{7,6},{8,9},{9,8},{10,11... | collective-permute-start | bytes 200 | tf_op jit(solution)/shard_map/ppermute | solution.py:72
  45.2 33.0 %collective-permute-start.13 = (bf16[2,3584,128]{2,1,0:T(8,128)(2,1)S(1)}, bf16[2,3584,128]{2,1,0:T(8,128)(2,1)S(1)}, u32[]{:S(2)}, u32[]{:S(2)}) collective-permute-start(bf16[2,3584,128]{2,1,0:T(8,128)(2,1)S(1)} %dynamic-slice_bitcast_fusion), channel_id=1, source_target_pairs={{0,1},{1,0},{2,3},{3,2},{4,5},{5,4},{6,7},{7,6},{8,9},{9,8},{10,11... | collective-permute-start | bytes 5505032 | tf_op jit(solution)/shard_map/ppermute | solution.py:72
  46.2 6.9 %collective-permute-start.7 = (bf16[16,3712]{1,0:T(8,128)(2,1)S(1)}, bf16[16,3712]{1,0:T(8,128)(2,1)S(1)}, u32[]{:S(2)}, u32[]{:S(2)}) collective-permute-start(bf16[16,3712]{1,0:T(8,128)(2,1)S(1)} %get-tuple-element.54), channel_id=1, source_target_pairs={{2,0},{9,1},{4,2},{11,3},{6,4},{13,5},{0,6},{15,7},{10,8},{17,9},{... | collective-permute-start | bytes 356360 | tf_op jit(solution)/shard_map/ppermute | solution.py:68
  50.0 5.3 %collective-permute-start.8 = (bf16[16,3712]{1,0:T(8,128)(2,1)S(1)}, bf16[16,3712]{1,0:T(8,128)(2,1)S(1)}, u32[]{:S(2)}, u32[]{:S(2)}) collective-permute-start(bf16[16,3712]{1,0:T(8,128)(2,1)S(1)} %get-tuple-element.54), channel_id=1, source_target_pairs={{4,0},{17,1},{6,2},{19,3},{0,4},{21,5},{2,6},{23,7},{12,8},{25,9},... | collective-permute-start | bytes 356360 | tf_op jit(solution)/shard_map/ppermute | solution.py:68
  50.0 6.2 %collective-permute-start.9 = (bf16[16,3712]{1,0:T(8,128)(2,1)S(1)}, bf16[16,3712]{1,0:T(8,128)(2,1)S(1)}, u32[]{:S(2)}, u32[]{:S(2)}) collective-permute-start(bf16[16,3712]{1,0:T(8,128)(2,1)S(1)} %get-tuple-element.54), channel_id=1, source_target_pairs={{6,0},{25,1},{0,2},{27,3},{2,4},{29,5},{4,6},{31,7},{14,8},{1,9},{... | collective-permute-start | bytes 356360 | tf_op jit(solution)/shard_map/ppermute | solution.py:68
  50.8 69.1 %collective-permute-start.20 = (bf16[128,3584]{1,0:T(8,128)(2,1)S(1)}, bf16[128,3584]{1,0:T(8,128)(2,1)S(1)}, u32[]{:S(2)}, u32[]{:S(2)}) collective-permute-start(bf16[128,3584]{1,0:T(8,128)(2,1)S(1)} %get-tuple-element.39), channel_id=1, source_target_pairs={{0,1},{1,0},{2,3},{3,2},{4,5},{5,4},{6,7},{7,6},{8,9},{9,8},{10,11... | collective-permute-start | bytes 2752520 | tf_op jit(solution)/shard_map/ppermute | solution.py:72
  56.3 12.9 %collective-permute-start.10 = (bf16[64,3712]{1,0:T(8,128)(2,1)S(1)}, bf16[64,3712]{1,0:T(8,128)(2,1)S(1)}, u32[]{:S(2)}, u32[]{:S(2)}) collective-permute-start(bf16[64,3712]{1,0:T(8,128)(2,1)S(1)} %bitcast.169), channel_id=1, source_target_pairs={{32,0},{3,1},{34,2},{5,3},{36,4},{7,5},{38,6},{1,7},{40,8},{11,9},... | collective-permute-start | bytes 1425416 | tf_op jit(solution)/shard_map/ppermute | solution.py:68
  58.5 10.7 %collective-permute-start.11 = (bf16[64,3712]{1,0:T(8,128)(2,1)S(1)}, bf16[64,3712]{1,0:T(8,128)(2,1)S(1)}, u32[]{:S(2)}, u32[]{:S(2)}) collective-permute-start(bf16[64,3712]{1,0:T(8,128)(2,1)S(1)} %bitcast.170), channel_id=1, source_target_pairs={{64,0},{5,1},{66,2},{7,3},{68,4},{1,5},{70,6},{3,7},{72,8},{13,9},... | collective-permute-start | bytes 1425416 | tf_op jit(solution)/shard_map/ppermute | solution.py:68
  58.5 14.1 %collective-permute-start.12 = (bf16[64,3712]{1,0:T(8,128)(2,1)S(1)}, bf16[64,3712]{1,0:T(8,128)(2,1)S(1)}, u32[]{:S(2)}, u32[]{:S(2)}) collective-permute-start(bf16[64,3712]{1,0:T(8,128)(2,1)S(1)} %bitcast.171), channel_id=1, source_target_pairs={{96,0},{7,1},{98,2},{1,3},{100,4},{3,5},{102,6},{5,7},{104,8},{15,... | collective-permute-start | bytes 1425416 | tf_op jit(solution)/shard_map/ppermute | solution.py:68
  73.1 13.2 %collective-permute-start.28 = (bf16[128,3712]{1,0:T(8,128)(2,1)S(1)}, bf16[128,3712]{1,0:T(8,128)(2,1)S(1)}, u32[]{:S(2)}, u32[]{:S(2)}) collective-permute-start(bf16[128,3712]{1,0:T(8,128)(2,1)S(1)} %bitcast.153), channel_id=1, source_target_pairs={{8,0},{33,1},{10,2},{35,3},{12,4},{37,5},{14,6},{39,7},{16,8},{41,... | collective-permute-start | bytes 2850824 | tf_op jit(solution)/shard_map/ppermute | solution.py:68
  75.6 14.2 %collective-permute-start.30 = (bf16[128,3712]{1,0:T(8,128)(2,1)S(1)}, bf16[128,3712]{1,0:T(8,128)(2,1)S(1)}, u32[]{:S(2)}, u32[]{:S(2)}) collective-permute-start(bf16[128,3712]{1,0:T(8,128)(2,1)S(1)} %bitcast.154), channel_id=1, source_target_pairs={{24,0},{97,1},{26,2},{99,3},{28,4},{101,5},{30,6},{103,7},{0,8},{1... | collective-permute-start | bytes 2850824 | tf_op jit(solution)/shard_map/ppermute | solution.py:68
  75.6 20.9 %collective-permute-start.14 = (bf16[128,3712]{1,0:T(8,128)(2,1)S(1)}, bf16[128,3712]{1,0:T(8,128)(2,1)S(1)}, u32[]{:S(2)}, u32[]{:S(2)}) collective-permute-start(bf16[128,3712]{1,0:T(8,128)(2,1)S(1)} %bitcast.157), channel_id=1, source_target_pairs={{8,0},{33,1},{10,2},{35,3},{12,4},{37,5},{14,6},{39,7},{16,8},{41,... | collective-permute-start | bytes 2850824 | tf_op jit(solution)/shard_map/ppermute | solution.py:68
  78.3 21.6 %collective-permute-start.16 = (bf16[128,3712]{1,0:T(8,128)(2,1)S(1)}, bf16[128,3712]{1,0:T(8,128)(2,1)S(1)}, u32[]{:S(2)}, u32[]{:S(2)}) collective-permute-start(bf16[128,3712]{1,0:T(8,128)(2,1)S(1)} %bitcast.158), channel_id=1, source_target_pairs={{24,0},{97,1},{26,2},{99,3},{28,4},{101,5},{30,6},{103,7},{0,8},{1... | collective-permute-start | bytes 2850824 | tf_op jit(solution)/shard_map/ppermute | solution.py:68
  86.3 16.0 %collective-permute-start.29 = (bf16[64,3712]{1,0:T(8,128)(2,1)S(1)}, bf16[64,3712]{1,0:T(8,128)(2,1)S(1)}, u32[]{:S(2)}, u32[]{:S(2)}) collective-permute-start(bf16[64,3712]{1,0:T(8,128)(2,1)S(1)} %slice.367), channel_id=1, source_target_pairs={{8,0},{33,1},{10,2},{35,3},{12,4},{37,5},{14,6},{39,7},{16,8},{41,... | collective-permute-start | bytes 1425416 | tf_op jit(solution)/shard_map/ppermute | solution.py:68
  89.8 15.1 %collective-permute-start.31 = (bf16[64,3712]{1,0:T(8,128)(2,1)S(1)}, bf16[64,3712]{1,0:T(8,128)(2,1)S(1)}, u32[]{:S(2)}, u32[]{:S(2)}) collective-permute-start(bf16[64,3712]{1,0:T(8,128)(2,1)S(1)} %slice.368), channel_id=1, source_target_pairs={{24,0},{97,1},{26,2},{99,3},{28,4},{101,5},{30,6},{103,7},{0,8},{1... | collective-permute-start | bytes 1425416 | tf_op jit(solution)/shard_map/ppermute | solution.py:68
  100.7 9.7 %collective-permute-start.15 = (bf16[64,3712]{1,0:T(8,128)(2,1)S(1)}, bf16[64,3712]{1,0:T(8,128)(2,1)S(1)}, u32[]{:S(2)}, u32[]{:S(2)}) collective-permute-start(bf16[64,3712]{1,0:T(8,128)(2,1)S(1)} %slice.339), channel_id=1, source_target_pairs={{8,0},{33,1},{10,2},{35,3},{12,4},{37,5},{14,6},{39,7},{16,8},{41,... | collective-permute-start | bytes 1425416 | tf_op jit(solution)/shard_map/ppermute | solution.py:68
  101.5 9.1 %collective-permute-start.17 = (bf16[64,3712]{1,0:T(8,128)(2,1)S(1)}, bf16[64,3712]{1,0:T(8,128)(2,1)S(1)}, u32[]{:S(2)}, u32[]{:S(2)}) collective-permute-start(bf16[64,3712]{1,0:T(8,128)(2,1)S(1)} %slice.340), channel_id=1, source_target_pairs={{24,0},{97,1},{26,2},{99,3},{28,4},{101,5},{30,6},{103,7},{0,8},{1... | collective-permute-start | bytes 1425416 | tf_op jit(solution)/shard_map/ppermute | solution.py:68
  105.7 11.4 %collective-permute-start.32 = (bf16[512,256]{1,0:T(8,128)(2,1)S(1)}, bf16[512,256]{1,0:T(8,128)(2,1)S(1)}, u32[]{:S(2)}, u32[]{:S(2)}) collective-permute-start(bf16[512,256]{1,0:T(8,128)(2,1)S(1)} %pad_maximum_fusion.10), channel_id=1, source_target_pairs={{0,1},{1,0},{2,3},{3,2},{4,5},{5,4},{6,7},{7,6},{8,9},{9,8},{10,11... | collective-permute-start | bytes 786440 | tf_op jit(solution)/shard_map/ppermute | solution.py:72
  111.4 6.7 %collective-permute-start.18 = (bf16[512,256]{1,0:T(8,128)(2,1)S(1)}, bf16[512,256]{1,0:T(8,128)(2,1)S(1)}, u32[]{:S(2)}, u32[]{:S(2)}) collective-permute-start(bf16[512,256]{1,0:T(8,128)(2,1)S(1)} %pad_maximum_fusion.9), channel_id=1, source_target_pairs={{0,1},{1,0},{2,3},{3,2},{4,5},{5,4},{6,7},{7,6},{8,9},{9,8},{10,11... | collective-permute-start | bytes 786440 | tf_op jit(solution)/shard_map/ppermute | solution.py:72
  118.4 1.4 collective-permute-start.33
  119.2 4.8 %collective-permute-start.19 = (bf16[512,128]{1,0:T(8,128)(2,1)S(1)}, bf16[512,128]{1,0:T(8,128)(2,1)S(1)}, u32[]{:S(2)}, u32[]{:S(2)}) collective-permute-start(bf16[512,128]{1,0:T(8,128)(2,1)S(1)} %fusion.21), channel_id=1, source_target_pairs={{0,1},{1,0},{2,3},{3,2},{4,5},{5,4},{6,7},{7,6},{8,9},{9,8},{10,11... | collective-permute-start | bytes 393224 | tf_op jit(solution)/shard_map/ppermute | solution.py:72
  121.2 8.9 %collective-permute-start.34 = (bf16[64,3584]{1,0:T(8,128)(2,1)S(1)}, bf16[64,3584]{1,0:T(8,128)(2,1)S(1)}, u32[]{:S(2)}, u32[]{:S(2)}) collective-permute-start(bf16[64,3584]{1,0:T(8,128)(2,1)S(1)} %get-tuple-element.28), channel_id=1, source_target_pairs={{24,0},{97,1},{26,2},{99,3},{28,4},{101,5},{30,6},{103,7},{0,8},{1... | collective-permute-start | bytes 1376264 | tf_op jit(solution)/shard_map/ppermute | solution.py:68
  121.3 8.8 %collective-permute-start.36 = (bf16[64,3584]{1,0:T(8,128)(2,1)S(1)}, bf16[64,3584]{1,0:T(8,128)(2,1)S(1)}, u32[]{:S(2)}, u32[]{:S(2)}) collective-permute-start(bf16[64,3584]{1,0:T(8,128)(2,1)S(1)} %get-tuple-element.29), channel_id=1, source_target_pairs={{8,0},{33,1},{10,2},{35,3},{12,4},{37,5},{14,6},{39,7},{16,8},{41,... | collective-permute-start | bytes 1376264 | tf_op jit(solution)/shard_map/ppermute | solution.py:68
  125.3 9.8 %collective-permute-start.21 = (bf16[64,3584]{1,0:T(8,128)(2,1)S(1)}, bf16[64,3584]{1,0:T(8,128)(2,1)S(1)}, u32[]{:S(2)}, u32[]{:S(2)}) collective-permute-start(bf16[64,3584]{1,0:T(8,128)(2,1)S(1)} %get-tuple-element.22), channel_id=1, source_target_pairs={{24,0},{97,1},{26,2},{99,3},{28,4},{101,5},{30,6},{103,7},{0,8},{1... | collective-permute-start | bytes 1376264 | tf_op jit(solution)/shard_map/ppermute | solution.py:68
  125.3 9.7 %collective-permute-start.23 = (bf16[64,3584]{1,0:T(8,128)(2,1)S(1)}, bf16[64,3584]{1,0:T(8,128)(2,1)S(1)}, u32[]{:S(2)}, u32[]{:S(2)}) collective-permute-start(bf16[64,3584]{1,0:T(8,128)(2,1)S(1)} %get-tuple-element.23), channel_id=1, source_target_pairs={{8,0},{33,1},{10,2},{35,3},{12,4},{37,5},{14,6},{39,7},{16,8},{41,... | collective-permute-start | bytes 1376264 | tf_op jit(solution)/shard_map/ppermute | solution.py:68
  130.4 14.5 %collective-permute-start.35 = (bf16[128,3584]{1,0:T(8,128)(2,1)S(1)}, bf16[128,3584]{1,0:T(8,128)(2,1)S(1)}, u32[]{:S(2)}, u32[]{:S(2)}) collective-permute-start(bf16[128,3584]{1,0:T(8,128)(2,1)S(1)} %pad_maximum_fusion.6), channel_id=1, source_target_pairs={{24,0},{97,1},{26,2},{99,3},{28,4},{101,5},{30,6},{103,7},{0,8},{1... | collective-permute-start | bytes 2752520 | tf_op jit(solution)/shard_map/ppermute | solution.py:68
  130.6 14.3 %collective-permute-start.37 = (bf16[128,3584]{1,0:T(8,128)(2,1)S(1)}, bf16[128,3584]{1,0:T(8,128)(2,1)S(1)}, u32[]{:S(2)}, u32[]{:S(2)}) collective-permute-start(bf16[128,3584]{1,0:T(8,128)(2,1)S(1)} %pad_maximum_fusion.7), channel_id=1, source_target_pairs={{8,0},{33,1},{10,2},{35,3},{12,4},{37,5},{14,6},{39,7},{16,8},{41,... | collective-permute-start | bytes 2752520 | tf_op jit(solution)/shard_map/ppermute | solution.py:68
  135.3 24.0 %collective-permute-start.22 = (bf16[128,3584]{1,0:T(8,128)(2,1)S(1)}, bf16[128,3584]{1,0:T(8,128)(2,1)S(1)}, u32[]{:S(2)}, u32[]{:S(2)}) collective-permute-start(bf16[128,3584]{1,0:T(8,128)(2,1)S(1)} %pad_maximum_fusion.4), channel_id=1, source_target_pairs={{24,0},{97,1},{26,2},{99,3},{28,4},{101,5},{30,6},{103,7},{0,8},{1... | collective-permute-start | bytes 2752520 | tf_op jit(solution)/shard_map/ppermute | solution.py:68
  135.5 23.9 %collective-permute-start.24 = (bf16[128,3584]{1,0:T(8,128)(2,1)S(1)}, bf16[128,3584]{1,0:T(8,128)(2,1)S(1)}, u32[]{:S(2)}, u32[]{:S(2)}) collective-permute-start(bf16[128,3584]{1,0:T(8,128)(2,1)S(1)} %pad_maximum_fusion.5), channel_id=1, source_target_pairs={{8,0},{33,1},{10,2},{35,3},{12,4},{37,5},{14,6},{39,7},{16,8},{41,... | collective-permute-start | bytes 2752520 | tf_op jit(solution)/shard_map/ppermute | solution.py:68
  145.3 16.4 %collective-permute-start.38 = (bf16[32,3584]{1,0:T(8,128)(2,1)S(1)}, bf16[32,3584]{1,0:T(8,128)(2,1)S(1)}, u32[]{:S(2)}, u32[]{:S(2)}) collective-permute-start(bf16[32,3584]{1,0:T(8,128)(2,1)S(1)} %get-tuple-element.43), channel_id=1, source_target_pairs={{96,0},{7,1},{98,2},{1,3},{100,4},{3,5},{102,6},{5,7},{104,8},{15,... | collective-permute-start | bytes 688136 | tf_op jit(solution)/shard_map/ppermute | solution.py:68
  145.3 17.3 %collective-permute-start.39 = (bf16[32,3584]{1,0:T(8,128)(2,1)S(1)}, bf16[32,3584]{1,0:T(8,128)(2,1)S(1)}, u32[]{:S(2)}, u32[]{:S(2)}) collective-permute-start(bf16[32,3584]{1,0:T(8,128)(2,1)S(1)} %get-tuple-element.45), channel_id=1, source_target_pairs={{64,0},{5,1},{66,2},{7,3},{68,4},{1,5},{70,6},{3,7},{72,8},{13,9},... | collective-permute-start | bytes 688136 | tf_op jit(solution)/shard_map/ppermute | solution.py:68
  147.1 15.5 %collective-permute-start.40 = (bf16[32,3584]{1,0:T(8,128)(2,1)S(1)}, bf16[32,3584]{1,0:T(8,128)(2,1)S(1)}, u32[]{:S(2)}, u32[]{:S(2)}) collective-permute-start(bf16[32,3584]{1,0:T(8,128)(2,1)S(1)} %get-tuple-element.44), channel_id=1, source_target_pairs={{32,0},{3,1},{34,2},{5,3},{36,4},{7,5},{38,6},{1,7},{40,8},{11,9},... | collective-permute-start | bytes 688136 | tf_op jit(solution)/shard_map/ppermute | solution.py:68
  159.7 8.6 %collective-permute-start.25 = (bf16[32,3584]{1,0:T(8,128)(2,1)S(1)}, bf16[32,3584]{1,0:T(8,128)(2,1)S(1)}, u32[]{:S(2)}, u32[]{:S(2)}) collective-permute-start(bf16[32,3584]{1,0:T(8,128)(2,1)S(1)} %get-tuple-element.40), channel_id=1, source_target_pairs={{96,0},{7,1},{98,2},{1,3},{100,4},{3,5},{102,6},{5,7},{104,8},{15,... | collective-permute-start | bytes 688136 | tf_op jit(solution)/shard_map/ppermute | solution.py:68
  159.8 8.5 %collective-permute-start.26 = (bf16[32,3584]{1,0:T(8,128)(2,1)S(1)}, bf16[32,3584]{1,0:T(8,128)(2,1)S(1)}, u32[]{:S(2)}, u32[]{:S(2)}) collective-permute-start(bf16[32,3584]{1,0:T(8,128)(2,1)S(1)} %get-tuple-element.42), channel_id=1, source_target_pairs={{64,0},{5,1},{66,2},{7,3},{68,4},{1,5},{70,6},{3,7},{72,8},{13,9},... | collective-permute-start | bytes 688136 | tf_op jit(solution)/shard_map/ppermute | solution.py:68
  161.6 7.4 %collective-permute-start.27 = (bf16[32,3584]{1,0:T(8,128)(2,1)S(1)}, bf16[32,3584]{1,0:T(8,128)(2,1)S(1)}, u32[]{:S(2)}, u32[]{:S(2)}) collective-permute-start(bf16[32,3584]{1,0:T(8,128)(2,1)S(1)} %get-tuple-element.41), channel_id=1, source_target_pairs={{32,0},{3,1},{34,2},{5,3},{36,4},{7,5},{38,6},{1,7},{40,8},{11,9},... | collective-permute-start | bytes 688136 | tf_op jit(solution)/shard_map/ppermute | solution.py:68
  169.1 6.2 %collective-permute-start.41 = (bf16[2,8,3584]{2,1,0:T(8,128)(2,1)S(1)}, bf16[2,8,3584]{2,1,0:T(8,128)(2,1)S(1)}, u32[]{:S(2)}, u32[]{:S(2)}) collective-permute-start(bf16[2,8,3584]{2,1,0:T(8,128)(2,1)S(1)} %get-tuple-element.49), channel_id=1, source_target_pairs={{6,0},{25,1},{0,2},{27,3},{2,4},{29,5},{4,6},{31,7},{14,8},{1,9},{... | collective-permute-start | bytes 344072 | tf_op jit(solution)/shard_map/ppermute | solution.py:68
  169.2 6.1 %collective-permute-start.42 = (bf16[2,8,3584]{2,1,0:T(8,128)(2,1)S(1)}, bf16[2,8,3584]{2,1,0:T(8,128)(2,1)S(1)}, u32[]{:S(2)}, u32[]{:S(2)}) collective-permute-start(bf16[2,8,3584]{2,1,0:T(8,128)(2,1)S(1)} %get-tuple-element.51), channel_id=1, source_target_pairs={{4,0},{17,1},{6,2},{19,3},{0,4},{21,5},{2,6},{23,7},{12,8},{25,9},... | collective-permute-start | bytes 344072 | tf_op jit(solution)/shard_map/ppermute | solution.py:68
  169.3 6.6 %collective-permute-start.43 = (bf16[2,8,3584]{2,1,0:T(8,128)(2,1)S(1)}, bf16[2,8,3584]{2,1,0:T(8,128)(2,1)S(1)}, u32[]{:S(2)}, u32[]{:S(2)}) collective-permute-start(bf16[2,8,3584]{2,1,0:T(8,128)(2,1)S(1)} %get-tuple-element.50), channel_id=1, source_target_pairs={{2,0},{9,1},{4,2},{11,3},{6,4},{13,5},{0,6},{15,7},{10,8},{17,9},{... | collective-permute-start | bytes 344072 | tf_op jit(solution)/shard_map/ppermute | solution.py:68
  171.9 4.2 %collective-permute-start.4 = (bf16[8,3584]{1,0:T(8,128)(2,1)S(1)}, bf16[8,3584]{1,0:T(8,128)(2,1)S(1)}, u32[]{:S(2)}, u32[]{:S(2)}) collective-permute-start(bf16[8,3584]{1,0:T(8,128)(2,1)S(1)} %get-tuple-element.55), channel_id=1, source_target_pairs={{0,1},{1,0},{2,3},{3,2},{4,5},{5,4},{6,7},{7,6},{8,9},{9,8},{10,11... | collective-permute-start | bytes 172040 | tf_op jit(solution)/shard_map/ppermute | solution.py:72
  176.0 1.3 collective-permute-start.44
  (20 other events, 175.0 us)

commit v8 on v7

--- a/solution.py
+++ b/solution.py
@@ -197,6 +197,7 @@
     width = half + lanes
     group = gather_near(payload, first_axis).reshape(8 * rows, width)
     near = gather_near(group, near_axis).reshape(4, 4, 2, rows, width)
+    near, weight_out = lax.optimization_barrier((near, weight_out))
 
     chunks = [near[:, :, c].reshape(16 * rows, width) for c in range(2)]
     hidden = weight_in.shape[1] // 2

time: 178 us -> 178 us (level)
  waiting for transfers between devices: 81.2 us -> 83.1 us
  transfers between devices with their start and end apart: 46 -> 46, of which waited for: 27 -> 27; matrix products, arithmetic and copies ran while one was open for 15% -> 13% of each run, Pallas kernels for 0% -> 0%
where the time goes in v8:
time: 178 us
  waiting for transfers between devices  83.1 us (47%)
  starting transfers between devices  60.7 us (34%)
  matrix products  21.6 us (12%)
  other arithmetic  8.15 us (5%)
  local copies, waits for them, and re-layouts  2.83 us (2%)
    ppermute x34, waiting for transfers between devices, shift(): return lax.ppermute(value, ('y', 'z', 'x', 'core'), ring(axes, distance))  69.7 us
    ppermute x34, starting transfers between devices, shift(): return lax.ppermute(value, ('y', 'z', 'x', 'core'), ring(axes, distance))  40.2 us
    ppermute x11, starting transfers between devices, swap(): return lax.ppermute(value, 'core', [(0, 1), (1, 0)])  14.7 us
    all_to_all x1, waiting for transfers between devices, per_device(): lax.all_to_all(latent_out, ('x', 'core'), split_axis=1, concat_axis=0, ti...  8.63 us
    dot_general x1, matrix products, per_device(): projected = jnp.dot(values, out_proj, preferred_element_type=f32)  7.91 us
    all_to_all x1, starting transfers between devices, per_device(): lax.all_to_all(latent_out, ('x', 'core'), split_axis=1, concat_axis=0, ti...  5.8 us
    dot_general x8, matrix products, per_device(): jnp.dot(b, weight_in, preferred_element_type=f32)  5.36 us
    ppermute x11, waiting for transfers between devices, swap(): return lax.ppermute(value, 'core', [(0, 1), (1, 0)])  4.74 us
  transfers between devices with their start and end apart: 46, of which 27 were waited for; matrix products, arithmetic and copies ran while one was open for 13% of the time, Pallas kernels for 0%

profile of v8, /device:TPU:1, one launch (start us, length us, event | category | flops | bytes accessed | tf_op | source)
XLA Modules:
  0.0 178.1 jit_solution(2709465747003862870)
XLA Ops:
  1.5 1.7 fusion.59
  3.2 3.0 %fusion.73 = (f32[8,64]{1,0:T(8,128)S(1)}, f32[8,64,384]{2,1,0:T(8,128)S(1)}) fusion(bf16[8,64,576]{2,1,0:T(8,128)(2,1)} %param.14, bf16[8,384,576]{1,2,0:T(8,128)(2,1)} %param.15, s32[8]{0:T(128)} %param.17), kind=kOutput, calls=%fused_computation.173 | convolution fusion | flops 227278336 | bytes 4917280 | tf_op jit(solution)/shard_map/rhc,rtc->rht/dot_general | solution.py:15
  6.6 1.1 fusion.12
  7.7 1.1 copy.55
  8.8 5.8 %all-to-all-start = ((bf16[8,64,512]{2,0,1:T(8,128)(2,1)}), bf16[8,64,512]{2,0,1:T(8,128)(2,1)S(1)}, u32[]{:S(2)}, u32[]{:S(2)}) async-start(bf16[8,64,512]{2,0,1:T(8,128)(2,1)} %copy.55), calls=%async_computation | async-start | bytes 1048576 | tf_op jit(solution)/shard_map/all_to_all | solution.py:150
  15.5 8.6 %all-to-all-done = bf16[8,64,512]{2,0,1:T(8,128)(2,1)S(1)} async-done(((bf16[8,64,512]{2,0,1:T(8,128)(2,1)}), bf16[8,64,512]{2,0,1:T(8,128)(2,1)S(1)}, u32[]{:S(2)}, u32[]{:S(2)}) %all-to-all-start) | async-done | bytes 524320 | tf_op jit(solution)/shard_map/all_to_all | solution.py:150
  24.5 7.9 %fusion.41 = f32[64,7168]{1,0:T(8,128)S(1)} fusion(bf16[1024,7168]{1,0:T(8,128)(2,1)} %param.19, bf16[8,8,8,128]{3,2,1,0:T(8,128)(2,1)S(1)} %fusion.16), kind=kOutput, calls=%fused_computation.94 | convolution fusion | flops 939524096 | bytes 16646144 | tf_op jit(solution)/shard_map/dot_general | solution.py:175
  33.5 1.4 collective-permute-done
  35.4 1.8 %collective-permute-start.2 = (bf16[16,3584]{1,0:T(8,128)(2,1)S(1)}, bf16[16,3584]{1,0:T(8,128)(2,1)S(1)}, u32[]{:S(2)}, u32[]{:S(2)}) collective-permute-start(bf16[16,3584]{1,0:T(8,128)(2,1)S(1)} %get-tuple-element.52), channel_id=1, source_target_pairs={{4,0},{5,1},{6,2},{7,3},{0,4},{1,5},{2,6},{3,7},{12,8},{13,9},{14,... | collective-permute-start | bytes 344072 | tf_op jit(solution)/shard_map/ppermute | solution.py:68
  38.0 1.0 collective-permute-start.13
  39.0 2.3 %collective-permute-done.1 = bf16[16,3584]{1,0:T(8,128)(2,1)S(1)} collective-permute-done((bf16[16,3584]{1,0:T(8,128)(2,1)S(1)}, bf16[16,3584]{1,0:T(8,128)(2,1)S(1)}, u32[]{:S(2)}, u32[]{:S(2)}) %collective-permute-start.1) | collective-permute-done | bytes 114720 | tf_op jit(solution)/shard_map/ppermute | solution.py:68
  41.3 1.3 collective-permute-done.2
  42.5 1.0 collective-permute-done.3
  43.7 1.5 collective-permute-start.6
  46.2 3.8 %collective-permute-start.7 = (bf16[16,3712]{1,0:T(8,128)(2,1)S(1)}, bf16[16,3712]{1,0:T(8,128)(2,1)S(1)}, u32[]{:S(2)}, u32[]{:S(2)}) collective-permute-start(bf16[16,3712]{1,0:T(8,128)(2,1)S(1)} %get-tuple-element.58), channel_id=1, source_target_pairs={{2,0},{9,1},{4,2},{11,3},{6,4},{13,5},{0,6},{15,7},{10,8},{17,9},{... | collective-permute-start | bytes 356360 | tf_op jit(solution)/shard_map/ppermute | solution.py:68
  50.9 2.1 %collective-permute-done.7 = bf16[16,3712]{1,0:T(8,128)(2,1)S(1)} collective-permute-done((bf16[16,3712]{1,0:T(8,128)(2,1)S(1)}, bf16[16,3712]{1,0:T(8,128)(2,1)S(1)}, u32[]{:S(2)}, u32[]{:S(2)}) %collective-permute-start.7) | collective-permute-done | bytes 118816 | tf_op jit(solution)/shard_map/ppermute | solution.py:68
  53.1 2.2 %collective-permute-done.8 = bf16[16,3712]{1,0:T(8,128)(2,1)S(1)} collective-permute-done((bf16[16,3712]{1,0:T(8,128)(2,1)S(1)}, bf16[16,3712]{1,0:T(8,128)(2,1)S(1)}, u32[]{:S(2)}, u32[]{:S(2)}) %collective-permute-start.8) | collective-permute-done | bytes 118816 | tf_op jit(solution)/shard_map/ppermute | solution.py:68
  56.3 2.2 %collective-permute-start.10 = (bf16[64,3712]{1,0:T(8,128)(2,1)S(1)}, bf16[64,3712]{1,0:T(8,128)(2,1)S(1)}, u32[]{:S(2)}, u32[]{:S(2)}) collective-permute-start(bf16[64,3712]{1,0:T(8,128)(2,1)S(1)} %bitcast.173), channel_id=1, source_target_pairs={{32,0},{3,1},{34,2},{5,3},{36,4},{7,5},{38,6},{1,7},{40,8},{11,9},... | collective-permute-start | bytes 1425416 | tf_op jit(solution)/shard_map/ppermute | solution.py:68
  59.3 9.9 %collective-permute-done.10 = bf16[64,3712]{1,0:T(8,128)(2,1)S(1)} collective-permute-done((bf16[64,3712]{1,0:T(8,128)(2,1)S(1)}, bf16[64,3712]{1,0:T(8,128)(2,1)S(1)}, u32[]{:S(2)}, u32[]{:S(2)}) %collective-permute-start.10) | collective-permute-done | bytes 475168 | tf_op jit(solution)/shard_map/ppermute | solution.py:68
  69.2 3.4 %collective-permute-done.12 = bf16[64,3712]{1,0:T(8,128)(2,1)S(1)} collective-permute-done((bf16[64,3712]{1,0:T(8,128)(2,1)S(1)}, bf16[64,3712]{1,0:T(8,128)(2,1)S(1)}, u32[]{:S(2)}, u32[]{:S(2)}) %collective-permute-start.12) | collective-permute-done | bytes 475168 | tf_op jit(solution)/shard_map/ppermute | solution.py:68
  73.1 2.5 %collective-permute-start.28 = (bf16[128,3712]{1,0:T(8,128)(2,1)S(1)}, bf16[128,3712]{1,0:T(8,128)(2,1)S(1)}, u32[]{:S(2)}, u32[]{:S(2)}) collective-permute-start(bf16[128,3712]{1,0:T(8,128)(2,1)S(1)} %bitcast.155), channel_id=1, source_target_pairs={{8,0},{33,1},{10,2},{35,3},{12,4},{37,5},{14,6},{39,7},{16,8},{41,... | collective-permute-start | bytes 2850824 | tf_op jit(solution)/shard_map/ppermute | solution.py:68
  75.6 2.7 %collective-permute-start.15 = (bf16[128,3712]{1,0:T(8,128)(2,1)S(1)}, bf16[128,3712]{1,0:T(8,128)(2,1)S(1)}, u32[]{:S(2)}, u32[]{:S(2)}) collective-permute-start(bf16[128,3712]{1,0:T(8,128)(2,1)S(1)} %bitcast.159), channel_id=1, source_target_pairs={{8,0},{33,1},{10,2},{35,3},{12,4},{37,5},{14,6},{39,7},{16,8},{41,... | collective-permute-start | bytes 2850824 | tf_op jit(solution)/shard_map/ppermute | solution.py:68
  78.4 2.2 %fusion.6 = bf16[3712,512]{1,0:T(8,128)(2,1)S(1)} fusion(bf16[3584,128]{1,0:T(8,128)(2,1)S(1)} %get-tuple-element.41, bf16[3584,128]{1,0:T(8,128)(2,1)S(1)} %get-tuple-element.40, bf16[3584,128]{1,0:T(8,128)(2,1)S(1)} %get-tuple-element.37, bf16[3584,128]{1,0:T(8,128)(2,1)S(1)} %get-tuple-element.36), kind=kLoop, calls=%fused_computation.9 | loop fusion | flops 24707072 | bytes 7471104 | tf_op jit(solution)/shard_map/concatenate | solution.py:159
  82.0 4.3 %collective-permute-done.28 = bf16[128,3712]{1,0:T(8,128)(2,1)S(1)} collective-permute-done((bf16[128,3712]{1,0:T(8,128)(2,1)S(1)}, bf16[128,3712]{1,0:T(8,128)(2,1)S(1)}, u32[]{:S(2)}, u32[]{:S(2)}) %collective-permute-start.28) | collective-permute-done | bytes 950304 | tf_op jit(solution)/shard_map/ppermute | solution.py:68
  86.3 3.5 %collective-permute-start.29 = (bf16[64,3712]{1,0:T(8,128)(2,1)S(1)}, bf16[64,3712]{1,0:T(8,128)(2,1)S(1)}, u32[]{:S(2)}, u32[]{:S(2)}) collective-permute-start(bf16[64,3712]{1,0:T(8,128)(2,1)S(1)} %slice.365), channel_id=1, source_target_pairs={{8,0},{33,1},{10,2},{35,3},{12,4},{37,5},{14,6},{39,7},{16,8},{41,... | collective-permute-start | bytes 1425416 | tf_op jit(solution)/shard_map/ppermute | solution.py:68
  91.3 5.1 %collective-permute-done.15 = bf16[128,3712]{1,0:T(8,128)(2,1)S(1)} collective-permute-done((bf16[128,3712]{1,0:T(8,128)(2,1)S(1)}, bf16[128,3712]{1,0:T(8,128)(2,1)S(1)}, u32[]{:S(2)}, u32[]{:S(2)}) %collective-permute-start.15) | collective-permute-done | bytes 950304 | tf_op jit(solution)/shard_map/ppermute | solution.py:68
  97.1 2.7 %collective-permute-done.17 = bf16[128,3712]{1,0:T(8,128)(2,1)S(1)} collective-permute-done((bf16[128,3712]{1,0:T(8,128)(2,1)S(1)}, bf16[128,3712]{1,0:T(8,128)(2,1)S(1)}, u32[]{:S(2)}, u32[]{:S(2)}) %collective-permute-start.17) | collective-permute-done | bytes 950304 | tf_op jit(solution)/shard_map/ppermute | solution.py:68
  102.4 2.6 %collective-permute-done.31 = bf16[64,3712]{1,0:T(8,128)(2,1)S(1)} collective-permute-done((bf16[64,3712]{1,0:T(8,128)(2,1)S(1)}, bf16[64,3712]{1,0:T(8,128)(2,1)S(1)}, u32[]{:S(2)}, u32[]{:S(2)}) %collective-permute-start.31) | collective-permute-done | bytes 475168 | tf_op jit(solution)/shard_map/ppermute | solution.py:68
  105.7 4.7 %collective-permute-start.32 = (bf16[512,256]{1,0:T(8,128)(2,1)S(1)}, bf16[512,256]{1,0:T(8,128)(2,1)S(1)}, u32[]{:S(2)}, u32[]{:S(2)}) collective-permute-start(bf16[512,256]{1,0:T(8,128)(2,1)S(1)} %pad_maximum_fusion.8), channel_id=1, source_target_pairs={{0,1},{1,0},{2,3},{3,2},{4,5},{5,4},{6,7},{7,6},{8,9},{9,8},{10,11... | collective-permute-start | bytes 786440 | tf_op jit(solution)/shard_map/ppermute | solution.py:72
  111.4 5.5 %collective-permute-start.19 = (bf16[512,256]{1,0:T(8,128)(2,1)S(1)}, bf16[512,256]{1,0:T(8,128)(2,1)S(1)}, u32[]{:S(2)}, u32[]{:S(2)}) collective-permute-start(bf16[512,256]{1,0:T(8,128)(2,1)S(1)} %pad_maximum_fusion.7), channel_id=1, source_target_pairs={{0,1},{1,0},{2,3},{3,2},{4,5},{5,4},{6,7},{7,6},{8,9},{9,8},{10,11... | collective-permute-start | bytes 786440 | tf_op jit(solution)/shard_map/ppermute | solution.py:72
  119.9 1.1 multiply_convert_fusion
  121.3 2.7 %collective-permute-start.36 = (bf16[64,3584]{1,0:T(8,128)(2,1)S(1)}, bf16[64,3584]{1,0:T(8,128)(2,1)S(1)}, u32[]{:S(2)}, u32[]{:S(2)}) collective-permute-start(bf16[64,3584]{1,0:T(8,128)(2,1)S(1)} %get-tuple-element.33), channel_id=1, source_target_pairs={{8,0},{33,1},{10,2},{35,3},{12,4},{37,5},{14,6},{39,7},{16,8},{41,... | collective-permute-start | bytes 1376264 | tf_op jit(solution)/shard_map/ppermute | solution.py:68
  124.0 1.1 multiply_convert_fusion.1
  125.3 2.7 %collective-permute-start.23 = (bf16[64,3584]{1,0:T(8,128)(2,1)S(1)}, bf16[64,3584]{1,0:T(8,128)(2,1)S(1)}, u32[]{:S(2)}, u32[]{:S(2)}) collective-permute-start(bf16[64,3584]{1,0:T(8,128)(2,1)S(1)} %get-tuple-element.27), channel_id=1, source_target_pairs={{8,0},{33,1},{10,2},{35,3},{12,4},{37,5},{14,6},{39,7},{16,8},{41,... | collective-permute-start | bytes 1376264 | tf_op jit(solution)/shard_map/ppermute | solution.py:68
  128.0 2.1 %collective-permute-done.34 = bf16[64,3584]{1,0:T(8,128)(2,1)S(1)} collective-permute-done((bf16[64,3584]{1,0:T(8,128)(2,1)S(1)}, bf16[64,3584]{1,0:T(8,128)(2,1)S(1)}, u32[]{:S(2)}, u32[]{:S(2)}) %collective-permute-start.34) | collective-permute-done | bytes 458784 | tf_op jit(solution)/shard_map/ppermute | solution.py:68
  130.5 2.7 %collective-permute-start.37 = (bf16[128,3584]{1,0:T(8,128)(2,1)S(1)}, bf16[128,3584]{1,0:T(8,128)(2,1)S(1)}, u32[]{:S(2)}, u32[]{:S(2)}) collective-permute-start(bf16[128,3584]{1,0:T(8,128)(2,1)S(1)} %pad_maximum_fusion.5), channel_id=1, source_target_pairs={{8,0},{33,1},{10,2},{35,3},{12,4},{37,5},{14,6},{39,7},{16,8},{41,... | collective-permute-start | bytes 2752520 | tf_op jit(solution)/shard_map/ppermute | solution.py:68
  133.3 1.7 collective-permute-done.21
  135.4 2.7 %collective-permute-start.24 = (bf16[128,3584]{1,0:T(8,128)(2,1)S(1)}, bf16[128,3584]{1,0:T(8,128)(2,1)S(1)}, u32[]{:S(2)}, u32[]{:S(2)}) collective-permute-start(bf16[128,3584]{1,0:T(8,128)(2,1)S(1)} %pad_maximum_fusion.3), channel_id=1, source_target_pairs={{8,0},{33,1},{10,2},{35,3},{12,4},{37,5},{14,6},{39,7},{16,8},{41,... | collective-permute-start | bytes 2752520 | tf_op jit(solution)/shard_map/ppermute | solution.py:68
  138.2 6.6 %collective-permute-done.35 = bf16[128,3584]{1,0:T(8,128)(2,1)S(1)} collective-permute-done((bf16[128,3584]{1,0:T(8,128)(2,1)S(1)}, bf16[128,3584]{1,0:T(8,128)(2,1)S(1)}, u32[]{:S(2)}, u32[]{:S(2)}) %collective-permute-start.35) | collective-permute-done | bytes 917536 | tf_op jit(solution)/shard_map/ppermute | solution.py:68
  145.3 1.8 collective-permute-start.39
  147.1 1.0 collective-permute-start.40
  148.1 11.2 %collective-permute-done.22 = bf16[128,3584]{1,0:T(8,128)(2,1)S(1)} collective-permute-done((bf16[128,3584]{1,0:T(8,128)(2,1)S(1)}, bf16[128,3584]{1,0:T(8,128)(2,1)S(1)}, u32[]{:S(2)}, u32[]{:S(2)}) %collective-permute-start.22) | collective-permute-done | bytes 917536 | tf_op jit(solution)/shard_map/ppermute | solution.py:68
  159.8 1.8 collective-permute-start.26
  161.6 1.0 collective-permute-start.27
  162.7 5.6 %collective-permute-done.25 = bf16[32,3584]{1,0:T(8,128)(2,1)S(1)} collective-permute-done((bf16[32,3584]{1,0:T(8,128)(2,1)S(1)}, bf16[32,3584]{1,0:T(8,128)(2,1)S(1)}, u32[]{:S(2)}, u32[]{:S(2)}) %collective-permute-start.25) | collective-permute-done | bytes 229408 | tf_op jit(solution)/shard_map/ppermute | solution.py:68
  169.3 2.6 %collective-permute-start.43 = (bf16[2,8,3584]{2,1,0:T(8,128)(2,1)S(1)}, bf16[2,8,3584]{2,1,0:T(8,128)(2,1)S(1)}, u32[]{:S(2)}, u32[]{:S(2)}) collective-permute-start(bf16[2,8,3584]{2,1,0:T(8,128)(2,1)S(1)} %get-tuple-element.54), channel_id=1, source_target_pairs={{2,0},{9,1},{4,2},{11,3},{6,4},{13,5},{0,6},{15,7},{10,8},{17,9},{... | collective-permute-start | bytes 344072 | tf_op jit(solution)/shard_map/ppermute | solution.py:68
  172.0 3.3 %collective-permute-done.41 = bf16[2,8,3584]{2,1,0:T(8,128)(2,1)S(1)} collective-permute-done((bf16[2,8,3584]{2,1,0:T(8,128)(2,1)S(1)}, bf16[2,8,3584]{2,1,0:T(8,128)(2,1)S(1)}, u32[]{:S(2)}, u32[]{:S(2)}) %collective-permute-start.41) | collective-permute-done | bytes 114720 | tf_op jit(solution)/shard_map/ppermute | solution.py:68
  176.1 1.2 collective-permute-done.44
  (187 shorter events, 24.5 us)
Async XLA Ops:
  0.6 23.5 %copy-start = (bf16[8,512,128]{2,1,0:T(8,128)(2,1)S(1)}, bf16[8,512,128]{2,1,0:T(8,128)(2,1)}, u32[]{:S(2)}) copy-start(bf16[8,512,128]{2,1,0:T(8,128)(2,1)} %param.18) | copy-start | bytes 3145732
  8.8 15.3 %all-to-all-start = ((bf16[8,64,512]{2,0,1:T(8,128)(2,1)}), bf16[8,64,512]{2,0,1:T(8,128)(2,1)S(1)}, u32[]{:S(2)}, u32[]{:S(2)}) async-start(bf16[8,64,512]{2,0,1:T(8,128)(2,1)} %copy.55), calls=%async_computation | async-start | bytes 1048576 | tf_op jit(solution)/shard_map/all_to_all | solution.py:150
  15.3 18.2 %collective-permute-start.5 = (bf16[8,3712]{1,0:T(8,128)(2,1)S(1)}, bf16[8,3712]{1,0:T(8,128)(2,1)S(1)}, u32[]{:S(2)}, u32[]{:S(2)}) collective-permute-start(bf16[8,3712]{1,0:T(8,128)(2,1)S(1)} %get-tuple-element.68), channel_id=1, source_target_pairs={{0,1},{1,0},{2,3},{3,2},{4,5},{5,4},{6,7},{7,6},{8,9},{9,8},{10,11... | collective-permute-start | bytes 178184 | tf_op jit(solution)/shard_map/ppermute | solution.py:72
  32.5 2.4 %collective-permute-start = (bf16[64,3584]{1,0:T(8,128)(2,1)S(1)}, bf16[64,3584]{1,0:T(8,128)(2,1)S(1)}, u32[]{:S(2)}, u32[]{:S(2)}) collective-permute-start(bf16[64,3584]{1,0:T(8,128)(2,1)S(1)} %dynamic-slice_convert_fusion), channel_id=1, source_target_pairs={{0,1},{1,0},{2,3},{3,2},{4,5},{5,4},{6,7},{7,6},{8,9},{9,8},{10,11... | collective-permute-start | bytes 1376264 | tf_op jit(solution)/shard_map/ppermute | solution.py:72
  35.0 6.2 %collective-permute-start.1 = (bf16[16,3584]{1,0:T(8,128)(2,1)S(1)}, bf16[16,3584]{1,0:T(8,128)(2,1)S(1)}, u32[]{:S(2)}, u32[]{:S(2)}) collective-permute-start(bf16[16,3584]{1,0:T(8,128)(2,1)S(1)} %get-tuple-element.50), channel_id=1, source_target_pairs={{6,0},{7,1},{0,2},{1,3},{2,4},{3,5},{4,6},{5,7},{14,8},{15,9},{8,1... | collective-permute-start | bytes 344072 | tf_op jit(solution)/shard_map/ppermute | solution.py:68
  35.4 7.1 %collective-permute-start.2 = (bf16[16,3584]{1,0:T(8,128)(2,1)S(1)}, bf16[16,3584]{1,0:T(8,128)(2,1)S(1)}, u32[]{:S(2)}, u32[]{:S(2)}) collective-permute-start(bf16[16,3584]{1,0:T(8,128)(2,1)S(1)} %get-tuple-element.52), channel_id=1, source_target_pairs={{4,0},{5,1},{6,2},{7,3},{0,4},{1,5},{2,6},{3,7},{12,8},{13,9},{14,... | collective-permute-start | bytes 344072 | tf_op jit(solution)/shard_map/ppermute | solution.py:68
  37.2 6.3 %collective-permute-start.3 = (bf16[16,3584]{1,0:T(8,128)(2,1)S(1)}, bf16[16,3584]{1,0:T(8,128)(2,1)S(1)}, u32[]{:S(2)}, u32[]{:S(2)}) collective-permute-start(bf16[16,3584]{1,0:T(8,128)(2,1)S(1)} %get-tuple-element.51), channel_id=1, source_target_pairs={{2,0},{3,1},{4,2},{5,3},{6,4},{7,5},{0,6},{1,7},{10,8},{11,9},{12,... | collective-permute-start | bytes 344072 | tf_op jit(solution)/shard_map/ppermute | solution.py:68
  38.0 21.2 %collective-permute-start.13 = (bf16[128,3584]{1,0:T(8,128)(2,1)S(1)}, bf16[128,3584]{1,0:T(8,128)(2,1)S(1)}, u32[]{:S(2)}, u32[]{:S(2)}) collective-permute-start(bf16[128,3584]{1,0:T(8,128)(2,1)S(1)} %get-tuple-element.43), channel_id=1, source_target_pairs={{0,1},{1,0},{2,3},{3,2},{4,5},{5,4},{6,7},{7,6},{8,9},{9,8},{10,11... | collective-permute-start | bytes 2752520 | tf_op jit(solution)/shard_map/ppermute | solution.py:72
  43.7 2.4 %collective-permute-start.6 = (f32[16,1]{0,1:T(1,128)S(1)}, f32[16,1]{0,1:T(1,128)S(1)}, u32[]{:S(2)}, u32[]{:S(2)}) collective-permute-start(f32[16,1]{0,1:T(1,128)S(1)} %bitcast.201), channel_id=1, source_target_pairs={{0,1},{1,0},{2,3},{3,2},{4,5},{5,4},{6,7},{7,6},{8,9},{9,8},{10,11... | collective-permute-start | bytes 200 | tf_op jit(solution)/shard_map/ppermute | solution.py:72
  46.2 6.9 %collective-permute-start.7 = (bf16[16,3712]{1,0:T(8,128)(2,1)S(1)}, bf16[16,3712]{1,0:T(8,128)(2,1)S(1)}, u32[]{:S(2)}, u32[]{:S(2)}) collective-permute-start(bf16[16,3712]{1,0:T(8,128)(2,1)S(1)} %get-tuple-element.58), channel_id=1, source_target_pairs={{2,0},{9,1},{4,2},{11,3},{6,4},{13,5},{0,6},{15,7},{10,8},{17,9},{... | collective-permute-start | bytes 356360 | tf_op jit(solution)/shard_map/ppermute | solution.py:68
  50.0 5.3 %collective-permute-start.8 = (bf16[16,3712]{1,0:T(8,128)(2,1)S(1)}, bf16[16,3712]{1,0:T(8,128)(2,1)S(1)}, u32[]{:S(2)}, u32[]{:S(2)}) collective-permute-start(bf16[16,3712]{1,0:T(8,128)(2,1)S(1)} %get-tuple-element.58), channel_id=1, source_target_pairs={{4,0},{17,1},{6,2},{19,3},{0,4},{21,5},{2,6},{23,7},{12,8},{25,9},... | collective-permute-start | bytes 356360 | tf_op jit(solution)/shard_map/ppermute | solution.py:68
  50.0 6.2 %collective-permute-start.9 = (bf16[16,3712]{1,0:T(8,128)(2,1)S(1)}, bf16[16,3712]{1,0:T(8,128)(2,1)S(1)}, u32[]{:S(2)}, u32[]{:S(2)}) collective-permute-start(bf16[16,3712]{1,0:T(8,128)(2,1)S(1)} %get-tuple-element.58), channel_id=1, source_target_pairs={{6,0},{25,1},{0,2},{27,3},{2,4},{29,5},{4,6},{31,7},{14,8},{1,9},{... | collective-permute-start | bytes 356360 | tf_op jit(solution)/shard_map/ppermute | solution.py:68
  50.8 27.4 %collective-permute-start.14 = (bf16[2,3584,128]{2,1,0:T(8,128)(2,1)S(1)}, bf16[2,3584,128]{2,1,0:T(8,128)(2,1)S(1)}, u32[]{:S(2)}, u32[]{:S(2)}) collective-permute-start(bf16[2,3584,128]{2,1,0:T(8,128)(2,1)S(1)} %dynamic-slice_bitcast_fusion), channel_id=1, source_target_pairs={{0,1},{1,0},{2,3},{3,2},{4,5},{5,4},{6,7},{7,6},{8,9},{9,8},{10,11... | collective-permute-start | bytes 5505032 | tf_op jit(solution)/shard_map/ppermute | solution.py:72
  56.3 12.9 %collective-permute-start.10 = (bf16[64,3712]{1,0:T(8,128)(2,1)S(1)}, bf16[64,3712]{1,0:T(8,128)(2,1)S(1)}, u32[]{:S(2)}, u32[]{:S(2)}) collective-permute-start(bf16[64,3712]{1,0:T(8,128)(2,1)S(1)} %bitcast.173), channel_id=1, source_target_pairs={{32,0},{3,1},{34,2},{5,3},{36,4},{7,5},{38,6},{1,7},{40,8},{11,9},... | collective-permute-start | bytes 1425416 | tf_op jit(solution)/shard_map/ppermute | solution.py:68
  58.5 10.7 %collective-permute-start.11 = (bf16[64,3712]{1,0:T(8,128)(2,1)S(1)}, bf16[64,3712]{1,0:T(8,128)(2,1)S(1)}, u32[]{:S(2)}, u32[]{:S(2)}) collective-permute-start(bf16[64,3712]{1,0:T(8,128)(2,1)S(1)} %bitcast.174), channel_id=1, source_target_pairs={{64,0},{5,1},{66,2},{7,3},{68,4},{1,5},{70,6},{3,7},{72,8},{13,9},... | collective-permute-start | bytes 1425416 | tf_op jit(solution)/shard_map/ppermute | solution.py:68
  58.5 14.1 %collective-permute-start.12 = (bf16[64,3712]{1,0:T(8,128)(2,1)S(1)}, bf16[64,3712]{1,0:T(8,128)(2,1)S(1)}, u32[]{:S(2)}, u32[]{:S(2)}) collective-permute-start(bf16[64,3712]{1,0:T(8,128)(2,1)S(1)} %bitcast.175), channel_id=1, source_target_pairs={{96,0},{7,1},{98,2},{1,3},{100,4},{3,5},{102,6},{5,7},{104,8},{15,... | collective-permute-start | bytes 1425416 | tf_op jit(solution)/shard_map/ppermute | solution.py:68
  73.1 13.2 %collective-permute-start.28 = (bf16[128,3712]{1,0:T(8,128)(2,1)S(1)}, bf16[128,3712]{1,0:T(8,128)(2,1)S(1)}, u32[]{:S(2)}, u32[]{:S(2)}) collective-permute-start(bf16[128,3712]{1,0:T(8,128)(2,1)S(1)} %bitcast.155), channel_id=1, source_target_pairs={{8,0},{33,1},{10,2},{35,3},{12,4},{37,5},{14,6},{39,7},{16,8},{41,... | collective-permute-start | bytes 2850824 | tf_op jit(solution)/shard_map/ppermute | solution.py:68
  75.6 14.2 %collective-permute-start.30 = (bf16[128,3712]{1,0:T(8,128)(2,1)S(1)}, bf16[128,3712]{1,0:T(8,128)(2,1)S(1)}, u32[]{:S(2)}, u32[]{:S(2)}) collective-permute-start(bf16[128,3712]{1,0:T(8,128)(2,1)S(1)} %bitcast.156), channel_id=1, source_target_pairs={{24,0},{97,1},{26,2},{99,3},{28,4},{101,5},{30,6},{103,7},{0,8},{1... | collective-permute-start | bytes 2850824 | tf_op jit(solution)/shard_map/ppermute | solution.py:68
  75.6 20.9 %collective-permute-start.15 = (bf16[128,3712]{1,0:T(8,128)(2,1)S(1)}, bf16[128,3712]{1,0:T(8,128)(2,1)S(1)}, u32[]{:S(2)}, u32[]{:S(2)}) collective-permute-start(bf16[128,3712]{1,0:T(8,128)(2,1)S(1)} %bitcast.159), channel_id=1, source_target_pairs={{8,0},{33,1},{10,2},{35,3},{12,4},{37,5},{14,6},{39,7},{16,8},{41,... | collective-permute-start | bytes 2850824 | tf_op jit(solution)/shard_map/ppermute | solution.py:68
  78.2 21.6 %collective-permute-start.17 = (bf16[128,3712]{1,0:T(8,128)(2,1)S(1)}, bf16[128,3712]{1,0:T(8,128)(2,1)S(1)}, u32[]{:S(2)}, u32[]{:S(2)}) collective-permute-start(bf16[128,3712]{1,0:T(8,128)(2,1)S(1)} %bitcast.160), channel_id=1, source_target_pairs={{24,0},{97,1},{26,2},{99,3},{28,4},{101,5},{30,6},{103,7},{0,8},{1... | collective-permute-start | bytes 2850824 | tf_op jit(solution)/shard_map/ppermute | solution.py:68
  86.3 16.0 %collective-permute-start.29 = (bf16[64,3712]{1,0:T(8,128)(2,1)S(1)}, bf16[64,3712]{1,0:T(8,128)(2,1)S(1)}, u32[]{:S(2)}, u32[]{:S(2)}) collective-permute-start(bf16[64,3712]{1,0:T(8,128)(2,1)S(1)} %slice.365), channel_id=1, source_target_pairs={{8,0},{33,1},{10,2},{35,3},{12,4},{37,5},{14,6},{39,7},{16,8},{41,... | collective-permute-start | bytes 1425416 | tf_op jit(solution)/shard_map/ppermute | solution.py:68
  89.8 15.1 %collective-permute-start.31 = (bf16[64,3712]{1,0:T(8,128)(2,1)S(1)}, bf16[64,3712]{1,0:T(8,128)(2,1)S(1)}, u32[]{:S(2)}, u32[]{:S(2)}) collective-permute-start(bf16[64,3712]{1,0:T(8,128)(2,1)S(1)} %slice.366), channel_id=1, source_target_pairs={{24,0},{97,1},{26,2},{99,3},{28,4},{101,5},{30,6},{103,7},{0,8},{1... | collective-permute-start | bytes 1425416 | tf_op jit(solution)/shard_map/ppermute | solution.py:68
  100.7 9.7 %collective-permute-start.16 = (bf16[64,3712]{1,0:T(8,128)(2,1)S(1)}, bf16[64,3712]{1,0:T(8,128)(2,1)S(1)}, u32[]{:S(2)}, u32[]{:S(2)}) collective-permute-start(bf16[64,3712]{1,0:T(8,128)(2,1)S(1)} %slice.338), channel_id=1, source_target_pairs={{8,0},{33,1},{10,2},{35,3},{12,4},{37,5},{14,6},{39,7},{16,8},{41,... | collective-permute-start | bytes 1425416 | tf_op jit(solution)/shard_map/ppermute | solution.py:68
  101.5 9.1 %collective-permute-start.18 = (bf16[64,3712]{1,0:T(8,128)(2,1)S(1)}, bf16[64,3712]{1,0:T(8,128)(2,1)S(1)}, u32[]{:S(2)}, u32[]{:S(2)}) collective-permute-start(bf16[64,3712]{1,0:T(8,128)(2,1)S(1)} %slice.339), channel_id=1, source_target_pairs={{24,0},{97,1},{26,2},{99,3},{28,4},{101,5},{30,6},{103,7},{0,8},{1... | collective-permute-start | bytes 1425416 | tf_op jit(solution)/shard_map/ppermute | solution.py:68
  105.7 11.4 %collective-permute-start.32 = (bf16[512,256]{1,0:T(8,128)(2,1)S(1)}, bf16[512,256]{1,0:T(8,128)(2,1)S(1)}, u32[]{:S(2)}, u32[]{:S(2)}) collective-permute-start(bf16[512,256]{1,0:T(8,128)(2,1)S(1)} %pad_maximum_fusion.8), channel_id=1, source_target_pairs={{0,1},{1,0},{2,3},{3,2},{4,5},{5,4},{6,7},{7,6},{8,9},{9,8},{10,11... | collective-permute-start | bytes 786440 | tf_op jit(solution)/shard_map/ppermute | solution.py:72
  111.4 6.7 %collective-permute-start.19 = (bf16[512,256]{1,0:T(8,128)(2,1)S(1)}, bf16[512,256]{1,0:T(8,128)(2,1)S(1)}, u32[]{:S(2)}, u32[]{:S(2)}) collective-permute-start(bf16[512,256]{1,0:T(8,128)(2,1)S(1)} %pad_maximum_fusion.7), channel_id=1, source_target_pairs={{0,1},{1,0},{2,3},{3,2},{4,5},{5,4},{6,7},{7,6},{8,9},{9,8},{10,11... | collective-permute-start | bytes 786440 | tf_op jit(solution)/shard_map/ppermute | solution.py:72
  118.4 1.4 collective-permute-start.33
  119.2 4.8 %collective-permute-start.20 = (bf16[512,128]{1,0:T(8,128)(2,1)S(1)}, bf16[512,128]{1,0:T(8,128)(2,1)S(1)}, u32[]{:S(2)}, u32[]{:S(2)}) collective-permute-start(bf16[512,128]{1,0:T(8,128)(2,1)S(1)} %fusion.21), channel_id=1, source_target_pairs={{0,1},{1,0},{2,3},{3,2},{4,5},{5,4},{6,7},{7,6},{8,9},{9,8},{10,11... | collective-permute-start | bytes 393224 | tf_op jit(solution)/shard_map/ppermute | solution.py:72
  121.2 8.9 %collective-permute-start.34 = (bf16[64,3584]{1,0:T(8,128)(2,1)S(1)}, bf16[64,3584]{1,0:T(8,128)(2,1)S(1)}, u32[]{:S(2)}, u32[]{:S(2)}) collective-permute-start(bf16[64,3584]{1,0:T(8,128)(2,1)S(1)} %get-tuple-element.32), channel_id=1, source_target_pairs={{24,0},{97,1},{26,2},{99,3},{28,4},{101,5},{30,6},{103,7},{0,8},{1... | collective-permute-start | bytes 1376264 | tf_op jit(solution)/shard_map/ppermute | solution.py:68
  121.3 8.8 %collective-permute-start.36 = (bf16[64,3584]{1,0:T(8,128)(2,1)S(1)}, bf16[64,3584]{1,0:T(8,128)(2,1)S(1)}, u32[]{:S(2)}, u32[]{:S(2)}) collective-permute-start(bf16[64,3584]{1,0:T(8,128)(2,1)S(1)} %get-tuple-element.33), channel_id=1, source_target_pairs={{8,0},{33,1},{10,2},{35,3},{12,4},{37,5},{14,6},{39,7},{16,8},{41,... | collective-permute-start | bytes 1376264 | tf_op jit(solution)/shard_map/ppermute | solution.py:68
  125.2 9.8 %collective-permute-start.21 = (bf16[64,3584]{1,0:T(8,128)(2,1)S(1)}, bf16[64,3584]{1,0:T(8,128)(2,1)S(1)}, u32[]{:S(2)}, u32[]{:S(2)}) collective-permute-start(bf16[64,3584]{1,0:T(8,128)(2,1)S(1)} %get-tuple-element.26), channel_id=1, source_target_pairs={{24,0},{97,1},{26,2},{99,3},{28,4},{101,5},{30,6},{103,7},{0,8},{1... | collective-permute-start | bytes 1376264 | tf_op jit(solution)/shard_map/ppermute | solution.py:68
  125.3 9.7 %collective-permute-start.23 = (bf16[64,3584]{1,0:T(8,128)(2,1)S(1)}, bf16[64,3584]{1,0:T(8,128)(2,1)S(1)}, u32[]{:S(2)}, u32[]{:S(2)}) collective-permute-start(bf16[64,3584]{1,0:T(8,128)(2,1)S(1)} %get-tuple-element.27), channel_id=1, source_target_pairs={{8,0},{33,1},{10,2},{35,3},{12,4},{37,5},{14,6},{39,7},{16,8},{41,... | collective-permute-start | bytes 1376264 | tf_op jit(solution)/shard_map/ppermute | solution.py:68
  130.4 14.5 %collective-permute-start.35 = (bf16[128,3584]{1,0:T(8,128)(2,1)S(1)}, bf16[128,3584]{1,0:T(8,128)(2,1)S(1)}, u32[]{:S(2)}, u32[]{:S(2)}) collective-permute-start(bf16[128,3584]{1,0:T(8,128)(2,1)S(1)} %pad_maximum_fusion.4), channel_id=1, source_target_pairs={{24,0},{97,1},{26,2},{99,3},{28,4},{101,5},{30,6},{103,7},{0,8},{1... | collective-permute-start | bytes 2752520 | tf_op jit(solution)/shard_map/ppermute | solution.py:68
  130.5 14.3 %collective-permute-start.37 = (bf16[128,3584]{1,0:T(8,128)(2,1)S(1)}, bf16[128,3584]{1,0:T(8,128)(2,1)S(1)}, u32[]{:S(2)}, u32[]{:S(2)}) collective-permute-start(bf16[128,3584]{1,0:T(8,128)(2,1)S(1)} %pad_maximum_fusion.5), channel_id=1, source_target_pairs={{8,0},{33,1},{10,2},{35,3},{12,4},{37,5},{14,6},{39,7},{16,8},{41,... | collective-permute-start | bytes 2752520 | tf_op jit(solution)/shard_map/ppermute | solution.py:68
  135.3 24.0 %collective-permute-start.22 = (bf16[128,3584]{1,0:T(8,128)(2,1)S(1)}, bf16[128,3584]{1,0:T(8,128)(2,1)S(1)}, u32[]{:S(2)}, u32[]{:S(2)}) collective-permute-start(bf16[128,3584]{1,0:T(8,128)(2,1)S(1)} %pad_maximum_fusion.2), channel_id=1, source_target_pairs={{24,0},{97,1},{26,2},{99,3},{28,4},{101,5},{30,6},{103,7},{0,8},{1... | collective-permute-start | bytes 2752520 | tf_op jit(solution)/shard_map/ppermute | solution.py:68
  135.4 23.9 %collective-permute-start.24 = (bf16[128,3584]{1,0:T(8,128)(2,1)S(1)}, bf16[128,3584]{1,0:T(8,128)(2,1)S(1)}, u32[]{:S(2)}, u32[]{:S(2)}) collective-permute-start(bf16[128,3584]{1,0:T(8,128)(2,1)S(1)} %pad_maximum_fusion.3), channel_id=1, source_target_pairs={{8,0},{33,1},{10,2},{35,3},{12,4},{37,5},{14,6},{39,7},{16,8},{41,... | collective-permute-start | bytes 2752520 | tf_op jit(solution)/shard_map/ppermute | solution.py:68
  145.2 16.3 %collective-permute-start.38 = (bf16[32,3584]{1,0:T(8,128)(2,1)S(1)}, bf16[32,3584]{1,0:T(8,128)(2,1)S(1)}, u32[]{:S(2)}, u32[]{:S(2)}) collective-permute-start(bf16[32,3584]{1,0:T(8,128)(2,1)S(1)} %get-tuple-element.47), channel_id=1, source_target_pairs={{96,0},{7,1},{98,2},{1,3},{100,4},{3,5},{102,6},{5,7},{104,8},{15,... | collective-permute-start | bytes 688136 | tf_op jit(solution)/shard_map/ppermute | solution.py:68
  145.3 17.3 %collective-permute-start.39 = (bf16[32,3584]{1,0:T(8,128)(2,1)S(1)}, bf16[32,3584]{1,0:T(8,128)(2,1)S(1)}, u32[]{:S(2)}, u32[]{:S(2)}) collective-permute-start(bf16[32,3584]{1,0:T(8,128)(2,1)S(1)} %get-tuple-element.49), channel_id=1, source_target_pairs={{64,0},{5,1},{66,2},{7,3},{68,4},{1,5},{70,6},{3,7},{72,8},{13,9},... | collective-permute-start | bytes 688136 | tf_op jit(solution)/shard_map/ppermute | solution.py:68
  147.1 15.5 %collective-permute-start.40 = (bf16[32,3584]{1,0:T(8,128)(2,1)S(1)}, bf16[32,3584]{1,0:T(8,128)(2,1)S(1)}, u32[]{:S(2)}, u32[]{:S(2)}) collective-permute-start(bf16[32,3584]{1,0:T(8,128)(2,1)S(1)} %get-tuple-element.48), channel_id=1, source_target_pairs={{32,0},{3,1},{34,2},{5,3},{36,4},{7,5},{38,6},{1,7},{40,8},{11,9},... | collective-permute-start | bytes 688136 | tf_op jit(solution)/shard_map/ppermute | solution.py:68
  159.3 18.7 %copy-start.1 = (bf16[8,512,128]{2,1,0:T(8,128)(2,1)S(1)}, bf16[8,512,128]{2,1,0:T(8,128)(2,1)}, u32[]{:S(2)}) copy-start(bf16[8,512,128]{2,1,0:T(8,128)(2,1)} %param.18) | copy-start | bytes 3145732
  159.7 8.6 %collective-permute-start.25 = (bf16[32,3584]{1,0:T(8,128)(2,1)S(1)}, bf16[32,3584]{1,0:T(8,128)(2,1)S(1)}, u32[]{:S(2)}, u32[]{:S(2)}) collective-permute-start(bf16[32,3584]{1,0:T(8,128)(2,1)S(1)} %get-tuple-element.44), channel_id=1, source_target_pairs={{96,0},{7,1},{98,2},{1,3},{100,4},{3,5},{102,6},{5,7},{104,8},{15,... | collective-permute-start | bytes 688136 | tf_op jit(solution)/shard_map/ppermute | solution.py:68
  159.8 8.5 %collective-permute-start.26 = (bf16[32,3584]{1,0:T(8,128)(2,1)S(1)}, bf16[32,3584]{1,0:T(8,128)(2,1)S(1)}, u32[]{:S(2)}, u32[]{:S(2)}) collective-permute-start(bf16[32,3584]{1,0:T(8,128)(2,1)S(1)} %get-tuple-element.46), channel_id=1, source_target_pairs={{64,0},{5,1},{66,2},{7,3},{68,4},{1,5},{70,6},{3,7},{72,8},{13,9},... | collective-permute-start | bytes 688136 | tf_op jit(solution)/shard_map/ppermute | solution.py:68
  161.6 7.4 %collective-permute-start.27 = (bf16[32,3584]{1,0:T(8,128)(2,1)S(1)}, bf16[32,3584]{1,0:T(8,128)(2,1)S(1)}, u32[]{:S(2)}, u32[]{:S(2)}) collective-permute-start(bf16[32,3584]{1,0:T(8,128)(2,1)S(1)} %get-tuple-element.45), channel_id=1, source_target_pairs={{32,0},{3,1},{34,2},{5,3},{36,4},{7,5},{38,6},{1,7},{40,8},{11,9},... | collective-permute-start | bytes 688136 | tf_op jit(solution)/shard_map/ppermute | solution.py:68
  169.1 6.2 %collective-permute-start.41 = (bf16[2,8,3584]{2,1,0:T(8,128)(2,1)S(1)}, bf16[2,8,3584]{2,1,0:T(8,128)(2,1)S(1)}, u32[]{:S(2)}, u32[]{:S(2)}) collective-permute-start(bf16[2,8,3584]{2,1,0:T(8,128)(2,1)S(1)} %get-tuple-element.53), channel_id=1, source_target_pairs={{6,0},{25,1},{0,2},{27,3},{2,4},{29,5},{4,6},{31,7},{14,8},{1,9},{... | collective-permute-start | bytes 344072 | tf_op jit(solution)/shard_map/ppermute | solution.py:68
  169.2 6.1 %collective-permute-start.42 = (bf16[2,8,3584]{2,1,0:T(8,128)(2,1)S(1)}, bf16[2,8,3584]{2,1,0:T(8,128)(2,1)S(1)}, u32[]{:S(2)}, u32[]{:S(2)}) collective-permute-start(bf16[2,8,3584]{2,1,0:T(8,128)(2,1)S(1)} %get-tuple-element.55), channel_id=1, source_target_pairs={{4,0},{17,1},{6,2},{19,3},{0,4},{21,5},{2,6},{23,7},{12,8},{25,9},... | collective-permute-start | bytes 344072 | tf_op jit(solution)/shard_map/ppermute | solution.py:68
  169.3 6.6 %collective-permute-start.43 = (bf16[2,8,3584]{2,1,0:T(8,128)(2,1)S(1)}, bf16[2,8,3584]{2,1,0:T(8,128)(2,1)S(1)}, u32[]{:S(2)}, u32[]{:S(2)}) collective-permute-start(bf16[2,8,3584]{2,1,0:T(8,128)(2,1)S(1)} %get-tuple-element.54), channel_id=1, source_target_pairs={{2,0},{9,1},{4,2},{11,3},{6,4},{13,5},{0,6},{15,7},{10,8},{17,9},{... | collective-permute-start | bytes 344072 | tf_op jit(solution)/shard_map/ppermute | solution.py:68
  171.9 4.2 %collective-permute-start.4 = (bf16[8,3584]{1,0:T(8,128)(2,1)S(1)}, bf16[8,3584]{1,0:T(8,128)(2,1)S(1)}, u32[]{:S(2)}, u32[]{:S(2)}) collective-permute-start(bf16[8,3584]{1,0:T(8,128)(2,1)S(1)} %get-tuple-element.59), channel_id=1, source_target_pairs={{0,1},{1,0},{2,3},{3,2},{4,5},{5,4},{6,7},{7,6},{8,9},{9,8},{10,11... | collective-permute-start | bytes 172040 | tf_op jit(solution)/shard_map/ppermute | solution.py:72
  176.0 1.3 collective-permute-start.44
  (20 other events, 155.6 us)
